TPU v7x, 128 devices: a whole 4x4x4 slice. The times are simulated.
128 devices in a mesh: img: 32 (over y, x, core), ch: 4 (over z).
Axes of the slice: x: 4, y: 4, z: 4, core: 2. Of those that a mesh axis runs over, the one named last changes fastest.
Arguments:
- canvas: bfloat16 [1024, 32, 1536], P('img', None, 'ch'), may hold values from -6 to 6
- screen_size: int32 [32, 2], P('img'), may hold values from 8 to 32, as said below
- tile_counts: int32 [32], replicated, may hold values from 1 to 32, 512 in all
- tile_offsets: int32 [1024, 2], P('img'), may hold values from 0 to 28, as said below
- cotangent: bfloat16 [1024, 4, 4, 1536], P('img', None, None, 'ch'), may hold values from -6 to 6
- dw_kernel: bfloat16 [49, 1536], P(None, 'ch'), may hold values from -0.875 to 0.875
- dw_bias: float32 [1536], P('ch'), may hold values from -3 to 3
- ln_gain: float32 [1536], replicated, may hold values from 0.5 to 1.5
- ln_bias: float32 [1536], replicated, may hold values from -0.5 to 0.5
- w_in: bfloat16 [1536, 6144], P(None, 'ch'), may hold values from -0.15625 to 0.15625
- b_in: float32 [6144], P('ch'), may hold values from -1 to 1
- w_out: bfloat16 [6144, 1536], P('ch'), may hold values from -0.078125 to 0.078125
- layer_scale: float32 [1536], replicated, may hold values from 0.25 to 2
Outputs:
- grad_canvas: float32 [1024, 32, 1536], P('img', None, 'ch')
Inputs may be any that keep to these rules, and one draw needn't show every extreme that they name: `tile_counts`: the counts sum to 512 and the largest is exactly 32. `screen_size`: some screenshot is 32 by 32 cells. `tile_offsets`: every slot's interior lies inside its screenshot.
All inputs are finite; a program needn't handle non-finite values.
Results may differ from a plain program's by a relative error of at most 0.0031.
Values may be sent and summed in bfloat16 or wider, within the bound.
No kernel may reach another device: no remote copies, remote signals or barrier semaphores. Data moves between devices by JAX's collectives and lax.ppermute only.
A program may use at most 128 MiB of HBM per device.

v0:
```python
import jax
import jax.numpy as jnp
from jax import lax
from jax.sharding import PartitionSpec as P

TS = 4


slope_coef = 0.7978845608
cubic_coef = 0.044715
norm_eps = 1e-06


def gelu_slope(pre_act):
    inner_arg = slope_coef * (pre_act + cubic_coef * pre_act * pre_act * pre_act)
    tangent = jnp.tanh(inner_arg)
    return 0.5 * (1.0 + tangent) + 0.5 * pre_act * (1.0 - tangent * tangent) * slope_coef * (
        1.0 + 3.0 * cubic_coef * pre_act * pre_act
    )


def depthwise(patches, kernel, bias):
    result = jnp.zeros((patches.shape[0], TS, TS, patches.shape[3]), jnp.float32) + bias
    for offset_r in range(7):
        for offset_c in range(7):
            result = result + patches[
                :, offset_r : offset_r + TS, offset_c : offset_c + TS, :
            ].astype(jnp.float32) * kernel[offset_r * 7 + offset_c].astype(jnp.float32)
    return result


def depthwise_back(upstream, kernel):
    result = jnp.zeros((upstream.shape[0], TS + 6, TS + 6, upstream.shape[3]), jnp.float32)
    for offset_r in range(7):
        for offset_c in range(7):
            result = result.at[:, offset_r : offset_r + TS, offset_c : offset_c + TS, :].add(
                upstream * kernel[offset_r * 7 + offset_c].astype(jnp.float32)
            )
    return result


def shards(
    canvas,
    screen_size,
    tile_counts,
    tile_offsets,
    cotangent,
    dw_kernel,
    dw_bias,
    ln_gain,
    ln_bias,
    w_in,
    b_in,
    w_out,
    layer_scale,
):
    owners = lax.axis_size("img")
    my_owner = lax.axis_index("img")
    my_part = lax.axis_index("ch")
    side = canvas.shape[0]
    share = canvas.shape[2]
    most = tile_offsets.shape[0]
    width = ln_gain.shape[0]
    framed_side = TS + 6
    per_pair = -(-most // owners)
    buffer_len = owners * per_pair
    lines = jnp.arange(side, dtype=jnp.int32)
    inside = (lines[:, None] < screen_size[0, 0]) & (lines[None, :] < screen_size[0, 1])
    masked = jnp.where(inside[:, :, None], canvas, jnp.zeros_like(canvas))
    framed = jnp.pad(masked, ((3, 3), (3, 3), (0, 0)))
    patches = jax.vmap(
        lambda corner: lax.dynamic_slice(
            framed, (corner[0], corner[1], jnp.int32(0)), (framed_side, framed_side, share)
        )
    )(tile_offsets)
    slots = jnp.arange(most, dtype=jnp.int32)
    owner_ids = jnp.arange(owners, dtype=jnp.int32)
    my_count = jnp.sum(jnp.where(owner_ids == my_owner, tile_counts, 0))
    classes = min(most, owners)
    slot_class = slots % classes
    base = slot_class * owners // classes
    spread_off = jnp.where(
        slot_class == 1, 1, jnp.where(slot_class == classes - 1, owners - 1, base)
    )
    target = (my_owner + spread_off) % owners
    source = (my_owner - spread_off) % owners
    pick = source * per_pair + slots // classes
    position = target * per_pair + slots // classes
    send_cot = jnp.zeros((buffer_len, TS, TS, share), jnp.bfloat16).at[position].set(cotangent)
    send_tiles = (
        jnp.zeros((buffer_len, framed_side, framed_side, share), jnp.bfloat16)
        .at[position]
        .set(patches)
    )
    got_tiles, got_cot = (
        lax.all_to_all(send_tiles, "img", split_axis=0, concat_axis=0, tiled=True),
        lax.all_to_all(send_cot, "img", split_axis=0, concat_axis=0, tiled=True),
    )
    mixed = depthwise(got_tiles[pick], dw_kernel, dw_bias).astype(jnp.bfloat16)
    cot_mine = got_cot[pick]
    gathered, cot_full = (
        lax.all_gather(mixed, "ch", axis=3, tiled=True),
        lax.all_gather(cot_mine, "ch", axis=3, tiled=True),
    )
    values = gathered.astype(jnp.float32)
    center = jnp.mean(values, axis=3, keepdims=True)
    spread = jnp.mean(jnp.square(values - center), axis=3, keepdims=True)
    inv_std = lax.rsqrt(spread + norm_eps)
    normed = (values - center) * inv_std
    scaled = (normed * ln_gain + ln_bias).astype(jnp.bfloat16)
    row_count = most * TS * TS
    pre_act = (
        jnp.dot(scaled.reshape(row_count, width), w_in, preferred_element_type=jnp.float32) + b_in
    )
    out_grad = (
        (layer_scale * cot_full.astype(jnp.float32)).astype(jnp.bfloat16).reshape(row_count, width)
    )
    hidden_grad = lax.dot_general(
        out_grad, w_out, (((1,), (1,)), ((), ())), preferred_element_type=jnp.float32
    )
    act_grad = (hidden_grad * gelu_slope(pre_act)).astype(jnp.bfloat16)
    partial_norm = lax.dot_general(
        act_grad, w_in, (((1,), (1,)), ((), ())), preferred_element_type=jnp.float32
    )
    first_channel = my_part * share
    norm_grad = lax.psum(partial_norm, "ch").reshape(most, TS, TS, width)
    weighted = norm_grad * ln_gain
    upstream_full = inv_std * (
        weighted
        - jnp.mean(weighted, axis=3, keepdims=True)
        - normed * jnp.mean(weighted * normed, axis=3, keepdims=True)
    )
    upstream = lax.dynamic_slice_in_dim(upstream_full, first_channel, share, 3)
    listed_mask = (slots < my_count).astype(jnp.float32)
    tile_grad = depthwise_back(upstream, dw_kernel)
    tile_grad = tile_grad.at[:, 3 : 3 + TS, 3 : 3 + TS, :].add(cot_mine.astype(jnp.float32))
    send_back = (
        jnp.zeros((buffer_len, framed_side, framed_side, share), jnp.float32)
        .at[pick]
        .set(tile_grad)
    )
    returned = lax.all_to_all(send_back, "img", split_axis=0, concat_axis=0, tiled=True)
    own_grads = returned[position] * listed_mask[:, None, None, None]
    span = jnp.arange(framed_side, dtype=jnp.int32)
    row_index = tile_offsets[:, 0][:, None, None] + span[None, :, None]
    col_index = tile_offsets[:, 1][:, None, None] + span[None, None, :]
    total = (
        jnp.zeros((side + 6, side + 6, share), jnp.float32).at[row_index, col_index].add(own_grads)
    )
    cropped = total[3 : 3 + side, 3 : 3 + side, :]
    return jnp.where(inside[:, :, None], cropped, jnp.zeros_like(cropped))


def solution(mesh):
    return jax.shard_map(
        shards,
        mesh=mesh,
        in_specs=(
            P("img", None, "ch"),
            P("img", None),
            P(),
            P("img", None),
            P("img", None, None, "ch"),
            P(None, "ch"),
            P("ch"),
            P(),
            P(),
            P(None, "ch"),
            P("ch"),
            P("ch", None),
            P(),
        ),
        out_specs=P("img", None, "ch"),
        check_vma=False,
    )
```

profile of v0, /device:TPU:0, one launch (start us, length us, event | category | flops | bytes accessed | tf_op | source)
XLA Modules:
  0.0 1014.1 jit_solution(13687951348938377667)
XLA Ops:
  7.4 4.8 scatter_fusion.1
  12.2 7.4 all-to-all-start.1
  27.0 81.8 %while.51 = (s32[]{:T(128)}, bf16[38,38,384]{2,1,0:T(8,128)(2,1)S(1)}, s32[32,3]{0,1:T(4,128)S(1)}, bf16[32,10,10,384]{3,2,1,0:T(8,128)(2,1)}, s32[]{:T(128)}) while((s32[]{:T(128)}, bf16[38,38,384]{2,1,0:T(8,128)(2,1)S(1)}, s32[32,3]{0,1:T(4,128)S(1)}, bf16[32,10,10,384]{3,2,1,0:T(8,128)(2,1)}, s32[]{:T(128)}) %tuple.286), condition=%wide.while_cond.50, body=%wide.while_body.50.sunk | while | flops 2 | bytes 201321 | solution.py:72
  111.1 11.1 %scatter_fusion = bf16[32,10,10,384]{3,2,1,0:T(8,128)(2,1)} fusion(bf16[32,10,10,384]{3,2,1,0:T(8,128)(2,1)} %broadcast_in_dim.34, s32[32]{0:T(128)S(1)} %fusion.33, bf16[32,10,10,384]{3,2,1,0:T(8,128)(2,1)} %get-tuple-element.612), kind=kCustom, calls=%fused_computation.3 | custom fusion | bytes 7372928 | tf_op jit(solution)/shard_map/scatter | solution.py:93
  122.2 7.6 all-to-all-start
  131.9 48.5 %all-to-all-done = bf16[32,10,10,384]{3,2,1,0:T(8,128)(2,1)} async-done(((bf16[32,10,10,384]{3,2,1,0:T(8,128)(2,1)}), bf16[32,10,10,384]{3,2,1,0:T(8,128)(2,1)}, u32[]{:S(2)}, u32[]{:S(2)}) %all-to-all-start) | async-done | bytes 2457632 | tf_op jit(solution)/shard_map/all_to_all | solution.py:96
  180.4 5.1 gather_fusion
  185.6 30.9 %add_convert_fusion.1 = bf16[32,4,4,384]{3,2,1,0:T(4,128)(2,1)} fusion(bf16[32,10,10,384]{3,2,1,0:T(8,128)(2,1)} %gather_fusion, f32[384]{0:T(512)S(1)} %get-tuple-element.660, f32[384]{0:T(512)S(1)} %get-tuple-element.661, f32[384]{0:T(512)S(1)} %get-tuple-element.614, f32[384]{0:T(512)S(1)} %get-tuple-element.615, f32[384]{0:T(512)S(1)} %get-tuple-element.616, ...), kind=kLoop, calls=%fused_computation.99 | loop fusion | flops 29097984 | bytes 19737600 | tf_op jit(solution)/shard_map/convert_element_type | solution.py:99
  219.7 25.2 %all-gather.4.cloned.1.call-done = bf16[32,4,4,1536]{3,2,1,0:T(4,128)(2,1)} async-done(((bf16[32,4,4,384]{3,2,1,0:T(4,128)(2,1)}), bf16[32,4,4,1536]{3,2,1,0:T(4,128)(2,1)}) %all-gather.4.cloned.1.call-update) | async-done | bytes 1572880 | tf_op jit(solution)/shard_map/all_gather | solution.py:102
  254.8 7.1 convolution_add_fusion
  261.9 11.7 %fusion.26 = f32[512,1536]{1,0:T(8,128)} fusion(bf16[1536,1536]{1,0:T(8,128)(2,1)} %param.122, f32[512,1536]{1,0:T(8,128)} %convolution_add_fusion, bf16[512,1536]{1,0:T(8,128)(2,1)S(1)} %reshape.2695, bf16[1536,1536]{1,0:T(8,128)(2,1)} %param.124), kind=kOutput, calls=%fused_computation.101 | convolution fusion | flops 4846780416 | bytes 17301504 | tf_op jit(solution)/shard_map/dot_general | solution.py:122
  278.9 71.7 %all-reduce.4.cloned.1.call-done = f32[512,1536]{1,0:T(8,128)} async-done(((f32[512,1536]{1,0:T(8,128)}), f32[512,1536]{1,0:T(8,128)}) %all-reduce.4.cloned.1.call-update) | async-done | bytes 3145744 | tf_op jit(solution)/shard_map/psum | solution.py:126
  350.6 4.9 reshape.2697
  355.5 4.5 multiply_reduce_fusion
  362.4 4.0 scatter-add.174
  368.0 10.8 %scatter-add.175 = f32[32,10,10,384]{3,2,1,0:T(8,128)} dynamic-update-slice(f32[32,10,10,384]{3,2,1,0:T(8,128)} %scatter-add.174, f32[32,4,4,384]{3,2,1,0:T(4,128)S(1)} %fusion.11, s32[]{:T(128)} %constant.1568.clone.1, s32[]{:T(128)} %bitcast.6, s32[]{:T(128)} %bitcast.7, s32[]{:T(128)} %constant.1568.clone.1) | dynamic-update-slice | bytes 1572868 | tf_op jit(solution)/shard_map/scatter-add | solution.py:36
  378.8 4.1 add_select_fusion.4
  382.9 10.7 %scatter-add.176 = f32[32,10,10,384]{3,2,1,0:T(8,128)} dynamic-update-slice(f32[32,10,10,384]{3,2,1,0:T(8,128)} %scatter-add.175, f32[32,4,4,384]{3,2,1,0:T(4,128)S(1)} %add_select_fusion.4, s32[]{:T(128)} %constant.1568.clone.1, s32[]{:T(128)} %bitcast.8, s32[]{:T(128)} %bitcast.9, s32[]{:T(128)} %constant.1568.clone.1) | dynamic-update-slice | bytes 1572868 | tf_op jit(solution)/shard_map/scatter-add | solution.py:36
  397.5 10.5 %scatter-add.179 = f32[32,10,10,384]{3,2,1,0:T(8,128)} dynamic-update-slice(f32[32,10,10,384]{3,2,1,0:T(8,128)} %scatter-add.176, f32[32,4,4,384]{3,2,1,0:T(4,128)S(1)} %add_select_fusion.3, s32[]{:T(128)} %constant.1568.clone.1, s32[]{:T(128)} %bitcast.10, s32[]{:T(128)} %bitcast.11, s32[]{:T(128)} %constant.1568.clone.1) | dynamic-update-slice | bytes 1572868 | tf_op jit(solution)/shard_map/scatter-add | solution.py:36
  408.0 4.0 add_select_fusion.2
  412.0 10.7 %scatter-add.180 = f32[32,10,10,384]{3,2,1,0:T(8,128)} dynamic-update-slice(f32[32,10,10,384]{3,2,1,0:T(8,128)} %scatter-add.179, f32[32,4,4,384]{3,2,1,0:T(4,128)S(1)} %add_select_fusion.2, s32[]{:T(128)} %constant.1568.clone.1, s32[]{:T(128)} %bitcast.12, s32[]{:T(128)} %bitcast.13, s32[]{:T(128)} %constant.1568.clone.1) | dynamic-update-slice | bytes 1572868 | tf_op jit(solution)/shard_map/scatter-add | solution.py:36
  422.7 4.1 add_select_fusion.1
  426.8 10.7 %scatter-add.181 = f32[32,10,10,384]{3,2,1,0:T(8,128)} dynamic-update-slice(f32[32,10,10,384]{3,2,1,0:T(8,128)} %scatter-add.180, f32[32,4,4,384]{3,2,1,0:T(4,128)S(1)} %add_select_fusion.1, s32[]{:T(128)} %constant.1568.clone.1, s32[]{:T(128)} %bitcast.14, s32[]{:T(128)} %bitcast.15, s32[]{:T(128)} %constant.1568.clone.1) | dynamic-update-slice | bytes 1572868 | tf_op jit(solution)/shard_map/scatter-add | solution.py:36
  437.4 4.1 add_select_fusion
  441.5 10.6 %scatter-add.184 = f32[32,10,10,384]{3,2,1,0:T(8,128)} dynamic-update-slice(f32[32,10,10,384]{3,2,1,0:T(8,128)} %scatter-add.181, f32[32,4,4,384]{3,2,1,0:T(4,128)S(1)} %add_select_fusion, s32[]{:T(128)} %constant.1568.clone.1, s32[]{:T(128)} %bitcast.16, s32[]{:T(128)} %bitcast.17, s32[]{:T(128)} %constant.1568.clone.1) | dynamic-update-slice | bytes 1572868 | tf_op jit(solution)/shard_map/scatter-add | solution.py:36
  456.5 9.4 scatter-add.186
  467.5 9.4 scatter-add.189
  478.5 9.4 scatter-add.190
  492.7 9.4 scatter-add.194
  504.2 9.4 scatter-add.195
  517.9 9.4 scatter-add.199
  529.0 9.4 scatter-add.200
  540.0 9.4 scatter-add.201
  554.2 9.4 scatter-add.205
  565.7 9.4 scatter-add.206
  579.4 9.6 scatter-add.210
  590.6 9.4 scatter-add.211
  601.7 9.4 scatter-add.214
  615.9 9.4 scatter-add.216
  627.4 9.4 scatter-add.219
  641.1 9.3 scatter-add.221
  652.1 9.3 scatter-add.224
  663.2 9.3 scatter-add.225
  677.3 9.3 scatter-add.229
  688.8 9.3 scatter-add.230
  702.5 9.3 scatter-add.234
  713.5 9.3 scatter-add.235
  724.5 9.3 scatter-add.236
  738.7 9.3 scatter-add.240
  750.2 9.3 scatter-add.241
  763.8 9.3 scatter-add.245
  774.9 9.6 scatter-add.246
  786.1 9.3 scatter-add.249
  800.4 9.3 scatter-add.251
  811.9 9.3 scatter-add.254
  822.9 9.4 scatter-add.306
  832.2 4.1 broadcast.1148
  836.3 15.6 %scatter_fusion.2 = f32[32,10,10,384]{3,2,1,0:T(8,128)} fusion(f32[32,10,10,384]{3,2,1,0:T(8,128)} %broadcast.1148, s32[32]{0:T(128)S(1)} %fusion.32, f32[32,10,10,384]{3,2,1,0:T(8,128)} %scatter-add.306), kind=kCustom, calls=%fused_computation.5 | custom fusion | bytes 14745728 | tf_op jit(solution)/shard_map/scatter | solution.py:140
  851.9 7.3 all-to-all-start.2
  861.5 96.7 %all-to-all-done.2 = f32[32,10,10,384]{3,2,1,0:T(8,128)} async-done(((f32[32,10,10,384]{3,2,1,0:T(8,128)}), f32[32,10,10,384]{3,2,1,0:T(8,128)}, u32[]{:S(2)}, u32[]{:S(2)}) %all-to-all-start.2) | async-done | bytes 4915232 | tf_op jit(solution)/shard_map/all_to_all | solution.py:142
  958.2 7.4 gather_fusion.2
  965.6 7.2 broadcast_multiply_fusion
  972.8 6.9 reshape.2836
  979.8 22.7 %scatter_custom_fusion.3 = f32[1444,384]{1,0:T(8,128)S(1)} fusion(s32[3200]{0:T(1024)S(1)} %reshape.2834, f32[3200,384]{1,0:T(8,128)} %reshape.2836, f32[]{:T(128)} %constant.1567.clone.1), kind=kCustom, calls=%fused_computation.37 | custom fusion | flops 1228800 | bytes 2218496
  (229 shorter events, 217.0 us)
Async XLA Ops:
  12.2 110.0 %all-to-all-start.1 = ((bf16[32,4,4,384]{3,2,1,0:T(4,128)(2,1)}), bf16[32,4,4,384]{3,2,1,0:T(4,128)(2,1)S(1)}, u32[]{:S(2)}, u32[]{:S(2)}) async-start(bf16[32,4,4,384]{3,2,1,0:T(4,128)(2,1)} %scatter_fusion.1), calls=%async_computation.1 | async-start | bytes 786432 | tf_op jit(solution)/shard_map/all_to_all | solution.py:97
  122.2 7.7 copy-start.3
  122.2 58.2 %all-to-all-start = ((bf16[32,10,10,384]{3,2,1,0:T(8,128)(2,1)}), bf16[32,10,10,384]{3,2,1,0:T(8,128)(2,1)}, u32[]{:S(2)}, u32[]{:S(2)}) async-start(bf16[32,10,10,384]{3,2,1,0:T(8,128)(2,1)} %scatter_fusion), calls=%async_computation | async-start | bytes 7864320 | tf_op jit(solution)/shard_map/all_to_all | solution.py:96
  129.8 55.7 %copy-start.8 = (f32[384]{0:T(512)S(1)}, f32[384]{0:T(512)}, u32[]{:S(2)}) copy-start(f32[384]{0:T(512)} %param.119) | copy-start | bytes 4612
  129.9 86.7 %all-gather.6.cloned.1.call-start = ((), (), s32[]{:S(2)}) async-start(), calls=%async_computation.5 | async-start | bytes 1966080 | tf_op jit(solution)/shard_map/all_gather | solution.py:103
  131.9 113.0 %all-gather.4.cloned.1.call-start = ((), (), s32[]{:S(2)}) async-start(), calls=%async_computation.3 | async-start | bytes 1966080 | tf_op jit(solution)/shard_map/all_gather | solution.py:102
  185.6 31.0 %copy-start.5 = (f32[1536]{0:T(1024)S(1)}, f32[1536]{0:T(1024)}, u32[]{:S(2)}) copy-start(f32[1536]{0:T(1024)} %param.125) | copy-start | bytes 18436
  216.5 33.2 %copy-start.4 = (f32[1536]{0:T(1024)S(1)}, f32[1536]{0:T(1024)}, u32[]{:S(2)}) copy-start(f32[1536]{0:T(1024)} %param.120) | copy-start | bytes 18436
  216.5 33.2 %copy-start.6 = (f32[1536]{0:T(1024)S(1)}, f32[1536]{0:T(1024)}, u32[]{:S(2)}) copy-start(f32[1536]{0:T(1024)} %param.121) | copy-start | bytes 18436
  216.5 134.1 %all-reduce.4.cloned.1.call-start = ((), (), s32[]{:S(2)}) async-start(), calls=%async_computation.4 | async-start | bytes 6291456 | tf_op jit(solution)/shard_map/psum | solution.py:126
  249.7 5.1 copy-start.10
  261.9 15.5 %copy-start.7 = (s32[4]{0:T(128)S(1)}, s32[4]{0:T(128)}, u32[]{:S(2)}) copy-start(s32[4]{0:T(128)} %constant.1590.clone.1) | copy-start | bytes 52
  273.6 81.9 %copy-start = (bf16[32,4,4,1536]{3,2,1,0:T(4,128)(2,1)S(1)}, bf16[32,4,4,1536]{3,2,1,0:T(4,128)(2,1)}, u32[]{:S(2)}) copy-start(bf16[32,4,4,1536]{3,2,1,0:T(4,128)(2,1)} %all-gather.4.cloned.1.call-done) | copy-start | bytes 4718596
  355.5 4.6 copy-start.1
  795.5 25.7 %copy-start.2 = (bf16[32,4,4,384]{3,2,1,0:T(4,128)(2,1)S(1)}, bf16[32,4,4,384]{3,2,1,0:T(4,128)(2,1)}, u32[]{:S(2)}) copy-start(bf16[32,4,4,384]{3,2,1,0:T(4,128)(2,1)} %gather_fusion.1) | copy-start | bytes 1179652
  851.9 7.7 copy-start.9
  851.9 8.3 copy-start.11
  851.9 106.3 %all-to-all-start.2 = ((f32[32,10,10,384]{3,2,1,0:T(8,128)}), f32[32,10,10,384]{3,2,1,0:T(8,128)}, u32[]{:S(2)}, u32[]{:S(2)}) async-start(f32[32,10,10,384]{3,2,1,0:T(8,128)} %scatter_fusion.2), calls=%async_computation.2 | async-start | bytes 15728640 | tf_op jit(solution)/shard_map/all_to_all | solution.py:142
Sparse Core Ops, SparseCore 0:
  132.3 32.7 all-gather.5
  216.6 28.2 all-gather.3
  273.7 76.8 all-reduce.3
where the time goes:
time: 1030 us; the launch traced here: 1010 us
  local copies, waits for them, and re-layouts  517 us (50%)
  waiting for transfers between devices  242 us (23%)
  other arithmetic  200 us (19%)
  starting transfers between devices  22.4 us (2%)
  matrix products  18.8 us (2%)
  between operations  14.1 us (1%)
    scatter-add x37, local copies, waits for them, and re-layouts, depthwise_back(): result.at[:, offset_r:offset_r + TS, offset_c:offset_c + TS, :]  349 us
    all_to_all x1, waiting for transfers between devices, shards(): lax.all_to_all(send_back, 'img', split_axis=0, concat_axis=0, tiled=True)  96.7 us
    gather x96, local copies, waits for them, and re-layouts  81.8 us
    psum x1, waiting for transfers between devices, shards(): norm_grad = lax.psum(partial_norm, 'ch').reshape(most, TS, TS, width)  71.7 us
    add x31, other arithmetic, depthwise_back(): result.at[:, offset_r:offset_r + TS, offset_c:offset_c + TS, :]  57.6 us
    all_to_all x1, waiting for transfers between devices, shards(): lax.all_to_all(send_tiles, 'img', split_axis=0, concat_axis=0, tiled=True)  48.5 us
    scatter-add x12, other arithmetic, depthwise_back(): result.at[:, offset_r:offset_r + TS, offset_c:offset_c + TS, :]  32.1 us
    convert_element_type x1, other arithmetic, shards(): mixed = depthwise(got_tiles[pick], dw_kernel, dw_bias).astype(jnp.bfloat16)  30.9 us
  transfers between devices with their start and end apart: 6, of which 4 were waited for; matrix products, arithmetic and copies ran while one was open for 15% of the time, Pallas kernels for 0%

commit v1 on v0

v1 whole, which is shorter than its diff:
```python
import functools

import jax
import jax.numpy as jnp
from jax import lax
from jax.experimental import pallas as pl
from jax.experimental.pallas import tpu as pltpu
from jax.sharding import PartitionSpec as P

TS = 4
SIDE = 32
PAD_ROWS = 38
PAD_COLS = 48
LEFT = 8

slope_coef = 0.7978845608
cubic_coef = 0.044715
norm_eps = 1e-06

VMEM = pl.BlockSpec(memory_space=pltpu.VMEM)
SMEM = pl.BlockSpec(memory_space=pltpu.SMEM)
LIMIT = 56 * 1024 * 1024


def call(kernel, out_shape, in_specs, scratch=()):
    many = isinstance(out_shape, (list, tuple))
    return pl.pallas_call(
        kernel,
        out_shape=out_shape,
        in_specs=in_specs,
        out_specs=[VMEM] * len(out_shape) if many else VMEM,
        scratch_shapes=list(scratch),
        compiler_params=pltpu.CompilerParams(vmem_limit_bytes=LIMIT),
    )


def inside_of(rows, row, height, width):
    column = lax.broadcasted_iota(jnp.int32, (rows, 128), 0)
    return (column < width) & (row < height)


def depthwise_kernel(offsets, screen, canvas, dwk, bias, mixed, framed, taps):
    lanes = canvas.shape[2] // 128
    height, width = screen[0, 0], screen[0, 1]
    low = lax.broadcasted_iota(jnp.int32, (8, 128), 0) < 4
    for b in range(lanes):
        cut = slice(b * 128, (b + 1) * 128)
        blank = jnp.zeros((PAD_COLS, 128), jnp.float32)
        for y in (0, 1, 2, SIDE + 3, SIDE + 4, SIDE + 5):
            framed[b, y] = blank

        def fill(y, carry):
            framed[b, y + 3, 0:LEFT, :] = blank[:LEFT]
            framed[b, y + 3, LEFT + SIDE : PAD_COLS, :] = blank[: PAD_COLS - LEFT - SIDE]
            row = canvas[y, :, cut].astype(jnp.float32)
            framed[b, y + 3, LEFT : LEFT + SIDE, :] = jnp.where(
                inside_of(SIDE, y, height, width), row, 0.0
            )
            return carry

        lax.fori_loop(0, SIDE, fill, 0, unroll=2)
        kern = dwk[:, cut].astype(jnp.float32)
        for i in range(7):
            for j in range(4):
                first = jnp.broadcast_to(kern[7 * i + j][None], (8, 128))
                if j < 3:
                    second = jnp.broadcast_to(kern[7 * i + j + 4][None], (8, 128))
                else:
                    second = jnp.zeros((8, 128), jnp.float32)
                taps[i * 4 + j] = jnp.where(low, first, second)
        start = jnp.broadcast_to(bias[:, cut], (8, 128))

        def tile(t, carry):
            r, q = offsets[t, 0], offsets[t, 1]
            sums = [None] * 4
            for p in range(10):
                for j in range(4):
                    seen = framed[b, r + p, pl.ds(q + (LEFT - 3 + j), 8), :]
                    for y in range(max(0, p - 6), min(3, p) + 1):
                        term = seen * taps[(p - y) * 4 + j]
                        sums[y] = term if sums[y] is None else sums[y] + term
            folded = [s + pltpu.roll(s, 4, 0) + start for s in sums]
            pair = [jnp.where(low, folded[y], folded[y + 1]) for y in (0, 2)]
            rows = pl.ds(pl.multiple_of(t * 16, 16), 16)
            mixed[rows, cut] = jnp.concatenate(pair, 0).astype(jnp.bfloat16)
            return carry

        lax.fori_loop(0, offsets.shape[0], tile, 0)


def assemble(full, place, blocks, change):
    own, left, right, opp_a, opp_b = blocks
    share = own.shape[1]
    half = opp_a.shape[0]
    rows = own.shape[0]
    for ref, shift, span in (
        (own, 0, (0, rows)),
        (left, 3, (0, rows)),
        (right, 1, (0, rows)),
        (opp_a, 2, (0, half)),
        (opp_b, 2, (half, rows)),
    ):
        begin = pl.multiple_of(lax.rem(place + shift, 4) * share, 128)
        full[span[0] : span[1], pl.ds(begin, share)] = change(ref[...], begin, share)


def hidden_kernel(place, own, left, right, opp_a, opp_b, scale, w_out, hidden, full):
    def scaled(block, begin, share):
        return (scale[:, pl.ds(begin, share)] * block.astype(jnp.float32)).astype(jnp.bfloat16)

    assemble(full, place[0], (own, left, right, opp_a, opp_b), scaled)
    step = 512
    for n in range(0, hidden.shape[1], step):
        hidden[:, n : n + step] = lax.dot_general(
            full[...],
            w_out[n : n + step, :],
            (((1,), (1,)), ((), ())),
            preferred_element_type=jnp.float32,
        )


def gelu_slope(v):
    square = v * v
    t = jnp.tanh(slope_coef * (v + cubic_coef * square * v))
    return 0.5 * (1.0 + t) + 0.5 * v * (1.0 - t * t) * slope_coef * (1.0 + 3.0 * cubic_coef * square)


def as_rows(column):
    count = column.shape[0] // 128
    eye = lax.broadcasted_iota(jnp.int32, (128, 128), 0) == lax.broadcasted_iota(jnp.int32, (128, 128), 1)
    return jnp.concatenate(
        [
            jnp.sum(jnp.where(eye, column[g * 128 : (g + 1) * 128], 0.0), axis=0, keepdims=True)
            for g in range(count)
        ],
        0,
    )


def as_column(rows):
    eye = lax.broadcasted_iota(jnp.int32, (128, 128), 0) == lax.broadcasted_iota(jnp.int32, (128, 128), 1)
    return jnp.concatenate(
        [
            jnp.sum(jnp.where(eye, rows[g : g + 1], 0.0), axis=1, keepdims=True)
            for g in range(rows.shape[0])
        ],
        0,
    )


def block_kernel(
    place, own, left, right, opp_a, opp_b, gain, bias, w_in, b_in, hidden,
    to_right, to_left, next_right, next_left, mine, centers, inverses, full, scaled, act,
):
    rows, width = full.shape
    share = own.shape[1]
    half = rows // 2
    assemble(full, place[0], (own, left, right, opp_a, opp_b), lambda block, begin, share: block)
    step = 64
    for m in range(0, rows, step):
        values = full[m : m + step, :].astype(jnp.float32)
        center = jnp.mean(values, axis=1, keepdims=True)
        apart = values - center
        inverse = lax.rsqrt(jnp.mean(apart * apart, axis=1, keepdims=True) + norm_eps)
        centers[m : m + step, :] = center
        inverses[m : m + step, :] = inverse
        scaled[m : m + step, :] = (apart * inverse * gain[...] + bias[...]).astype(jnp.bfloat16)
    step = 512
    for n in range(0, width, step):
        pre = jnp.dot(scaled[...], w_in[:, n : n + step], preferred_element_type=jnp.float32)
        pre = pre + b_in[:, n : n + step]
        act[:, n : n + step] = (hidden[:, n : n + step] * gelu_slope(pre)).astype(jnp.bfloat16)
    first = jnp.zeros((rows, 1), jnp.float32)
    second = jnp.zeros((rows, 1), jnp.float32)
    for shift in (2, 1, 3, 0):
        begin = pl.multiple_of(lax.rem(place[0] + shift, 4) * share, 128)
        part = lax.dot_general(
            act[...],
            w_in[pl.ds(begin, share), :],
            (((1,), (1,)), ((), ())),
            preferred_element_type=jnp.float32,
        )
        if shift == 2:
            to_right[:half, :] = part[:half].astype(jnp.bfloat16)
            to_left[:half, :] = part[half:].astype(jnp.bfloat16)
        elif shift == 1:
            next_right[...] = part.astype(jnp.bfloat16)
        elif shift == 3:
            next_left[...] = part.astype(jnp.bfloat16)
        else:
            mine[...] = part
        weighted = part * gain[:, pl.ds(begin, share)]
        normed = (full[:, pl.ds(begin, share)].astype(jnp.float32) - centers[...]) * inverses[...]
        first = first + jnp.sum(weighted, axis=1, keepdims=True)
        second = second + jnp.sum(weighted * normed, axis=1, keepdims=True)
    packed = []
    for column in (first, second):
        line = as_rows(column)
        high = line.astype(jnp.bfloat16).astype(jnp.float32)
        packed += [high, line - high]
    sums = jnp.concatenate(packed, 0).astype(jnp.bfloat16)
    for out in (to_right, to_left):
        out[half : half + 16, :] = jnp.zeros((16, share), jnp.bfloat16)
        out[half : half + 16, :128] = sums


def middle_kernel(from_left, from_right, next_right, next_left, go_right, go_left):
    rows = next_right.shape[0]
    half = rows // 2

    def add(a, b):
        return (a.astype(jnp.float32) + b.astype(jnp.float32)).astype(jnp.bfloat16)

    go_right[:half, :] = add(next_right[:half, :], from_left[:half, :])
    go_right[half:rows, :] = next_right[half:, :]
    go_right[rows : rows + 16, :] = from_left[half : half + 16, :]
    go_left[:half, :] = next_left[:half, :]
    go_left[half:, :] = add(next_left[half:, :], from_right[:half, :])


def canvas_kernel(
    place, offsets, screen, counts,
    mine, got_left, got_right, from_left, from_right, to_right, mixed, centers, inverses, gain, cot, dwk,
    grad, upstream, grown, taken, taps,
):
    rows, share = mixed.shape
    half = rows // 2
    lanes = share // 128
    total = gain.shape[1]
    height, width = screen[0, 0], screen[0, 1]
    listed = counts[0, place[1]]
    begin = pl.multiple_of(place[0] * share, 128)
    packed = (
        to_right[half : half + 16, :128].astype(jnp.float32)
        + from_left[half : half + 16, :128].astype(jnp.float32)
        + from_right[half : half + 16, :128].astype(jnp.float32)
        + got_left[rows : rows + 16, :128].astype(jnp.float32)
    )
    first = as_column((packed[0:4] + packed[4:8]) * (1.0 / total))
    second = as_column((packed[8:12] + packed[12:16]) * (1.0 / total))
    step = 64
    for m in range(0, rows, step):
        span = slice(m, m + step)
        norm_grad = (
            mine[span, :]
            + got_left[span, :].astype(jnp.float32)
            + got_right[span, :].astype(jnp.float32)
        )
        inverse = inverses[span, :]
        normed = (mixed[span, :].astype(jnp.float32) - centers[span, :]) * inverse
        weighted = norm_grad * gain[:, pl.ds(begin, share)]
        upstream[span, :] = inverse * (weighted - first[span] - normed * second[span])

    low = lax.broadcasted_iota(jnp.int32, (8, 128), 0) < 4
    grown[...] = jnp.zeros_like(grown)
    taken[...] = jnp.zeros_like(taken)

    def tile(t, carry):
        r, q = offsets[t, 0], offsets[t, 1]
        for b in range(lanes):
            cut = slice(b * 128, (b + 1) * 128)
            span = pl.ds(pl.multiple_of(t * 16, 16), 16)
            up = upstream[span, cut]
            direct = cot[span, cut].astype(jnp.float32)
            for values, canvas, top in ((up, grown, 3), (direct, taken, 0)):
                for y in range(4):
                    pair = values[8 * (y // 2) : 8 * (y // 2) + 8]
                    pair = pltpu.roll(pair, 4, 0) if y % 2 else pair
                    columns = pl.ds(q + LEFT, 8)
                    canvas[b, r + top + y, columns, :] += jnp.where(low, pair, 0.0)
        return carry

    lax.fori_loop(0, listed, tile, 0)
    pairs = 2
    for b in range(lanes):
        cut = slice(b * 128, (b + 1) * 128)
        kern = dwk[:, cut].astype(jnp.float32)
        for k in range(49):
            taps[k] = jnp.broadcast_to(kern[k][None], (8, 128))

        def line(step, carry):
            y = step * pairs
            sums = [[None] * 4 for _ in range(pairs)]
            for p in range(6 + pairs):
                for j in range(7):
                    seen = [
                        grown[b, y + p, LEFT + 3 - j + 8 * x : LEFT + 3 - j + 8 * x + 8, :]
                        for x in range(4)
                    ]
                    for d in range(pairs):
                        i = 6 + d - p
                        if 0 <= i < 7:
                            tap = taps[7 * i + j]
                            for x in range(4):
                                term = seen[x] * tap
                                sums[d][x] = term if sums[d][x] is None else sums[d][x] + term
            for d in range(pairs):
                whole = jnp.concatenate(sums[d], 0) + taken[b, y + d, LEFT : LEFT + SIDE, :]
                grad[y + d, :, cut] = jnp.where(inside_of(SIDE, y + d, height, width), whole, 0.0)
            return carry

        lax.fori_loop(0, SIDE // pairs, line, 0)


def shift(x, by):
    n = lax.axis_size("ch")
    return lax.ppermute(x, "ch", [(i, (i + by) % n) for i in range(n)])


def ring_gather(x):
    half = x.shape[0] // 2
    left, right = shift(x, 1), shift(x, -1)
    return x, left, right, shift(left[:half], 1), shift(right[half:], -1)


def shards(
    canvas,
    screen_size,
    tile_counts,
    tile_offsets,
    cotangent,
    dw_kernel,
    dw_bias,
    ln_gain,
    ln_bias,
    w_in,
    b_in,
    w_out,
    layer_scale,
):
    f32, bf16 = jnp.float32, jnp.bfloat16
    struct = jax.ShapeDtypeStruct
    slots = tile_offsets.shape[0]
    share = canvas.shape[2]
    width = ln_gain.shape[0]
    hid = w_in.shape[1]
    rows = slots * TS * TS
    half = rows // 2
    lanes = share // 128
    place = jnp.stack([lax.axis_index("ch"), lax.axis_index("img")]).astype(jnp.int32)
    line = lambda v: v.reshape(1, -1)

    cot = cotangent.reshape(rows, share)
    cots = ring_gather(cot)
    mixed = call(
        depthwise_kernel,
        struct((rows, share), bf16),
        [SMEM, SMEM, VMEM, VMEM, VMEM],
        [
            pltpu.VMEM((lanes, PAD_ROWS, PAD_COLS, 128), f32),
            pltpu.VMEM((28, 8, 128), f32),
        ],
    )(tile_offsets, screen_size, canvas, dw_kernel, line(dw_bias))
    mixes = ring_gather(mixed)
    hidden = call(
        hidden_kernel,
        struct((rows, hid), f32),
        [SMEM] + [VMEM] * 7,
        [pltpu.VMEM((rows, width), bf16)],
    )(place, *cots, line(layer_scale), w_out)
    to_right, to_left, next_right, next_left, mine, centers, inverses = call(
        block_kernel,
        [
            struct((half + 16, share), bf16),
            struct((half + 16, share), bf16),
            struct((rows, share), bf16),
            struct((rows, share), bf16),
            struct((rows, share), f32),
            struct((rows, 1), f32),
            struct((rows, 1), f32),
        ],
        [SMEM] + [VMEM] * 10,
        [
            pltpu.VMEM((rows, width), bf16),
            pltpu.VMEM((rows, width), bf16),
            pltpu.VMEM((rows, hid), bf16),
        ],
    )(place, *mixes, line(ln_gain), line(ln_bias), w_in, line(b_in), hidden)
    from_left, from_right = shift(to_right, 1), shift(to_left, -1)
    go_right, go_left = call(
        middle_kernel,
        [struct((rows + 16, share), bf16), struct((rows, share), bf16)],
        [VMEM] * 4,
    )(from_left, from_right, next_right, next_left)
    got_left, got_right = shift(go_right, 1), shift(go_left, -1)
    return call(
        canvas_kernel,
        struct(canvas.shape, f32),
        [SMEM] * 4 + [VMEM] * 12,
        [
            pltpu.VMEM((rows, share), f32),
            pltpu.VMEM((lanes, PAD_ROWS, PAD_COLS, 128), f32),
            pltpu.VMEM((lanes, SIDE, PAD_COLS, 128), f32),
            pltpu.VMEM((49, 8, 128), f32),
        ],
    )(
        place, tile_offsets, screen_size, line(tile_counts),
        mine, got_left, got_right, from_left, from_right, to_right, mixed, centers, inverses,
        line(ln_gain), cot, dw_kernel,
    )


def solution(mesh):
    return jax.shard_map(
        shards,
        mesh=mesh,
        in_specs=(
            P("img", None, "ch"),
            P("img", None),
            P(),
            P("img", None),
            P("img", None, None, "ch"),
            P(None, "ch"),
            P("ch"),
            P(),
            P(),
            P(None, "ch"),
            P("ch"),
            P("ch", None),
            P(),
        ),
        out_specs=P("img", None, "ch"),
        check_vma=False,
    )
```

time: 1030 us -> 95.8 us (0.09)
  the two profiles are of different devices: /device:TPU:0 before, /device:TPU:28 now
where the time goes in v1:
time: 95.8 us; the launch traced here: 95.1 us
  Pallas kernels  40.4 us (42%)
  starting transfers between devices  21.1 us (22%)
  waiting for transfers between devices  19.8 us (21%)
  local copies, waits for them, and re-layouts  13.1 us (14%)
    ppermute x12, starting transfers between devices, shift(): return lax.ppermute(x, 'ch', [(i, (i + by) % n) for i in range(n)])  21.1 us
    ppermute x12, waiting for transfers between devices, shift(): return lax.ppermute(x, 'ch', [(i, (i + by) % n) for i in range(n)])  19.8 us
    pallas_call x1, Pallas kernels, shards(): call(block_kernel, [struct((half + 16, share), bf16), struct((half + 16,...  13.3 us
    pallas_call x1, Pallas kernels, shards(): call(canvas_kernel, struct(canvas.shape, f32), [SMEM] * 4 + [VMEM] * 12,...  10.7 us
    pallas_call x1, Pallas kernels, shards(): call(hidden_kernel, struct((rows, hid), f32), [SMEM] + [VMEM] * 7, [pltpu...  7.33 us
    pallas_call x1, Pallas kernels, shards(): call(depthwise_kernel, struct((rows, share), bf16), [SMEM, SMEM, VMEM, VM...  6.78 us
    reshape x5, local copies, waits for them, and re-layouts, shards(): line = lambda v: v.reshape(1, -1)  6.42 us
    unnamed x27, local copies, waits for them, and re-layouts  5.52 us
  transfers between devices with their start and end apart: 12, of which 5 were waited for; matrix products, arithmetic and copies ran while one was open for 9% of the time, Pallas kernels for 15%

profile of v1, /device:TPU:28, one launch (start us, length us, event | category | flops | bytes accessed | tf_op | source)
XLA Modules:
  0.0 95.1 jit_solution(16755053773154683027)
XLA Ops:
  0.0 1.1 %reshape.27.own.cot = bf16[512,384]{1,0:T(8,128)(2,1)S(1)} reshape(bf16[32,4,4,384]{3,2,1,0:T(4,128)(2,1)} %param.17) | data formatting | bytes 786432 | tf_op jit(solution)/shard_map/reshape | solution.py:343
  1.1 0.0 copy-start
  1.1 4.1 %collective-permute-start.5 = (bf16[512,384]{1,0:T(8,128)(2,1)S(1)}, bf16[512,384]{1,0:T(8,128)(2,1)S(1)}, u32[]{:S(2)}, u32[]{:S(2)}) collective-permute-start(bf16[512,384]{1,0:T(8,128)(2,1)S(1)} %reshape.27.own.cot), channel_id=1, source_target_pairs={{0,3},{1,0},{2,1},{3,2},{4,7},{5,4},{6,5},{7,6},{8,11},{9,8},{10,9... | collective-permute-start | bytes 1179656 | tf_op jit(solution)/shard_map/ppermute | solution.py:307
  5.2 0.0 collective-permute-start.4
  5.2 1.2 %reshape.23.bias = f32[1,384]{1,0:T(1,128)} reshape(f32[384]{0:T(512)} %param.19) | data formatting | bytes 3072 | tf_op jit(solution)/shard_map/reshape | solution.py:341
  6.5 1.4 %copy.15.offsets = s32[32,2]{1,0:T(8,128)} copy(s32[32,2]{0,1:T(2,128)} %param.16) | data formatting | bytes 512 | tf_op args[3]
  7.8 6.8 %shard_map.127.own.mixed = bf16[512,384]{1,0:T(8,128)(2,1)} custom-call(s32[32,2]{1,0:T(8,128)} %copy.15.offsets, s32[1,2]{1,0:T(1,128)} %screen.3, bf16[32,32,384]{2,1,0:T(8,128)(2,1)} %canvas.1, bf16[49,384]{1,0:T(8,128)(2,1)} %dwk.3, f32[1,384]{1,0:T(1,128)} %reshape.23.bias), custom_call_target="tpu_custom_call" | custom-call | tf_op jit(solution)/shard_map/pallas_call | solution.py:345
  14.6 3.2 %collective-permute-start.1 = (bf16[512,384]{1,0:T(8,128)(2,1)}, bf16[512,384]{1,0:T(8,128)(2,1)S(1)}, u32[]{:S(2)}, u32[]{:S(2)}) collective-permute-start(bf16[512,384]{1,0:T(8,128)(2,1)} %shard_map.127.own.mixed), channel_id=1, source_target_pairs={{0,3},{1,0},{2,1},{3,2},{4,7},{5,4},{6,5},{7,6},{8,11},{9,8},{10,9... | collective-permute-start | bytes 1179656 | tf_op jit(solution)/shard_map/ppermute | solution.py:307
  17.8 0.0 collective-permute-start
  17.8 0.0 collective-permute-done.5.right
  17.8 0.0 copy-start.1
  17.9 3.3 %collective-permute-start.7 = (bf16[256,384]{1,0:T(8,128)(2,1)S(1)}, bf16[256,384]{1,0:T(8,128)(2,1)S(1)}, u32[]{:S(2)}, u32[]{:S(2)}) collective-permute-start(bf16[256,384]{1,0:T(8,128)(2,1)S(1)} %slice.19), channel_id=1, source_target_pairs={{0,3},{1,0},{2,1},{3,2},{4,7},{5,4},{6,5},{7,6},{8,11},{9,8},{10,9... | collective-permute-start | bytes 589832 | tf_op jit(solution)/shard_map/ppermute | solution.py:307
  21.2 0.0 collective-permute-done.4.left
  21.2 0.0 copy-start.2
  21.2 0.1 collective-permute-start.6
  21.3 6.4 %collective-permute-done.1.right = bf16[512,384]{1,0:T(8,128)(2,1)S(1)} collective-permute-done((bf16[512,384]{1,0:T(8,128)(2,1)}, bf16[512,384]{1,0:T(8,128)(2,1)S(1)}, u32[]{:S(2)}, u32[]{:S(2)}) %collective-permute-start.1) | collective-permute-done | bytes 393248 | tf_op jit(solution)/shard_map/ppermute | solution.py:307
  27.7 0.0 copy-start.3
  27.7 3.7 %collective-permute-start.3 = (bf16[256,384]{1,0:T(8,128)(2,1)S(1)}, bf16[256,384]{1,0:T(8,128)(2,1)S(1)}, u32[]{:S(2)}, u32[]{:S(2)}) collective-permute-start(bf16[256,384]{1,0:T(8,128)(2,1)S(1)} %slice.17), channel_id=1, source_target_pairs={{0,3},{1,0},{2,1},{3,2},{4,7},{5,4},{6,5},{7,6},{8,11},{9,8},{10,9... | collective-permute-start | bytes 589832 | tf_op jit(solution)/shard_map/ppermute | solution.py:307
  31.4 0.0 collective-permute-done.left
  31.4 0.0 copy-start.4
  31.4 0.3 collective-permute-start.2
  31.7 1.3 %reshape.24.gain = f32[1,1536]{1,0:T(1,128)} reshape(f32[1536]{0:T(1024)} %param.20) | data formatting | bytes 12288 | tf_op jit(solution)/shard_map/reshape | solution.py:341
  33.0 1.3 %reshape.25.bias = f32[1,1536]{1,0:T(1,128)} reshape(f32[1536]{0:T(1024)} %param.21) | data formatting | bytes 12288 | tf_op jit(solution)/shard_map/reshape | solution.py:341
  34.3 1.3 %reshape.26.b_in = f32[1,1536]{1,0:T(1,128)} reshape(f32[1536]{0:T(1024)} %param.23) | data formatting | bytes 12288 | tf_op jit(solution)/shard_map/reshape | solution.py:341
  35.6 1.3 %reshape.28.scale = f32[1,1536]{1,0:T(1,128)} reshape(f32[1536]{0:T(1024)} %param.25) | data formatting | bytes 12288 | tf_op jit(solution)/shard_map/reshape | solution.py:341
  36.9 0.6 pad_add_fusion.place
  37.5 0.0 collective-permute-done.7.opp_b
  37.5 0.0 copy-start.10
  37.5 0.0 collective-permute-done.6.opp_a
  37.5 0.0 copy-done
  37.5 0.0 copy-done.1
  37.5 0.0 copy-done.2
  37.5 0.7 copy-done.10
  38.2 0.0 copy-start.12
  38.2 0.7 copy-done.12
  38.9 7.3 %shard_map.128.hidden = f32[512,1536]{1,0:T(8,128)} custom-call(s32[2]{0:T(128)} %pad_add_fusion.place, bf16[512,384]{1,0:T(8,128)(2,1)} %copy-done, bf16[512,384]{1,0:T(8,128)(2,1)} %copy-done.2, bf16[512,384]{1,0:T(8,128)(2,1)} %copy-done.1, bf16[256,384]{1,0:T(8,128)(2,1)} %copy-done.12, bf16[256,384]{1,0:T(8,128)(2,1)} %copy-done.10, ...), custom_call_target="tpu_custom_call" | custom-call | tf_op jit(solution)/shard_map/pallas_call | solution.py:355
  46.2 0.0 copy-done.3
  46.2 0.0 copy-done.4
  46.2 0.0 collective-permute-done.3.opp_b
  46.2 0.0 copy-start.9
  46.2 0.0 collective-permute-done.2.opp_a
  46.2 0.7 copy-done.9
  46.9 0.0 copy-start.11
  46.9 0.7 copy-done.11
  47.6 13.3 %shard_map.129 = (bf16[272,384]{1,0:T(8,128)(2,1)}, bf16[272,384]{1,0:T(8,128)(2,1)}, bf16[512,384]{1,0:T(8,128)(2,1)}, bf16[512,384]{1,0:T(8,128)(2,1)}, f32[51...) custom-call(s32[2]{0:T(128)} %pad_add_fusion.place, bf16[512,384]{1,0:T(8,128)(2,1)} %shard_map.127.own.mixed, ...), custom_call_target="tpu_custom_call" | custom-call | tf_op jit(solution)/shard_map/pallas_call | solution.py:361
  60.9 3.2 %collective-permute-start.9 = (bf16[272,384]{1,0:T(8,128)(2,1)}, bf16[272,384]{1,0:T(8,128)(2,1)S(1)}, u32[]{:S(2)}, u32[]{:S(2)}) collective-permute-start(bf16[272,384]{1,0:T(8,128)(2,1)} %get-tuple-element.16), channel_id=1, source_target_pairs={{0,3},{1,0},{2,1},{3,2},{4,7},{5,4},{6,5},{7,6},{8,11},{9,8},{10,9... | collective-permute-start | bytes 626696 | tf_op jit(solution)/shard_map/ppermute | solution.py:307
  64.1 0.0 collective-permute-start.8
  64.1 3.6 %collective-permute-done.9.from_right = bf16[272,384]{1,0:T(8,128)(2,1)S(1)} collective-permute-done((bf16[272,384]{1,0:T(8,128)(2,1)}, bf16[272,384]{1,0:T(8,128)(2,1)S(1)}, u32[]{:S(2)}, u32[]{:S(2)}) %collective-permute-start.9) | collective-permute-done | bytes 208928 | tf_op jit(solution)/shard_map/ppermute | solution.py:307
  67.8 0.0 copy-start.5
  67.8 3.6 %collective-permute-done.8.from_left = bf16[272,384]{1,0:T(8,128)(2,1)S(1)} collective-permute-done((bf16[272,384]{1,0:T(8,128)(2,1)}, bf16[272,384]{1,0:T(8,128)(2,1)S(1)}, u32[]{:S(2)}, u32[]{:S(2)}) %collective-permute-start.8) | collective-permute-done | bytes 208928 | tf_op jit(solution)/shard_map/ppermute | solution.py:307
  71.3 0.0 copy-start.6
  71.3 0.0 copy-done.5
  71.4 0.7 copy-done.6
  72.0 2.3 %shard_map.130 = (bf16[528,384]{1,0:T(8,128)(2,1)}, bf16[512,384]{1,0:T(8,128)(2,1)}) custom-call(bf16[272,384]{1,0:T(8,128)(2,1)} %copy-done.6, bf16[272,384]{1,0:T(8,128)(2,1)} %copy-done.5, bf16[512,384]{1,0:T(8,128)(2,1)} %get-tuple-element.17.next_right, bf16[512,384]{1,0:T(8,128)(2,1)} %get-tuple-element.18.next_left), custom_call_target="tpu_custom_call" | custom-call | tf_op jit(solution)/shard_map/pallas_call | solution.py:380
  74.3 0.0 collective-permute-start.10
  74.3 3.2 %collective-permute-start.11 = (bf16[512,384]{1,0:T(8,128)(2,1)}, bf16[512,384]{1,0:T(8,128)(2,1)S(1)}, u32[]{:S(2)}, u32[]{:S(2)}) collective-permute-start(bf16[512,384]{1,0:T(8,128)(2,1)} %get-tuple-element.20), channel_id=1, source_target_pairs={{0,3},{1,0},{2,1},{3,2},{4,7},{5,4},{6,5},{7,6},{8,11},{9,8},{10,9... | collective-permute-start | bytes 1179656 | tf_op jit(solution)/shard_map/ppermute | solution.py:307
  77.6 5.6 %collective-permute-done.11.got_right = bf16[512,384]{1,0:T(8,128)(2,1)S(1)} collective-permute-done((bf16[512,384]{1,0:T(8,128)(2,1)}, bf16[512,384]{1,0:T(8,128)(2,1)S(1)}, u32[]{:S(2)}, u32[]{:S(2)}) %collective-permute-start.11) | collective-permute-done | bytes 393248 | tf_op jit(solution)/shard_map/ppermute | solution.py:307
  83.2 0.0 copy-start.8
  83.2 0.5 collective-permute-done.10.got_left
  83.6 0.0 copy-start.7
  83.7 0.3 copy-done.8
  83.9 0.5 copy-done.7
  84.4 10.7 %shard_map.131 = f32[32,32,384]{2,1,0:T(8,128)} custom-call(s32[2]{0:T(128)} %pad_add_fusion.place, s32[32,2]{1,0:T(8,128)} %copy.15.offsets, s32[1,2]{1,0:T(1,128)} %screen.3, s32[1,32]{1,0:T(1,128)} %bitcast.3, f32[512,384]{1,0:T(8,128)} %get-tuple-element.14.mine, bf16[528,384]{1,0:T(8,128)(2,1)} %copy-done.7, bf16[512,384]{1,0:T(8,128)(2,1)} %copy-done.8, ...), custom_call_target="tpu_custom_call" | custom-call | tf_op jit(solution)/shard_map/pallas_call | solution.py:386
  (4 shorter events, 0.1 us)
Async XLA Ops:
  1.1 36.4 %copy-start = (bf16[512,384]{1,0:T(8,128)(2,1)}, bf16[512,384]{1,0:T(8,128)(2,1)S(1)}, u32[]{:S(2)}) copy-start(bf16[512,384]{1,0:T(8,128)(2,1)S(1)} %reshape.27.own.cot) | copy-start | bytes 1179652
  1.1 16.7 %collective-permute-start.5 = (bf16[512,384]{1,0:T(8,128)(2,1)S(1)}, bf16[512,384]{1,0:T(8,128)(2,1)S(1)}, u32[]{:S(2)}, u32[]{:S(2)}) collective-permute-start(bf16[512,384]{1,0:T(8,128)(2,1)S(1)} %reshape.27.own.cot), channel_id=1, source_target_pairs={{0,3},{1,0},{2,1},{3,2},{4,7},{5,4},{6,5},{7,6},{8,11},{9,8},{10,9... | collective-permute-start | bytes 1179656 | tf_op jit(solution)/shard_map/ppermute | solution.py:307
  5.2 16.0 %collective-permute-start.4 = (bf16[512,384]{1,0:T(8,128)(2,1)S(1)}, bf16[512,384]{1,0:T(8,128)(2,1)S(1)}, u32[]{:S(2)}, u32[]{:S(2)}) collective-permute-start(bf16[512,384]{1,0:T(8,128)(2,1)S(1)} %reshape.27.own.cot), channel_id=1, source_target_pairs={{0,1},{1,2},{2,3},{3,0},{4,5},{5,6},{6,7},{7,4},{8,9},{9,10},{10,1... | collective-permute-start | bytes 1179656 | tf_op jit(solution)/shard_map/ppermute | solution.py:307
  14.6 13.1 %collective-permute-start.1 = (bf16[512,384]{1,0:T(8,128)(2,1)}, bf16[512,384]{1,0:T(8,128)(2,1)S(1)}, u32[]{:S(2)}, u32[]{:S(2)}) collective-permute-start(bf16[512,384]{1,0:T(8,128)(2,1)} %shard_map.127.own.mixed), channel_id=1, source_target_pairs={{0,3},{1,0},{2,1},{3,2},{4,7},{5,4},{6,5},{7,6},{8,11},{9,8},{10,9... | collective-permute-start | bytes 1179656 | tf_op jit(solution)/shard_map/ppermute | solution.py:307
  17.8 13.6 %collective-permute-start = (bf16[512,384]{1,0:T(8,128)(2,1)}, bf16[512,384]{1,0:T(8,128)(2,1)S(1)}, u32[]{:S(2)}, u32[]{:S(2)}) collective-permute-start(bf16[512,384]{1,0:T(8,128)(2,1)} %shard_map.127.own.mixed), channel_id=1, source_target_pairs={{0,1},{1,2},{2,3},{3,0},{4,5},{5,6},{6,7},{7,4},{8,9},{9,10},{10,1... | collective-permute-start | bytes 1179656 | tf_op jit(solution)/shard_map/ppermute | solution.py:307
  17.8 19.7 %copy-start.1 = (bf16[512,384]{1,0:T(8,128)(2,1)}, bf16[512,384]{1,0:T(8,128)(2,1)S(1)}, u32[]{:S(2)}) copy-start(bf16[512,384]{1,0:T(8,128)(2,1)S(1)} %collective-permute-done.5.right) | copy-start | bytes 1179652
  17.9 19.6 %collective-permute-start.7 = (bf16[256,384]{1,0:T(8,128)(2,1)S(1)}, bf16[256,384]{1,0:T(8,128)(2,1)S(1)}, u32[]{:S(2)}, u32[]{:S(2)}) collective-permute-start(bf16[256,384]{1,0:T(8,128)(2,1)S(1)} %slice.19), channel_id=1, source_target_pairs={{0,3},{1,0},{2,1},{3,2},{4,7},{5,4},{6,5},{7,6},{8,11},{9,8},{10,9... | collective-permute-start | bytes 589832 | tf_op jit(solution)/shard_map/ppermute | solution.py:307
  21.2 16.4 %copy-start.2 = (bf16[512,384]{1,0:T(8,128)(2,1)}, bf16[512,384]{1,0:T(8,128)(2,1)S(1)}, u32[]{:S(2)}) copy-start(bf16[512,384]{1,0:T(8,128)(2,1)S(1)} %collective-permute-done.4.left) | copy-start | bytes 1179652
  21.2 16.3 %collective-permute-start.6 = (bf16[256,384]{1,0:T(8,128)(2,1)S(1)}, bf16[256,384]{1,0:T(8,128)(2,1)S(1)}, u32[]{:S(2)}, u32[]{:S(2)}) collective-permute-start(bf16[256,384]{1,0:T(8,128)(2,1)S(1)} %slice.18), channel_id=1, source_target_pairs={{0,1},{1,2},{2,3},{3,0},{4,5},{5,6},{6,7},{7,4},{8,9},{9,10},{10,1... | collective-permute-start | bytes 589832 | tf_op jit(solution)/shard_map/ppermute | solution.py:307
  27.7 18.5 %copy-start.3 = (bf16[512,384]{1,0:T(8,128)(2,1)}, bf16[512,384]{1,0:T(8,128)(2,1)S(1)}, u32[]{:S(2)}) copy-start(bf16[512,384]{1,0:T(8,128)(2,1)S(1)} %collective-permute-done.1.right) | copy-start | bytes 1179652
  27.7 18.5 %collective-permute-start.3 = (bf16[256,384]{1,0:T(8,128)(2,1)S(1)}, bf16[256,384]{1,0:T(8,128)(2,1)S(1)}, u32[]{:S(2)}, u32[]{:S(2)}) collective-permute-start(bf16[256,384]{1,0:T(8,128)(2,1)S(1)} %slice.17), channel_id=1, source_target_pairs={{0,3},{1,0},{2,1},{3,2},{4,7},{5,4},{6,5},{7,6},{8,11},{9,8},{10,9... | collective-permute-start | bytes 589832 | tf_op jit(solution)/shard_map/ppermute | solution.py:307
  31.4 14.8 %copy-start.4 = (bf16[512,384]{1,0:T(8,128)(2,1)}, bf16[512,384]{1,0:T(8,128)(2,1)S(1)}, u32[]{:S(2)}) copy-start(bf16[512,384]{1,0:T(8,128)(2,1)S(1)} %collective-permute-done.left) | copy-start | bytes 1179652
  31.4 14.8 %collective-permute-start.2 = (bf16[256,384]{1,0:T(8,128)(2,1)S(1)}, bf16[256,384]{1,0:T(8,128)(2,1)S(1)}, u32[]{:S(2)}, u32[]{:S(2)}) collective-permute-start(bf16[256,384]{1,0:T(8,128)(2,1)S(1)} %slice.16), channel_id=1, source_target_pairs={{0,1},{1,2},{2,3},{3,0},{4,5},{5,6},{6,7},{7,4},{8,9},{9,10},{10,1... | collective-permute-start | bytes 589832 | tf_op jit(solution)/shard_map/ppermute | solution.py:307
  37.5 0.7 copy-start.10
  38.2 0.7 copy-start.12
  46.2 0.7 copy-start.9
  46.9 0.7 copy-start.11
  60.9 6.9 %collective-permute-start.9 = (bf16[272,384]{1,0:T(8,128)(2,1)}, bf16[272,384]{1,0:T(8,128)(2,1)S(1)}, u32[]{:S(2)}, u32[]{:S(2)}) collective-permute-start(bf16[272,384]{1,0:T(8,128)(2,1)} %get-tuple-element.16), channel_id=1, source_target_pairs={{0,3},{1,0},{2,1},{3,2},{4,7},{5,4},{6,5},{7,6},{8,11},{9,8},{10,9... | collective-permute-start | bytes 626696 | tf_op jit(solution)/shard_map/ppermute | solution.py:307
  64.1 7.2 %collective-permute-start.8 = (bf16[272,384]{1,0:T(8,128)(2,1)}, bf16[272,384]{1,0:T(8,128)(2,1)S(1)}, u32[]{:S(2)}, u32[]{:S(2)}) collective-permute-start(bf16[272,384]{1,0:T(8,128)(2,1)} %get-tuple-element.15.to_right), channel_id=1, source_target_pairs={{0,1},{1,2},{2,3},{3,0},{4,5},{5,6},{6,7},{7,4},{8,9},{9,10},{10,1... | collective-permute-start | bytes 626696 | tf_op jit(solution)/shard_map/ppermute | solution.py:307
  67.8 3.6 %copy-start.5 = (bf16[272,384]{1,0:T(8,128)(2,1)}, bf16[272,384]{1,0:T(8,128)(2,1)S(1)}, u32[]{:S(2)}) copy-start(bf16[272,384]{1,0:T(8,128)(2,1)S(1)} %collective-permute-done.9.from_right) | copy-start | bytes 626692
  71.3 0.7 copy-start.6
  74.3 9.3 %collective-permute-start.10 = (bf16[528,384]{1,0:T(8,128)(2,1)}, bf16[528,384]{1,0:T(8,128)(2,1)S(1)}, u32[]{:S(2)}, u32[]{:S(2)}) collective-permute-start(bf16[528,384]{1,0:T(8,128)(2,1)} %get-tuple-element.19), channel_id=1, source_target_pairs={{0,1},{1,2},{2,3},{3,0},{4,5},{5,6},{6,7},{7,4},{8,9},{9,10},{10,1... | collective-permute-start | bytes 1216520 | tf_op jit(solution)/shard_map/ppermute | solution.py:307
  74.3 8.8 %collective-permute-start.11 = (bf16[512,384]{1,0:T(8,128)(2,1)}, bf16[512,384]{1,0:T(8,128)(2,1)S(1)}, u32[]{:S(2)}, u32[]{:S(2)}) collective-permute-start(bf16[512,384]{1,0:T(8,128)(2,1)} %get-tuple-element.20), channel_id=1, source_target_pairs={{0,3},{1,0},{2,1},{3,2},{4,7},{5,4},{6,5},{7,6},{8,11},{9,8},{10,9... | collective-permute-start | bytes 1179656 | tf_op jit(solution)/shard_map/ppermute | solution.py:307
  83.2 0.7 copy-start.8
  83.6 0.8 copy-start.7

commit v2 on v1

--- a/solution.py
+++ b/solution.py
@@ -19,19 +19,28 @@
 
 VMEM = pl.BlockSpec(memory_space=pltpu.VMEM)
 SMEM = pl.BlockSpec(memory_space=pltpu.SMEM)
-LIMIT = 56 * 1024 * 1024
-
-
-def call(kernel, out_shape, in_specs, scratch=()):
-    many = isinstance(out_shape, (list, tuple))
-    return pl.pallas_call(
+HBM = pl.BlockSpec(memory_space=pltpu.HBM)
+
+
+def call(kernel, out_shape, in_specs, scratch=(), limit=16, out_specs=None):
+    run = pl.pallas_call(
         kernel,
         out_shape=out_shape,
         in_specs=in_specs,
-        out_specs=[VMEM] * len(out_shape) if many else VMEM,
+        out_specs=out_specs or [VMEM] * len(out_shape),
         scratch_shapes=list(scratch),
-        compiler_params=pltpu.CompilerParams(vmem_limit_bytes=LIMIT),
-    )
+        compiler_params=pltpu.CompilerParams(vmem_limit_bytes=limit << 20),
+    )
+
+    def held(*args):
+        return run(
+            *(
+                pltpu.with_memory_space_constraint(a, pltpu.VMEM if spec is VMEM else pltpu.HBM)
+                for spec, a in zip(in_specs, args, strict=True)
+            )
+        )
+
+    return held
 
 
 def inside_of(rows, row, height, width):
@@ -39,7 +48,15 @@
     return (column < width) & (row < height)
 
 
-def depthwise_kernel(offsets, screen, canvas, dwk, bias, mixed, framed, taps):
+def depthwise_kernel(
+    offsets, screen, canvas, dwk, bias, w_in, w_out, mixed, near_in, near_out, framed, taps, sems
+):
+    fetches = [
+        pltpu.make_async_copy(w_out, near_out, sems.at[0]),
+        pltpu.make_async_copy(w_in, near_in, sems.at[1]),
+    ]
+    for fetch in fetches:
+        fetch.start()
     lanes = canvas.shape[2] // 128
     height, width = screen[0, 0], screen[0, 1]
     low = lax.broadcasted_iota(jnp.int32, (8, 128), 0) < 4
@@ -68,10 +85,10 @@
                 else:
                     second = jnp.zeros((8, 128), jnp.float32)
                 taps[i * 4 + j] = jnp.where(low, first, second)
-        start = jnp.broadcast_to(bias[:, cut], (8, 128))
+        start = jnp.broadcast_to(bias[cut][None], (8, 128))
 
         def tile(t, carry):
-            r, q = offsets[t, 0], offsets[t, 1]
+            r, q = offsets[0, t], offsets[1, t]
             sums = [None] * 4
             for p in range(10):
                 for j in range(4):
@@ -85,11 +102,14 @@
             mixed[rows, cut] = jnp.concatenate(pair, 0).astype(jnp.bfloat16)
             return carry
 
-        lax.fori_loop(0, offsets.shape[0], tile, 0)
-
-
-def assemble(full, place, blocks, change):
+        lax.fori_loop(0, offsets.shape[1], tile, 0)
+    for fetch in fetches:
+        fetch.wait()
+
+
+def assemble(full, blocks, change):
     own, left, right, opp_a, opp_b = blocks
+    place = lax.axis_index("ch")
     share = own.shape[1]
     half = opp_a.shape[0]
     rows = own.shape[0]
@@ -104,11 +124,33 @@
         full[span[0] : span[1], pl.ds(begin, share)] = change(ref[...], begin, share)
 
 
-def hidden_kernel(place, own, left, right, opp_a, opp_b, scale, w_out, hidden, full):
+def place_tiles(offsets, listed, values, canvas, top):
+    low = lax.broadcasted_iota(jnp.int32, (8, 128), 0) < 4
+
+    def tile(t, carry):
+        r, q = offsets[0, t], offsets[1, t]
+        columns = pl.ds(q + LEFT, 8)
+        span = pl.ds(pl.multiple_of(t * 16, 16), 16)
+        for b in range(values.shape[1] // 128):
+            cells = values[span, b * 128 : (b + 1) * 128].astype(jnp.float32)
+            for y in range(4):
+                pair = cells[8 * (y // 2) : 8 * (y // 2) + 8]
+                pair = pltpu.roll(pair, 4, 0) if y % 2 else pair
+                canvas[b, r + top + y, columns, :] += jnp.where(low, pair, 0.0)
+        return carry
+
+    lax.fori_loop(0, listed, tile, 0)
+
+
+def hidden_kernel(
+    offsets, counts, own, left, right, opp_a, opp_b, scale, w_out, hidden, taken, full
+):
     def scaled(block, begin, share):
-        return (scale[:, pl.ds(begin, share)] * block.astype(jnp.float32)).astype(jnp.bfloat16)
-
-    assemble(full, place[0], (own, left, right, opp_a, opp_b), scaled)
+        return (scale[pl.ds(begin, share)][None] * block.astype(jnp.float32)).astype(jnp.bfloat16)
+
+    taken[...] = jnp.zeros_like(taken)
+    place_tiles(offsets, counts[lax.axis_index("img")], own, taken, 0)
+    assemble(full, (own, left, right, opp_a, opp_b), scaled)
     step = 512
     for n in range(0, hidden.shape[1], step):
         hidden[:, n : n + step] = lax.dot_general(
@@ -149,13 +191,14 @@
 
 
 def block_kernel(
-    place, own, left, right, opp_a, opp_b, gain, bias, w_in, b_in, hidden,
+    own, left, right, opp_a, opp_b, gain, bias, w_in, b_in, hidden,
     to_right, to_left, next_right, next_left, mine, centers, inverses, full, scaled, act,
 ):
     rows, width = full.shape
     share = own.shape[1]
+    place = lax.axis_index("ch")
     half = rows // 2
-    assemble(full, place[0], (own, left, right, opp_a, opp_b), lambda block, begin, share: block)
+    assemble(full, (own, left, right, opp_a, opp_b), lambda block, begin, share: block)
     step = 64
     for m in range(0, rows, step):
         values = full[m : m + step, :].astype(jnp.float32)
@@ -164,16 +207,16 @@
         inverse = lax.rsqrt(jnp.mean(apart * apart, axis=1, keepdims=True) + norm_eps)
         centers[m : m + step, :] = center
         inverses[m : m + step, :] = inverse
-        scaled[m : m + step, :] = (apart * inverse * gain[...] + bias[...]).astype(jnp.bfloat16)
+        scaled[m : m + step, :] = (apart * inverse * gain[...][None] + bias[...][None]).astype(jnp.bfloat16)
     step = 512
     for n in range(0, width, step):
         pre = jnp.dot(scaled[...], w_in[:, n : n + step], preferred_element_type=jnp.float32)
-        pre = pre + b_in[:, n : n + step]
+        pre = pre + b_in[n : n + step][None]
         act[:, n : n + step] = (hidden[:, n : n + step] * gelu_slope(pre)).astype(jnp.bfloat16)
     first = jnp.zeros((rows, 1), jnp.float32)
     second = jnp.zeros((rows, 1), jnp.float32)
     for shift in (2, 1, 3, 0):
-        begin = pl.multiple_of(lax.rem(place[0] + shift, 4) * share, 128)
+        begin = pl.multiple_of(lax.rem(place + shift, 4) * share, 128)
         part = lax.dot_general(
             act[...],
             w_in[pl.ds(begin, share), :],
@@ -189,7 +232,7 @@
             next_left[...] = part.astype(jnp.bfloat16)
         else:
             mine[...] = part
-        weighted = part * gain[:, pl.ds(begin, share)]
+        weighted = part * gain[pl.ds(begin, share)][None]
         normed = (full[:, pl.ds(begin, share)].astype(jnp.float32) - centers[...]) * inverses[...]
         first = first + jnp.sum(weighted, axis=1, keepdims=True)
         second = second + jnp.sum(weighted * normed, axis=1, keepdims=True)
@@ -219,17 +262,16 @@
 
 
 def canvas_kernel(
-    place, offsets, screen, counts,
-    mine, got_left, got_right, from_left, from_right, to_right, mixed, centers, inverses, gain, cot, dwk,
-    grad, upstream, grown, taken, taps,
+    offsets, screen, counts,
+    mine, got_left, got_right, from_left, from_right, to_right, mixed, centers, inverses, gain, taken, dwk,
+    grad, upstream, grown, taps, stage, sems,
 ):
     rows, share = mixed.shape
     half = rows // 2
     lanes = share // 128
-    total = gain.shape[1]
+    total = gain.shape[0]
     height, width = screen[0, 0], screen[0, 1]
-    listed = counts[0, place[1]]
-    begin = pl.multiple_of(place[0] * share, 128)
+    begin = pl.multiple_of(lax.axis_index("ch") * share, 128)
     packed = (
         to_right[half : half + 16, :128].astype(jnp.float32)
         + from_left[half : half + 16, :128].astype(jnp.float32)
@@ -248,29 +290,12 @@
         )
         inverse = inverses[span, :]
         normed = (mixed[span, :].astype(jnp.float32) - centers[span, :]) * inverse
-        weighted = norm_grad * gain[:, pl.ds(begin, share)]
+        weighted = norm_grad * gain[pl.ds(begin, share)][None]
         upstream[span, :] = inverse * (weighted - first[span] - normed * second[span])
 
-    low = lax.broadcasted_iota(jnp.int32, (8, 128), 0) < 4
     grown[...] = jnp.zeros_like(grown)
-    taken[...] = jnp.zeros_like(taken)
-
-    def tile(t, carry):
-        r, q = offsets[t, 0], offsets[t, 1]
-        for b in range(lanes):
-            cut = slice(b * 128, (b + 1) * 128)
-            span = pl.ds(pl.multiple_of(t * 16, 16), 16)
-            up = upstream[span, cut]
-            direct = cot[span, cut].astype(jnp.float32)
-            for values, canvas, top in ((up, grown, 3), (direct, taken, 0)):
-                for y in range(4):
-                    pair = values[8 * (y // 2) : 8 * (y // 2) + 8]
-                    pair = pltpu.roll(pair, 4, 0) if y % 2 else pair
-                    columns = pl.ds(q + LEFT, 8)
-                    canvas[b, r + top + y, columns, :] += jnp.where(low, pair, 0.0)
-        return carry
-
-    lax.fori_loop(0, listed, tile, 0)
+    place_tiles(offsets, counts[lax.axis_index("img")], upstream, grown, 3)
+    stores = []
     pairs = 2
     for b in range(lanes):
         cut = slice(b * 128, (b + 1) * 128)
@@ -296,10 +321,15 @@
                                 sums[d][x] = term if sums[d][x] is None else sums[d][x] + term
             for d in range(pairs):
                 whole = jnp.concatenate(sums[d], 0) + taken[b, y + d, LEFT : LEFT + SIDE, :]
-                grad[y + d, :, cut] = jnp.where(inside_of(SIDE, y + d, height, width), whole, 0.0)
+                stage[y + d, :, cut] = jnp.where(inside_of(SIDE, y + d, height, width), whole, 0.0)
             return carry
 
         lax.fori_loop(0, SIDE // pairs, line, 0)
+        store = pltpu.make_async_copy(stage.at[:, :, cut], grad.at[:, :, cut], sems.at[b])
+        store.start()
+        stores.append(store)
+    for store in stores:
+        store.wait()
 
 
 def shift(x, by):
@@ -329,7 +359,7 @@
     layer_scale,
 ):
     f32, bf16 = jnp.float32, jnp.bfloat16
-    struct = jax.ShapeDtypeStruct
+    struct = pltpu.VMEM
     slots = tile_offsets.shape[0]
     share = canvas.shape[2]
     width = ln_gain.shape[0]
@@ -337,27 +367,26 @@
     rows = slots * TS * TS
     half = rows // 2
     lanes = share // 128
-    place = jnp.stack([lax.axis_index("ch"), lax.axis_index("img")]).astype(jnp.int32)
-    line = lambda v: v.reshape(1, -1)
-
+    offsets = tile_offsets.T
     cot = cotangent.reshape(rows, share)
     cots = ring_gather(cot)
-    mixed = call(
+    mixed, near_in, near_out = call(
         depthwise_kernel,
-        struct((rows, share), bf16),
-        [SMEM, SMEM, VMEM, VMEM, VMEM],
+        [struct((rows, share), bf16), struct(w_in.shape, bf16), struct(w_out.shape, bf16)],
+        [SMEM, SMEM, VMEM, VMEM, VMEM, HBM, HBM],
         [
             pltpu.VMEM((lanes, PAD_ROWS, PAD_COLS, 128), f32),
             pltpu.VMEM((28, 8, 128), f32),
-        ],
-    )(tile_offsets, screen_size, canvas, dw_kernel, line(dw_bias))
+            pltpu.SemaphoreType.DMA((2,)),
+        ],
+    )(offsets, screen_size, canvas, dw_kernel, dw_bias, w_in, w_out)
     mixes = ring_gather(mixed)
-    hidden = call(
+    hidden, taken = call(
         hidden_kernel,
-        struct((rows, hid), f32),
-        [SMEM] + [VMEM] * 7,
+        [struct((rows, hid), f32), struct((lanes, SIDE, PAD_COLS, 128), f32)],
+        [SMEM] * 2 + [VMEM] * 7,
         [pltpu.VMEM((rows, width), bf16)],
-    )(place, *cots, line(layer_scale), w_out)
+    )(offsets, tile_counts, *cots, layer_scale, near_out)
     to_right, to_left, next_right, next_left, mine, centers, inverses = call(
         block_kernel,
         [
@@ -369,13 +398,14 @@
             struct((rows, 1), f32),
             struct((rows, 1), f32),
         ],
-        [SMEM] + [VMEM] * 10,
+        [VMEM] * 10,
         [
             pltpu.VMEM((rows, width), bf16),
             pltpu.VMEM((rows, width), bf16),
             pltpu.VMEM((rows, hid), bf16),
         ],
-    )(place, *mixes, line(ln_gain), line(ln_bias), w_in, line(b_in), hidden)
+        limit=24,
+    )(*mixes, ln_gain, ln_bias, near_in, b_in, hidden)
     from_left, from_right = shift(to_right, 1), shift(to_left, -1)
     go_right, go_left = call(
         middle_kernel,
@@ -385,18 +415,20 @@
     got_left, got_right = shift(go_right, 1), shift(go_left, -1)
     return call(
         canvas_kernel,
-        struct(canvas.shape, f32),
-        [SMEM] * 4 + [VMEM] * 12,
+        jax.ShapeDtypeStruct(canvas.shape, f32),
+        [SMEM] * 3 + [VMEM] * 12,
         [
             pltpu.VMEM((rows, share), f32),
             pltpu.VMEM((lanes, PAD_ROWS, PAD_COLS, 128), f32),
-            pltpu.VMEM((lanes, SIDE, PAD_COLS, 128), f32),
             pltpu.VMEM((49, 8, 128), f32),
-        ],
+            pltpu.VMEM(canvas.shape, f32),
+            pltpu.SemaphoreType.DMA((lanes,)),
+        ],
+        out_specs=HBM,
     )(
-        place, tile_offsets, screen_size, line(tile_counts),
+        offsets, screen_size, tile_counts,
         mine, got_left, got_right, from_left, from_right, to_right, mixed, centers, inverses,
-        line(ln_gain), cot, dw_kernel,
+        ln_gain, taken, dw_kernel,
     )
 
 

time: 95.8 us -> 69.9 us (0.73)
  Pallas kernels: 40.4 us -> 26.8 us
  local copies, waits for them, and re-layouts: 13.1 us -> 3.8 us
  waiting for transfers between devices: 19.8 us -> 17 us
    pallas_call x5, Pallas kernels: 40.4 us -> 26.8 us  [held(): run(*(pltpu.with_memory_space_constraint(a, pltpu.VMEM if spec is VMEM el...]
    reshape x5 -> x0, local copies, waits for them, and re-layouts: 6.42 us -> none  [shards(): line = lambda v: v.reshape(1, -1)]
    unnamed x27 -> x16, local copies, waits for them, and re-layouts: 5.52 us -> 2.63 us
    ppermute x12, waiting for transfers between devices: 19.8 us -> 17 us  [shift(): return lax.ppermute(x, 'ch', [(i, (i + by) % n) for i in range(n)])]
  transfers between devices with their start and end apart: 12 -> 12, of which waited for: 5 -> 4; matrix products, arithmetic and copies ran while one was open for 9% -> 0% of each run, Pallas kernels for 15% -> 14%
where the time goes in v2:
time: 69.9 us; the launch traced here: 69 us
  Pallas kernels  26.8 us (38%)
  starting transfers between devices  21.1 us (30%)
  waiting for transfers between devices  17 us (24%)
  local copies, waits for them, and re-layouts  3.8 us (5%)
    pallas_call x5, Pallas kernels, held(): run(*(pltpu.with_memory_space_constraint(a, pltpu.VMEM if spec is VMEM el...  26.8 us
    ppermute x12, starting transfers between devices, shift(): return lax.ppermute(x, 'ch', [(i, (i + by) % n) for i in range(n)])  21.1 us
    ppermute x12, waiting for transfers between devices, shift(): return lax.ppermute(x, 'ch', [(i, (i + by) % n) for i in range(n)])  17 us
    unnamed x16, local copies, waits for them, and re-layouts  2.63 us
  transfers between devices with their start and end apart: 12, of which 4 were waited for; matrix products, arithmetic and copies ran while one was open for 0% of the time, Pallas kernels for 14%

profile of v2, /device:TPU:28, one launch (start us, length us, event | category | flops | bytes accessed | tf_op | source)
XLA Modules:
  0.0 69.0 jit_solution(5326590644262144758)
XLA Ops:
  0.0 1.1 %reshape.3.own = bf16[512,384]{1,0:T(8,128)(2,1)S(1)} reshape(bf16[32,4,4,384]{3,2,1,0:T(4,128)(2,1)} %param.17) | data formatting | bytes 786432 | tf_op jit(solution)/shard_map/reshape | solution.py:371
  1.1 2.0 %collective-permute-start.4 = (bf16[512,384]{1,0:T(8,128)(2,1)S(1)}, bf16[512,384]{1,0:T(8,128)(2,1)S(1)}, u32[]{:S(2)}, u32[]{:S(2)}) collective-permute-start(bf16[512,384]{1,0:T(8,128)(2,1)S(1)} %reshape.3.own), channel_id=1, source_target_pairs={{0,1},{1,2},{2,3},{3,0},{4,5},{5,6},{6,7},{7,4},{8,9},{9,10},{10,1... | collective-permute-start | bytes 1179656 | tf_op jit(solution)/shard_map/ppermute | solution.py:337
  3.1 2.2 %collective-permute-start.5 = (bf16[512,384]{1,0:T(8,128)(2,1)S(1)}, bf16[512,384]{1,0:T(8,128)(2,1)S(1)}, u32[]{:S(2)}, u32[]{:S(2)}) collective-permute-start(bf16[512,384]{1,0:T(8,128)(2,1)S(1)} %reshape.3.own), channel_id=1, source_target_pairs={{0,3},{1,0},{2,1},{3,2},{4,7},{5,4},{6,5},{7,6},{8,11},{9,8},{10,9... | collective-permute-start | bytes 1179656 | tf_op jit(solution)/shard_map/ppermute | solution.py:337
  5.3 0.0 copy-start
  5.3 1.1 %copy-done = bf16[32,32,384]{2,1,0:T(8,128)(2,1)S(1)} copy-done((bf16[32,32,384]{2,1,0:T(8,128)(2,1)S(1)}, bf16[32,32,384]{2,1,0:T(8,128)(2,1)}, u32[]{:S(2)}) %copy-start) | copy-done | bytes 786456
  6.4 0.0 copy-start.1
  6.4 0.8 %copy-done.1 = bf16[49,384]{1,0:T(8,128)(2,1)S(1)} copy-done((bf16[49,384]{1,0:T(8,128)(2,1)S(1)}, bf16[49,384]{1,0:T(8,128)(2,1)}, u32[]{:S(2)}) %copy-start.1) | copy-done | bytes 37656
  7.2 0.0 copy-start.7
  7.2 0.7 copy-done.7
  7.9 0.0 copy-start.4
  7.9 5.7 %shard_map.127 = (bf16[512,384]{1,0:T(8,128)(2,1)S(1)}, bf16[1536,1536]{1,0:T(8,128)(2,1)S(1)}, bf16[1536,1536]{1,0:T(8,128)(2,1)S(1)}) custom-call(s32[2,32]{1,0:T(2,128)} %bitcast.1, s32[1,2]{1,0:T(1,128)} %screen.3, bf16[32,32,384]{2,1,0:T(8,128)(2,1)S(1)} %copy-done, bf16[49,384]{1,0:T(8,128)(2,1)S(1)} %copy-done.1, f32[384]{0:T(512)S(1)} %copy-done.7, ...), custom_call_target="tpu_custom_call" | custom-call | tf_op jit(solution)/shard_map/pallas_call | solution.py:36
  13.6 0.0 copy-start.3
  13.6 0.0 copy-start.5
  13.7 0.0 copy-start.6
  13.7 0.1 collective-permute-start
  13.7 3.2 %collective-permute-start.1 = (bf16[512,384]{1,0:T(8,128)(2,1)S(1)}, bf16[512,384]{1,0:T(8,128)(2,1)S(1)}, u32[]{:S(2)}, u32[]{:S(2)}) collective-permute-start(bf16[512,384]{1,0:T(8,128)(2,1)S(1)} %get-tuple-element.19.own.mixed), channel_id=1, source_target_pairs={{0,3},{1,0},{2,1},{3,2},{4,7},{5,4},{6,5},{7,6},{8,11},{9,8},{10,9... | collective-permute-start | bytes 1179656 | tf_op jit(solution)/shard_map/ppermute | solution.py:337
  17.0 0.0 collective-permute-done.4.left
  17.0 0.1 collective-permute-start.6
  17.1 0.0 collective-permute-done.5.right
  17.1 3.3 %collective-permute-start.7 = (bf16[256,384]{1,0:T(8,128)(2,1)S(1)}, bf16[256,384]{1,0:T(8,128)(2,1)S(1)}, u32[]{:S(2)}, u32[]{:S(2)}) collective-permute-start(bf16[256,384]{1,0:T(8,128)(2,1)S(1)} %slice.19), channel_id=1, source_target_pairs={{0,3},{1,0},{2,1},{3,2},{4,7},{5,4},{6,5},{7,6},{8,11},{9,8},{10,9... | collective-permute-start | bytes 589832 | tf_op jit(solution)/shard_map/ppermute | solution.py:337
  20.4 6.6 %collective-permute-done.left = bf16[512,384]{1,0:T(8,128)(2,1)S(1)} collective-permute-done((bf16[512,384]{1,0:T(8,128)(2,1)S(1)}, bf16[512,384]{1,0:T(8,128)(2,1)S(1)}, u32[]{:S(2)}, u32[]{:S(2)}) %collective-permute-start) | collective-permute-done | bytes 393248 | tf_op jit(solution)/shard_map/ppermute | solution.py:337
  27.0 0.1 collective-permute-start.2
  27.1 0.0 collective-permute-done.1.right
  27.1 3.3 %collective-permute-start.3 = (bf16[256,384]{1,0:T(8,128)(2,1)S(1)}, bf16[256,384]{1,0:T(8,128)(2,1)S(1)}, u32[]{:S(2)}, u32[]{:S(2)}) collective-permute-start(bf16[256,384]{1,0:T(8,128)(2,1)S(1)} %slice.17), channel_id=1, source_target_pairs={{0,3},{1,0},{2,1},{3,2},{4,7},{5,4},{6,5},{7,6},{8,11},{9,8},{10,9... | collective-permute-start | bytes 589832 | tf_op jit(solution)/shard_map/ppermute | solution.py:337
  30.4 0.8 %collective-permute-done.6.opp_a = bf16[256,384]{1,0:T(8,128)(2,1)S(1)} collective-permute-done((bf16[256,384]{1,0:T(8,128)(2,1)S(1)}, bf16[256,384]{1,0:T(8,128)(2,1)S(1)}, u32[]{:S(2)}, u32[]{:S(2)}) %collective-permute-start.6) | collective-permute-done | bytes 196640 | tf_op jit(solution)/shard_map/ppermute | solution.py:337
  31.2 0.0 collective-permute-done.7.opp_b
  31.2 0.0 copy-done.4
  31.2 4.0 %shard_map.128 = (f32[512,1536]{1,0:T(8,128)S(1)}, f32[3,32,48,128]{3,2,1,0:T(8,128)S(1)}) custom-call(s32[2,32]{1,0:T(2,128)} %bitcast.2, s32[32]{0:T(128)} %counts.3, bf16[512,384]{1,0:T(8,128)(2,1)S(1)} %reshape.3.own, bf16[512,384]{1,0:T(8,128)(2,1)S(1)} %collective-permute-done.4.left, bf16[512,384]{1,0:T(8,128)(2,1)S(1)} %collective-permute-done.5.right, ...), custom_call_target="tpu_custom_call" | custom-call | tf_op jit(solution)/shard_map/pallas_call | solution.py:36
  35.2 0.0 collective-permute-done.2.opp_a
  35.2 0.0 collective-permute-done.3.opp_b
  35.2 0.0 copy-done.3
  35.2 0.0 copy-done.5
  35.3 0.0 copy-done.6
  35.3 0.0 copy-start.2
  35.3 8.2 %shard_map.129 = (bf16[272,384]{1,0:T(8,128)(2,1)S(1)}, bf16[272,384]{1,0:T(8,128)(2,1)S(1)}, bf16[512,384]{1,0:T(8,128)(2,1)S(1)}, bf16[512,384]{1,0:T(8,128)(2...) custom-call(bf16[512,384]{1,0:T(8,128)(2,1)S(1)} %get-tuple-element.19.own.mixed, ...), custom_call_target="tpu_custom_call" | custom-call | tf_op jit(solution)/shard_map/pallas_call | solution.py:36
  43.5 0.6 collective-permute-start.8
  44.1 2.7 %collective-permute-start.9 = (bf16[272,384]{1,0:T(8,128)(2,1)S(1)}, bf16[272,384]{1,0:T(8,128)(2,1)S(1)}, u32[]{:S(2)}, u32[]{:S(2)}) collective-permute-start(bf16[272,384]{1,0:T(8,128)(2,1)S(1)} %get-tuple-element.25), channel_id=1, source_target_pairs={{0,3},{1,0},{2,1},{3,2},{4,7},{5,4},{6,5},{7,6},{8,11},{9,8},{10,9... | collective-permute-start | bytes 626696 | tf_op jit(solution)/shard_map/ppermute | solution.py:337
  46.8 3.8 %collective-permute-done.8.from_left = bf16[272,384]{1,0:T(8,128)(2,1)S(1)} collective-permute-done((bf16[272,384]{1,0:T(8,128)(2,1)S(1)}, bf16[272,384]{1,0:T(8,128)(2,1)S(1)}, u32[]{:S(2)}, u32[]{:S(2)}) %collective-permute-start.8) | collective-permute-done | bytes 208928 | tf_op jit(solution)/shard_map/ppermute | solution.py:337
  50.6 0.0 collective-permute-done.9.from_right
  50.6 0.1 shard_map.130
  50.7 1.2 %collective-permute-start.10 = (bf16[528,384]{1,0:T(8,128)(2,1)S(1)}, bf16[528,384]{1,0:T(8,128)(2,1)S(1)}, u32[]{:S(2)}, u32[]{:S(2)}) collective-permute-start(bf16[528,384]{1,0:T(8,128)(2,1)S(1)} %get-tuple-element.28), channel_id=1, source_target_pairs={{0,1},{1,2},{2,3},{3,0},{4,5},{5,6},{6,7},{7,4},{8,9},{9,10},{10,1... | collective-permute-start | bytes 1216520 | tf_op jit(solution)/shard_map/ppermute | solution.py:337
  52.0 2.3 %collective-permute-start.11 = (bf16[512,384]{1,0:T(8,128)(2,1)S(1)}, bf16[512,384]{1,0:T(8,128)(2,1)S(1)}, u32[]{:S(2)}, u32[]{:S(2)}) collective-permute-start(bf16[512,384]{1,0:T(8,128)(2,1)S(1)} %get-tuple-element.29), channel_id=1, source_target_pairs={{0,3},{1,0},{2,1},{3,2},{4,7},{5,4},{6,5},{7,6},{8,11},{9,8},{10,9... | collective-permute-start | bytes 1179656 | tf_op jit(solution)/shard_map/ppermute | solution.py:337
  54.3 5.8 %collective-permute-done.11.got_right = bf16[512,384]{1,0:T(8,128)(2,1)S(1)} collective-permute-done((bf16[512,384]{1,0:T(8,128)(2,1)S(1)}, bf16[512,384]{1,0:T(8,128)(2,1)S(1)}, u32[]{:S(2)}, u32[]{:S(2)}) %collective-permute-start.11) | collective-permute-done | bytes 393248 | tf_op jit(solution)/shard_map/ppermute | solution.py:337
  60.1 0.0 collective-permute-done.10.got_left
  60.1 0.0 copy-done.2
  60.1 8.8 %shard_map.131 = f32[32,32,384]{2,1,0:T(8,128)} custom-call(s32[2,32]{1,0:T(2,128)} %bitcast.3, s32[1,2]{1,0:T(1,128)} %screen.3, s32[32]{0:T(128)} %counts.3, f32[512,384]{1,0:T(8,128)S(1)} %get-tuple-element.23.mine, bf16[528,384]{1,0:T(8,128)(2,1)S(1)} %collective-permute-done.10.got_left, bf16[512,384]{1,0:T(8,128)(2,1)S(1)} %collective-permute-done.11.got_right, ...), custom_call_target="tpu_custom_call" | custom-call | tf_op jit(solution)/shard_map/pallas_call | solution.py:36
  (4 shorter events, 0.1 us)
Async XLA Ops:
  1.1 15.9 %collective-permute-start.4 = (bf16[512,384]{1,0:T(8,128)(2,1)S(1)}, bf16[512,384]{1,0:T(8,128)(2,1)S(1)}, u32[]{:S(2)}, u32[]{:S(2)}) collective-permute-start(bf16[512,384]{1,0:T(8,128)(2,1)S(1)} %reshape.3.own), channel_id=1, source_target_pairs={{0,1},{1,2},{2,3},{3,0},{4,5},{5,6},{6,7},{7,4},{8,9},{9,10},{10,1... | collective-permute-start | bytes 1179656 | tf_op jit(solution)/shard_map/ppermute | solution.py:337
  3.1 14.0 %collective-permute-start.5 = (bf16[512,384]{1,0:T(8,128)(2,1)S(1)}, bf16[512,384]{1,0:T(8,128)(2,1)S(1)}, u32[]{:S(2)}, u32[]{:S(2)}) collective-permute-start(bf16[512,384]{1,0:T(8,128)(2,1)S(1)} %reshape.3.own), channel_id=1, source_target_pairs={{0,3},{1,0},{2,1},{3,2},{4,7},{5,4},{6,5},{7,6},{8,11},{9,8},{10,9... | collective-permute-start | bytes 1179656 | tf_op jit(solution)/shard_map/ppermute | solution.py:337
  5.3 1.1 %copy-start = (bf16[32,32,384]{2,1,0:T(8,128)(2,1)S(1)}, bf16[32,32,384]{2,1,0:T(8,128)(2,1)}, u32[]{:S(2)}) copy-start(bf16[32,32,384]{2,1,0:T(8,128)(2,1)} %canvas.1) | copy-start | bytes 2359300
  6.4 0.8 %copy-start.1 = (bf16[49,384]{1,0:T(8,128)(2,1)S(1)}, bf16[49,384]{1,0:T(8,128)(2,1)}, u32[]{:S(2)}) copy-start(bf16[49,384]{1,0:T(8,128)(2,1)} %dwk.3) | copy-start | bytes 112900
  7.2 0.7 copy-start.7
  7.9 23.3 %copy-start.4 = (f32[1536]{0:T(1024)S(1)}, f32[1536]{0:T(1024)}, u32[]{:S(2)}) copy-start(f32[1536]{0:T(1024)} %scale.1) | copy-start | bytes 18436
  13.6 21.6 %copy-start.3 = (f32[1536]{0:T(1024)S(1)}, f32[1536]{0:T(1024)}, u32[]{:S(2)}) copy-start(f32[1536]{0:T(1024)} %gain.3) | copy-start | bytes 18436
  13.6 21.6 %copy-start.5 = (f32[1536]{0:T(1024)S(1)}, f32[1536]{0:T(1024)}, u32[]{:S(2)}) copy-start(f32[1536]{0:T(1024)} %bias.3) | copy-start | bytes 18436
  13.7 21.6 %copy-start.6 = (f32[1536]{0:T(1024)S(1)}, f32[1536]{0:T(1024)}, u32[]{:S(2)}) copy-start(f32[1536]{0:T(1024)} %b_in.1) | copy-start | bytes 18436
  13.7 13.3 %collective-permute-start = (bf16[512,384]{1,0:T(8,128)(2,1)S(1)}, bf16[512,384]{1,0:T(8,128)(2,1)S(1)}, u32[]{:S(2)}, u32[]{:S(2)}) collective-permute-start(bf16[512,384]{1,0:T(8,128)(2,1)S(1)} %get-tuple-element.19.own.mixed), channel_id=1, source_target_pairs={{0,1},{1,2},{2,3},{3,0},{4,5},{5,6},{6,7},{7,4},{8,9},{9,10},{10,1... | collective-permute-start | bytes 1179656 | tf_op jit(solution)/shard_map/ppermute | solution.py:337
  13.7 13.3 %collective-permute-start.1 = (bf16[512,384]{1,0:T(8,128)(2,1)S(1)}, bf16[512,384]{1,0:T(8,128)(2,1)S(1)}, u32[]{:S(2)}, u32[]{:S(2)}) collective-permute-start(bf16[512,384]{1,0:T(8,128)(2,1)S(1)} %get-tuple-element.19.own.mixed), channel_id=1, source_target_pairs={{0,3},{1,0},{2,1},{3,2},{4,7},{5,4},{6,5},{7,6},{8,11},{9,8},{10,9... | collective-permute-start | bytes 1179656 | tf_op jit(solution)/shard_map/ppermute | solution.py:337
  17.0 14.2 %collective-permute-start.6 = (bf16[256,384]{1,0:T(8,128)(2,1)S(1)}, bf16[256,384]{1,0:T(8,128)(2,1)S(1)}, u32[]{:S(2)}, u32[]{:S(2)}) collective-permute-start(bf16[256,384]{1,0:T(8,128)(2,1)S(1)} %slice.18), channel_id=1, source_target_pairs={{0,1},{1,2},{2,3},{3,0},{4,5},{5,6},{6,7},{7,4},{8,9},{9,10},{10,1... | collective-permute-start | bytes 589832 | tf_op jit(solution)/shard_map/ppermute | solution.py:337
  17.1 14.1 %collective-permute-start.7 = (bf16[256,384]{1,0:T(8,128)(2,1)S(1)}, bf16[256,384]{1,0:T(8,128)(2,1)S(1)}, u32[]{:S(2)}, u32[]{:S(2)}) collective-permute-start(bf16[256,384]{1,0:T(8,128)(2,1)S(1)} %slice.19), channel_id=1, source_target_pairs={{0,3},{1,0},{2,1},{3,2},{4,7},{5,4},{6,5},{7,6},{8,11},{9,8},{10,9... | collective-permute-start | bytes 589832 | tf_op jit(solution)/shard_map/ppermute | solution.py:337
  27.0 8.2 %collective-permute-start.2 = (bf16[256,384]{1,0:T(8,128)(2,1)S(1)}, bf16[256,384]{1,0:T(8,128)(2,1)S(1)}, u32[]{:S(2)}, u32[]{:S(2)}) collective-permute-start(bf16[256,384]{1,0:T(8,128)(2,1)S(1)} %slice.16), channel_id=1, source_target_pairs={{0,1},{1,2},{2,3},{3,0},{4,5},{5,6},{6,7},{7,4},{8,9},{9,10},{10,1... | collective-permute-start | bytes 589832 | tf_op jit(solution)/shard_map/ppermute | solution.py:337
  27.1 8.1 %collective-permute-start.3 = (bf16[256,384]{1,0:T(8,128)(2,1)S(1)}, bf16[256,384]{1,0:T(8,128)(2,1)S(1)}, u32[]{:S(2)}, u32[]{:S(2)}) collective-permute-start(bf16[256,384]{1,0:T(8,128)(2,1)S(1)} %slice.17), channel_id=1, source_target_pairs={{0,3},{1,0},{2,1},{3,2},{4,7},{5,4},{6,5},{7,6},{8,11},{9,8},{10,9... | collective-permute-start | bytes 589832 | tf_op jit(solution)/shard_map/ppermute | solution.py:337
  35.3 24.8 %copy-start.2 = (bf16[49,384]{1,0:T(8,128)(2,1)S(1)}, bf16[49,384]{1,0:T(8,128)(2,1)}, u32[]{:S(2)}) copy-start(bf16[49,384]{1,0:T(8,128)(2,1)} %dwk.3) | copy-start | bytes 112900
  43.5 7.1 %collective-permute-start.8 = (bf16[272,384]{1,0:T(8,128)(2,1)S(1)}, bf16[272,384]{1,0:T(8,128)(2,1)S(1)}, u32[]{:S(2)}, u32[]{:S(2)}) collective-permute-start(bf16[272,384]{1,0:T(8,128)(2,1)S(1)} %get-tuple-element.24.to_right), channel_id=1, source_target_pairs={{0,1},{1,2},{2,3},{3,0},{4,5},{5,6},{6,7},{7,4},{8,9},{9,10},{10,1... | collective-permute-start | bytes 626696 | tf_op jit(solution)/shard_map/ppermute | solution.py:337
  44.1 6.5 %collective-permute-start.9 = (bf16[272,384]{1,0:T(8,128)(2,1)S(1)}, bf16[272,384]{1,0:T(8,128)(2,1)S(1)}, u32[]{:S(2)}, u32[]{:S(2)}) collective-permute-start(bf16[272,384]{1,0:T(8,128)(2,1)S(1)} %get-tuple-element.25), channel_id=1, source_target_pairs={{0,3},{1,0},{2,1},{3,2},{4,7},{5,4},{6,5},{7,6},{8,11},{9,8},{10,9... | collective-permute-start | bytes 626696 | tf_op jit(solution)/shard_map/ppermute | solution.py:337
  50.7 9.4 %collective-permute-start.10 = (bf16[528,384]{1,0:T(8,128)(2,1)S(1)}, bf16[528,384]{1,0:T(8,128)(2,1)S(1)}, u32[]{:S(2)}, u32[]{:S(2)}) collective-permute-start(bf16[528,384]{1,0:T(8,128)(2,1)S(1)} %get-tuple-element.28), channel_id=1, source_target_pairs={{0,1},{1,2},{2,3},{3,0},{4,5},{5,6},{6,7},{7,4},{8,9},{9,10},{10,1... | collective-permute-start | bytes 1216520 | tf_op jit(solution)/shard_map/ppermute | solution.py:337
  52.0 8.1 %collective-permute-start.11 = (bf16[512,384]{1,0:T(8,128)(2,1)S(1)}, bf16[512,384]{1,0:T(8,128)(2,1)S(1)}, u32[]{:S(2)}, u32[]{:S(2)}) collective-permute-start(bf16[512,384]{1,0:T(8,128)(2,1)S(1)} %get-tuple-element.29), channel_id=1, source_target_pairs={{0,3},{1,0},{2,1},{3,2},{4,7},{5,4},{6,5},{7,6},{8,11},{9,8},{10,9... | collective-permute-start | bytes 1179656 | tf_op jit(solution)/shard_map/ppermute | solution.py:337

commit v3 on v2

--- a/solution.py
+++ b/solution.py
@@ -49,34 +49,34 @@
 
 
 def depthwise_kernel(
-    offsets, screen, canvas, dwk, bias, w_in, w_out, mixed, near_in, near_out, framed, taps, sems
+    offsets, screen, canvas, dwk, bias, w_out, mixed_a, mixed_b, near_out, here, framed, taps, kern_bf, bias_row, sems
 ):
-    fetches = [
-        pltpu.make_async_copy(w_out, near_out, sems.at[0]),
-        pltpu.make_async_copy(w_in, near_in, sems.at[1]),
+    lanes = canvas.shape[2] // 128
+    parts = 4
+    deep = SIDE // parts
+    height, width = screen[0, 0], screen[0, 1]
+    small = [
+        pltpu.make_async_copy(dwk, kern_bf, sems.at[parts]),
+        pltpu.make_async_copy(bias, bias_row, sems.at[parts + 1]),
     ]
-    for fetch in fetches:
+    rows_in = [
+        pltpu.make_async_copy(
+            canvas.at[pl.ds(g * deep, deep)], here.at[pl.ds(g * deep, deep)], sems.at[g]
+        )
+        for g in range(parts)
+    ]
+    weights = pltpu.make_async_copy(w_out, near_out, sems.at[parts + 2])
+    for fetch in (*small, *rows_in, weights):
         fetch.start()
-    lanes = canvas.shape[2] // 128
-    height, width = screen[0, 0], screen[0, 1]
     low = lax.broadcasted_iota(jnp.int32, (8, 128), 0) < 4
+    blank = jnp.zeros((PAD_COLS, 128), jnp.float32)
     for b in range(lanes):
-        cut = slice(b * 128, (b + 1) * 128)
-        blank = jnp.zeros((PAD_COLS, 128), jnp.float32)
         for y in (0, 1, 2, SIDE + 3, SIDE + 4, SIDE + 5):
             framed[b, y] = blank
-
-        def fill(y, carry):
-            framed[b, y + 3, 0:LEFT, :] = blank[:LEFT]
-            framed[b, y + 3, LEFT + SIDE : PAD_COLS, :] = blank[: PAD_COLS - LEFT - SIDE]
-            row = canvas[y, :, cut].astype(jnp.float32)
-            framed[b, y + 3, LEFT : LEFT + SIDE, :] = jnp.where(
-                inside_of(SIDE, y, height, width), row, 0.0
-            )
-            return carry
-
-        lax.fori_loop(0, SIDE, fill, 0, unroll=2)
-        kern = dwk[:, cut].astype(jnp.float32)
+    for fetch in small:
+        fetch.wait()
+    for b in range(lanes):
+        kern = kern_bf[:, b * 128 : (b + 1) * 128].astype(jnp.float32)
         for i in range(7):
             for j in range(4):
                 first = jnp.broadcast_to(kern[7 * i + j][None], (8, 128))
@@ -84,44 +84,51 @@
                     second = jnp.broadcast_to(kern[7 * i + j + 4][None], (8, 128))
                 else:
                     second = jnp.zeros((8, 128), jnp.float32)
-                taps[i * 4 + j] = jnp.where(low, first, second)
-        start = jnp.broadcast_to(bias[cut][None], (8, 128))
-
-        def tile(t, carry):
-            r, q = offsets[0, t], offsets[1, t]
-            sums = [None] * 4
-            for p in range(10):
-                for j in range(4):
-                    seen = framed[b, r + p, pl.ds(q + (LEFT - 3 + j), 8), :]
-                    for y in range(max(0, p - 6), min(3, p) + 1):
-                        term = seen * taps[(p - y) * 4 + j]
-                        sums[y] = term if sums[y] is None else sums[y] + term
-            folded = [s + pltpu.roll(s, 4, 0) + start for s in sums]
-            pair = [jnp.where(low, folded[y], folded[y + 1]) for y in (0, 2)]
-            rows = pl.ds(pl.multiple_of(t * 16, 16), 16)
-            mixed[rows, cut] = jnp.concatenate(pair, 0).astype(jnp.bfloat16)
-            return carry
-
-        lax.fori_loop(0, offsets.shape[1], tile, 0)
-    for fetch in fetches:
-        fetch.wait()
+                taps[b, i * 4 + j] = jnp.where(low, first, second)
+
+    def fill(y, carry):
+        seen = inside_of(SIDE, y, height, width)
+        for b in range(lanes):
+            framed[b, y + 3, 0:LEFT, :] = blank[:LEFT]
+            framed[b, y + 3, LEFT + SIDE : PAD_COLS, :] = blank[: PAD_COLS - LEFT - SIDE]
+            row = here[y, :, b * 128 : (b + 1) * 128].astype(jnp.float32)
+            framed[b, y + 3, LEFT : LEFT + SIDE, :] = jnp.where(seen, row, 0.0)
+        return carry
+
+    for g in range(parts):
+        rows_in[g].wait()
+        lax.fori_loop(g * deep, (g + 1) * deep, fill, 0, unroll=4)
+    count = mixed_a.shape[0] // 16
+    for b in range(lanes):
+        cut = slice(b * 128, (b + 1) * 128)
+        start = jnp.broadcast_to(bias_row[cut][None], (8, 128))
+        for mixed, base in ((mixed_a, 0), (mixed_b, count)):
+
+            def tile(t, carry):
+                r, q = offsets[0, base + t], offsets[1, base + t]
+                sums = [None] * 4
+                for p in range(10):
+                    for j in range(4):
+                        seen = framed[b, r + p, pl.ds(q + (LEFT - 3 + j), 8), :]
+                        for y in range(max(0, p - 6), min(3, p) + 1):
+                            term = seen * taps[b, (p - y) * 4 + j]
+                            sums[y] = term if sums[y] is None else sums[y] + term
+                folded = [s + pltpu.roll(s, 4, 0) + start for s in sums]
+                pair = [jnp.where(low, folded[y], folded[y + 1]) for y in (0, 2)]
+                rows = pl.ds(pl.multiple_of(t * 16, 16), 16)
+                mixed[rows, cut] = jnp.concatenate(pair, 0).astype(jnp.bfloat16)
+                return carry
+
+            lax.fori_loop(0, count, tile, 0, unroll=2)
+    weights.wait()
 
 
 def assemble(full, blocks, change):
-    own, left, right, opp_a, opp_b = blocks
     place = lax.axis_index("ch")
-    share = own.shape[1]
-    half = opp_a.shape[0]
-    rows = own.shape[0]
-    for ref, shift, span in (
-        (own, 0, (0, rows)),
-        (left, 3, (0, rows)),
-        (right, 1, (0, rows)),
-        (opp_a, 2, (0, half)),
-        (opp_b, 2, (half, rows)),
-    ):
-        begin = pl.multiple_of(lax.rem(place + shift, 4) * share, 128)
-        full[span[0] : span[1], pl.ds(begin, share)] = change(ref[...], begin, share)
+    for ref, ahead, row in blocks:
+        rows, share = ref.shape
+        begin = pl.multiple_of(lax.rem(place + ahead, 4) * share, 128)
+        full[row : row + rows, pl.ds(begin, share)] = change(ref[...], begin, share)
 
 
 def place_tiles(offsets, listed, values, canvas, top):
@@ -142,15 +149,26 @@
     lax.fori_loop(0, listed, tile, 0)
 
 
+def two_parts(row):
+    high = row.astype(jnp.bfloat16).astype(jnp.float32)
+    return [high, row - high]
+
+
 def hidden_kernel(
-    offsets, counts, own, left, right, opp_a, opp_b, scale, w_out, hidden, taken, full
+    offsets, counts, own, left, right, opp_a, opp_b, scale, gain, bias, b_in, w_out, w_in,
+    hidden, taken, near_in, sides, full, sem,
 ):
+    fetch = pltpu.make_async_copy(w_in, near_in, sem)
+    fetch.start()
+
     def scaled(block, begin, share):
         return (scale[pl.ds(begin, share)][None] * block.astype(jnp.float32)).astype(jnp.bfloat16)
 
     taken[...] = jnp.zeros_like(taken)
     place_tiles(offsets, counts[lax.axis_index("img")], own, taken, 0)
-    assemble(full, (own, left, right, opp_a, opp_b), scaled)
+    half = opp_a.shape[0]
+    blocks = ((own, 0, 0), (left, 3, 0), (right, 1, 0), (opp_a, 2, 0), (opp_b, 2, half))
+    assemble(full, blocks, scaled)
     step = 512
     for n in range(0, hidden.shape[1], step):
         hidden[:, n : n + step] = lax.dot_general(
@@ -159,6 +177,13 @@
             (((1,), (1,)), ((), ())),
             preferred_element_type=jnp.float32,
         )
+    width = gain.shape[0]
+    lines = two_parts(gain[...][None]) + two_parts(bias[...][None])
+    lines = jnp.concatenate(lines + [jnp.zeros((12, width), jnp.float32)], 0).astype(jnp.bfloat16)
+    fetch.wait()
+    both = jnp.dot(lines, near_in[...], preferred_element_type=jnp.float32)
+    sides[0:1, :] = both[0:1] + both[1:2]
+    sides[1:2, :] = both[2:3] + both[3:4] + b_in[...][None]
 
 
 def gelu_slope(v):
@@ -190,15 +215,26 @@
     )
 
 
+def part_of(act, w_in, ahead):
+    share = w_in.shape[0] // 4
+    begin = pl.multiple_of(lax.rem(lax.axis_index("ch") + ahead, 4) * share, 128)
+    return lax.dot_general(
+        act[...],
+        w_in[pl.ds(begin, share), :],
+        (((1,), (1,)), ((), ())),
+        preferred_element_type=jnp.float32,
+    )
+
+
 def block_kernel(
-    own, left, right, opp_a, opp_b, gain, bias, w_in, b_in, hidden,
-    to_right, to_left, next_right, next_left, mine, centers, inverses, full, scaled, act,
+    own_a, own_b, left_a, left_b, right_a, right_b, opp_a, opp_b, gain, bias, w_in, b_in, hidden, sides,
+    to_right, to_left, act, centers, inverses, full, scaled,
 ):
     rows, width = full.shape
-    share = own.shape[1]
-    place = lax.axis_index("ch")
-    half = rows // 2
-    assemble(full, (own, left, right, opp_a, opp_b), lambda block, begin, share: block)
+    half, share = own_a.shape
+    pairs = ((own_a, own_b, 0), (left_a, left_b, 3), (right_a, right_b, 1), (opp_a, opp_b, 2))
+    blocks = [(ref, ahead, row) for a, b, ahead in pairs for ref, row in ((a, 0), (b, half))]
+    assemble(full, blocks, lambda block, begin, share: block)
     step = 64
     for m in range(0, rows, step):
         values = full[m : m + step, :].astype(jnp.float32)
@@ -207,44 +243,40 @@
         inverse = lax.rsqrt(jnp.mean(apart * apart, axis=1, keepdims=True) + norm_eps)
         centers[m : m + step, :] = center
         inverses[m : m + step, :] = inverse
-        scaled[m : m + step, :] = (apart * inverse * gain[...][None] + bias[...][None]).astype(jnp.bfloat16)
+        scaled[m : m + step, :] = (apart * inverse * gain[...][None] + bias[...][None]).astype(
+            jnp.bfloat16
+        )
     step = 512
+    first = jnp.zeros((rows, 128), jnp.float32)
+    second = jnp.zeros((rows, 128), jnp.float32)
     for n in range(0, width, step):
-        pre = jnp.dot(scaled[...], w_in[:, n : n + step], preferred_element_type=jnp.float32)
-        pre = pre + b_in[n : n + step][None]
-        act[:, n : n + step] = (hidden[:, n : n + step] * gelu_slope(pre)).astype(jnp.bfloat16)
-    first = jnp.zeros((rows, 1), jnp.float32)
-    second = jnp.zeros((rows, 1), jnp.float32)
-    for shift in (2, 1, 3, 0):
-        begin = pl.multiple_of(lax.rem(place + shift, 4) * share, 128)
-        part = lax.dot_general(
-            act[...],
-            w_in[pl.ds(begin, share), :],
-            (((1,), (1,)), ((), ())),
-            preferred_element_type=jnp.float32,
-        )
-        if shift == 2:
-            to_right[:half, :] = part[:half].astype(jnp.bfloat16)
-            to_left[:half, :] = part[half:].astype(jnp.bfloat16)
-        elif shift == 1:
-            next_right[...] = part.astype(jnp.bfloat16)
-        elif shift == 3:
-            next_left[...] = part.astype(jnp.bfloat16)
-        else:
-            mine[...] = part
-        weighted = part * gain[pl.ds(begin, share)][None]
-        normed = (full[:, pl.ds(begin, share)].astype(jnp.float32) - centers[...]) * inverses[...]
-        first = first + jnp.sum(weighted, axis=1, keepdims=True)
-        second = second + jnp.sum(weighted * normed, axis=1, keepdims=True)
+        span = slice(n, n + step)
+        product = jnp.dot(scaled[...], w_in[:, span], preferred_element_type=jnp.float32)
+        pre = product + b_in[span][None]
+        rounded = (hidden[:, span] * gelu_slope(pre)).astype(jnp.bfloat16)
+        act[:, span] = rounded
+        value = rounded.astype(jnp.float32)
+        one = value * sides[0:1, span]
+        two = value * (pre - sides[1:2, span])
+        for k in range(0, step, 128):
+            first = first + one[:, k : k + 128]
+            second = second + two[:, k : k + 128]
+    part = part_of(act, w_in, 2)
+    to_right[:half, :] = part[:half].astype(jnp.bfloat16)
+    to_left[:half, :] = part[half:].astype(jnp.bfloat16)
     packed = []
-    for column in (first, second):
-        line = as_rows(column)
-        high = line.astype(jnp.bfloat16).astype(jnp.float32)
-        packed += [high, line - high]
+    for sums in (first, second):
+        packed += two_parts(as_rows(jnp.sum(sums, axis=1, keepdims=True)))
     sums = jnp.concatenate(packed, 0).astype(jnp.bfloat16)
     for out in (to_right, to_left):
         out[half : half + 16, :] = jnp.zeros((16, share), jnp.bfloat16)
         out[half : half + 16, :128] = sums
+
+
+def parts_kernel(act, w_in, next_right, next_left, mine):
+    next_right[...] = part_of(act, w_in, 1).astype(jnp.bfloat16)
+    next_left[...] = part_of(act, w_in, 3).astype(jnp.bfloat16)
+    mine[...] = part_of(act, w_in, 0)
 
 
 def middle_kernel(from_left, from_right, next_right, next_left, go_right, go_left):
@@ -263,11 +295,11 @@
 
 def canvas_kernel(
     offsets, screen, counts,
-    mine, got_left, got_right, from_left, from_right, to_right, mixed, centers, inverses, gain, taken, dwk,
+    mine, got_left, got_right, from_left, from_right, to_right, mixed_a, mixed_b, centers, inverses, gain, taken, dwk,
     grad, upstream, grown, taps, stage, sems,
 ):
-    rows, share = mixed.shape
-    half = rows // 2
+    half, share = mixed_a.shape
+    rows = 2 * half
     lanes = share // 128
     total = gain.shape[0]
     height, width = screen[0, 0], screen[0, 1]
@@ -289,14 +321,15 @@
             + got_right[span, :].astype(jnp.float32)
         )
         inverse = inverses[span, :]
-        normed = (mixed[span, :].astype(jnp.float32) - centers[span, :]) * inverse
+        mixed = mixed_a[span, :] if m < half else mixed_b[m - half : m - half + step, :]
+        normed = (mixed.astype(jnp.float32) - centers[span, :]) * inverse
         weighted = norm_grad * gain[pl.ds(begin, share)][None]
         upstream[span, :] = inverse * (weighted - first[span] - normed * second[span])
 
     grown[...] = jnp.zeros_like(grown)
     place_tiles(offsets, counts[lax.axis_index("img")], upstream, grown, 3)
     stores = []
-    pairs = 2
+    pairs = 4
     for b in range(lanes):
         cut = slice(b * 128, (b + 1) * 128)
         kern = dwk[:, cut].astype(jnp.float32)
@@ -370,43 +403,55 @@
     offsets = tile_offsets.T
     cot = cotangent.reshape(rows, share)
     cots = ring_gather(cot)
-    mixed, near_in, near_out = call(
+    mixed_a, mixed_b, near_out = call(
         depthwise_kernel,
-        [struct((rows, share), bf16), struct(w_in.shape, bf16), struct(w_out.shape, bf16)],
-        [SMEM, SMEM, VMEM, VMEM, VMEM, HBM, HBM],
+        [struct((half, share), bf16), struct((half, share), bf16), struct(w_out.shape, bf16)],
+        [SMEM, SMEM, HBM, HBM, HBM, HBM],
         [
+            pltpu.VMEM(canvas.shape, bf16),
             pltpu.VMEM((lanes, PAD_ROWS, PAD_COLS, 128), f32),
-            pltpu.VMEM((28, 8, 128), f32),
-            pltpu.SemaphoreType.DMA((2,)),
+            pltpu.VMEM((lanes, 28, 8, 128), f32),
+            pltpu.VMEM(dw_kernel.shape, bf16),
+            pltpu.VMEM(dw_bias.shape, f32),
+            pltpu.SemaphoreType.DMA((7,)),
         ],
-    )(offsets, screen_size, canvas, dw_kernel, dw_bias, w_in, w_out)
-    mixes = ring_gather(mixed)
-    hidden, taken = call(
+    )(offsets, screen_size, canvas, dw_kernel, dw_bias, w_out)
+    left_a, right_b = shift(mixed_a, 1), shift(mixed_b, -1)
+    left_b, right_a = shift(mixed_b, 1), shift(mixed_a, -1)
+    opp_a, opp_b = shift(left_a, 1), shift(right_b, -1)
+    hidden, taken, near_in, sides = call(
         hidden_kernel,
-        [struct((rows, hid), f32), struct((lanes, SIDE, PAD_COLS, 128), f32)],
-        [SMEM] * 2 + [VMEM] * 7,
-        [pltpu.VMEM((rows, width), bf16)],
-    )(offsets, tile_counts, *cots, layer_scale, near_out)
-    to_right, to_left, next_right, next_left, mine, centers, inverses = call(
+        [
+            struct((rows, hid), f32),
+            struct((lanes, SIDE, PAD_COLS, 128), f32),
+            struct(w_in.shape, bf16),
+            struct((8, hid), f32),
+        ],
+        [SMEM] * 2 + [VMEM] * 10 + [HBM],
+        [pltpu.VMEM((rows, width), bf16), pltpu.SemaphoreType.DMA(())],
+    )(offsets, tile_counts, *cots, layer_scale, ln_gain, ln_bias, b_in, near_out, w_in)
+    to_right, to_left, act, centers, inverses = call(
         block_kernel,
         [
             struct((half + 16, share), bf16),
             struct((half + 16, share), bf16),
-            struct((rows, share), bf16),
-            struct((rows, share), bf16),
-            struct((rows, share), f32),
+            struct((rows, hid), bf16),
             struct((rows, 1), f32),
             struct((rows, 1), f32),
         ],
-        [VMEM] * 10,
-        [
-            pltpu.VMEM((rows, width), bf16),
-            pltpu.VMEM((rows, width), bf16),
-            pltpu.VMEM((rows, hid), bf16),
-        ],
+        [VMEM] * 14,
+        [pltpu.VMEM((rows, width), bf16), pltpu.VMEM((rows, width), bf16)],
         limit=24,
-    )(*mixes, ln_gain, ln_bias, near_in, b_in, hidden)
+    )(
+        mixed_a, mixed_b, left_a, left_b, right_a, right_b, opp_a, opp_b,
+        ln_gain, ln_bias, near_in, b_in, hidden, sides,
+    )
     from_left, from_right = shift(to_right, 1), shift(to_left, -1)
+    next_right, next_left, mine = call(
+        parts_kernel,
+        [struct((rows, share), bf16), struct((rows, share), bf16), struct((rows, share), f32)],
+        [VMEM] * 2,
+    )(act, near_in)
     go_right, go_left = call(
         middle_kernel,
         [struct((rows + 16, share), bf16), struct((rows, share), bf16)],
@@ -416,7 +461,7 @@
     return call(
         canvas_kernel,
         jax.ShapeDtypeStruct(canvas.shape, f32),
-        [SMEM] * 3 + [VMEM] * 12,
+        [SMEM] * 3 + [VMEM] * 13,
         [
             pltpu.VMEM((rows, share), f32),
             pltpu.VMEM((lanes, PAD_ROWS, PAD_COLS, 128), f32),
@@ -427,7 +472,7 @@
         out_specs=HBM,
     )(
         offsets, screen_size, tile_counts,
-        mine, got_left, got_right, from_left, from_right, to_right, mixed, centers, inverses,
+        mine, got_left, got_right, from_left, from_right, to_right, mixed_a, mixed_b, centers, inverses,
         ln_gain, taken, dw_kernel,
     )
 

time: 69.9 us -> 63.8 us (0.913)
  waiting for transfers between devices: 17 us -> 14 us
  local copies, waits for them, and re-layouts: 3.8 us -> 1.2 us
    ppermute x12 -> x14, waiting for transfers between devices: 17 us -> 14 us  [shift(): return lax.ppermute(x, 'ch', [(i, (i + by) % n) for i in range(n)])]
    unnamed x16 -> x10, local copies, waits for them, and re-layouts: 2.63 us -> 0.02 us
    pallas_call x5 -> x6, Pallas kernels: 26.8 us -> 27.2 us  [held(): run(*(pltpu.with_memory_space_constraint(a, pltpu.VMEM if spec is VMEM el...]
    ppermute x12 -> x14, starting transfers between devices: 21.1 us -> 20.9 us  [shift(): return lax.ppermute(x, 'ch', [(i, (i + by) % n) for i in range(n)])]
  transfers between devices with their start and end apart: 12 -> 14, of which waited for: 4 -> 6; matrix products, arithmetic and copies ran while one was open for 0% -> 0% of each run, Pallas kernels for 14% -> 21%
where the time goes in v3:
time: 63.8 us; the launch traced here: 63.6 us
  Pallas kernels  27.2 us (43%)
  starting transfers between devices  20.9 us (33%)
  waiting for transfers between devices  14 us (22%)
  local copies, waits for them, and re-layouts  1.2 us (2%)
    pallas_call x6, Pallas kernels, held(): run(*(pltpu.with_memory_space_constraint(a, pltpu.VMEM if spec is VMEM el...  27.2 us
    ppermute x14, starting transfers between devices, shift(): return lax.ppermute(x, 'ch', [(i, (i + by) % n) for i in range(n)])  20.9 us
    ppermute x14, waiting for transfers between devices, shift(): return lax.ppermute(x, 'ch', [(i, (i + by) % n) for i in range(n)])  14 us
  transfers between devices with their start and end apart: 14, of which 6 were waited for; matrix products, arithmetic and copies ran while one was open for 0% of the time, Pallas kernels for 21%

profile of v3, /device:TPU:28, one launch (start us, length us, event | category | flops | bytes accessed | tf_op | source)
XLA Modules:
  0.0 63.6 jit_solution(9746037941039172444)
XLA Ops:
  0.0 0.0 copy-start.1
  0.0 0.0 copy-start.2
  0.0 0.0 copy-start.3
  0.0 0.0 copy-start.4
  0.0 1.1 %reshape.3.own = bf16[512,384]{1,0:T(8,128)(2,1)S(1)} reshape(bf16[32,4,4,384]{3,2,1,0:T(4,128)(2,1)} %param.17) | data formatting | bytes 786432 | tf_op jit(solution)/shard_map/reshape | solution.py:404
  1.2 2.0 %collective-permute-start.6 = (bf16[512,384]{1,0:T(8,128)(2,1)S(1)}, bf16[512,384]{1,0:T(8,128)(2,1)S(1)}, u32[]{:S(2)}, u32[]{:S(2)}) collective-permute-start(bf16[512,384]{1,0:T(8,128)(2,1)S(1)} %reshape.3.own), channel_id=1, source_target_pairs={{0,1},{1,2},{2,3},{3,0},{4,5},{5,6},{6,7},{7,4},{8,9},{9,10},{10,1... | collective-permute-start | bytes 1179656 | tf_op jit(solution)/shard_map/ppermute | solution.py:370
  3.1 2.2 %collective-permute-start.7 = (bf16[512,384]{1,0:T(8,128)(2,1)S(1)}, bf16[512,384]{1,0:T(8,128)(2,1)S(1)}, u32[]{:S(2)}, u32[]{:S(2)}) collective-permute-start(bf16[512,384]{1,0:T(8,128)(2,1)S(1)} %reshape.3.own), channel_id=1, source_target_pairs={{0,3},{1,0},{2,1},{3,2},{4,7},{5,4},{6,5},{7,6},{8,11},{9,8},{10,9... | collective-permute-start | bytes 1179656 | tf_op jit(solution)/shard_map/ppermute | solution.py:370
  5.3 5.8 %shard_map.127 = (bf16[256,384]{1,0:T(8,128)(2,1)S(1)}, bf16[256,384]{1,0:T(8,128)(2,1)S(1)}, bf16[1536,1536]{1,0:T(8,128)(2,1)S(1)}) custom-call(s32[2,32]{1,0:T(2,128)} %bitcast.1, s32[1,2]{1,0:T(1,128)} %screen.3, bf16[32,32,384]{2,1,0:T(8,128)(2,1)} %canvas.1, bf16[49,384]{1,0:T(8,128)(2,1)} %dwk.3, f32[384]{0:T(512)} %bias.3, bf16[1536,1536]{1,0:T(8,128)(2,1)} %w_out.1), custom_call_target="tpu_custom_call" | custom-call | tf_op jit(solution)/shard_map/pallas_call | solution.py:36
  11.1 0.1 collective-permute-start
  11.2 3.2 %collective-permute-start.3 = (bf16[256,384]{1,0:T(8,128)(2,1)S(1)}, bf16[256,384]{1,0:T(8,128)(2,1)S(1)}, u32[]{:S(2)}, u32[]{:S(2)}) collective-permute-start(bf16[256,384]{1,0:T(8,128)(2,1)S(1)} %get-tuple-element.23.own_b.mixed_b), channel_id=1, source_target_pairs={{0,3},{1,0},{2,1},{3,2},{4,7},{5,4},{6,5},{7,6},{8,11},{9,8},{10,9... | collective-permute-start | bytes 589832 | tf_op jit(solution)/shard_map/ppermute | solution.py:370
  14.4 0.0 collective-permute-done.6.left
  14.5 0.1 collective-permute-start.8
  14.6 0.0 collective-permute-done.7.right
  14.6 3.3 %collective-permute-start.9 = (bf16[256,384]{1,0:T(8,128)(2,1)S(1)}, bf16[256,384]{1,0:T(8,128)(2,1)S(1)}, u32[]{:S(2)}, u32[]{:S(2)}) collective-permute-start(bf16[256,384]{1,0:T(8,128)(2,1)S(1)} %slice.9), channel_id=1, source_target_pairs={{0,3},{1,0},{2,1},{3,2},{4,7},{5,4},{6,5},{7,6},{8,11},{9,8},{10,9... | collective-permute-start | bytes 589832 | tf_op jit(solution)/shard_map/ppermute | solution.py:370
  17.9 0.0 collective-permute-start.1
  17.9 2.1 %collective-permute-done.left_a = bf16[256,384]{1,0:T(8,128)(2,1)S(1)} collective-permute-done((bf16[256,384]{1,0:T(8,128)(2,1)S(1)}, bf16[256,384]{1,0:T(8,128)(2,1)S(1)}, u32[]{:S(2)}, u32[]{:S(2)}) %collective-permute-start) | collective-permute-done | bytes 196640 | tf_op jit(solution)/shard_map/ppermute | solution.py:370
  19.9 1.4 %collective-permute-start.2 = (bf16[256,384]{1,0:T(8,128)(2,1)S(1)}, bf16[256,384]{1,0:T(8,128)(2,1)S(1)}, u32[]{:S(2)}, u32[]{:S(2)}) collective-permute-start(bf16[256,384]{1,0:T(8,128)(2,1)S(1)} %get-tuple-element.22.own_a.mixed_a), channel_id=1, source_target_pairs={{0,3},{1,0},{2,1},{3,2},{4,7},{5,4},{6,5},{7,6},{8,11},{9,8},{10,9... | collective-permute-start | bytes 589832 | tf_op jit(solution)/shard_map/ppermute | solution.py:370
  21.4 0.0 collective-permute-done.3.right_b
  21.4 0.6 collective-permute-start.4
  22.0 2.2 %collective-permute-done.8.opp_a = bf16[256,384]{1,0:T(8,128)(2,1)S(1)} collective-permute-done((bf16[256,384]{1,0:T(8,128)(2,1)S(1)}, bf16[256,384]{1,0:T(8,128)(2,1)S(1)}, u32[]{:S(2)}, u32[]{:S(2)}) %collective-permute-start.8) | collective-permute-done | bytes 196640 | tf_op jit(solution)/shard_map/ppermute | solution.py:370
  24.2 1.4 %collective-permute-start.5 = (bf16[256,384]{1,0:T(8,128)(2,1)S(1)}, bf16[256,384]{1,0:T(8,128)(2,1)S(1)}, u32[]{:S(2)}, u32[]{:S(2)}) collective-permute-start(bf16[256,384]{1,0:T(8,128)(2,1)S(1)} %collective-permute-done.3.right_b), channel_id=1, source_target_pairs={{0,3},{1,0},{2,1},{3,2},{4,7},{5,4},{6,5},{7,6},{8,11},{9,8},{10,9... | collective-permute-start | bytes 589832 | tf_op jit(solution)/shard_map/ppermute | solution.py:370
  25.6 0.0 collective-permute-done.9.opp_b
  25.6 0.0 copy-done.1
  25.6 0.0 copy-done.2
  25.6 0.0 copy-done.3
  25.6 0.0 copy-done.4
  25.6 4.9 %shard_map.128 = (f32[512,1536]{1,0:T(8,128)S(1)}, f32[3,32,48,128]{3,2,1,0:T(8,128)S(1)}, bf16[1536,1536]{1,0:T(8,128)(2,1)S(1)}, f32[8,1536]{1,0:T(8,128)S(1)}) custom-call(s32[2,32]{1,0:T(2,128)} %bitcast.2, s32[32]{0:T(128)} %counts.3, bf16[512,384]{1,0:T(8,128)(2,1)S(1)} %reshape.3.own, bf16[512,384]{1,0:T(8,128)(2,1)S(1)} %collective-permute-done.6.left, ...), custom_call_target="tpu_custom_call" | custom-call | tf_op jit(solution)/shard_map/pallas_call | solution.py:36
  30.5 0.0 collective-permute-done.1.left_b
  30.5 0.0 collective-permute-done.2.right_a
  30.5 0.9 %collective-permute-done.4.opp_a = bf16[256,384]{1,0:T(8,128)(2,1)S(1)} collective-permute-done((bf16[256,384]{1,0:T(8,128)(2,1)S(1)}, bf16[256,384]{1,0:T(8,128)(2,1)S(1)}, u32[]{:S(2)}, u32[]{:S(2)}) %collective-permute-start.4) | collective-permute-done | bytes 196640 | tf_op jit(solution)/shard_map/ppermute | solution.py:370
  31.4 0.0 collective-permute-done.5.opp_b
  31.4 5.7 %shard_map.129 = (bf16[272,384]{1,0:T(8,128)(2,1)S(1)}, bf16[272,384]{1,0:T(8,128)(2,1)S(1)}, bf16[512,1536]{1,0:T(8,128)(2,1)S(1)}, f32[512,1]{1,0:T(8,128)S(1)}, f32[512,1]{1,0:T(8,128)S(1)}) custom-call(bf16[256,384]{1,0:T(8,128)(2,1)S(1)} %get-tuple-element.22.own_a.mixed_a, bf16[256,384]{1,0:T(8,128)(2,1)S(1)} %get-tuple-element.23.own_b.mixed_b, ...), custom_call_target="tpu_custom_call" | custom-call | tf_op jit(solution)/shard_map/pallas_call | solution.py:36
  37.2 0.0 copy-start
  37.2 1.1 %collective-permute-start.10 = (bf16[272,384]{1,0:T(8,128)(2,1)S(1)}, bf16[272,384]{1,0:T(8,128)(2,1)S(1)}, u32[]{:S(2)}, u32[]{:S(2)}) collective-permute-start(bf16[272,384]{1,0:T(8,128)(2,1)S(1)} %get-tuple-element.30.to_right), channel_id=1, source_target_pairs={{0,1},{1,2},{2,3},{3,0},{4,5},{5,6},{6,7},{7,4},{8,9},{9,10},{10,1... | collective-permute-start | bytes 626696 | tf_op jit(solution)/shard_map/ppermute | solution.py:370
  38.3 2.2 %collective-permute-start.11 = (bf16[272,384]{1,0:T(8,128)(2,1)S(1)}, bf16[272,384]{1,0:T(8,128)(2,1)S(1)}, u32[]{:S(2)}, u32[]{:S(2)}) collective-permute-start(bf16[272,384]{1,0:T(8,128)(2,1)S(1)} %get-tuple-element.31), channel_id=1, source_target_pairs={{0,3},{1,0},{2,1},{3,2},{4,7},{5,4},{6,5},{7,6},{8,11},{9,8},{10,9... | collective-permute-start | bytes 626696 | tf_op jit(solution)/shard_map/ppermute | solution.py:370
  40.5 2.6 %shard_map.130 = (bf16[512,384]{1,0:T(8,128)(2,1)S(1)}, bf16[512,384]{1,0:T(8,128)(2,1)S(1)}, f32[512,384]{1,0:T(8,128)S(1)}) custom-call(bf16[512,1536]{1,0:T(8,128)(2,1)S(1)} %get-tuple-element.28.act, bf16[1536,1536]{1,0:T(8,128)(2,1)S(1)} %get-tuple-element.25.w_in), custom_call_target="tpu_custom_call" | custom-call | tf_op jit(solution)/shard_map/pallas_call | solution.py:36
  43.1 1.5 %collective-permute-done.10.from_left = bf16[272,384]{1,0:T(8,128)(2,1)S(1)} collective-permute-done((bf16[272,384]{1,0:T(8,128)(2,1)S(1)}, bf16[272,384]{1,0:T(8,128)(2,1)S(1)}, u32[]{:S(2)}, u32[]{:S(2)}) %collective-permute-start.10) | collective-permute-done | bytes 208928 | tf_op jit(solution)/shard_map/ppermute | solution.py:370
  44.6 0.0 collective-permute-done.11.from_right
  44.6 0.1 shard_map.131
  44.7 1.3 %collective-permute-start.12 = (bf16[528,384]{1,0:T(8,128)(2,1)S(1)}, bf16[528,384]{1,0:T(8,128)(2,1)S(1)}, u32[]{:S(2)}, u32[]{:S(2)}) collective-permute-start(bf16[528,384]{1,0:T(8,128)(2,1)S(1)} %get-tuple-element.34), channel_id=1, source_target_pairs={{0,1},{1,2},{2,3},{3,0},{4,5},{5,6},{6,7},{7,4},{8,9},{9,10},{10,1... | collective-permute-start | bytes 1216520 | tf_op jit(solution)/shard_map/ppermute | solution.py:370
  46.0 2.0 %collective-permute-start.13 = (bf16[512,384]{1,0:T(8,128)(2,1)S(1)}, bf16[512,384]{1,0:T(8,128)(2,1)S(1)}, u32[]{:S(2)}, u32[]{:S(2)}) collective-permute-start(bf16[512,384]{1,0:T(8,128)(2,1)S(1)} %get-tuple-element.35), channel_id=1, source_target_pairs={{0,3},{1,0},{2,1},{3,2},{4,7},{5,4},{6,5},{7,6},{8,11},{9,8},{10,9... | collective-permute-start | bytes 1179656 | tf_op jit(solution)/shard_map/ppermute | solution.py:370
  48.0 6.6 %collective-permute-done.13.got_right = bf16[512,384]{1,0:T(8,128)(2,1)S(1)} collective-permute-done((bf16[512,384]{1,0:T(8,128)(2,1)S(1)}, bf16[512,384]{1,0:T(8,128)(2,1)S(1)}, u32[]{:S(2)}, u32[]{:S(2)}) %collective-permute-start.13) | collective-permute-done | bytes 393248 | tf_op jit(solution)/shard_map/ppermute | solution.py:370
  54.6 0.8 %collective-permute-done.12.got_left = bf16[528,384]{1,0:T(8,128)(2,1)S(1)} collective-permute-done((bf16[528,384]{1,0:T(8,128)(2,1)S(1)}, bf16[528,384]{1,0:T(8,128)(2,1)S(1)}, u32[]{:S(2)}, u32[]{:S(2)}) %collective-permute-start.12) | collective-permute-done | bytes 405536 | tf_op jit(solution)/shard_map/ppermute | solution.py:370
  55.4 0.0 copy-done
  55.4 8.0 %shard_map.132 = f32[32,32,384]{2,1,0:T(8,128)} custom-call(s32[2,32]{1,0:T(2,128)} %bitcast.3, s32[1,2]{1,0:T(1,128)} %screen.3, s32[32]{0:T(128)} %counts.3, f32[512,384]{1,0:T(8,128)S(1)} %get-tuple-element.29.mine, bf16[528,384]{1,0:T(8,128)(2,1)S(1)} %collective-permute-done.12.got_left, bf16[512,384]{1,0:T(8,128)(2,1)S(1)} %collective-permute-done.13.got_right, ...), custom_call_target="tpu_custom_call" | custom-call | tf_op jit(solution)/shard_map/pallas_call | solution.py:36
  (2 shorter events, 0.0 us)
Async XLA Ops:
  0.0 25.6 %copy-start.1 = (f32[1536]{0:T(1024)S(1)}, f32[1536]{0:T(1024)}, u32[]{:S(2)}) copy-start(f32[1536]{0:T(1024)} %gain.5) | copy-start | bytes 18436
  0.0 25.6 %copy-start.2 = (f32[1536]{0:T(1024)S(1)}, f32[1536]{0:T(1024)}, u32[]{:S(2)}) copy-start(f32[1536]{0:T(1024)} %bias.5) | copy-start | bytes 18436
  0.0 25.6 %copy-start.3 = (f32[1536]{0:T(1024)S(1)}, f32[1536]{0:T(1024)}, u32[]{:S(2)}) copy-start(f32[1536]{0:T(1024)} %b_in.3) | copy-start | bytes 18436
  0.0 25.6 %copy-start.4 = (f32[1536]{0:T(1024)S(1)}, f32[1536]{0:T(1024)}, u32[]{:S(2)}) copy-start(f32[1536]{0:T(1024)} %scale.1) | copy-start | bytes 18436
  1.2 13.3 %collective-permute-start.6 = (bf16[512,384]{1,0:T(8,128)(2,1)S(1)}, bf16[512,384]{1,0:T(8,128)(2,1)S(1)}, u32[]{:S(2)}, u32[]{:S(2)}) collective-permute-start(bf16[512,384]{1,0:T(8,128)(2,1)S(1)} %reshape.3.own), channel_id=1, source_target_pairs={{0,1},{1,2},{2,3},{3,0},{4,5},{5,6},{6,7},{7,4},{8,9},{9,10},{10,1... | collective-permute-start | bytes 1179656 | tf_op jit(solution)/shard_map/ppermute | solution.py:370
  3.1 11.4 %collective-permute-start.7 = (bf16[512,384]{1,0:T(8,128)(2,1)S(1)}, bf16[512,384]{1,0:T(8,128)(2,1)S(1)}, u32[]{:S(2)}, u32[]{:S(2)}) collective-permute-start(bf16[512,384]{1,0:T(8,128)(2,1)S(1)} %reshape.3.own), channel_id=1, source_target_pairs={{0,3},{1,0},{2,1},{3,2},{4,7},{5,4},{6,5},{7,6},{8,11},{9,8},{10,9... | collective-permute-start | bytes 1179656 | tf_op jit(solution)/shard_map/ppermute | solution.py:370
  11.1 8.8 %collective-permute-start = (bf16[256,384]{1,0:T(8,128)(2,1)S(1)}, bf16[256,384]{1,0:T(8,128)(2,1)S(1)}, u32[]{:S(2)}, u32[]{:S(2)}) collective-permute-start(bf16[256,384]{1,0:T(8,128)(2,1)S(1)} %get-tuple-element.22.own_a.mixed_a), channel_id=1, source_target_pairs={{0,1},{1,2},{2,3},{3,0},{4,5},{5,6},{6,7},{7,4},{8,9},{9,10},{10,1... | collective-permute-start | bytes 589832 | tf_op jit(solution)/shard_map/ppermute | solution.py:370
  11.2 10.2 %collective-permute-start.3 = (bf16[256,384]{1,0:T(8,128)(2,1)S(1)}, bf16[256,384]{1,0:T(8,128)(2,1)S(1)}, u32[]{:S(2)}, u32[]{:S(2)}) collective-permute-start(bf16[256,384]{1,0:T(8,128)(2,1)S(1)} %get-tuple-element.23.own_b.mixed_b), channel_id=1, source_target_pairs={{0,3},{1,0},{2,1},{3,2},{4,7},{5,4},{6,5},{7,6},{8,11},{9,8},{10,9... | collective-permute-start | bytes 589832 | tf_op jit(solution)/shard_map/ppermute | solution.py:370
  14.5 9.7 %collective-permute-start.8 = (bf16[256,384]{1,0:T(8,128)(2,1)S(1)}, bf16[256,384]{1,0:T(8,128)(2,1)S(1)}, u32[]{:S(2)}, u32[]{:S(2)}) collective-permute-start(bf16[256,384]{1,0:T(8,128)(2,1)S(1)} %slice.8), channel_id=1, source_target_pairs={{0,1},{1,2},{2,3},{3,0},{4,5},{5,6},{6,7},{7,4},{8,9},{9,10},{10,1... | collective-permute-start | bytes 589832 | tf_op jit(solution)/shard_map/ppermute | solution.py:370
  14.6 11.0 %collective-permute-start.9 = (bf16[256,384]{1,0:T(8,128)(2,1)S(1)}, bf16[256,384]{1,0:T(8,128)(2,1)S(1)}, u32[]{:S(2)}, u32[]{:S(2)}) collective-permute-start(bf16[256,384]{1,0:T(8,128)(2,1)S(1)} %slice.9), channel_id=1, source_target_pairs={{0,3},{1,0},{2,1},{3,2},{4,7},{5,4},{6,5},{7,6},{8,11},{9,8},{10,9... | collective-permute-start | bytes 589832 | tf_op jit(solution)/shard_map/ppermute | solution.py:370
  17.9 12.7 %collective-permute-start.1 = (bf16[256,384]{1,0:T(8,128)(2,1)S(1)}, bf16[256,384]{1,0:T(8,128)(2,1)S(1)}, u32[]{:S(2)}, u32[]{:S(2)}) collective-permute-start(bf16[256,384]{1,0:T(8,128)(2,1)S(1)} %get-tuple-element.23.own_b.mixed_b), channel_id=1, source_target_pairs={{0,1},{1,2},{2,3},{3,0},{4,5},{5,6},{6,7},{7,4},{8,9},{9,10},{10,1... | collective-permute-start | bytes 589832 | tf_op jit(solution)/shard_map/ppermute | solution.py:370
  19.9 10.6 %collective-permute-start.2 = (bf16[256,384]{1,0:T(8,128)(2,1)S(1)}, bf16[256,384]{1,0:T(8,128)(2,1)S(1)}, u32[]{:S(2)}, u32[]{:S(2)}) collective-permute-start(bf16[256,384]{1,0:T(8,128)(2,1)S(1)} %get-tuple-element.22.own_a.mixed_a), channel_id=1, source_target_pairs={{0,3},{1,0},{2,1},{3,2},{4,7},{5,4},{6,5},{7,6},{8,11},{9,8},{10,9... | collective-permute-start | bytes 589832 | tf_op jit(solution)/shard_map/ppermute | solution.py:370
  21.4 10.1 %collective-permute-start.4 = (bf16[256,384]{1,0:T(8,128)(2,1)S(1)}, bf16[256,384]{1,0:T(8,128)(2,1)S(1)}, u32[]{:S(2)}, u32[]{:S(2)}) collective-permute-start(bf16[256,384]{1,0:T(8,128)(2,1)S(1)} %collective-permute-done.left_a), channel_id=1, source_target_pairs={{0,1},{1,2},{2,3},{3,0},{4,5},{5,6},{6,7},{7,4},{8,9},{9,10},{10,1... | collective-permute-start | bytes 589832 | tf_op jit(solution)/shard_map/ppermute | solution.py:370
  24.2 7.3 %collective-permute-start.5 = (bf16[256,384]{1,0:T(8,128)(2,1)S(1)}, bf16[256,384]{1,0:T(8,128)(2,1)S(1)}, u32[]{:S(2)}, u32[]{:S(2)}) collective-permute-start(bf16[256,384]{1,0:T(8,128)(2,1)S(1)} %collective-permute-done.3.right_b), channel_id=1, source_target_pairs={{0,3},{1,0},{2,1},{3,2},{4,7},{5,4},{6,5},{7,6},{8,11},{9,8},{10,9... | collective-permute-start | bytes 589832 | tf_op jit(solution)/shard_map/ppermute | solution.py:370
  37.2 18.2 %copy-start = (bf16[49,384]{1,0:T(8,128)(2,1)S(1)}, bf16[49,384]{1,0:T(8,128)(2,1)}, u32[]{:S(2)}) copy-start(bf16[49,384]{1,0:T(8,128)(2,1)} %dwk.3) | copy-start | bytes 112900
  37.2 7.4 %collective-permute-start.10 = (bf16[272,384]{1,0:T(8,128)(2,1)S(1)}, bf16[272,384]{1,0:T(8,128)(2,1)S(1)}, u32[]{:S(2)}, u32[]{:S(2)}) collective-permute-start(bf16[272,384]{1,0:T(8,128)(2,1)S(1)} %get-tuple-element.30.to_right), channel_id=1, source_target_pairs={{0,1},{1,2},{2,3},{3,0},{4,5},{5,6},{6,7},{7,4},{8,9},{9,10},{10,1... | collective-permute-start | bytes 626696 | tf_op jit(solution)/shard_map/ppermute | solution.py:370
  38.3 6.3 %collective-permute-start.11 = (bf16[272,384]{1,0:T(8,128)(2,1)S(1)}, bf16[272,384]{1,0:T(8,128)(2,1)S(1)}, u32[]{:S(2)}, u32[]{:S(2)}) collective-permute-start(bf16[272,384]{1,0:T(8,128)(2,1)S(1)} %get-tuple-element.31), channel_id=1, source_target_pairs={{0,3},{1,0},{2,1},{3,2},{4,7},{5,4},{6,5},{7,6},{8,11},{9,8},{10,9... | collective-permute-start | bytes 626696 | tf_op jit(solution)/shard_map/ppermute | solution.py:370
  44.7 10.7 %collective-permute-start.12 = (bf16[528,384]{1,0:T(8,128)(2,1)S(1)}, bf16[528,384]{1,0:T(8,128)(2,1)S(1)}, u32[]{:S(2)}, u32[]{:S(2)}) collective-permute-start(bf16[528,384]{1,0:T(8,128)(2,1)S(1)} %get-tuple-element.34), channel_id=1, source_target_pairs={{0,1},{1,2},{2,3},{3,0},{4,5},{5,6},{6,7},{7,4},{8,9},{9,10},{10,1... | collective-permute-start | bytes 1216520 | tf_op jit(solution)/shard_map/ppermute | solution.py:370
  46.0 8.6 %collective-permute-start.13 = (bf16[512,384]{1,0:T(8,128)(2,1)S(1)}, bf16[512,384]{1,0:T(8,128)(2,1)S(1)}, u32[]{:S(2)}, u32[]{:S(2)}) collective-permute-start(bf16[512,384]{1,0:T(8,128)(2,1)S(1)} %get-tuple-element.35), channel_id=1, source_target_pairs={{0,3},{1,0},{2,1},{3,2},{4,7},{5,4},{6,5},{7,6},{8,11},{9,8},{10,9... | collective-permute-start | bytes 1179656 | tf_op jit(solution)/shard_map/ppermute | solution.py:370

commit v4 on v3

--- a/solution.py
+++ b/solution.py
@@ -49,7 +49,7 @@
 
 
 def depthwise_kernel(
-    offsets, screen, canvas, dwk, bias, w_out, mixed_a, mixed_b, near_out, here, framed, taps, kern_bf, bias_row, sems
+    offsets, screen, canvas, dwk, bias, w_out, mixed_a, mixed_b, near_out, taps, here, framed, kern_bf, bias_row, sems
 ):
     lanes = canvas.shape[2] // 128
     parts = 4
@@ -123,60 +123,55 @@
     weights.wait()
 
 
-def assemble(full, blocks, change):
-    place = lax.axis_index("ch")
-    for ref, ahead, row in blocks:
-        rows, share = ref.shape
-        begin = pl.multiple_of(lax.rem(place + ahead, 4) * share, 128)
-        full[row : row + rows, pl.ds(begin, share)] = change(ref[...], begin, share)
-
-
-def place_tiles(offsets, listed, values, canvas, top):
-    low = lax.broadcasted_iota(jnp.int32, (8, 128), 0) < 4
-
-    def tile(t, carry):
-        r, q = offsets[0, t], offsets[1, t]
-        columns = pl.ds(q + LEFT, 8)
-        span = pl.ds(pl.multiple_of(t * 16, 16), 16)
-        for b in range(values.shape[1] // 128):
-            cells = values[span, b * 128 : (b + 1) * 128].astype(jnp.float32)
-            for y in range(4):
-                pair = cells[8 * (y // 2) : 8 * (y // 2) + 8]
-                pair = pltpu.roll(pair, 4, 0) if y % 2 else pair
-                canvas[b, r + top + y, columns, :] += jnp.where(low, pair, 0.0)
-        return carry
-
-    lax.fori_loop(0, listed, tile, 0)
-
-
 def two_parts(row):
     high = row.astype(jnp.bfloat16).astype(jnp.float32)
     return [high, row - high]
 
 
+def scaled_rows(cells, scale, begin):
+    share = cells.shape[3]
+    flat = cells[...].astype(jnp.float32).reshape(cells.shape[0] * 16, share)
+    return (scale[pl.ds(begin, share)][None] * flat).astype(jnp.bfloat16)
+
+
+def channels_of(ahead, share):
+    return pl.multiple_of(lax.rem(lax.axis_index("ch") + ahead, 4) * share, 128)
+
+
 def hidden_kernel(
-    offsets, counts, own, left, right, opp_a, opp_b, scale, gain, bias, b_in, w_out, w_in,
-    hidden, taken, near_in, sides, full, sem,
+    offsets, counts, own, left, right, scale, gain, bias, b_in, w_out, w_in,
+    hidden, taken, near_in, sides, flat, sem,
 ):
     fetch = pltpu.make_async_copy(w_in, near_in, sem)
     fetch.start()
-
-    def scaled(block, begin, share):
-        return (scale[pl.ds(begin, share)][None] * block.astype(jnp.float32)).astype(jnp.bfloat16)
-
+    share = own.shape[3]
     taken[...] = jnp.zeros_like(taken)
-    place_tiles(offsets, counts[lax.axis_index("img")], own, taken, 0)
-    half = opp_a.shape[0]
-    blocks = ((own, 0, 0), (left, 3, 0), (right, 1, 0), (opp_a, 2, 0), (opp_b, 2, half))
-    assemble(full, blocks, scaled)
+
+    def tile(t, carry):
+        r, q = offsets[0, t], offsets[1, t]
+        for y in range(4):
+            cells = own[t, y].astype(jnp.float32)
+            for b in range(share // 128):
+                taken[b, r + 3 + y, pl.ds(q + LEFT, 4), :] += cells[:, b * 128 : (b + 1) * 128]
+        return carry
+
+    lax.fori_loop(0, counts[lax.axis_index("img")], tile, 0)
+    begins = []
+    for k, (cells, ahead) in enumerate(((own, 0), (left, 3), (right, 1))):
+        begins.append(channels_of(ahead, share))
+        flat[k] = scaled_rows(cells, scale, begins[k])
     step = 512
     for n in range(0, hidden.shape[1], step):
-        hidden[:, n : n + step] = lax.dot_general(
-            full[...],
-            w_out[n : n + step, :],
-            (((1,), (1,)), ((), ())),
-            preferred_element_type=jnp.float32,
-        )
+        total = None
+        for k, begin in enumerate(begins):
+            product = lax.dot_general(
+                flat[k],
+                w_out[n : n + step, pl.ds(begin, share)],
+                (((1,), (1,)), ((), ())),
+                preferred_element_type=jnp.float32,
+            )
+            total = product if total is None else total + product
+        hidden[:, n : n + step] = total
     width = gain.shape[0]
     lines = two_parts(gain[...][None]) + two_parts(bias[...][None])
     lines = jnp.concatenate(lines + [jnp.zeros((12, width), jnp.float32)], 0).astype(jnp.bfloat16)
@@ -217,24 +212,28 @@
 
 def part_of(act, w_in, ahead):
     share = w_in.shape[0] // 4
-    begin = pl.multiple_of(lax.rem(lax.axis_index("ch") + ahead, 4) * share, 128)
     return lax.dot_general(
         act[...],
-        w_in[pl.ds(begin, share), :],
+        w_in[pl.ds(channels_of(ahead, share), share), :],
         (((1,), (1,)), ((), ())),
         preferred_element_type=jnp.float32,
     )
 
 
 def block_kernel(
-    own_a, own_b, left_a, left_b, right_a, right_b, opp_a, opp_b, gain, bias, w_in, b_in, hidden, sides,
-    to_right, to_left, act, centers, inverses, full, scaled,
+    own_a, own_b, left_a, left_b, right_a, right_b, opp_a, opp_b, cot_a, cot_b,
+    gain, bias, scale, w_in, b_in, w_out, hidden, sides,
+    to_right, to_left, act, centers, inverses, full, scaled, flat,
 ):
     rows, width = full.shape
     half, share = own_a.shape
-    pairs = ((own_a, own_b, 0), (left_a, left_b, 3), (right_a, right_b, 1), (opp_a, opp_b, 2))
-    blocks = [(ref, ahead, row) for a, b, ahead in pairs for ref, row in ((a, 0), (b, half))]
-    assemble(full, blocks, lambda block, begin, share: block)
+    for a, b, ahead in ((own_a, own_b, 0), (left_a, left_b, 3), (right_a, right_b, 1), (opp_a, opp_b, 2)):
+        columns = pl.ds(channels_of(ahead, share), share)
+        full[:half, columns] = a[...]
+        full[half:, columns] = b[...]
+    opposite = channels_of(2, share)
+    flat[:half, :] = scaled_rows(cot_a, scale, opposite)
+    flat[half:, :] = scaled_rows(cot_b, scale, opposite)
     step = 64
     for m in range(0, rows, step):
         values = full[m : m + step, :].astype(jnp.float32)
@@ -253,7 +252,13 @@
         span = slice(n, n + step)
         product = jnp.dot(scaled[...], w_in[:, span], preferred_element_type=jnp.float32)
         pre = product + b_in[span][None]
-        rounded = (hidden[:, span] * gelu_slope(pre)).astype(jnp.bfloat16)
+        rest = lax.dot_general(
+            flat[...],
+            w_out[span, pl.ds(opposite, share)],
+            (((1,), (1,)), ((), ())),
+            preferred_element_type=jnp.float32,
+        )
+        rounded = ((hidden[:, span] + rest) * gelu_slope(pre)).astype(jnp.bfloat16)
         act[:, span] = rounded
         value = rounded.astype(jnp.float32)
         one = value * sides[0:1, span]
@@ -273,92 +278,102 @@
         out[half : half + 16, :128] = sums
 
 
-def parts_kernel(act, w_in, next_right, next_left, mine):
-    next_right[...] = part_of(act, w_in, 1).astype(jnp.bfloat16)
-    next_left[...] = part_of(act, w_in, 3).astype(jnp.bfloat16)
+def parts_kernel(act, w_in, keep_right, own_right, own_left, keep_left):
+    half = keep_right.shape[0]
+    for ahead, top, bottom in ((1, keep_right, own_right), (3, own_left, keep_left)):
+        part = part_of(act, w_in, ahead).astype(jnp.bfloat16)
+        top[:half, :] = part[:half]
+        bottom[:half, :] = part[half:]
+    for own in (own_right, own_left):
+        own[half:, :] = jnp.zeros_like(own[half:, :])
+
+
+def mine_kernel(act, w_in, keep, mine):
+    del keep
     mine[...] = part_of(act, w_in, 0)
 
 
-def middle_kernel(from_left, from_right, next_right, next_left, go_right, go_left):
-    rows = next_right.shape[0]
-    half = rows // 2
+def middle_kernel(from_left, from_right, keep_right, keep_left, mine, go_right, go_left):
+    del mine
+    half = keep_right.shape[0]
 
     def add(a, b):
         return (a.astype(jnp.float32) + b.astype(jnp.float32)).astype(jnp.bfloat16)
 
-    go_right[:half, :] = add(next_right[:half, :], from_left[:half, :])
-    go_right[half:rows, :] = next_right[half:, :]
-    go_right[rows : rows + 16, :] = from_left[half : half + 16, :]
-    go_left[:half, :] = next_left[:half, :]
-    go_left[half:, :] = add(next_left[half:, :], from_right[:half, :])
+    go_right[:half, :] = add(keep_right[...], from_left[:half, :])
+    go_right[half : half + 16, :] = from_left[half : half + 16, :]
+    go_left[...] = add(keep_left[...], from_right[:half, :])
 
 
 def canvas_kernel(
     offsets, screen, counts,
-    mine, got_left, got_right, from_left, from_right, to_right, mixed_a, mixed_b, centers, inverses, gain, taken, dwk,
-    grad, upstream, grown, taps, stage, sems,
+    own_right, own_left, sum_left, sum_right, mine, from_left, from_right, to_right,
+    mixed_a, mixed_b, centers, inverses, gain, taken, taps,
+    grad, upstream, grown, stage, sems,
 ):
     half, share = mixed_a.shape
     rows = 2 * half
     lanes = share // 128
     total = gain.shape[0]
     height, width = screen[0, 0], screen[0, 1]
-    begin = pl.multiple_of(lax.axis_index("ch") * share, 128)
+    grown[...] = taken[...]
     packed = (
         to_right[half : half + 16, :128].astype(jnp.float32)
         + from_left[half : half + 16, :128].astype(jnp.float32)
         + from_right[half : half + 16, :128].astype(jnp.float32)
-        + got_left[rows : rows + 16, :128].astype(jnp.float32)
+        + sum_left[half : half + 16, :128].astype(jnp.float32)
     )
     first = as_column((packed[0:4] + packed[4:8]) * (1.0 / total))
     second = as_column((packed[8:12] + packed[12:16]) * (1.0 / total))
+    weight = gain[pl.ds(channels_of(0, share), share)][None]
     step = 64
     for m in range(0, rows, step):
         span = slice(m, m + step)
-        norm_grad = (
-            mine[span, :]
-            + got_left[span, :].astype(jnp.float32)
-            + got_right[span, :].astype(jnp.float32)
-        )
+        if m < half:
+            here = span
+            mixed, one, two = mixed_a, sum_left, own_left
+        else:
+            here = slice(m - half, m - half + step)
+            mixed, one, two = mixed_b, own_right, sum_right
+        norm_grad = mine[span, :] + one[here, :].astype(jnp.float32) + two[here, :].astype(jnp.float32)
         inverse = inverses[span, :]
-        mixed = mixed_a[span, :] if m < half else mixed_b[m - half : m - half + step, :]
-        normed = (mixed.astype(jnp.float32) - centers[span, :]) * inverse
-        weighted = norm_grad * gain[pl.ds(begin, share)][None]
-        upstream[span, :] = inverse * (weighted - first[span] - normed * second[span])
-
-    grown[...] = jnp.zeros_like(grown)
-    place_tiles(offsets, counts[lax.axis_index("img")], upstream, grown, 3)
+        normed = (mixed[here, :].astype(jnp.float32) - centers[span, :]) * inverse
+        upstream[span, :] = inverse * (norm_grad * weight - first[span] - normed * second[span])
+
+    low = lax.broadcasted_iota(jnp.int32, (8, 128), 0) < 4
+
+    def tile(t, carry):
+        r, q = offsets[0, t], offsets[1, t]
+        for b in range(lanes):
+            doubled = []
+            for h in range(2):
+                pair = upstream[pl.ds(pl.multiple_of(t * 16 + 8 * h, 8), 8), b * 128 : (b + 1) * 128]
+                turned = pltpu.roll(pair, 4, 0)
+                doubled += [jnp.where(low, pair, turned), jnp.where(low, turned, pair)]
+            for j in range(4):
+                columns = pl.ds(q + (LEFT - 3 + j), 8)
+                for y in range(10):
+                    seen = grown[b, r + y, columns, :]
+                    for k in range(max(0, y - 6), min(3, y) + 1):
+                        seen = seen + doubled[k] * taps[b, (y - k) * 4 + j]
+                    grown[b, r + y, columns, :] = seen
+        return carry
+
+    lax.fori_loop(0, counts[lax.axis_index("img")], tile, 0)
     stores = []
-    pairs = 4
-    for b in range(lanes):
-        cut = slice(b * 128, (b + 1) * 128)
-        kern = dwk[:, cut].astype(jnp.float32)
-        for k in range(49):
-            taps[k] = jnp.broadcast_to(kern[k][None], (8, 128))
-
-        def line(step, carry):
-            y = step * pairs
-            sums = [[None] * 4 for _ in range(pairs)]
-            for p in range(6 + pairs):
-                for j in range(7):
-                    seen = [
-                        grown[b, y + p, LEFT + 3 - j + 8 * x : LEFT + 3 - j + 8 * x + 8, :]
-                        for x in range(4)
-                    ]
-                    for d in range(pairs):
-                        i = 6 + d - p
-                        if 0 <= i < 7:
-                            tap = taps[7 * i + j]
-                            for x in range(4):
-                                term = seen[x] * tap
-                                sums[d][x] = term if sums[d][x] is None else sums[d][x] + term
-            for d in range(pairs):
-                whole = jnp.concatenate(sums[d], 0) + taken[b, y + d, LEFT : LEFT + SIDE, :]
-                stage[y + d, :, cut] = jnp.where(inside_of(SIDE, y + d, height, width), whole, 0.0)
+    deep = SIDE // 4
+    for g in range(4):
+
+        def line(y, carry):
+            seen = inside_of(SIDE, y, height, width)
+            for b in range(lanes):
+                whole = grown[b, y + 3, LEFT : LEFT + SIDE, :]
+                stage[y, :, b * 128 : (b + 1) * 128] = jnp.where(seen, whole, 0.0)
             return carry
 
-        lax.fori_loop(0, SIDE // pairs, line, 0)
-        store = pltpu.make_async_copy(stage.at[:, :, cut], grad.at[:, :, cut], sems.at[b])
+        lax.fori_loop(g * deep, (g + 1) * deep, line, 0, unroll=4)
+        part = pl.ds(g * deep, deep)
+        store = pltpu.make_async_copy(stage.at[part], grad.at[part], sems.at[g])
         store.start()
         stores.append(store)
     for store in stores:
@@ -368,12 +383,6 @@
 def shift(x, by):
     n = lax.axis_size("ch")
     return lax.ppermute(x, "ch", [(i, (i + by) % n) for i in range(n)])
-
-
-def ring_gather(x):
-    half = x.shape[0] // 2
-    left, right = shift(x, 1), shift(x, -1)
-    return x, left, right, shift(left[:half], 1), shift(right[half:], -1)
 
 
 def shards(
@@ -401,35 +410,41 @@
     half = rows // 2
     lanes = share // 128
     offsets = tile_offsets.T
-    cot = cotangent.reshape(rows, share)
-    cots = ring_gather(cot)
-    mixed_a, mixed_b, near_out = call(
+    left, right = shift(cotangent, 1), shift(cotangent, -1)
+    mixed_a, mixed_b, near_out, taps = call(
         depthwise_kernel,
-        [struct((half, share), bf16), struct((half, share), bf16), struct(w_out.shape, bf16)],
+        [
+            struct((half, share), bf16),
+            struct((half, share), bf16),
+            struct(w_out.shape, bf16),
+            struct((lanes, 28, 8, 128), f32),
+        ],
         [SMEM, SMEM, HBM, HBM, HBM, HBM],
         [
             pltpu.VMEM(canvas.shape, bf16),
             pltpu.VMEM((lanes, PAD_ROWS, PAD_COLS, 128), f32),
-            pltpu.VMEM((lanes, 28, 8, 128), f32),
             pltpu.VMEM(dw_kernel.shape, bf16),
             pltpu.VMEM(dw_bias.shape, f32),
             pltpu.SemaphoreType.DMA((7,)),
         ],
     )(offsets, screen_size, canvas, dw_kernel, dw_bias, w_out)
     left_a, right_b = shift(mixed_a, 1), shift(mixed_b, -1)
+    cot_a, cot_b = shift(left[: slots // 2], 1), shift(right[slots // 2 :], -1)
     left_b, right_a = shift(mixed_b, 1), shift(mixed_a, -1)
     opp_a, opp_b = shift(left_a, 1), shift(right_b, -1)
     hidden, taken, near_in, sides = call(
         hidden_kernel,
         [
             struct((rows, hid), f32),
-            struct((lanes, SIDE, PAD_COLS, 128), f32),
+            struct((lanes, PAD_ROWS, PAD_COLS, 128), f32),
             struct(w_in.shape, bf16),
             struct((8, hid), f32),
         ],
-        [SMEM] * 2 + [VMEM] * 10 + [HBM],
-        [pltpu.VMEM((rows, width), bf16), pltpu.SemaphoreType.DMA(())],
-    )(offsets, tile_counts, *cots, layer_scale, ln_gain, ln_bias, b_in, near_out, w_in)
+        [SMEM] * 2 + [VMEM] * 8 + [HBM],
+        [pltpu.VMEM((3, rows, share), bf16), pltpu.SemaphoreType.DMA(())],
+    )(
+        offsets, tile_counts, cotangent, left, right, layer_scale, ln_gain, ln_bias, b_in, near_out, w_in
+    )
     to_right, to_left, act, centers, inverses = call(
         block_kernel,
         [
@@ -439,41 +454,46 @@
             struct((rows, 1), f32),
             struct((rows, 1), f32),
         ],
-        [VMEM] * 14,
-        [pltpu.VMEM((rows, width), bf16), pltpu.VMEM((rows, width), bf16)],
+        [VMEM] * 18,
+        [
+            pltpu.VMEM((rows, width), bf16),
+            pltpu.VMEM((rows, width), bf16),
+            pltpu.VMEM((rows, share), bf16),
+        ],
         limit=24,
     )(
-        mixed_a, mixed_b, left_a, left_b, right_a, right_b, opp_a, opp_b,
-        ln_gain, ln_bias, near_in, b_in, hidden, sides,
+        mixed_a, mixed_b, left_a, left_b, right_a, right_b, opp_a, opp_b, cot_a, cot_b,
+        ln_gain, ln_bias, layer_scale, near_in, b_in, near_out, hidden, sides,
     )
     from_left, from_right = shift(to_right, 1), shift(to_left, -1)
-    next_right, next_left, mine = call(
+    keep_right, own_right, own_left, keep_left = call(
         parts_kernel,
-        [struct((rows, share), bf16), struct((rows, share), bf16), struct((rows, share), f32)],
+        [struct((half + more, share), bf16) for more in (0, 16, 16, 0)],
         [VMEM] * 2,
     )(act, near_in)
+    got_left, got_right = shift(own_right, 1), shift(own_left, -1)
+    (mine,) = call(mine_kernel, [struct((rows, share), f32)], [VMEM] * 3)(act, near_in, keep_right)
     go_right, go_left = call(
         middle_kernel,
-        [struct((rows + 16, share), bf16), struct((rows, share), bf16)],
-        [VMEM] * 4,
-    )(from_left, from_right, next_right, next_left)
-    got_left, got_right = shift(go_right, 1), shift(go_left, -1)
+        [struct((half + 16, share), bf16), struct((half, share), bf16)],
+        [VMEM] * 5,
+    )(from_left, from_right, keep_right, keep_left, mine)
+    sum_left, sum_right = shift(go_right, 1), shift(go_left, -1)
     return call(
         canvas_kernel,
         jax.ShapeDtypeStruct(canvas.shape, f32),
-        [SMEM] * 3 + [VMEM] * 13,
+        [SMEM] * 3 + [VMEM] * 15,
         [
             pltpu.VMEM((rows, share), f32),
             pltpu.VMEM((lanes, PAD_ROWS, PAD_COLS, 128), f32),
-            pltpu.VMEM((49, 8, 128), f32),
             pltpu.VMEM(canvas.shape, f32),
-            pltpu.SemaphoreType.DMA((lanes,)),
+            pltpu.SemaphoreType.DMA((4,)),
         ],
         out_specs=HBM,
     )(
         offsets, screen_size, tile_counts,
-        mine, got_left, got_right, from_left, from_right, to_right, mixed_a, mixed_b, centers, inverses,
-        ln_gain, taken, dw_kernel,
+        got_left, got_right, sum_left, sum_right, mine, from_left, from_right, to_right,
+        mixed_a, mixed_b, centers, inverses, ln_gain, taken, taps,
     )
 
 

time: 63.8 us -> 64.6 us (1.013)
  starting transfers between devices: 20.9 us -> 24.4 us
  waiting for transfers between devices: 14 us -> 11.6 us
  local copies, waits for them, and re-layouts: 1.2 us -> 0.16 us
  Pallas kernels: 27.2 us -> 28 us
    ppermute x14 -> x16, starting transfers between devices: 20.9 us -> 24.4 us  [shift(): return lax.ppermute(x, 'ch', [(i, (i + by) % n) for i in range(n)])]
    ppermute x14 -> x16, waiting for transfers between devices: 14 us -> 11.6 us  [shift(): return lax.ppermute(x, 'ch', [(i, (i + by) % n) for i in range(n)])]
    reshape x1 -> x0, local copies, waits for them, and re-layouts: 1.13 us -> none  [shards(): cot = cotangent.reshape(rows, share)]
    pallas_call x6 -> x7, Pallas kernels: 27.2 us -> 28 us  [held(): run(*(pltpu.with_memory_space_constraint(a, pltpu.VMEM if spec is VMEM el...]
  transfers between devices with their start and end apart: 14 -> 16, of which waited for: 6 -> 8; matrix products, arithmetic and copies ran while one was open for 0% -> 0% of each run, Pallas kernels for 21% -> 21%
where the time goes in v4:
time: 64.6 us; the launch traced here: 64.5 us
  Pallas kernels  28 us (43%)
  starting transfers between devices  24.4 us (38%)
  waiting for transfers between devices  11.6 us (18%)
    pallas_call x7, Pallas kernels, held(): run(*(pltpu.with_memory_space_constraint(a, pltpu.VMEM if spec is VMEM el...  28 us
    ppermute x16, starting transfers between devices, shift(): return lax.ppermute(x, 'ch', [(i, (i + by) % n) for i in range(n)])  24.4 us
    ppermute x16, waiting for transfers between devices, shift(): return lax.ppermute(x, 'ch', [(i, (i + by) % n) for i in range(n)])  11.6 us
  transfers between devices with their start and end apart: 16, of which 8 were waited for; matrix products, arithmetic and copies ran while one was open for 0% of the time, Pallas kernels for 21%

profile of v4, /device:TPU:28, one launch (start us, length us, event | category | flops | bytes accessed | tf_op | source)
XLA Modules:
  0.0 64.5 jit_solution(53439497372074653)
XLA Ops:
  0.0 0.0 copy-start
  0.0 0.0 copy-start.1
  0.0 0.0 copy-start.3
  0.0 0.0 copy-start.4
  0.0 0.0 copy-start.2
  0.0 2.0 %collective-permute-start.6 = (bf16[32,4,4,384]{3,2,1,0:T(4,128)(2,1)}, bf16[32,4,4,384]{3,2,1,0:T(4,128)(2,1)S(1)}, u32[]{:S(2)}, u32[]{:S(2)}) collective-permute-start(bf16[32,4,4,384]{3,2,1,0:T(4,128)(2,1)} %own.1), channel_id=1, source_target_pairs={{0,1},{1,2},{2,3},{3,0},{4,5},{5,6},{6,7},{7,4},{8,9},{9,10},{10,1... | collective-permute-start | bytes 1179656 | tf_op jit(solution)/shard_map/ppermute | solution.py:385
  2.0 2.2 %collective-permute-start.8 = (bf16[32,4,4,384]{3,2,1,0:T(4,128)(2,1)}, bf16[32,4,4,384]{3,2,1,0:T(4,128)(2,1)S(1)}, u32[]{:S(2)}, u32[]{:S(2)}) collective-permute-start(bf16[32,4,4,384]{3,2,1,0:T(4,128)(2,1)} %own.1), channel_id=1, source_target_pairs={{0,3},{1,0},{2,1},{3,2},{4,7},{5,4},{6,5},{7,6},{8,11},{9,8},{10,9... | collective-permute-start | bytes 1179656 | tf_op jit(solution)/shard_map/ppermute | solution.py:385
  4.2 5.8 %shard_map.127 = (bf16[256,384]{1,0:T(8,128)(2,1)S(1)}, bf16[256,384]{1,0:T(8,128)(2,1)S(1)}, bf16[1536,1536]{1,0:T(8,128)(2,1)S(1)}, f32[3,28,8,128]{3,2,1,0:T(8,128)S(1)}) custom-call(s32[2,32]{1,0:T(2,128)} %bitcast.1, s32[1,2]{1,0:T(1,128)} %screen.3, bf16[32,32,384]{2,1,0:T(8,128)(2,1)} %canvas.1, bf16[49,384]{1,0:T(8,128)(2,1)} %dwk.1, f32[384]{0:T(512)} %bias.3, ...), custom_call_target="tpu_custom_call" | custom-call | tf_op jit(solution)/shard_map/pallas_call | solution.py:36
  10.0 0.1 collective-permute-start
  10.1 3.2 %collective-permute-start.3 = (bf16[256,384]{1,0:T(8,128)(2,1)S(1)}, bf16[256,384]{1,0:T(8,128)(2,1)S(1)}, u32[]{:S(2)}, u32[]{:S(2)}) collective-permute-start(bf16[256,384]{1,0:T(8,128)(2,1)S(1)} %get-tuple-element.25.own_b.mixed_b), channel_id=1, source_target_pairs={{0,3},{1,0},{2,1},{3,2},{4,7},{5,4},{6,5},{7,6},{8,11},{9,8},{10,9... | collective-permute-start | bytes 589832 | tf_op jit(solution)/shard_map/ppermute | solution.py:385
  13.3 0.7 %collective-permute-start.2 = (bf16[256,384]{1,0:T(8,128)(2,1)S(1)}, bf16[256,384]{1,0:T(8,128)(2,1)S(1)}, u32[]{:S(2)}, u32[]{:S(2)}) collective-permute-start(bf16[256,384]{1,0:T(8,128)(2,1)S(1)} %get-tuple-element.24.own_a.mixed_a), channel_id=1, source_target_pairs={{0,3},{1,0},{2,1},{3,2},{4,7},{5,4},{6,5},{7,6},{8,11},{9,8},{10,9... | collective-permute-start | bytes 589832 | tf_op jit(solution)/shard_map/ppermute | solution.py:385
  14.0 3.6 %collective-permute-done.left_a = bf16[256,384]{1,0:T(8,128)(2,1)S(1)} collective-permute-done((bf16[256,384]{1,0:T(8,128)(2,1)S(1)}, bf16[256,384]{1,0:T(8,128)(2,1)S(1)}, u32[]{:S(2)}, u32[]{:S(2)}) %collective-permute-start) | collective-permute-done | bytes 196640 | tf_op jit(solution)/shard_map/ppermute | solution.py:385
  17.7 0.0 collective-permute-start.1
  17.7 1.0 %collective-permute-done.3.right_b = bf16[256,384]{1,0:T(8,128)(2,1)S(1)} collective-permute-done((bf16[256,384]{1,0:T(8,128)(2,1)S(1)}, bf16[256,384]{1,0:T(8,128)(2,1)S(1)}, u32[]{:S(2)}, u32[]{:S(2)}) %collective-permute-start.3) | collective-permute-done | bytes 196640 | tf_op jit(solution)/shard_map/ppermute | solution.py:385
  18.7 1.6 %collective-permute-start.4 = (bf16[256,384]{1,0:T(8,128)(2,1)S(1)}, bf16[256,384]{1,0:T(8,128)(2,1)S(1)}, u32[]{:S(2)}, u32[]{:S(2)}) collective-permute-start(bf16[256,384]{1,0:T(8,128)(2,1)S(1)} %collective-permute-done.left_a), channel_id=1, source_target_pairs={{0,1},{1,2},{2,3},{3,0},{4,5},{5,6},{6,7},{7,4},{8,9},{9,10},{10,1... | collective-permute-start | bytes 589832 | tf_op jit(solution)/shard_map/ppermute | solution.py:385
  20.2 0.0 collective-permute-done.6.left
  20.2 2.1 %collective-permute-start.5 = (bf16[256,384]{1,0:T(8,128)(2,1)S(1)}, bf16[256,384]{1,0:T(8,128)(2,1)S(1)}, u32[]{:S(2)}, u32[]{:S(2)}) collective-permute-start(bf16[256,384]{1,0:T(8,128)(2,1)S(1)} %collective-permute-done.3.right_b), channel_id=1, source_target_pairs={{0,3},{1,0},{2,1},{3,2},{4,7},{5,4},{6,5},{7,6},{8,11},{9,8},{10,9... | collective-permute-start | bytes 589832 | tf_op jit(solution)/shard_map/ppermute | solution.py:385
  22.4 0.1 slice.8
  22.4 0.0 collective-permute-done.8.right
  22.4 0.1 collective-permute-start.7
  22.5 0.1 slice.9
  22.6 0.1 collective-permute-done.2.right_a
  22.7 3.7 %collective-permute-start.9 = (bf16[16,4,4,384]{3,2,1,0:T(4,128)(2,1)S(1)}, bf16[16,4,4,384]{3,2,1,0:T(4,128)(2,1)S(1)}, u32[]{:S(2)}, u32[]{:S(2)}) collective-permute-start(bf16[16,4,4,384]{3,2,1,0:T(4,128)(2,1)S(1)} %slice.9), channel_id=1, source_target_pairs={{0,3},{1,0},{2,1},{3,2},{4,7},{5,4},{6,5},{7,6},{8,11},{9,8},{10,9... | collective-permute-start | bytes 589832 | tf_op jit(solution)/shard_map/ppermute | solution.py:385
  26.4 0.0 copy-done
  26.4 0.0 copy-done.1
  26.4 0.0 copy-done.3
  26.4 0.0 copy-done.4
  26.4 0.0 copy-done.2
  26.5 4.9 %shard_map.128 = (f32[512,1536]{1,0:T(8,128)S(1)}, f32[3,38,48,128]{3,2,1,0:T(8,128)S(1)}, bf16[1536,1536]{1,0:T(8,128)(2,1)S(1)}, f32[8,1536]{1,0:T(8,128)S(1)}) custom-call(s32[2,32]{1,0:T(2,128)} %bitcast.2, s32[32]{0:T(128)} %counts.3, bf16[32,4,4,384]{3,2,1,0:T(4,128)(2,1)S(1)} %copy-done, bf16[32,4,4,384]{3,2,1,0:T(4,128)(2,1)S(1)} %collective-permute-done.6.left, ...), custom_call_target="tpu_custom_call" | custom-call | tf_op jit(solution)/shard_map/pallas_call | solution.py:36
  31.3 0.0 collective-permute-done.1.left_b
  31.4 0.0 collective-permute-done.4.opp_a
  31.4 0.0 collective-permute-done.5.opp_b
  31.4 1.4 %collective-permute-done.7.cot_a = bf16[16,4,4,384]{3,2,1,0:T(4,128)(2,1)S(1)} collective-permute-done((bf16[16,4,4,384]{3,2,1,0:T(4,128)(2,1)S(1)}, bf16[16,4,4,384]{3,2,1,0:T(4,128)(2,1)S(1)}, u32[]{:S(2)}, u32[]{:S(2)}) %collective-permute-start.7) | collective-permute-done | bytes 196640 | tf_op jit(solution)/shard_map/ppermute | solution.py:385
  32.8 0.0 collective-permute-done.9.cot_b
  32.8 7.4 %shard_map.129 = (bf16[272,384]{1,0:T(8,128)(2,1)S(1)}, bf16[272,384]{1,0:T(8,128)(2,1)S(1)}, bf16[512,1536]{1,0:T(8,128)(2,1)S(1)}, f32[512,1]{1,0:T(8,128)S(1)}, f32[512,1]{1,0:T(8,128)S(1)}) custom-call(bf16[256,384]{1,0:T(8,128)(2,1)S(1)} %get-tuple-element.24.own_a.mixed_a, bf16[256,384]{1,0:T(8,128)(2,1)S(1)} %get-tuple-element.25.own_b.mixed_b, ...), custom_call_target="tpu_custom_call" | custom-call | tf_op jit(solution)/shard_map/pallas_call | solution.py:36
  40.2 0.9 %collective-permute-start.13 = (bf16[272,384]{1,0:T(8,128)(2,1)S(1)}, bf16[272,384]{1,0:T(8,128)(2,1)S(1)}, u32[]{:S(2)}, u32[]{:S(2)}) collective-permute-start(bf16[272,384]{1,0:T(8,128)(2,1)S(1)} %get-tuple-element.34), channel_id=1, source_target_pairs={{0,3},{1,0},{2,1},{3,2},{4,7},{5,4},{6,5},{7,6},{8,11},{9,8},{10,9... | collective-permute-start | bytes 626696 | tf_op jit(solution)/shard_map/ppermute | solution.py:385
  41.1 1.2 %collective-permute-start.12 = (bf16[272,384]{1,0:T(8,128)(2,1)S(1)}, bf16[272,384]{1,0:T(8,128)(2,1)S(1)}, u32[]{:S(2)}, u32[]{:S(2)}) collective-permute-start(bf16[272,384]{1,0:T(8,128)(2,1)S(1)} %get-tuple-element.33.to_right), channel_id=1, source_target_pairs={{0,1},{1,2},{2,3},{3,0},{4,5},{5,6},{6,7},{7,4},{8,9},{9,10},{10,1... | collective-permute-start | bytes 626696 | tf_op jit(solution)/shard_map/ppermute | solution.py:385
  42.3 1.8 %shard_map.130 = (bf16[256,384]{1,0:T(8,128)(2,1)S(1)}, bf16[272,384]{1,0:T(8,128)(2,1)S(1)}, bf16[272,384]{1,0:T(8,128)(2,1)S(1)}, bf16[256,384]{1,0:T(8,128)(2,1)S(1)}) custom-call(bf16[512,1536]{1,0:T(8,128)(2,1)S(1)} %get-tuple-element.30.act, bf16[1536,1536]{1,0:T(8,128)(2,1)S(1)} %get-tuple-element.27.w_in), custom_call_target="tpu_custom_call" | custom-call | tf_op jit(solution)/shard_map/pallas_call | solution.py:36
  44.1 1.0 %shard_map.131.mine = f32[512,384]{1,0:T(8,128)S(1)} custom-call(bf16[512,1536]{1,0:T(8,128)(2,1)S(1)} %get-tuple-element.30.act, bf16[1536,1536]{1,0:T(8,128)(2,1)S(1)} %get-tuple-element.27.w_in, bf16[256,384]{1,0:T(8,128)(2,1)S(1)} %get-tuple-element.35.keep.keep_right), custom_call_target="tpu_custom_call" | custom-call | tf_op jit(solution)/shard_map/pallas_call | solution.py:36
  45.1 0.1 collective-permute-start.10
  45.2 3.2 %collective-permute-start.11 = (bf16[272,384]{1,0:T(8,128)(2,1)S(1)}, bf16[272,384]{1,0:T(8,128)(2,1)S(1)}, u32[]{:S(2)}, u32[]{:S(2)}) collective-permute-start(bf16[272,384]{1,0:T(8,128)(2,1)S(1)} %get-tuple-element.32), channel_id=1, source_target_pairs={{0,3},{1,0},{2,1},{3,2},{4,7},{5,4},{6,5},{7,6},{8,11},{9,8},{10,9... | collective-permute-start | bytes 626696 | tf_op jit(solution)/shard_map/ppermute | solution.py:385
  48.4 0.0 collective-permute-done.13.from_right
  48.4 1.6 %collective-permute-done.12.from_left = bf16[272,384]{1,0:T(8,128)(2,1)S(1)} collective-permute-done((bf16[272,384]{1,0:T(8,128)(2,1)S(1)}, bf16[272,384]{1,0:T(8,128)(2,1)S(1)}, u32[]{:S(2)}, u32[]{:S(2)}) %collective-permute-start.12) | collective-permute-done | bytes 208928 | tf_op jit(solution)/shard_map/ppermute | solution.py:385
  50.0 0.1 shard_map.132
  50.1 0.3 collective-permute-start.14
  50.4 3.0 %collective-permute-start.15 = (bf16[256,384]{1,0:T(8,128)(2,1)S(1)}, bf16[256,384]{1,0:T(8,128)(2,1)S(1)}, u32[]{:S(2)}, u32[]{:S(2)}) collective-permute-start(bf16[256,384]{1,0:T(8,128)(2,1)S(1)} %get-tuple-element.38), channel_id=1, source_target_pairs={{0,3},{1,0},{2,1},{3,2},{4,7},{5,4},{6,5},{7,6},{8,11},{9,8},{10,9... | collective-permute-start | bytes 589832 | tf_op jit(solution)/shard_map/ppermute | solution.py:385
  53.4 1.1 %collective-permute-done.10.own_right = bf16[272,384]{1,0:T(8,128)(2,1)S(1)} collective-permute-done((bf16[272,384]{1,0:T(8,128)(2,1)S(1)}, bf16[272,384]{1,0:T(8,128)(2,1)S(1)}, u32[]{:S(2)}, u32[]{:S(2)}) %collective-permute-start.10) | collective-permute-done | bytes 208928 | tf_op jit(solution)/shard_map/ppermute | solution.py:385
  54.5 0.0 collective-permute-done.11.own_left
  54.5 2.1 %collective-permute-done.15.sum_right = bf16[256,384]{1,0:T(8,128)(2,1)S(1)} collective-permute-done((bf16[256,384]{1,0:T(8,128)(2,1)S(1)}, bf16[256,384]{1,0:T(8,128)(2,1)S(1)}, u32[]{:S(2)}, u32[]{:S(2)}) %collective-permute-start.15) | collective-permute-done | bytes 196640 | tf_op jit(solution)/shard_map/ppermute | solution.py:385
  56.6 0.6 collective-permute-done.14.sum_left
  57.2 7.1 %shard_map.133 = f32[32,32,384]{2,1,0:T(8,128)} custom-call(s32[2,32]{1,0:T(2,128)} %bitcast.3, s32[1,2]{1,0:T(1,128)} %screen.3, s32[32]{0:T(128)} %counts.3, bf16[272,384]{1,0:T(8,128)(2,1)S(1)} %collective-permute-done.10.own_right, bf16[272,384]{1,0:T(8,128)(2,1)S(1)} %collective-permute-done.11.own_left, ...), custom_call_target="tpu_custom_call" | custom-call | tf_op jit(solution)/shard_map/pallas_call | solution.py:36
Async XLA Ops:
  0.0 26.4 %copy-start = (bf16[32,4,4,384]{3,2,1,0:T(4,128)(2,1)S(1)}, bf16[32,4,4,384]{3,2,1,0:T(4,128)(2,1)}, u32[]{:S(2)}) copy-start(bf16[32,4,4,384]{3,2,1,0:T(4,128)(2,1)} %own.1) | copy-start | bytes 1179652
  0.0 26.4 %copy-start.1 = (f32[1536]{0:T(1024)S(1)}, f32[1536]{0:T(1024)}, u32[]{:S(2)}) copy-start(f32[1536]{0:T(1024)} %gain.5) | copy-start | bytes 18436
  0.0 26.4 %copy-start.3 = (f32[1536]{0:T(1024)S(1)}, f32[1536]{0:T(1024)}, u32[]{:S(2)}) copy-start(f32[1536]{0:T(1024)} %scale.3) | copy-start | bytes 18436
  0.0 26.4 %copy-start.4 = (f32[1536]{0:T(1024)S(1)}, f32[1536]{0:T(1024)}, u32[]{:S(2)}) copy-start(f32[1536]{0:T(1024)} %b_in.3) | copy-start | bytes 18436
  0.0 26.4 %copy-start.2 = (f32[1536]{0:T(1024)S(1)}, f32[1536]{0:T(1024)}, u32[]{:S(2)}) copy-start(f32[1536]{0:T(1024)} %bias.5) | copy-start | bytes 18436
  0.0 20.2 %collective-permute-start.6 = (bf16[32,4,4,384]{3,2,1,0:T(4,128)(2,1)}, bf16[32,4,4,384]{3,2,1,0:T(4,128)(2,1)S(1)}, u32[]{:S(2)}, u32[]{:S(2)}) collective-permute-start(bf16[32,4,4,384]{3,2,1,0:T(4,128)(2,1)} %own.1), channel_id=1, source_target_pairs={{0,1},{1,2},{2,3},{3,0},{4,5},{5,6},{6,7},{7,4},{8,9},{9,10},{10,1... | collective-permute-start | bytes 1179656 | tf_op jit(solution)/shard_map/ppermute | solution.py:385
  2.0 20.4 %collective-permute-start.8 = (bf16[32,4,4,384]{3,2,1,0:T(4,128)(2,1)}, bf16[32,4,4,384]{3,2,1,0:T(4,128)(2,1)S(1)}, u32[]{:S(2)}, u32[]{:S(2)}) collective-permute-start(bf16[32,4,4,384]{3,2,1,0:T(4,128)(2,1)} %own.1), channel_id=1, source_target_pairs={{0,3},{1,0},{2,1},{3,2},{4,7},{5,4},{6,5},{7,6},{8,11},{9,8},{10,9... | collective-permute-start | bytes 1179656 | tf_op jit(solution)/shard_map/ppermute | solution.py:385
  10.0 7.7 %collective-permute-start = (bf16[256,384]{1,0:T(8,128)(2,1)S(1)}, bf16[256,384]{1,0:T(8,128)(2,1)S(1)}, u32[]{:S(2)}, u32[]{:S(2)}) collective-permute-start(bf16[256,384]{1,0:T(8,128)(2,1)S(1)} %get-tuple-element.24.own_a.mixed_a), channel_id=1, source_target_pairs={{0,1},{1,2},{2,3},{3,0},{4,5},{5,6},{6,7},{7,4},{8,9},{9,10},{10,1... | collective-permute-start | bytes 589832 | tf_op jit(solution)/shard_map/ppermute | solution.py:385
  10.1 8.6 %collective-permute-start.3 = (bf16[256,384]{1,0:T(8,128)(2,1)S(1)}, bf16[256,384]{1,0:T(8,128)(2,1)S(1)}, u32[]{:S(2)}, u32[]{:S(2)}) collective-permute-start(bf16[256,384]{1,0:T(8,128)(2,1)S(1)} %get-tuple-element.25.own_b.mixed_b), channel_id=1, source_target_pairs={{0,3},{1,0},{2,1},{3,2},{4,7},{5,4},{6,5},{7,6},{8,11},{9,8},{10,9... | collective-permute-start | bytes 589832 | tf_op jit(solution)/shard_map/ppermute | solution.py:385
  13.3 9.4 %collective-permute-start.2 = (bf16[256,384]{1,0:T(8,128)(2,1)S(1)}, bf16[256,384]{1,0:T(8,128)(2,1)S(1)}, u32[]{:S(2)}, u32[]{:S(2)}) collective-permute-start(bf16[256,384]{1,0:T(8,128)(2,1)S(1)} %get-tuple-element.24.own_a.mixed_a), channel_id=1, source_target_pairs={{0,3},{1,0},{2,1},{3,2},{4,7},{5,4},{6,5},{7,6},{8,11},{9,8},{10,9... | collective-permute-start | bytes 589832 | tf_op jit(solution)/shard_map/ppermute | solution.py:385
  17.7 13.7 %collective-permute-start.1 = (bf16[256,384]{1,0:T(8,128)(2,1)S(1)}, bf16[256,384]{1,0:T(8,128)(2,1)S(1)}, u32[]{:S(2)}, u32[]{:S(2)}) collective-permute-start(bf16[256,384]{1,0:T(8,128)(2,1)S(1)} %get-tuple-element.25.own_b.mixed_b), channel_id=1, source_target_pairs={{0,1},{1,2},{2,3},{3,0},{4,5},{5,6},{6,7},{7,4},{8,9},{9,10},{10,1... | collective-permute-start | bytes 589832 | tf_op jit(solution)/shard_map/ppermute | solution.py:385
  18.7 12.7 %collective-permute-start.4 = (bf16[256,384]{1,0:T(8,128)(2,1)S(1)}, bf16[256,384]{1,0:T(8,128)(2,1)S(1)}, u32[]{:S(2)}, u32[]{:S(2)}) collective-permute-start(bf16[256,384]{1,0:T(8,128)(2,1)S(1)} %collective-permute-done.left_a), channel_id=1, source_target_pairs={{0,1},{1,2},{2,3},{3,0},{4,5},{5,6},{6,7},{7,4},{8,9},{9,10},{10,1... | collective-permute-start | bytes 589832 | tf_op jit(solution)/shard_map/ppermute | solution.py:385
  20.2 11.2 %collective-permute-start.5 = (bf16[256,384]{1,0:T(8,128)(2,1)S(1)}, bf16[256,384]{1,0:T(8,128)(2,1)S(1)}, u32[]{:S(2)}, u32[]{:S(2)}) collective-permute-start(bf16[256,384]{1,0:T(8,128)(2,1)S(1)} %collective-permute-done.3.right_b), channel_id=1, source_target_pairs={{0,3},{1,0},{2,1},{3,2},{4,7},{5,4},{6,5},{7,6},{8,11},{9,8},{10,9... | collective-permute-start | bytes 589832 | tf_op jit(solution)/shard_map/ppermute | solution.py:385
  22.4 10.4 %collective-permute-start.7 = (bf16[16,4,4,384]{3,2,1,0:T(4,128)(2,1)S(1)}, bf16[16,4,4,384]{3,2,1,0:T(4,128)(2,1)S(1)}, u32[]{:S(2)}, u32[]{:S(2)}) collective-permute-start(bf16[16,4,4,384]{3,2,1,0:T(4,128)(2,1)S(1)} %slice.8), channel_id=1, source_target_pairs={{0,1},{1,2},{2,3},{3,0},{4,5},{5,6},{6,7},{7,4},{8,9},{9,10},{10,1... | collective-permute-start | bytes 589832 | tf_op jit(solution)/shard_map/ppermute | solution.py:385
  22.7 10.1 %collective-permute-start.9 = (bf16[16,4,4,384]{3,2,1,0:T(4,128)(2,1)S(1)}, bf16[16,4,4,384]{3,2,1,0:T(4,128)(2,1)S(1)}, u32[]{:S(2)}, u32[]{:S(2)}) collective-permute-start(bf16[16,4,4,384]{3,2,1,0:T(4,128)(2,1)S(1)} %slice.9), channel_id=1, source_target_pairs={{0,3},{1,0},{2,1},{3,2},{4,7},{5,4},{6,5},{7,6},{8,11},{9,8},{10,9... | collective-permute-start | bytes 589832 | tf_op jit(solution)/shard_map/ppermute | solution.py:385
  40.2 8.2 %collective-permute-start.13 = (bf16[272,384]{1,0:T(8,128)(2,1)S(1)}, bf16[272,384]{1,0:T(8,128)(2,1)S(1)}, u32[]{:S(2)}, u32[]{:S(2)}) collective-permute-start(bf16[272,384]{1,0:T(8,128)(2,1)S(1)} %get-tuple-element.34), channel_id=1, source_target_pairs={{0,3},{1,0},{2,1},{3,2},{4,7},{5,4},{6,5},{7,6},{8,11},{9,8},{10,9... | collective-permute-start | bytes 626696 | tf_op jit(solution)/shard_map/ppermute | solution.py:385
  41.1 8.9 %collective-permute-start.12 = (bf16[272,384]{1,0:T(8,128)(2,1)S(1)}, bf16[272,384]{1,0:T(8,128)(2,1)S(1)}, u32[]{:S(2)}, u32[]{:S(2)}) collective-permute-start(bf16[272,384]{1,0:T(8,128)(2,1)S(1)} %get-tuple-element.33.to_right), channel_id=1, source_target_pairs={{0,1},{1,2},{2,3},{3,0},{4,5},{5,6},{6,7},{7,4},{8,9},{9,10},{10,1... | collective-permute-start | bytes 626696 | tf_op jit(solution)/shard_map/ppermute | solution.py:385
  45.1 9.4 %collective-permute-start.10 = (bf16[272,384]{1,0:T(8,128)(2,1)S(1)}, bf16[272,384]{1,0:T(8,128)(2,1)S(1)}, u32[]{:S(2)}, u32[]{:S(2)}) collective-permute-start(bf16[272,384]{1,0:T(8,128)(2,1)S(1)} %get-tuple-element.31), channel_id=1, source_target_pairs={{0,1},{1,2},{2,3},{3,0},{4,5},{5,6},{6,7},{7,4},{8,9},{9,10},{10,1... | collective-permute-start | bytes 626696 | tf_op jit(solution)/shard_map/ppermute | solution.py:385
  45.2 9.3 %collective-permute-start.11 = (bf16[272,384]{1,0:T(8,128)(2,1)S(1)}, bf16[272,384]{1,0:T(8,128)(2,1)S(1)}, u32[]{:S(2)}, u32[]{:S(2)}) collective-permute-start(bf16[272,384]{1,0:T(8,128)(2,1)S(1)} %get-tuple-element.32), channel_id=1, source_target_pairs={{0,3},{1,0},{2,1},{3,2},{4,7},{5,4},{6,5},{7,6},{8,11},{9,8},{10,9... | collective-permute-start | bytes 626696 | tf_op jit(solution)/shard_map/ppermute | solution.py:385
  50.1 7.1 %collective-permute-start.14 = (bf16[272,384]{1,0:T(8,128)(2,1)S(1)}, bf16[272,384]{1,0:T(8,128)(2,1)S(1)}, u32[]{:S(2)}, u32[]{:S(2)}) collective-permute-start(bf16[272,384]{1,0:T(8,128)(2,1)S(1)} %get-tuple-element.37), channel_id=1, source_target_pairs={{0,1},{1,2},{2,3},{3,0},{4,5},{5,6},{6,7},{7,4},{8,9},{9,10},{10,1... | collective-permute-start | bytes 626696 | tf_op jit(solution)/shard_map/ppermute | solution.py:385
  50.4 6.2 %collective-permute-start.15 = (bf16[256,384]{1,0:T(8,128)(2,1)S(1)}, bf16[256,384]{1,0:T(8,128)(2,1)S(1)}, u32[]{:S(2)}, u32[]{:S(2)}) collective-permute-start(bf16[256,384]{1,0:T(8,128)(2,1)S(1)} %get-tuple-element.38), channel_id=1, source_target_pairs={{0,3},{1,0},{2,1},{3,2},{4,7},{5,4},{6,5},{7,6},{8,11},{9,8},{10,9... | collective-permute-start | bytes 589832 | tf_op jit(solution)/shard_map/ppermute | solution.py:385

commit v5 on v4

--- a/solution.py
+++ b/solution.py
@@ -139,12 +139,13 @@
 
 
 def hidden_kernel(
-    offsets, counts, own, left, right, scale, gain, bias, b_in, w_out, w_in,
-    hidden, taken, near_in, sides, flat, sem,
+    offsets, counts, own, left, right, cot_a, cot_b, scale, gain, bias, b_in, w_out, w_in,
+    hidden_a, hidden_b, taken, near_in, sides, full, sem,
 ):
     fetch = pltpu.make_async_copy(w_in, near_in, sem)
     fetch.start()
     share = own.shape[3]
+    half = hidden_a.shape[0]
     taken[...] = jnp.zeros_like(taken)
 
     def tile(t, carry):
@@ -156,22 +157,19 @@
         return carry
 
     lax.fori_loop(0, counts[lax.axis_index("img")], tile, 0)
-    begins = []
-    for k, (cells, ahead) in enumerate(((own, 0), (left, 3), (right, 1))):
-        begins.append(channels_of(ahead, share))
-        flat[k] = scaled_rows(cells, scale, begins[k])
+    for cells, ahead, row in ((own, 0, 0), (left, 3, 0), (right, 1, 0), (cot_a, 2, 0), (cot_b, 2, half)):
+        begin = channels_of(ahead, share)
+        full[row : row + 16 * cells.shape[0], pl.ds(begin, share)] = scaled_rows(cells, scale, begin)
     step = 512
-    for n in range(0, hidden.shape[1], step):
-        total = None
-        for k, begin in enumerate(begins):
-            product = lax.dot_general(
-                flat[k],
-                w_out[n : n + step, pl.ds(begin, share)],
-                (((1,), (1,)), ((), ())),
-                preferred_element_type=jnp.float32,
-            )
-            total = product if total is None else total + product
-        hidden[:, n : n + step] = total
+    for n in range(0, hidden_a.shape[1], step):
+        product = lax.dot_general(
+            full[...],
+            w_out[n : n + step, :],
+            (((1,), (1,)), ((), ())),
+            preferred_element_type=jnp.float32,
+        )
+        hidden_a[:, n : n + step] = product[:half]
+        hidden_b[:, n : n + step] = product[half:]
     width = gain.shape[0]
     lines = two_parts(gain[...][None]) + two_parts(bias[...][None])
     lines = jnp.concatenate(lines + [jnp.zeros((12, width), jnp.float32)], 0).astype(jnp.bfloat16)
@@ -221,19 +219,14 @@
 
 
 def block_kernel(
-    own_a, own_b, left_a, left_b, right_a, right_b, opp_a, opp_b, cot_a, cot_b,
-    gain, bias, scale, w_in, b_in, w_out, hidden, sides,
-    to_right, to_left, act, centers, inverses, full, scaled, flat,
-):
+    own, left, right, opp, gain, bias, w_in, b_in, hidden, sides, earlier,
+    away, act, centers, inverses, full, scaled,
+):
+    del earlier
     rows, width = full.shape
-    half, share = own_a.shape
-    for a, b, ahead in ((own_a, own_b, 0), (left_a, left_b, 3), (right_a, right_b, 1), (opp_a, opp_b, 2)):
-        columns = pl.ds(channels_of(ahead, share), share)
-        full[:half, columns] = a[...]
-        full[half:, columns] = b[...]
-    opposite = channels_of(2, share)
-    flat[:half, :] = scaled_rows(cot_a, scale, opposite)
-    flat[half:, :] = scaled_rows(cot_b, scale, opposite)
+    share = own.shape[1]
+    for ref, ahead in ((own, 0), (left, 3), (right, 1), (opp, 2)):
+        full[:, pl.ds(channels_of(ahead, share), share)] = ref[...]
     step = 64
     for m in range(0, rows, step):
         values = full[m : m + step, :].astype(jnp.float32)
@@ -252,13 +245,7 @@
         span = slice(n, n + step)
         product = jnp.dot(scaled[...], w_in[:, span], preferred_element_type=jnp.float32)
         pre = product + b_in[span][None]
-        rest = lax.dot_general(
-            flat[...],
-            w_out[span, pl.ds(opposite, share)],
-            (((1,), (1,)), ((), ())),
-            preferred_element_type=jnp.float32,
-        )
-        rounded = ((hidden[:, span] + rest) * gelu_slope(pre)).astype(jnp.bfloat16)
+        rounded = (hidden[:, span] * gelu_slope(pre)).astype(jnp.bfloat16)
         act[:, span] = rounded
         value = rounded.astype(jnp.float32)
         one = value * sides[0:1, span]
@@ -266,85 +253,57 @@
         for k in range(0, step, 128):
             first = first + one[:, k : k + 128]
             second = second + two[:, k : k + 128]
-    part = part_of(act, w_in, 2)
-    to_right[:half, :] = part[:half].astype(jnp.bfloat16)
-    to_left[:half, :] = part[half:].astype(jnp.bfloat16)
+    away[:rows, :] = part_of(act, w_in, 2).astype(jnp.bfloat16)
     packed = []
     for sums in (first, second):
         packed += two_parts(as_rows(jnp.sum(sums, axis=1, keepdims=True)))
-    sums = jnp.concatenate(packed, 0).astype(jnp.bfloat16)
-    for out in (to_right, to_left):
-        out[half : half + 16, :] = jnp.zeros((16, share), jnp.bfloat16)
-        out[half : half + 16, :128] = sums
-
-
-def parts_kernel(act, w_in, keep_right, own_right, own_left, keep_left):
-    half = keep_right.shape[0]
-    for ahead, top, bottom in ((1, keep_right, own_right), (3, own_left, keep_left)):
-        part = part_of(act, w_in, ahead).astype(jnp.bfloat16)
-        top[:half, :] = part[:half]
-        bottom[:half, :] = part[half:]
-    for own in (own_right, own_left):
-        own[half:, :] = jnp.zeros_like(own[half:, :])
-
-
-def mine_kernel(act, w_in, keep, mine):
-    del keep
+    packed += [jnp.zeros((16 - 4 * (rows // 128), 128), jnp.float32)]
+    away[rows : rows + 16, :] = jnp.zeros((16, share), jnp.bfloat16)
+    away[rows : rows + 16, :128] = jnp.concatenate(packed, 0).astype(jnp.bfloat16)
+
+
+def parts_kernel(keep_ahead, own_ahead, act, w_in, away, earlier, keep, own, mine):
+    del earlier
+    rows = act.shape[0]
+    own[:rows, :] = part_of(act, w_in, own_ahead).astype(jnp.bfloat16)
+    own[rows:, :] = away[rows:, :]
+    keep[...] = part_of(act, w_in, keep_ahead).astype(jnp.bfloat16)
     mine[...] = part_of(act, w_in, 0)
 
 
-def middle_kernel(from_left, from_right, keep_right, keep_left, mine, go_right, go_left):
-    del mine
-    half = keep_right.shape[0]
-
-    def add(a, b):
-        return (a.astype(jnp.float32) + b.astype(jnp.float32)).astype(jnp.bfloat16)
-
-    go_right[:half, :] = add(keep_right[...], from_left[:half, :])
-    go_right[half : half + 16, :] = from_left[half : half + 16, :]
-    go_left[...] = add(keep_left[...], from_right[:half, :])
-
-
-def canvas_kernel(
-    offsets, screen, counts,
-    own_right, own_left, sum_left, sum_right, mine, from_left, from_right, to_right,
-    mixed_a, mixed_b, centers, inverses, gain, taken, taps,
-    grad, upstream, grown, stage, sems,
-):
-    half, share = mixed_a.shape
-    rows = 2 * half
-    lanes = share // 128
-    total = gain.shape[0]
-    height, width = screen[0, 0], screen[0, 1]
-    grown[...] = taken[...]
-    packed = (
-        to_right[half : half + 16, :128].astype(jnp.float32)
-        + from_left[half : half + 16, :128].astype(jnp.float32)
-        + from_right[half : half + 16, :128].astype(jnp.float32)
-        + sum_left[half : half + 16, :128].astype(jnp.float32)
-    )
-    first = as_column((packed[0:4] + packed[4:8]) * (1.0 / total))
-    second = as_column((packed[8:12] + packed[12:16]) * (1.0 / total))
+def middle_kernel(come, keep, go):
+    rows = keep.shape[0]
+    total = keep[...].astype(jnp.float32) + come[:rows, :].astype(jnp.float32)
+    go[:rows, :] = total.astype(jnp.bfloat16)
+    go[rows:, :] = come[rows:, :]
+
+
+def add_tiles(
+    base, offsets, counts, mine, got, total, come, away, mixed, centers, inverses, gain, taps, upstream, grown
+):
+    rows, share = mixed.shape
+    width = gain.shape[0]
+    packed = None
+    for ref in (away, come, got, total):
+        lines = ref[rows : rows + 16, :128].astype(jnp.float32)
+        packed = lines if packed is None else packed + lines
+    n = rows // 128
+    first = as_column((packed[0:n] + packed[n : 2 * n]) * (1.0 / width))
+    second = as_column((packed[2 * n : 3 * n] + packed[3 * n : 4 * n]) * (1.0 / width))
     weight = gain[pl.ds(channels_of(0, share), share)][None]
     step = 64
     for m in range(0, rows, step):
         span = slice(m, m + step)
-        if m < half:
-            here = span
-            mixed, one, two = mixed_a, sum_left, own_left
-        else:
-            here = slice(m - half, m - half + step)
-            mixed, one, two = mixed_b, own_right, sum_right
-        norm_grad = mine[span, :] + one[here, :].astype(jnp.float32) + two[here, :].astype(jnp.float32)
+        norm_grad = mine[span, :] + got[span, :].astype(jnp.float32) + total[span, :].astype(jnp.float32)
         inverse = inverses[span, :]
-        normed = (mixed[here, :].astype(jnp.float32) - centers[span, :]) * inverse
+        normed = (mixed[span, :].astype(jnp.float32) - centers[span, :]) * inverse
         upstream[span, :] = inverse * (norm_grad * weight - first[span] - normed * second[span])
 
     low = lax.broadcasted_iota(jnp.int32, (8, 128), 0) < 4
 
     def tile(t, carry):
-        r, q = offsets[0, t], offsets[1, t]
-        for b in range(lanes):
+        r, q = offsets[0, base + t], offsets[1, base + t]
+        for b in range(share // 128):
             doubled = []
             for h in range(2):
                 pair = upstream[pl.ds(pl.multiple_of(t * 16 + 8 * h, 8), 8), b * 128 : (b + 1) * 128]
@@ -353,20 +312,44 @@
             for j in range(4):
                 columns = pl.ds(q + (LEFT - 3 + j), 8)
                 for y in range(10):
-                    seen = grown[b, r + y, columns, :]
+                    more = None
                     for k in range(max(0, y - 6), min(3, y) + 1):
-                        seen = seen + doubled[k] * taps[b, (y - k) * 4 + j]
-                    grown[b, r + y, columns, :] = seen
+                        term = doubled[k] * taps[b, (y - k) * 4 + j]
+                        more = term if more is None else more + term
+                    grown[b, r + y, columns, :] += more
         return carry
 
-    lax.fori_loop(0, counts[lax.axis_index("img")], tile, 0)
+    listed = counts[lax.axis_index("img")] - base
+    lax.fori_loop(0, jnp.clip(listed, 0, rows // 16), tile, 0)
+
+
+def first_tiles_kernel(
+    offsets, counts, mine, got, total, come, away, mixed, centers, inverses, gain, taps, before,
+    grown, upstream,
+):
+    grown[...] = before[...]
+    add_tiles(
+        0, offsets, counts, mine, got, total, come, away, mixed, centers, inverses, gain, taps, upstream, grown
+    )
+
+
+def last_tiles_kernel(
+    offsets, counts, screen, mine, got, total, come, away, mixed, centers, inverses, gain, taps, before,
+    grad, upstream, grown, stage, sems,
+):
+    grown[...] = before[...]
+    add_tiles(
+        mixed.shape[0] // 16,
+        offsets, counts, mine, got, total, come, away, mixed, centers, inverses, gain, taps, upstream, grown,
+    )
+    height, width = screen[0, 0], screen[0, 1]
     stores = []
     deep = SIDE // 4
     for g in range(4):
 
         def line(y, carry):
             seen = inside_of(SIDE, y, height, width)
-            for b in range(lanes):
+            for b in range(mixed.shape[1] // 128):
                 whole = grown[b, y + 3, LEFT : LEFT + SIDE, :]
                 stage[y, :, b * 128 : (b + 1) * 128] = jnp.where(seen, whole, 0.0)
             return carry
@@ -428,72 +411,79 @@
             pltpu.SemaphoreType.DMA((7,)),
         ],
     )(offsets, screen_size, canvas, dw_kernel, dw_bias, w_out)
-    left_a, right_b = shift(mixed_a, 1), shift(mixed_b, -1)
+    left_a, right_a = shift(mixed_a, 1), shift(mixed_a, -1)
     cot_a, cot_b = shift(left[: slots // 2], 1), shift(right[slots // 2 :], -1)
-    left_b, right_a = shift(mixed_b, 1), shift(mixed_a, -1)
-    opp_a, opp_b = shift(left_a, 1), shift(right_b, -1)
-    hidden, taken, near_in, sides = call(
+    opp_a, right_b = shift(left_a, 1), shift(mixed_b, -1)
+    left_b, opp_b = shift(mixed_b, 1), shift(right_b, -1)
+    canvas_like = struct((lanes, PAD_ROWS, PAD_COLS, 128), f32)
+    hidden_a, hidden_b, taken, near_in, sides = call(
         hidden_kernel,
         [
-            struct((rows, hid), f32),
-            struct((lanes, PAD_ROWS, PAD_COLS, 128), f32),
+            struct((half, hid), f32),
+            struct((half, hid), f32),
+            canvas_like,
             struct(w_in.shape, bf16),
             struct((8, hid), f32),
         ],
-        [SMEM] * 2 + [VMEM] * 8 + [HBM],
-        [pltpu.VMEM((3, rows, share), bf16), pltpu.SemaphoreType.DMA(())],
+        [SMEM] * 2 + [VMEM] * 10 + [HBM],
+        [pltpu.VMEM((rows, width), bf16), pltpu.SemaphoreType.DMA(())],
     )(
-        offsets, tile_counts, cotangent, left, right, layer_scale, ln_gain, ln_bias, b_in, near_out, w_in
-    )
-    to_right, to_left, act, centers, inverses = call(
-        block_kernel,
+        offsets, tile_counts, cotangent, left, right, cot_a, cot_b,
+        layer_scale, ln_gain, ln_bias, b_in, near_out, w_in,
+    )
+    message = struct((half + 16, share), bf16)
+
+    def block(blocks, hidden, earlier):
+        return call(
+            block_kernel,
+            [message, struct((half, hid), bf16), struct((half, 1), f32), struct((half, 1), f32)],
+            [VMEM] * 11,
+            [pltpu.VMEM((half, width), bf16), pltpu.VMEM((half, width), bf16)],
+        )(*blocks, ln_gain, ln_bias, near_in, b_in, hidden, sides, earlier)
+
+    def parts(keep_ahead, own_ahead, act, away, earlier):
+        return call(
+            functools.partial(parts_kernel, keep_ahead, own_ahead),
+            [struct((half, share), bf16), message, struct((half, share), f32)],
+            [VMEM] * 4,
+        )(act, near_in, away, earlier)
+
+    def middle(come, keep):
+        return call(middle_kernel, [message], [VMEM] * 2)(come, keep)[0]
+
+    away_a, act_a, centers_a, inverses_a = block((mixed_a, left_a, right_a, opp_a), hidden_a, mixed_b)
+    come_a = shift(away_a, 1)
+    keep_a, own_a, mine_a = parts(1, 3, act_a, away_a, away_a)
+    got_a = shift(own_a, -1)
+    away_b, act_b, centers_b, inverses_b = block((mixed_b, left_b, right_b, opp_b), hidden_b, keep_a)
+    come_b = shift(away_b, -1)
+    keep_b, own_b, mine_b = parts(3, 1, act_b, away_b, got_a)
+    got_b = shift(own_b, 1)
+    total_a = shift(middle(come_a, keep_a), 1)
+    total_b = shift(middle(come_b, keep_b), -1)
+    grown = call(
+        first_tiles_kernel,
+        [canvas_like],
+        [SMEM] * 2 + [VMEM] * 11,
+        [pltpu.VMEM((half, share), f32)],
+    )(
+        offsets, tile_counts, mine_a, got_a, total_a, come_a, away_a, mixed_a, centers_a, inverses_a,
+        ln_gain, taps, taken,
+    )[0]
+    return call(
+        last_tiles_kernel,
+        jax.ShapeDtypeStruct(canvas.shape, f32),
+        [SMEM] * 3 + [VMEM] * 11,
         [
-            struct((half + 16, share), bf16),
-            struct((half + 16, share), bf16),
-            struct((rows, hid), bf16),
-            struct((rows, 1), f32),
-            struct((rows, 1), f32),
-        ],
-        [VMEM] * 18,
-        [
-            pltpu.VMEM((rows, width), bf16),
-            pltpu.VMEM((rows, width), bf16),
-            pltpu.VMEM((rows, share), bf16),
-        ],
-        limit=24,
-    )(
-        mixed_a, mixed_b, left_a, left_b, right_a, right_b, opp_a, opp_b, cot_a, cot_b,
-        ln_gain, ln_bias, layer_scale, near_in, b_in, near_out, hidden, sides,
-    )
-    from_left, from_right = shift(to_right, 1), shift(to_left, -1)
-    keep_right, own_right, own_left, keep_left = call(
-        parts_kernel,
-        [struct((half + more, share), bf16) for more in (0, 16, 16, 0)],
-        [VMEM] * 2,
-    )(act, near_in)
-    got_left, got_right = shift(own_right, 1), shift(own_left, -1)
-    (mine,) = call(mine_kernel, [struct((rows, share), f32)], [VMEM] * 3)(act, near_in, keep_right)
-    go_right, go_left = call(
-        middle_kernel,
-        [struct((half + 16, share), bf16), struct((half, share), bf16)],
-        [VMEM] * 5,
-    )(from_left, from_right, keep_right, keep_left, mine)
-    sum_left, sum_right = shift(go_right, 1), shift(go_left, -1)
-    return call(
-        canvas_kernel,
-        jax.ShapeDtypeStruct(canvas.shape, f32),
-        [SMEM] * 3 + [VMEM] * 15,
-        [
-            pltpu.VMEM((rows, share), f32),
+            pltpu.VMEM((half, share), f32),
             pltpu.VMEM((lanes, PAD_ROWS, PAD_COLS, 128), f32),
             pltpu.VMEM(canvas.shape, f32),
             pltpu.SemaphoreType.DMA((4,)),
         ],
         out_specs=HBM,
     )(
-        offsets, screen_size, tile_counts,
-        got_left, got_right, sum_left, sum_right, mine, from_left, from_right, to_right,
-        mixed_a, mixed_b, centers, inverses, ln_gain, taken, taps,
+        offsets, tile_counts, screen_size, mine_b, got_b, total_b, come_b, away_b, mixed_b, centers_b, inverses_b,
+        ln_gain, taps, grown,
     )
 
 

time: 64.6 us -> 61 us (0.944)
  the two profiles are of different devices: /device:TPU:28 before, /device:TPU:16 now
where the time goes in v5:
time: 61 us; the launch traced here: 60.8 us
  Pallas kernels  28.2 us (46%)
  starting transfers between devices  23.8 us (39%)
  waiting for transfers between devices  8.33 us (14%)
    pallas_call x10, Pallas kernels, held(): run(*(pltpu.with_memory_space_constraint(a, pltpu.VMEM if spec is VMEM el...  28.2 us
    ppermute x16, starting transfers between devices, shift(): return lax.ppermute(x, 'ch', [(i, (i + by) % n) for i in range(n)])  23.8 us
    ppermute x16, waiting for transfers between devices, shift(): return lax.ppermute(x, 'ch', [(i, (i + by) % n) for i in range(n)])  8.33 us
  transfers between devices with their start and end apart: 16, of which 5 were waited for; matrix products, arithmetic and copies ran while one was open for 0% of the time, Pallas kernels for 39%

profile of v5, /device:TPU:16, one launch (start us, length us, event | category | flops | bytes accessed | tf_op | source)
XLA Modules:
  0.0 60.8 jit_solution(2821066207836140885)
XLA Ops:
  0.0 1.9 %collective-permute-start.3 = (bf16[32,4,4,384]{3,2,1,0:T(4,128)(2,1)}, bf16[32,4,4,384]{3,2,1,0:T(4,128)(2,1)S(1)}, u32[]{:S(2)}, u32[]{:S(2)}) collective-permute-start(bf16[32,4,4,384]{3,2,1,0:T(4,128)(2,1)} %own.1), channel_id=1, source_target_pairs={{0,1},{1,2},{2,3},{3,0},{4,5},{5,6},{6,7},{7,4},{8,9},{9,10},{10,1... | collective-permute-start | bytes 1179656 | tf_op jit(solution)/shard_map/ppermute | solution.py:368
  1.9 2.1 %collective-permute-start.4 = (bf16[32,4,4,384]{3,2,1,0:T(4,128)(2,1)}, bf16[32,4,4,384]{3,2,1,0:T(4,128)(2,1)S(1)}, u32[]{:S(2)}, u32[]{:S(2)}) collective-permute-start(bf16[32,4,4,384]{3,2,1,0:T(4,128)(2,1)} %own.1), channel_id=1, source_target_pairs={{0,3},{1,0},{2,1},{3,2},{4,7},{5,4},{6,5},{7,6},{8,11},{9,8},{10,9... | collective-permute-start | bytes 1179656 | tf_op jit(solution)/shard_map/ppermute | solution.py:368
  4.0 0.0 copy-start
  4.0 0.0 copy-start.1
  4.0 0.0 copy-start.2
  4.0 0.0 copy-start.3
  4.1 0.0 copy-start.4
  4.1 5.9 %shard_map.127 = (bf16[256,384]{1,0:T(8,128)(2,1)S(1)}, bf16[256,384]{1,0:T(8,128)(2,1)S(1)}, bf16[1536,1536]{1,0:T(8,128)(2,1)S(1)}, f32[3,28,8,128]{3,2,1,0:T(8,128)S(1)}) custom-call(s32[2,32]{1,0:T(2,128)} %bitcast.1, s32[1,2]{1,0:T(1,128)} %screen.3, bf16[32,32,384]{2,1,0:T(8,128)(2,1)} %canvas.1, bf16[49,384]{1,0:T(8,128)(2,1)} %dwk.1, f32[384]{0:T(512)} %bias.4, ...), custom_call_target="tpu_custom_call" | custom-call | tf_op jit(solution)/shard_map/pallas_call | solution.py:36
  10.0 0.1 collective-permute-start.7
  10.1 3.2 %collective-permute-start.1 = (bf16[256,384]{1,0:T(8,128)(2,1)S(1)}, bf16[256,384]{1,0:T(8,128)(2,1)S(1)}, u32[]{:S(2)}, u32[]{:S(2)}) collective-permute-start(bf16[256,384]{1,0:T(8,128)(2,1)S(1)} %get-tuple-element.28.earlier.own.mixed), channel_id=1, source_target_pairs={{0,3},{1,0},{2,1},{3,2},{4,7},{5,4},{6,5},{7,6},{8,11},{9,8},{10,9... | collective-permute-start | bytes 589832 | tf_op jit(solution)/shard_map/ppermute | solution.py:368
  13.3 0.1 collective-permute-done.3.left
  13.4 0.1 slice.8
  13.4 0.4 collective-permute-start.5
  13.8 0.0 collective-permute-done.4.right
  13.8 0.1 slice.9
  13.9 3.0 %collective-permute-start.6 = (bf16[16,4,4,384]{3,2,1,0:T(4,128)(2,1)S(1)}, bf16[16,4,4,384]{3,2,1,0:T(4,128)(2,1)S(1)}, u32[]{:S(2)}, u32[]{:S(2)}) collective-permute-start(bf16[16,4,4,384]{3,2,1,0:T(4,128)(2,1)S(1)} %slice.9), channel_id=1, source_target_pairs={{0,3},{1,0},{2,1},{3,2},{4,7},{5,4},{6,5},{7,6},{8,11},{9,8},{10,9... | collective-permute-start | bytes 589832 | tf_op jit(solution)/shard_map/ppermute | solution.py:368
  16.9 1.7 %collective-permute-start.8 = (bf16[256,384]{1,0:T(8,128)(2,1)S(1)}, bf16[256,384]{1,0:T(8,128)(2,1)S(1)}, u32[]{:S(2)}, u32[]{:S(2)}) collective-permute-start(bf16[256,384]{1,0:T(8,128)(2,1)S(1)} %get-tuple-element.33.own.mixed), channel_id=1, source_target_pairs={{0,3},{1,0},{2,1},{3,2},{4,7},{5,4},{6,5},{7,6},{8,11},{9,8},{10,9... | collective-permute-start | bytes 589832 | tf_op jit(solution)/shard_map/ppermute | solution.py:368
  18.6 0.0 collective-permute-done.7.left
  18.6 0.3 collective-permute-start.9
  18.9 0.0 collective-permute-done.1.right
  18.9 1.3 %collective-permute-start = (bf16[256,384]{1,0:T(8,128)(2,1)S(1)}, bf16[256,384]{1,0:T(8,128)(2,1)S(1)}, u32[]{:S(2)}, u32[]{:S(2)}) collective-permute-start(bf16[256,384]{1,0:T(8,128)(2,1)S(1)} %get-tuple-element.28.earlier.own.mixed), channel_id=1, source_target_pairs={{0,1},{1,2},{2,3},{3,0},{4,5},{5,6},{6,7},{7,4},{8,9},{9,10},{10,1... | collective-permute-start | bytes 589832 | tf_op jit(solution)/shard_map/ppermute | solution.py:368
  20.3 2.5 %collective-permute-done.5.cot_a = bf16[16,4,4,384]{3,2,1,0:T(4,128)(2,1)S(1)} collective-permute-done((bf16[16,4,4,384]{3,2,1,0:T(4,128)(2,1)S(1)}, bf16[16,4,4,384]{3,2,1,0:T(4,128)(2,1)S(1)}, u32[]{:S(2)}, u32[]{:S(2)}) %collective-permute-start.5) | collective-permute-done | bytes 196640 | tf_op jit(solution)/shard_map/ppermute | solution.py:368
  22.8 1.9 %collective-permute-start.2 = (bf16[256,384]{1,0:T(8,128)(2,1)S(1)}, bf16[256,384]{1,0:T(8,128)(2,1)S(1)}, u32[]{:S(2)}, u32[]{:S(2)}) collective-permute-start(bf16[256,384]{1,0:T(8,128)(2,1)S(1)} %collective-permute-done.1.right), channel_id=1, source_target_pairs={{0,3},{1,0},{2,1},{3,2},{4,7},{5,4},{6,5},{7,6},{8,11},{9,8},{10,9... | collective-permute-start | bytes 589832 | tf_op jit(solution)/shard_map/ppermute | solution.py:368
  24.7 0.0 collective-permute-done.6.cot_b
  24.7 0.0 copy-done
  24.7 0.0 copy-done.1
  24.7 0.0 copy-done.2
  24.7 0.0 copy-done.3
  24.7 0.0 copy-done.4
  24.7 4.9 %shard_map.128 = (f32[256,1536]{1,0:T(8,128)S(1)}, f32[256,1536]{1,0:T(8,128)S(1)}, f32[3,38,48,128]{3,2,1,0:T(8,128)S(1)}, bf16[1536,1536]{1,0:T(8,128)(2,1)S(1)}, f32[8,1536]{1,0:T(8,128)S(1)}) custom-call(s32[2,32]{1,0:T(2,128)} %bitcast.2, s32[32]{0:T(128)} %counts.5, bf16[32,4,4,384]{3,2,1,0:T(4,128)(2,1)S(1)} %copy-done, ...), custom_call_target="tpu_custom_call" | custom-call | tf_op jit(solution)/shard_map/pallas_call | solution.py:36
  29.6 0.0 collective-permute-done.8.right
  29.6 0.0 collective-permute-done.9.opp
  29.6 3.3 %shard_map.129 = (bf16[272,384]{1,0:T(8,128)(2,1)S(1)}, bf16[256,1536]{1,0:T(8,128)(2,1)S(1)}, f32[256,1]{1,0:T(8,128)S(1)}, f32[256,1]{1,0:T(8,128)S(1)}) custom-call(bf16[256,384]{1,0:T(8,128)(2,1)S(1)} %get-tuple-element.33.own.mixed, bf16[256,384]{1,0:T(8,128)(2,1)S(1)} %collective-permute-done.7.left, ...), custom_call_target="tpu_custom_call" | custom-call | tf_op jit(solution)/shard_map/pallas_call | solution.py:36
  32.9 0.2 collective-permute-start.14
  33.1 1.4 %shard_map.130 = (bf16[256,384]{1,0:T(8,128)(2,1)S(1)}, bf16[272,384]{1,0:T(8,128)(2,1)S(1)}, f32[256,384]{1,0:T(8,128)S(1)}) custom-call(bf16[256,1536]{1,0:T(8,128)(2,1)S(1)} %get-tuple-element.35.act, bf16[1536,1536]{1,0:T(8,128)(2,1)S(1)} %get-tuple-element.30.w_in, bf16[272,384]{1,0:T(8,128)(2,1)S(1)} %get-tuple-element.36.away.earlier, ...), custom_call_target="tpu_custom_call" | custom-call | tf_op jit(solution)/shard_map/pallas_call | solution.py:36
  34.5 3.4 %collective-permute-start.10 = (bf16[272,384]{1,0:T(8,128)(2,1)S(1)}, bf16[272,384]{1,0:T(8,128)(2,1)S(1)}, u32[]{:S(2)}, u32[]{:S(2)}) collective-permute-start(bf16[272,384]{1,0:T(8,128)(2,1)S(1)} %get-tuple-element.40), channel_id=1, source_target_pairs={{0,3},{1,0},{2,1},{3,2},{4,7},{5,4},{6,5},{7,6},{8,11},{9,8},{10,9... | collective-permute-start | bytes 626696 | tf_op jit(solution)/shard_map/ppermute | solution.py:368
  37.9 0.0 collective-permute-done.left
  37.9 0.0 collective-permute-done.2.opp
  37.9 3.3 %shard_map.131 = (bf16[272,384]{1,0:T(8,128)(2,1)S(1)}, bf16[256,1536]{1,0:T(8,128)(2,1)S(1)}, f32[256,1]{1,0:T(8,128)S(1)}, f32[256,1]{1,0:T(8,128)S(1)}) custom-call(bf16[256,384]{1,0:T(8,128)(2,1)S(1)} %get-tuple-element.28.earlier.own.mixed, bf16[256,384]{1,0:T(8,128)(2,1)S(1)} %collective-permute-done.left, ...), custom_call_target="tpu_custom_call" | custom-call | tf_op jit(solution)/shard_map/pallas_call | solution.py:36
  41.2 0.1 collective-permute-start.12
  41.3 0.0 collective-permute-done.14.come
  41.3 0.1 shard_map.134
  41.3 2.1 %collective-permute-start.15 = (bf16[272,384]{1,0:T(8,128)(2,1)S(1)}, bf16[272,384]{1,0:T(8,128)(2,1)S(1)}, u32[]{:S(2)}, u32[]{:S(2)}) collective-permute-start(bf16[272,384]{1,0:T(8,128)(2,1)S(1)} %shard_map.134), channel_id=1, source_target_pairs={{0,1},{1,2},{2,3},{3,0},{4,5},{5,6},{6,7},{7,4},{8,9},{9,10},{10,1... | collective-permute-start | bytes 626696 | tf_op jit(solution)/shard_map/ppermute | solution.py:368
  43.4 0.0 collective-permute-done.10.earlier.got
  43.4 1.4 %shard_map.132 = (bf16[256,384]{1,0:T(8,128)(2,1)S(1)}, bf16[272,384]{1,0:T(8,128)(2,1)S(1)}, f32[256,384]{1,0:T(8,128)S(1)}) custom-call(bf16[256,1536]{1,0:T(8,128)(2,1)S(1)} %get-tuple-element.38.act, bf16[1536,1536]{1,0:T(8,128)(2,1)S(1)} %get-tuple-element.30.w_in, bf16[272,384]{1,0:T(8,128)(2,1)S(1)} %get-tuple-element.39.away, ...), custom_call_target="tpu_custom_call" | custom-call | tf_op jit(solution)/shard_map/pallas_call | solution.py:36
  44.8 4.0 %collective-permute-done.12.come = bf16[272,384]{1,0:T(8,128)(2,1)S(1)} collective-permute-done((bf16[272,384]{1,0:T(8,128)(2,1)S(1)}, bf16[272,384]{1,0:T(8,128)(2,1)S(1)}, u32[]{:S(2)}, u32[]{:S(2)}) %collective-permute-start.12) | collective-permute-done | bytes 208928 | tf_op jit(solution)/shard_map/ppermute | solution.py:368
  48.9 0.1 shard_map.133
  48.9 0.1 collective-permute-start.13
  49.0 2.0 %collective-permute-start.11 = (bf16[272,384]{1,0:T(8,128)(2,1)S(1)}, bf16[272,384]{1,0:T(8,128)(2,1)S(1)}, u32[]{:S(2)}, u32[]{:S(2)}) collective-permute-start(bf16[272,384]{1,0:T(8,128)(2,1)S(1)} %get-tuple-element.42), channel_id=1, source_target_pairs={{0,1},{1,2},{2,3},{3,0},{4,5},{5,6},{6,7},{7,4},{8,9},{9,10},{10,1... | collective-permute-start | bytes 626696 | tf_op jit(solution)/shard_map/ppermute | solution.py:368
  51.0 0.0 collective-permute-done.15.total
  51.0 3.4 %shard_map.135.before = f32[3,38,48,128]{3,2,1,0:T(8,128)S(1)} custom-call(s32[2,32]{1,0:T(2,128)} %bitcast.3, s32[32]{0:T(128)} %counts.5, f32[256,384]{1,0:T(8,128)S(1)} %get-tuple-element.47.mine, bf16[272,384]{1,0:T(8,128)(2,1)S(1)} %collective-permute-done.10.earlier.got, bf16[272,384]{1,0:T(8,128)(2,1)S(1)} %collective-permute-done.15.total, ...), custom_call_target="tpu_custom_call" | custom-call | tf_op jit(solution)/shard_map/pallas_call | solution.py:36
  54.4 0.4 collective-permute-done.13.total
  54.8 1.3 %collective-permute-done.11.got = bf16[272,384]{1,0:T(8,128)(2,1)S(1)} collective-permute-done((bf16[272,384]{1,0:T(8,128)(2,1)S(1)}, bf16[272,384]{1,0:T(8,128)(2,1)S(1)}, u32[]{:S(2)}, u32[]{:S(2)}) %collective-permute-start.11) | collective-permute-done | bytes 208928 | tf_op jit(solution)/shard_map/ppermute | solution.py:368
  56.1 4.6 %shard_map.136 = f32[32,32,384]{2,1,0:T(8,128)} custom-call(s32[2,32]{1,0:T(2,128)} %bitcast.4, s32[32]{0:T(128)} %counts.5, s32[1,2]{1,0:T(1,128)} %screen.3, f32[256,384]{1,0:T(8,128)S(1)} %get-tuple-element.41.mine, bf16[272,384]{1,0:T(8,128)(2,1)S(1)} %collective-permute-done.11.got, bf16[272,384]{1,0:T(8,128)(2,1)S(1)} %collective-permute-done.13.total, ...), custom_call_target="tpu_custom_call" | custom-call | tf_op jit(solution)/shard_map/pallas_call | solution.py:36
Async XLA Ops:
  0.0 13.4 %collective-permute-start.3 = (bf16[32,4,4,384]{3,2,1,0:T(4,128)(2,1)}, bf16[32,4,4,384]{3,2,1,0:T(4,128)(2,1)S(1)}, u32[]{:S(2)}, u32[]{:S(2)}) collective-permute-start(bf16[32,4,4,384]{3,2,1,0:T(4,128)(2,1)} %own.1), channel_id=1, source_target_pairs={{0,1},{1,2},{2,3},{3,0},{4,5},{5,6},{6,7},{7,4},{8,9},{9,10},{10,1... | collective-permute-start | bytes 1179656 | tf_op jit(solution)/shard_map/ppermute | solution.py:368
  1.9 11.9 %collective-permute-start.4 = (bf16[32,4,4,384]{3,2,1,0:T(4,128)(2,1)}, bf16[32,4,4,384]{3,2,1,0:T(4,128)(2,1)S(1)}, u32[]{:S(2)}, u32[]{:S(2)}) collective-permute-start(bf16[32,4,4,384]{3,2,1,0:T(4,128)(2,1)} %own.1), channel_id=1, source_target_pairs={{0,3},{1,0},{2,1},{3,2},{4,7},{5,4},{6,5},{7,6},{8,11},{9,8},{10,9... | collective-permute-start | bytes 1179656 | tf_op jit(solution)/shard_map/ppermute | solution.py:368
  4.0 20.6 %copy-start = (bf16[32,4,4,384]{3,2,1,0:T(4,128)(2,1)S(1)}, bf16[32,4,4,384]{3,2,1,0:T(4,128)(2,1)}, u32[]{:S(2)}) copy-start(bf16[32,4,4,384]{3,2,1,0:T(4,128)(2,1)} %own.1) | copy-start | bytes 1179652
  4.0 20.6 %copy-start.1 = (f32[1536]{0:T(1024)S(1)}, f32[1536]{0:T(1024)}, u32[]{:S(2)}) copy-start(f32[1536]{0:T(1024)} %gain.9) | copy-start | bytes 18436
  4.0 20.6 %copy-start.2 = (f32[1536]{0:T(1024)S(1)}, f32[1536]{0:T(1024)}, u32[]{:S(2)}) copy-start(f32[1536]{0:T(1024)} %bias.7) | copy-start | bytes 18436
  4.0 20.7 %copy-start.3 = (f32[1536]{0:T(1024)S(1)}, f32[1536]{0:T(1024)}, u32[]{:S(2)}) copy-start(f32[1536]{0:T(1024)} %b_in.5) | copy-start | bytes 18436
  4.1 20.7 %copy-start.4 = (f32[1536]{0:T(1024)S(1)}, f32[1536]{0:T(1024)}, u32[]{:S(2)}) copy-start(f32[1536]{0:T(1024)} %scale.1) | copy-start | bytes 18436
  10.0 8.6 %collective-permute-start.7 = (bf16[256,384]{1,0:T(8,128)(2,1)S(1)}, bf16[256,384]{1,0:T(8,128)(2,1)S(1)}, u32[]{:S(2)}, u32[]{:S(2)}) collective-permute-start(bf16[256,384]{1,0:T(8,128)(2,1)S(1)} %get-tuple-element.33.own.mixed), channel_id=1, source_target_pairs={{0,1},{1,2},{2,3},{3,0},{4,5},{5,6},{6,7},{7,4},{8,9},{9,10},{10,1... | collective-permute-start | bytes 589832 | tf_op jit(solution)/shard_map/ppermute | solution.py:368
  10.1 8.9 %collective-permute-start.1 = (bf16[256,384]{1,0:T(8,128)(2,1)S(1)}, bf16[256,384]{1,0:T(8,128)(2,1)S(1)}, u32[]{:S(2)}, u32[]{:S(2)}) collective-permute-start(bf16[256,384]{1,0:T(8,128)(2,1)S(1)} %get-tuple-element.28.earlier.own.mixed), channel_id=1, source_target_pairs={{0,3},{1,0},{2,1},{3,2},{4,7},{5,4},{6,5},{7,6},{8,11},{9,8},{10,9... | collective-permute-start | bytes 589832 | tf_op jit(solution)/shard_map/ppermute | solution.py:368
  13.4 9.3 %collective-permute-start.5 = (bf16[16,4,4,384]{3,2,1,0:T(4,128)(2,1)S(1)}, bf16[16,4,4,384]{3,2,1,0:T(4,128)(2,1)S(1)}, u32[]{:S(2)}, u32[]{:S(2)}) collective-permute-start(bf16[16,4,4,384]{3,2,1,0:T(4,128)(2,1)S(1)} %slice.8), channel_id=1, source_target_pairs={{0,1},{1,2},{2,3},{3,0},{4,5},{5,6},{6,7},{7,4},{8,9},{9,10},{10,1... | collective-permute-start | bytes 589832 | tf_op jit(solution)/shard_map/ppermute | solution.py:368
  13.9 10.8 %collective-permute-start.6 = (bf16[16,4,4,384]{3,2,1,0:T(4,128)(2,1)S(1)}, bf16[16,4,4,384]{3,2,1,0:T(4,128)(2,1)S(1)}, u32[]{:S(2)}, u32[]{:S(2)}) collective-permute-start(bf16[16,4,4,384]{3,2,1,0:T(4,128)(2,1)S(1)} %slice.9), channel_id=1, source_target_pairs={{0,3},{1,0},{2,1},{3,2},{4,7},{5,4},{6,5},{7,6},{8,11},{9,8},{10,9... | collective-permute-start | bytes 589832 | tf_op jit(solution)/shard_map/ppermute | solution.py:368
  16.9 12.7 %collective-permute-start.8 = (bf16[256,384]{1,0:T(8,128)(2,1)S(1)}, bf16[256,384]{1,0:T(8,128)(2,1)S(1)}, u32[]{:S(2)}, u32[]{:S(2)}) collective-permute-start(bf16[256,384]{1,0:T(8,128)(2,1)S(1)} %get-tuple-element.33.own.mixed), channel_id=1, source_target_pairs={{0,3},{1,0},{2,1},{3,2},{4,7},{5,4},{6,5},{7,6},{8,11},{9,8},{10,9... | collective-permute-start | bytes 589832 | tf_op jit(solution)/shard_map/ppermute | solution.py:368
  18.6 11.0 %collective-permute-start.9 = (bf16[256,384]{1,0:T(8,128)(2,1)S(1)}, bf16[256,384]{1,0:T(8,128)(2,1)S(1)}, u32[]{:S(2)}, u32[]{:S(2)}) collective-permute-start(bf16[256,384]{1,0:T(8,128)(2,1)S(1)} %collective-permute-done.7.left), channel_id=1, source_target_pairs={{0,1},{1,2},{2,3},{3,0},{4,5},{5,6},{6,7},{7,4},{8,9},{9,10},{10,1... | collective-permute-start | bytes 589832 | tf_op jit(solution)/shard_map/ppermute | solution.py:368
  18.9 19.0 %collective-permute-start = (bf16[256,384]{1,0:T(8,128)(2,1)S(1)}, bf16[256,384]{1,0:T(8,128)(2,1)S(1)}, u32[]{:S(2)}, u32[]{:S(2)}) collective-permute-start(bf16[256,384]{1,0:T(8,128)(2,1)S(1)} %get-tuple-element.28.earlier.own.mixed), channel_id=1, source_target_pairs={{0,1},{1,2},{2,3},{3,0},{4,5},{5,6},{6,7},{7,4},{8,9},{9,10},{10,1... | collective-permute-start | bytes 589832 | tf_op jit(solution)/shard_map/ppermute | solution.py:368
  22.8 15.1 %collective-permute-start.2 = (bf16[256,384]{1,0:T(8,128)(2,1)S(1)}, bf16[256,384]{1,0:T(8,128)(2,1)S(1)}, u32[]{:S(2)}, u32[]{:S(2)}) collective-permute-start(bf16[256,384]{1,0:T(8,128)(2,1)S(1)} %collective-permute-done.1.right), channel_id=1, source_target_pairs={{0,3},{1,0},{2,1},{3,2},{4,7},{5,4},{6,5},{7,6},{8,11},{9,8},{10,9... | collective-permute-start | bytes 589832 | tf_op jit(solution)/shard_map/ppermute | solution.py:368
  32.9 8.4 %collective-permute-start.14 = (bf16[272,384]{1,0:T(8,128)(2,1)S(1)}, bf16[272,384]{1,0:T(8,128)(2,1)S(1)}, u32[]{:S(2)}, u32[]{:S(2)}) collective-permute-start(bf16[272,384]{1,0:T(8,128)(2,1)S(1)} %get-tuple-element.36.away.earlier), channel_id=1, source_target_pairs={{0,1},{1,2},{2,3},{3,0},{4,5},{5,6},{6,7},{7,4},{8,9},{9,10},{10,1... | collective-permute-start | bytes 626696 | tf_op jit(solution)/shard_map/ppermute | solution.py:368
  34.5 8.9 %collective-permute-start.10 = (bf16[272,384]{1,0:T(8,128)(2,1)S(1)}, bf16[272,384]{1,0:T(8,128)(2,1)S(1)}, u32[]{:S(2)}, u32[]{:S(2)}) collective-permute-start(bf16[272,384]{1,0:T(8,128)(2,1)S(1)} %get-tuple-element.40), channel_id=1, source_target_pairs={{0,3},{1,0},{2,1},{3,2},{4,7},{5,4},{6,5},{7,6},{8,11},{9,8},{10,9... | collective-permute-start | bytes 626696 | tf_op jit(solution)/shard_map/ppermute | solution.py:368
  41.2 7.7 %collective-permute-start.12 = (bf16[272,384]{1,0:T(8,128)(2,1)S(1)}, bf16[272,384]{1,0:T(8,128)(2,1)S(1)}, u32[]{:S(2)}, u32[]{:S(2)}) collective-permute-start(bf16[272,384]{1,0:T(8,128)(2,1)S(1)} %get-tuple-element.39.away), channel_id=1, source_target_pairs={{0,3},{1,0},{2,1},{3,2},{4,7},{5,4},{6,5},{7,6},{8,11},{9,8},{10,9... | collective-permute-start | bytes 626696 | tf_op jit(solution)/shard_map/ppermute | solution.py:368
  41.3 9.7 %collective-permute-start.15 = (bf16[272,384]{1,0:T(8,128)(2,1)S(1)}, bf16[272,384]{1,0:T(8,128)(2,1)S(1)}, u32[]{:S(2)}, u32[]{:S(2)}) collective-permute-start(bf16[272,384]{1,0:T(8,128)(2,1)S(1)} %shard_map.134), channel_id=1, source_target_pairs={{0,1},{1,2},{2,3},{3,0},{4,5},{5,6},{6,7},{7,4},{8,9},{9,10},{10,1... | collective-permute-start | bytes 626696 | tf_op jit(solution)/shard_map/ppermute | solution.py:368
  48.9 5.9 %collective-permute-start.13 = (bf16[272,384]{1,0:T(8,128)(2,1)S(1)}, bf16[272,384]{1,0:T(8,128)(2,1)S(1)}, u32[]{:S(2)}, u32[]{:S(2)}) collective-permute-start(bf16[272,384]{1,0:T(8,128)(2,1)S(1)} %shard_map.133), channel_id=1, source_target_pairs={{0,3},{1,0},{2,1},{3,2},{4,7},{5,4},{6,5},{7,6},{8,11},{9,8},{10,9... | collective-permute-start | bytes 626696 | tf_op jit(solution)/shard_map/ppermute | solution.py:368
  49.0 7.1 %collective-permute-start.11 = (bf16[272,384]{1,0:T(8,128)(2,1)S(1)}, bf16[272,384]{1,0:T(8,128)(2,1)S(1)}, u32[]{:S(2)}, u32[]{:S(2)}) collective-permute-start(bf16[272,384]{1,0:T(8,128)(2,1)S(1)} %get-tuple-element.42), channel_id=1, source_target_pairs={{0,1},{1,2},{2,3},{3,0},{4,5},{5,6},{6,7},{7,4},{8,9},{9,10},{10,1... | collective-permute-start | bytes 626696 | tf_op jit(solution)/shard_map/ppermute | solution.py:368

commit v6 on v5

--- a/solution.py
+++ b/solution.py
@@ -139,13 +139,12 @@
 
 
 def hidden_kernel(
-    offsets, counts, own, left, right, cot_a, cot_b, scale, gain, bias, b_in, w_out, w_in,
-    hidden_a, hidden_b, taken, near_in, sides, full, sem,
+    offsets, counts, own, left, right, scale, gain, bias, b_in, w_out, w_in,
+    hidden, taken, near_in, sides, flat, sem,
 ):
     fetch = pltpu.make_async_copy(w_in, near_in, sem)
     fetch.start()
     share = own.shape[3]
-    half = hidden_a.shape[0]
     taken[...] = jnp.zeros_like(taken)
 
     def tile(t, carry):
@@ -157,19 +156,22 @@
         return carry
 
     lax.fori_loop(0, counts[lax.axis_index("img")], tile, 0)
-    for cells, ahead, row in ((own, 0, 0), (left, 3, 0), (right, 1, 0), (cot_a, 2, 0), (cot_b, 2, half)):
-        begin = channels_of(ahead, share)
-        full[row : row + 16 * cells.shape[0], pl.ds(begin, share)] = scaled_rows(cells, scale, begin)
+    begins = []
+    for k, (cells, ahead) in enumerate(((own, 0), (left, 3), (right, 1))):
+        begins.append(channels_of(ahead, share))
+        flat[k] = scaled_rows(cells, scale, begins[k])
     step = 512
-    for n in range(0, hidden_a.shape[1], step):
-        product = lax.dot_general(
-            full[...],
-            w_out[n : n + step, :],
-            (((1,), (1,)), ((), ())),
-            preferred_element_type=jnp.float32,
-        )
-        hidden_a[:, n : n + step] = product[:half]
-        hidden_b[:, n : n + step] = product[half:]
+    for n in range(0, hidden.shape[1], step):
+        total = None
+        for k, begin in enumerate(begins):
+            product = lax.dot_general(
+                flat[k],
+                w_out[n : n + step, pl.ds(begin, share)],
+                (((1,), (1,)), ((), ())),
+                preferred_element_type=jnp.float32,
+            )
+            total = product if total is None else total + product
+        hidden[:, n : n + step] = total
     width = gain.shape[0]
     lines = two_parts(gain[...][None]) + two_parts(bias[...][None])
     lines = jnp.concatenate(lines + [jnp.zeros((12, width), jnp.float32)], 0).astype(jnp.bfloat16)
@@ -177,6 +179,24 @@
     both = jnp.dot(lines, near_in[...], preferred_element_type=jnp.float32)
     sides[0:1, :] = both[0:1] + both[1:2]
     sides[1:2, :] = both[2:3] + both[3:4] + b_in[...][None]
+
+
+def opposite_kernel(before, cot_a, cot_b, scale, w_out, hidden_a, hidden_b, flat):
+    rows, share = flat.shape
+    half = rows // 2
+    begin = channels_of(2, share)
+    flat[:half, :] = scaled_rows(cot_a, scale, begin)
+    flat[half:, :] = scaled_rows(cot_b, scale, begin)
+    step = 512
+    for n in range(0, before.shape[1], step):
+        product = lax.dot_general(
+            flat[...],
+            w_out[n : n + step, pl.ds(begin, share)],
+            (((1,), (1,)), ((), ())),
+            preferred_element_type=jnp.float32,
+        )
+        hidden_a[:, n : n + step] = before[:half, n : n + step] + product[:half]
+        hidden_b[:, n : n + step] = before[half:, n : n + step] + product[half:]
 
 
 def gelu_slope(v):
@@ -219,10 +239,9 @@
 
 
 def block_kernel(
-    own, left, right, opp, gain, bias, w_in, b_in, hidden, sides, earlier,
+    own, left, right, opp, gain, bias, w_in, b_in, hidden, sides,
     away, act, centers, inverses, full, scaled,
 ):
-    del earlier
     rows, width = full.shape
     share = own.shape[1]
     for ref, ahead in ((own, 0), (left, 3), (right, 1), (opp, 2)):
@@ -262,8 +281,7 @@
     away[rows : rows + 16, :128] = jnp.concatenate(packed, 0).astype(jnp.bfloat16)
 
 
-def parts_kernel(keep_ahead, own_ahead, act, w_in, away, earlier, keep, own, mine):
-    del earlier
+def parts_kernel(keep_ahead, own_ahead, act, w_in, away, keep, own, mine):
     rows = act.shape[0]
     own[:rows, :] = part_of(act, w_in, own_ahead).astype(jnp.bfloat16)
     own[rows:, :] = away[rows:, :]
@@ -413,51 +431,51 @@
     )(offsets, screen_size, canvas, dw_kernel, dw_bias, w_out)
     left_a, right_a = shift(mixed_a, 1), shift(mixed_a, -1)
     cot_a, cot_b = shift(left[: slots // 2], 1), shift(right[slots // 2 :], -1)
-    opp_a, right_b = shift(left_a, 1), shift(mixed_b, -1)
-    left_b, opp_b = shift(mixed_b, 1), shift(right_b, -1)
+    right_b, left_b = shift(mixed_b, -1), shift(mixed_b, 1)
     canvas_like = struct((lanes, PAD_ROWS, PAD_COLS, 128), f32)
-    hidden_a, hidden_b, taken, near_in, sides = call(
+    hidden, taken, near_in, sides = call(
         hidden_kernel,
-        [
-            struct((half, hid), f32),
-            struct((half, hid), f32),
-            canvas_like,
-            struct(w_in.shape, bf16),
-            struct((8, hid), f32),
-        ],
-        [SMEM] * 2 + [VMEM] * 10 + [HBM],
-        [pltpu.VMEM((rows, width), bf16), pltpu.SemaphoreType.DMA(())],
+        [struct((rows, hid), f32), canvas_like, struct(w_in.shape, bf16), struct((8, hid), f32)],
+        [SMEM] * 2 + [VMEM] * 8 + [HBM],
+        [pltpu.VMEM((3, rows, share), bf16), pltpu.SemaphoreType.DMA(())],
     )(
-        offsets, tile_counts, cotangent, left, right, cot_a, cot_b,
-        layer_scale, ln_gain, ln_bias, b_in, near_out, w_in,
-    )
+        offsets, tile_counts, cotangent, left, right, layer_scale, ln_gain, ln_bias, b_in, near_out, w_in
+    )
+    forward_a, forward_b, sides = lax.optimization_barrier((left_a, right_b, sides))
+    opp_a, opp_b = shift(forward_a, 1), shift(forward_b, -1)
+    hidden_a, hidden_b = call(
+        opposite_kernel,
+        [struct((half, hid), f32)] * 2,
+        [VMEM] * 5,
+        [pltpu.VMEM((rows, share), bf16)],
+    )(hidden, cot_a, cot_b, layer_scale, near_out)
     message = struct((half + 16, share), bf16)
 
-    def block(blocks, hidden, earlier):
+    def block(blocks, hidden):
         return call(
             block_kernel,
             [message, struct((half, hid), bf16), struct((half, 1), f32), struct((half, 1), f32)],
-            [VMEM] * 11,
+            [VMEM] * 10,
             [pltpu.VMEM((half, width), bf16), pltpu.VMEM((half, width), bf16)],
-        )(*blocks, ln_gain, ln_bias, near_in, b_in, hidden, sides, earlier)
-
-    def parts(keep_ahead, own_ahead, act, away, earlier):
+        )(*blocks, ln_gain, ln_bias, near_in, b_in, hidden, sides)
+
+    def parts(keep_ahead, own_ahead, act, away):
         return call(
             functools.partial(parts_kernel, keep_ahead, own_ahead),
             [struct((half, share), bf16), message, struct((half, share), f32)],
-            [VMEM] * 4,
-        )(act, near_in, away, earlier)
+            [VMEM] * 3,
+        )(act, near_in, away)
 
     def middle(come, keep):
         return call(middle_kernel, [message], [VMEM] * 2)(come, keep)[0]
 
-    away_a, act_a, centers_a, inverses_a = block((mixed_a, left_a, right_a, opp_a), hidden_a, mixed_b)
+    away_a, act_a, centers_a, inverses_a = block((mixed_a, left_a, right_a, opp_a), hidden_a)
     come_a = shift(away_a, 1)
-    keep_a, own_a, mine_a = parts(1, 3, act_a, away_a, away_a)
+    keep_a, own_a, mine_a = parts(1, 3, act_a, away_a)
     got_a = shift(own_a, -1)
-    away_b, act_b, centers_b, inverses_b = block((mixed_b, left_b, right_b, opp_b), hidden_b, keep_a)
+    away_b, act_b, centers_b, inverses_b = block((mixed_b, left_b, right_b, opp_b), hidden_b)
     come_b = shift(away_b, -1)
-    keep_b, own_b, mine_b = parts(3, 1, act_b, away_b, got_a)
+    keep_b, own_b, mine_b = parts(3, 1, act_b, away_b)
     got_b = shift(own_b, 1)
     total_a = shift(middle(come_a, keep_a), 1)
     total_b = shift(middle(come_b, keep_b), -1)

time: 61 us -> 57.7 us (0.946)
  the two profiles are of different devices: /device:TPU:16 before, /device:TPU:28 now
where the time goes in v6:
time: 57.7 us; the launch traced here: 57.5 us
  Pallas kernels  29.2 us (51%)
  starting transfers between devices  23.9 us (41%)
  waiting for transfers between devices  3.97 us (7%)
    pallas_call x11, Pallas kernels, held(): run(*(pltpu.with_memory_space_constraint(a, pltpu.VMEM if spec is VMEM el...  29.2 us
    ppermute x16, starting transfers between devices, shift(): return lax.ppermute(x, 'ch', [(i, (i + by) % n) for i in range(n)])  23.9 us
    ppermute x16, waiting for transfers between devices, shift(): return lax.ppermute(x, 'ch', [(i, (i + by) % n) for i in range(n)])  3.97 us
  transfers between devices with their start and end apart: 16, of which 3 were waited for; matrix products, arithmetic and copies ran while one was open for 0% of the time, Pallas kernels for 43%

profile of v6, /device:TPU:28, one launch (start us, length us, event | category | flops | bytes accessed | tf_op | source)
XLA Modules:
  0.0 57.5 jit_solution(5575440493177167619)
XLA Ops:
  0.0 1.9 %collective-permute-start.3 = (bf16[32,4,4,384]{3,2,1,0:T(4,128)(2,1)}, bf16[32,4,4,384]{3,2,1,0:T(4,128)(2,1)S(1)}, u32[]{:S(2)}, u32[]{:S(2)}) collective-permute-start(bf16[32,4,4,384]{3,2,1,0:T(4,128)(2,1)} %own.1), channel_id=1, source_target_pairs={{0,1},{1,2},{2,3},{3,0},{4,5},{5,6},{6,7},{7,4},{8,9},{9,10},{10,1... | collective-permute-start | bytes 1179656 | tf_op jit(solution)/shard_map/ppermute | solution.py:386
  1.9 2.1 %collective-permute-start.4 = (bf16[32,4,4,384]{3,2,1,0:T(4,128)(2,1)}, bf16[32,4,4,384]{3,2,1,0:T(4,128)(2,1)S(1)}, u32[]{:S(2)}, u32[]{:S(2)}) collective-permute-start(bf16[32,4,4,384]{3,2,1,0:T(4,128)(2,1)} %own.1), channel_id=1, source_target_pairs={{0,3},{1,0},{2,1},{3,2},{4,7},{5,4},{6,5},{7,6},{8,11},{9,8},{10,9... | collective-permute-start | bytes 1179656 | tf_op jit(solution)/shard_map/ppermute | solution.py:386
  4.0 0.0 copy-start
  4.0 0.0 copy-start.1
  4.0 0.0 copy-start.2
  4.0 0.0 copy-start.3
  4.1 0.0 copy-start.4
  4.1 5.9 %shard_map.127 = (bf16[256,384]{1,0:T(8,128)(2,1)S(1)}, bf16[256,384]{1,0:T(8,128)(2,1)S(1)}, bf16[1536,1536]{1,0:T(8,128)(2,1)S(1)}, f32[3,28,8,128]{3,2,1,0:T(8,128)S(1)}) custom-call(s32[2,32]{1,0:T(2,128)} %bitcast.1, s32[1,2]{1,0:T(1,128)} %screen.3, bf16[32,32,384]{2,1,0:T(8,128)(2,1)} %canvas.1, bf16[49,384]{1,0:T(8,128)(2,1)} %dwk.1, f32[384]{0:T(512)} %bias.4, ...), custom_call_target="tpu_custom_call" | custom-call | tf_op jit(solution)/shard_map/pallas_call | solution.py:36
  10.0 2.1 %collective-permute-start.1 = (bf16[256,384]{1,0:T(8,128)(2,1)S(1)}, bf16[256,384]{1,0:T(8,128)(2,1)S(1)}, u32[]{:S(2)}, u32[]{:S(2)}) collective-permute-start(bf16[256,384]{1,0:T(8,128)(2,1)S(1)} %get-tuple-element.32.own.mixed), channel_id=1, source_target_pairs={{0,3},{1,0},{2,1},{3,2},{4,7},{5,4},{6,5},{7,6},{8,11},{9,8},{10,9... | collective-permute-start | bytes 589832 | tf_op jit(solution)/shard_map/ppermute | solution.py:386
  12.1 0.0 collective-permute-start.2
  12.1 1.3 %collective-permute-done.3.left = bf16[32,4,4,384]{3,2,1,0:T(4,128)(2,1)S(1)} collective-permute-done((bf16[32,4,4,384]{3,2,1,0:T(4,128)(2,1)}, bf16[32,4,4,384]{3,2,1,0:T(4,128)(2,1)S(1)}, u32[]{:S(2)}, u32[]{:S(2)}) %collective-permute-start.3) | collective-permute-done | bytes 393248 | tf_op jit(solution)/shard_map/ppermute | solution.py:386
  13.4 0.1 slice.8
  13.4 0.1 collective-permute-start.6
  13.5 3.2 %collective-permute-start.11 = (bf16[256,384]{1,0:T(8,128)(2,1)S(1)}, bf16[256,384]{1,0:T(8,128)(2,1)S(1)}, u32[]{:S(2)}, u32[]{:S(2)}) collective-permute-start(bf16[256,384]{1,0:T(8,128)(2,1)S(1)} %get-tuple-element.33.own.mixed), channel_id=1, source_target_pairs={{0,3},{1,0},{2,1},{3,2},{4,7},{5,4},{6,5},{7,6},{8,11},{9,8},{10,9... | collective-permute-start | bytes 589832 | tf_op jit(solution)/shard_map/ppermute | solution.py:386
  16.7 0.0 collective-permute-done.4.right
  16.7 0.1 slice.9
  16.8 1.6 %collective-permute-start.7 = (bf16[16,4,4,384]{3,2,1,0:T(4,128)(2,1)S(1)}, bf16[16,4,4,384]{3,2,1,0:T(4,128)(2,1)S(1)}, u32[]{:S(2)}, u32[]{:S(2)}) collective-permute-start(bf16[16,4,4,384]{3,2,1,0:T(4,128)(2,1)S(1)} %slice.9), channel_id=1, source_target_pairs={{0,3},{1,0},{2,1},{3,2},{4,7},{5,4},{6,5},{7,6},{8,11},{9,8},{10,9... | collective-permute-start | bytes 589832 | tf_op jit(solution)/shard_map/ppermute | solution.py:386
  18.4 0.0 copy-done
  18.4 0.0 copy-done.1
  18.4 0.0 copy-done.2
  18.4 0.0 copy-done.3
  18.4 0.0 copy-done.4
  18.4 4.7 %shard_map.128 = (f32[512,1536]{1,0:T(8,128)S(1)}, f32[3,38,48,128]{3,2,1,0:T(8,128)S(1)}, bf16[1536,1536]{1,0:T(8,128)(2,1)S(1)}, f32[8,1536]{1,0:T(8,128)S(1)}) custom-call(s32[2,32]{1,0:T(2,128)} %bitcast.2, s32[32]{0:T(128)} %counts.5, bf16[32,4,4,384]{3,2,1,0:T(4,128)(2,1)S(1)} %copy-done, bf16[32,4,4,384]{3,2,1,0:T(4,128)(2,1)S(1)} %collective-permute-done.3.left, ...), custom_call_target="tpu_custom_call" | custom-call | tf_op jit(solution)/shard_map/pallas_call | solution.py:36
  23.1 0.0 collective-permute-done.1.right
  23.1 0.0 collective-permute-done.2.left
  23.1 0.6 %collective-permute-start.12 = (bf16[256,384]{1,0:T(8,128)(2,1)S(1)}, bf16[256,384]{1,0:T(8,128)(2,1)S(1)}, u32[]{:S(2)}, u32[]{:S(2)}) collective-permute-start(bf16[256,384]{1,0:T(8,128)(2,1)S(1)} %collective-permute-done.2.left), channel_id=1, source_target_pairs={{0,1},{1,2},{2,3},{3,0},{4,5},{5,6},{6,7},{7,4},{8,9},{9,10},{10,1... | collective-permute-start | bytes 589832 | tf_op jit(solution)/shard_map/ppermute | solution.py:386
  23.7 0.1 collective-permute-start
  23.8 0.0 collective-permute-done.6.cot_a
  23.8 3.2 %collective-permute-start.5 = (bf16[256,384]{1,0:T(8,128)(2,1)S(1)}, bf16[256,384]{1,0:T(8,128)(2,1)S(1)}, u32[]{:S(2)}, u32[]{:S(2)}) collective-permute-start(bf16[256,384]{1,0:T(8,128)(2,1)S(1)} %collective-permute-done.1.right), channel_id=1, source_target_pairs={{0,3},{1,0},{2,1},{3,2},{4,7},{5,4},{6,5},{7,6},{8,11},{9,8},{10,9... | collective-permute-start | bytes 589832 | tf_op jit(solution)/shard_map/ppermute | solution.py:386
  27.0 0.0 collective-permute-done.7.cot_b
  27.0 1.1 %shard_map.129 = (f32[256,1536]{1,0:T(8,128)S(1)}, f32[256,1536]{1,0:T(8,128)S(1)}) custom-call(f32[512,1536]{1,0:T(8,128)S(1)} %get-tuple-element.38.before, bf16[16,4,4,384]{3,2,1,0:T(4,128)(2,1)S(1)} %collective-permute-done.6.cot_a, bf16[16,4,4,384]{3,2,1,0:T(4,128)(2,1)S(1)} %collective-permute-done.7.cot_b, f32[1536]{0:T(1024)S(1)} %copy-done.4, ...), custom_call_target="tpu_custom_call" | custom-call | tf_op jit(solution)/shard_map/pallas_call | solution.py:36
  28.1 0.0 collective-permute-done.11.right
  28.1 2.2 %collective-permute-done.12.opp = bf16[256,384]{1,0:T(8,128)(2,1)S(1)} collective-permute-done((bf16[256,384]{1,0:T(8,128)(2,1)S(1)}, bf16[256,384]{1,0:T(8,128)(2,1)S(1)}, u32[]{:S(2)}, u32[]{:S(2)}) %collective-permute-start.12) | collective-permute-done | bytes 196640 | tf_op jit(solution)/shard_map/ppermute | solution.py:386
  30.3 3.3 %shard_map.133 = (bf16[272,384]{1,0:T(8,128)(2,1)S(1)}, bf16[256,1536]{1,0:T(8,128)(2,1)S(1)}, f32[256,1]{1,0:T(8,128)S(1)}, f32[256,1]{1,0:T(8,128)S(1)}) custom-call(bf16[256,384]{1,0:T(8,128)(2,1)S(1)} %get-tuple-element.33.own.mixed, bf16[256,384]{1,0:T(8,128)(2,1)S(1)} %collective-permute-done.2.left, ...), custom_call_target="tpu_custom_call" | custom-call | tf_op jit(solution)/shard_map/pallas_call | solution.py:36
  33.6 0.8 %collective-permute-start.14 = (bf16[272,384]{1,0:T(8,128)(2,1)S(1)}, bf16[272,384]{1,0:T(8,128)(2,1)S(1)}, u32[]{:S(2)}, u32[]{:S(2)}) collective-permute-start(bf16[272,384]{1,0:T(8,128)(2,1)S(1)} %get-tuple-element.52.away), channel_id=1, source_target_pairs={{0,1},{1,2},{2,3},{3,0},{4,5},{5,6},{6,7},{7,4},{8,9},{9,10},{10,1... | collective-permute-start | bytes 626696 | tf_op jit(solution)/shard_map/ppermute | solution.py:386
  34.3 0.0 collective-permute-done.left
  34.3 0.0 collective-permute-done.5.opp
  34.3 3.3 %shard_map.130 = (bf16[272,384]{1,0:T(8,128)(2,1)S(1)}, bf16[256,1536]{1,0:T(8,128)(2,1)S(1)}, f32[256,1]{1,0:T(8,128)S(1)}, f32[256,1]{1,0:T(8,128)S(1)}) custom-call(bf16[256,384]{1,0:T(8,128)(2,1)S(1)} %get-tuple-element.32.own.mixed, bf16[256,384]{1,0:T(8,128)(2,1)S(1)} %collective-permute-done.left, bf16[256,384]{1,0:T(8,128)(2,1)S(1)} %collective-permute-done.1.right, ...), custom_call_target="tpu_custom_call" | custom-call | tf_op jit(solution)/shard_map/pallas_call | solution.py:36
  37.6 2.8 %collective-permute-start.9 = (bf16[272,384]{1,0:T(8,128)(2,1)S(1)}, bf16[272,384]{1,0:T(8,128)(2,1)S(1)}, u32[]{:S(2)}, u32[]{:S(2)}) collective-permute-start(bf16[272,384]{1,0:T(8,128)(2,1)S(1)} %get-tuple-element.42.away), channel_id=1, source_target_pairs={{0,3},{1,0},{2,1},{3,2},{4,7},{5,4},{6,5},{7,6},{8,11},{9,8},{10,9... | collective-permute-start | bytes 626696 | tf_op jit(solution)/shard_map/ppermute | solution.py:386
  40.4 1.4 %shard_map.134 = (bf16[256,384]{1,0:T(8,128)(2,1)S(1)}, bf16[272,384]{1,0:T(8,128)(2,1)S(1)}, f32[256,384]{1,0:T(8,128)S(1)}) custom-call(bf16[256,1536]{1,0:T(8,128)(2,1)S(1)} %get-tuple-element.51.act, bf16[1536,1536]{1,0:T(8,128)(2,1)S(1)} %get-tuple-element.37.w_in, bf16[272,384]{1,0:T(8,128)(2,1)S(1)} %get-tuple-element.52.away), custom_call_target="tpu_custom_call" | custom-call | tf_op jit(solution)/shard_map/pallas_call | solution.py:36
  41.8 0.1 collective-permute-start.13
  41.9 0.0 collective-permute-done.14.come
  41.9 0.1 shard_map.135
  42.0 2.1 %collective-permute-start.15 = (bf16[272,384]{1,0:T(8,128)(2,1)S(1)}, bf16[272,384]{1,0:T(8,128)(2,1)S(1)}, u32[]{:S(2)}, u32[]{:S(2)}) collective-permute-start(bf16[272,384]{1,0:T(8,128)(2,1)S(1)} %shard_map.135), channel_id=1, source_target_pairs={{0,1},{1,2},{2,3},{3,0},{4,5},{5,6},{6,7},{7,4},{8,9},{9,10},{10,1... | collective-permute-start | bytes 626696 | tf_op jit(solution)/shard_map/ppermute | solution.py:386
  44.0 1.4 %shard_map.131 = (bf16[256,384]{1,0:T(8,128)(2,1)S(1)}, bf16[272,384]{1,0:T(8,128)(2,1)S(1)}, f32[256,384]{1,0:T(8,128)S(1)}) custom-call(bf16[256,1536]{1,0:T(8,128)(2,1)S(1)} %get-tuple-element.41.act, bf16[1536,1536]{1,0:T(8,128)(2,1)S(1)} %get-tuple-element.37.w_in, bf16[272,384]{1,0:T(8,128)(2,1)S(1)} %get-tuple-element.42.away), custom_call_target="tpu_custom_call" | custom-call | tf_op jit(solution)/shard_map/pallas_call | solution.py:36
  45.4 0.1 collective-permute-start.8
  45.5 0.0 collective-permute-done.9.come
  45.5 0.1 shard_map.132
  45.6 3.3 %collective-permute-start.10 = (bf16[272,384]{1,0:T(8,128)(2,1)S(1)}, bf16[272,384]{1,0:T(8,128)(2,1)S(1)}, u32[]{:S(2)}, u32[]{:S(2)}) collective-permute-start(bf16[272,384]{1,0:T(8,128)(2,1)S(1)} %shard_map.132), channel_id=1, source_target_pairs={{0,3},{1,0},{2,1},{3,2},{4,7},{5,4},{6,5},{7,6},{8,11},{9,8},{10,9... | collective-permute-start | bytes 626696 | tf_op jit(solution)/shard_map/ppermute | solution.py:386
  48.9 0.0 collective-permute-done.13.got
  48.9 0.5 collective-permute-done.15.total
  49.3 3.4 %shard_map.136.before = f32[3,38,48,128]{3,2,1,0:T(8,128)S(1)} custom-call(s32[2,32]{1,0:T(2,128)} %bitcast.3, s32[32]{0:T(128)} %counts.5, f32[256,384]{1,0:T(8,128)S(1)} %get-tuple-element.53.mine, bf16[272,384]{1,0:T(8,128)(2,1)S(1)} %collective-permute-done.13.got, bf16[272,384]{1,0:T(8,128)(2,1)S(1)} %collective-permute-done.15.total, ...), custom_call_target="tpu_custom_call" | custom-call | tf_op jit(solution)/shard_map/pallas_call | solution.py:36
  52.8 0.0 collective-permute-done.8.got
  52.8 0.0 collective-permute-done.10.total
  52.8 4.6 %shard_map.137 = f32[32,32,384]{2,1,0:T(8,128)} custom-call(s32[2,32]{1,0:T(2,128)} %bitcast.4, s32[32]{0:T(128)} %counts.5, s32[1,2]{1,0:T(1,128)} %screen.3, f32[256,384]{1,0:T(8,128)S(1)} %get-tuple-element.43.mine, bf16[272,384]{1,0:T(8,128)(2,1)S(1)} %collective-permute-done.8.got, bf16[272,384]{1,0:T(8,128)(2,1)S(1)} %collective-permute-done.10.total, ...), custom_call_target="tpu_custom_call" | custom-call | tf_op jit(solution)/shard_map/pallas_call | solution.py:36
Async XLA Ops:
  0.0 13.4 %collective-permute-start.3 = (bf16[32,4,4,384]{3,2,1,0:T(4,128)(2,1)}, bf16[32,4,4,384]{3,2,1,0:T(4,128)(2,1)S(1)}, u32[]{:S(2)}, u32[]{:S(2)}) collective-permute-start(bf16[32,4,4,384]{3,2,1,0:T(4,128)(2,1)} %own.1), channel_id=1, source_target_pairs={{0,1},{1,2},{2,3},{3,0},{4,5},{5,6},{6,7},{7,4},{8,9},{9,10},{10,1... | collective-permute-start | bytes 1179656 | tf_op jit(solution)/shard_map/ppermute | solution.py:386
  1.9 14.8 %collective-permute-start.4 = (bf16[32,4,4,384]{3,2,1,0:T(4,128)(2,1)}, bf16[32,4,4,384]{3,2,1,0:T(4,128)(2,1)S(1)}, u32[]{:S(2)}, u32[]{:S(2)}) collective-permute-start(bf16[32,4,4,384]{3,2,1,0:T(4,128)(2,1)} %own.1), channel_id=1, source_target_pairs={{0,3},{1,0},{2,1},{3,2},{4,7},{5,4},{6,5},{7,6},{8,11},{9,8},{10,9... | collective-permute-start | bytes 1179656 | tf_op jit(solution)/shard_map/ppermute | solution.py:386
  4.0 14.3 %copy-start = (bf16[32,4,4,384]{3,2,1,0:T(4,128)(2,1)S(1)}, bf16[32,4,4,384]{3,2,1,0:T(4,128)(2,1)}, u32[]{:S(2)}) copy-start(bf16[32,4,4,384]{3,2,1,0:T(4,128)(2,1)} %own.1) | copy-start | bytes 1179652
  4.0 14.3 %copy-start.1 = (f32[1536]{0:T(1024)S(1)}, f32[1536]{0:T(1024)}, u32[]{:S(2)}) copy-start(f32[1536]{0:T(1024)} %gain.9) | copy-start | bytes 18436
  4.0 14.3 %copy-start.2 = (f32[1536]{0:T(1024)S(1)}, f32[1536]{0:T(1024)}, u32[]{:S(2)}) copy-start(f32[1536]{0:T(1024)} %bias.7) | copy-start | bytes 18436
  4.0 14.3 %copy-start.3 = (f32[1536]{0:T(1024)S(1)}, f32[1536]{0:T(1024)}, u32[]{:S(2)}) copy-start(f32[1536]{0:T(1024)} %b_in.5) | copy-start | bytes 18436
  4.1 14.3 %copy-start.4 = (f32[1536]{0:T(1024)S(1)}, f32[1536]{0:T(1024)}, u32[]{:S(2)}) copy-start(f32[1536]{0:T(1024)} %scale.3) | copy-start | bytes 18436
  10.0 13.1 %collective-permute-start.1 = (bf16[256,384]{1,0:T(8,128)(2,1)S(1)}, bf16[256,384]{1,0:T(8,128)(2,1)S(1)}, u32[]{:S(2)}, u32[]{:S(2)}) collective-permute-start(bf16[256,384]{1,0:T(8,128)(2,1)S(1)} %get-tuple-element.32.own.mixed), channel_id=1, source_target_pairs={{0,3},{1,0},{2,1},{3,2},{4,7},{5,4},{6,5},{7,6},{8,11},{9,8},{10,9... | collective-permute-start | bytes 589832 | tf_op jit(solution)/shard_map/ppermute | solution.py:386
  12.1 11.0 %collective-permute-start.2 = (bf16[256,384]{1,0:T(8,128)(2,1)S(1)}, bf16[256,384]{1,0:T(8,128)(2,1)S(1)}, u32[]{:S(2)}, u32[]{:S(2)}) collective-permute-start(bf16[256,384]{1,0:T(8,128)(2,1)S(1)} %get-tuple-element.33.own.mixed), channel_id=1, source_target_pairs={{0,1},{1,2},{2,3},{3,0},{4,5},{5,6},{6,7},{7,4},{8,9},{9,10},{10,1... | collective-permute-start | bytes 589832 | tf_op jit(solution)/shard_map/ppermute | solution.py:386
  13.4 10.4 %collective-permute-start.6 = (bf16[16,4,4,384]{3,2,1,0:T(4,128)(2,1)S(1)}, bf16[16,4,4,384]{3,2,1,0:T(4,128)(2,1)S(1)}, u32[]{:S(2)}, u32[]{:S(2)}) collective-permute-start(bf16[16,4,4,384]{3,2,1,0:T(4,128)(2,1)S(1)} %slice.8), channel_id=1, source_target_pairs={{0,1},{1,2},{2,3},{3,0},{4,5},{5,6},{6,7},{7,4},{8,9},{9,10},{10,1... | collective-permute-start | bytes 589832 | tf_op jit(solution)/shard_map/ppermute | solution.py:386
  13.5 14.5 %collective-permute-start.11 = (bf16[256,384]{1,0:T(8,128)(2,1)S(1)}, bf16[256,384]{1,0:T(8,128)(2,1)S(1)}, u32[]{:S(2)}, u32[]{:S(2)}) collective-permute-start(bf16[256,384]{1,0:T(8,128)(2,1)S(1)} %get-tuple-element.33.own.mixed), channel_id=1, source_target_pairs={{0,3},{1,0},{2,1},{3,2},{4,7},{5,4},{6,5},{7,6},{8,11},{9,8},{10,9... | collective-permute-start | bytes 589832 | tf_op jit(solution)/shard_map/ppermute | solution.py:386
  16.8 10.2 %collective-permute-start.7 = (bf16[16,4,4,384]{3,2,1,0:T(4,128)(2,1)S(1)}, bf16[16,4,4,384]{3,2,1,0:T(4,128)(2,1)S(1)}, u32[]{:S(2)}, u32[]{:S(2)}) collective-permute-start(bf16[16,4,4,384]{3,2,1,0:T(4,128)(2,1)S(1)} %slice.9), channel_id=1, source_target_pairs={{0,3},{1,0},{2,1},{3,2},{4,7},{5,4},{6,5},{7,6},{8,11},{9,8},{10,9... | collective-permute-start | bytes 589832 | tf_op jit(solution)/shard_map/ppermute | solution.py:386
  23.1 7.1 %collective-permute-start.12 = (bf16[256,384]{1,0:T(8,128)(2,1)S(1)}, bf16[256,384]{1,0:T(8,128)(2,1)S(1)}, u32[]{:S(2)}, u32[]{:S(2)}) collective-permute-start(bf16[256,384]{1,0:T(8,128)(2,1)S(1)} %collective-permute-done.2.left), channel_id=1, source_target_pairs={{0,1},{1,2},{2,3},{3,0},{4,5},{5,6},{6,7},{7,4},{8,9},{9,10},{10,1... | collective-permute-start | bytes 589832 | tf_op jit(solution)/shard_map/ppermute | solution.py:386
  23.7 10.6 %collective-permute-start = (bf16[256,384]{1,0:T(8,128)(2,1)S(1)}, bf16[256,384]{1,0:T(8,128)(2,1)S(1)}, u32[]{:S(2)}, u32[]{:S(2)}) collective-permute-start(bf16[256,384]{1,0:T(8,128)(2,1)S(1)} %get-tuple-element.32.own.mixed), channel_id=1, source_target_pairs={{0,1},{1,2},{2,3},{3,0},{4,5},{5,6},{6,7},{7,4},{8,9},{9,10},{10,1... | collective-permute-start | bytes 589832 | tf_op jit(solution)/shard_map/ppermute | solution.py:386
  23.8 10.5 %collective-permute-start.5 = (bf16[256,384]{1,0:T(8,128)(2,1)S(1)}, bf16[256,384]{1,0:T(8,128)(2,1)S(1)}, u32[]{:S(2)}, u32[]{:S(2)}) collective-permute-start(bf16[256,384]{1,0:T(8,128)(2,1)S(1)} %collective-permute-done.1.right), channel_id=1, source_target_pairs={{0,3},{1,0},{2,1},{3,2},{4,7},{5,4},{6,5},{7,6},{8,11},{9,8},{10,9... | collective-permute-start | bytes 589832 | tf_op jit(solution)/shard_map/ppermute | solution.py:386
  33.6 8.3 %collective-permute-start.14 = (bf16[272,384]{1,0:T(8,128)(2,1)S(1)}, bf16[272,384]{1,0:T(8,128)(2,1)S(1)}, u32[]{:S(2)}, u32[]{:S(2)}) collective-permute-start(bf16[272,384]{1,0:T(8,128)(2,1)S(1)} %get-tuple-element.52.away), channel_id=1, source_target_pairs={{0,1},{1,2},{2,3},{3,0},{4,5},{5,6},{6,7},{7,4},{8,9},{9,10},{10,1... | collective-permute-start | bytes 626696 | tf_op jit(solution)/shard_map/ppermute | solution.py:386
  37.6 7.9 %collective-permute-start.9 = (bf16[272,384]{1,0:T(8,128)(2,1)S(1)}, bf16[272,384]{1,0:T(8,128)(2,1)S(1)}, u32[]{:S(2)}, u32[]{:S(2)}) collective-permute-start(bf16[272,384]{1,0:T(8,128)(2,1)S(1)} %get-tuple-element.42.away), channel_id=1, source_target_pairs={{0,3},{1,0},{2,1},{3,2},{4,7},{5,4},{6,5},{7,6},{8,11},{9,8},{10,9... | collective-permute-start | bytes 626696 | tf_op jit(solution)/shard_map/ppermute | solution.py:386
  41.8 7.1 %collective-permute-start.13 = (bf16[272,384]{1,0:T(8,128)(2,1)S(1)}, bf16[272,384]{1,0:T(8,128)(2,1)S(1)}, u32[]{:S(2)}, u32[]{:S(2)}) collective-permute-start(bf16[272,384]{1,0:T(8,128)(2,1)S(1)} %get-tuple-element.54), channel_id=1, source_target_pairs={{0,3},{1,0},{2,1},{3,2},{4,7},{5,4},{6,5},{7,6},{8,11},{9,8},{10,9... | collective-permute-start | bytes 626696 | tf_op jit(solution)/shard_map/ppermute | solution.py:386
  42.0 7.4 %collective-permute-start.15 = (bf16[272,384]{1,0:T(8,128)(2,1)S(1)}, bf16[272,384]{1,0:T(8,128)(2,1)S(1)}, u32[]{:S(2)}, u32[]{:S(2)}) collective-permute-start(bf16[272,384]{1,0:T(8,128)(2,1)S(1)} %shard_map.135), channel_id=1, source_target_pairs={{0,1},{1,2},{2,3},{3,0},{4,5},{5,6},{6,7},{7,4},{8,9},{9,10},{10,1... | collective-permute-start | bytes 626696 | tf_op jit(solution)/shard_map/ppermute | solution.py:386
  45.4 7.3 %collective-permute-start.8 = (bf16[272,384]{1,0:T(8,128)(2,1)S(1)}, bf16[272,384]{1,0:T(8,128)(2,1)S(1)}, u32[]{:S(2)}, u32[]{:S(2)}) collective-permute-start(bf16[272,384]{1,0:T(8,128)(2,1)S(1)} %get-tuple-element.44), channel_id=1, source_target_pairs={{0,1},{1,2},{2,3},{3,0},{4,5},{5,6},{6,7},{7,4},{8,9},{9,10},{10,1... | collective-permute-start | bytes 626696 | tf_op jit(solution)/shard_map/ppermute | solution.py:386
  45.6 7.2 %collective-permute-start.10 = (bf16[272,384]{1,0:T(8,128)(2,1)S(1)}, bf16[272,384]{1,0:T(8,128)(2,1)S(1)}, u32[]{:S(2)}, u32[]{:S(2)}) collective-permute-start(bf16[272,384]{1,0:T(8,128)(2,1)S(1)} %shard_map.132), channel_id=1, source_target_pairs={{0,3},{1,0},{2,1},{3,2},{4,7},{5,4},{6,5},{7,6},{8,11},{9,8},{10,9... | collective-permute-start | bytes 626696 | tf_op jit(solution)/shard_map/ppermute | solution.py:386

commit v7 on v6

--- a/solution.py
+++ b/solution.py
@@ -139,9 +139,10 @@
 
 
 def hidden_kernel(
-    offsets, counts, own, left, right, scale, gain, bias, b_in, w_out, w_in,
-    hidden, taken, near_in, sides, flat, sem,
-):
+    offsets, counts, own, left, right, scale, gain, bias, b_in, w_out, earlier, w_in,
+    hidden_a, hidden_b, taken, near_in, sides, flat, sem,
+):
+    del earlier
     fetch = pltpu.make_async_copy(w_in, near_in, sem)
     fetch.start()
     share = own.shape[3]
@@ -161,7 +162,7 @@
         begins.append(channels_of(ahead, share))
         flat[k] = scaled_rows(cells, scale, begins[k])
     step = 512
-    for n in range(0, hidden.shape[1], step):
+    for n in range(0, hidden_a.shape[1], step):
         total = None
         for k, begin in enumerate(begins):
             product = lax.dot_general(
@@ -171,7 +172,8 @@
                 preferred_element_type=jnp.float32,
             )
             total = product if total is None else total + product
-        hidden[:, n : n + step] = total
+        hidden_a[:, n : n + step] = total[: hidden_a.shape[0]]
+        hidden_b[:, n : n + step] = total[hidden_a.shape[0] :]
     width = gain.shape[0]
     lines = two_parts(gain[...][None]) + two_parts(bias[...][None])
     lines = jnp.concatenate(lines + [jnp.zeros((12, width), jnp.float32)], 0).astype(jnp.bfloat16)
@@ -181,22 +183,19 @@
     sides[1:2, :] = both[2:3] + both[3:4] + b_in[...][None]
 
 
-def opposite_kernel(before, cot_a, cot_b, scale, w_out, hidden_a, hidden_b, flat):
-    rows, share = flat.shape
-    half = rows // 2
+def opposite_kernel(before, cot, scale, w_out, earlier, hidden, flat):
+    del earlier
+    share = flat.shape[1]
     begin = channels_of(2, share)
-    flat[:half, :] = scaled_rows(cot_a, scale, begin)
-    flat[half:, :] = scaled_rows(cot_b, scale, begin)
+    flat[...] = scaled_rows(cot, scale, begin)
     step = 512
     for n in range(0, before.shape[1], step):
-        product = lax.dot_general(
+        hidden[:, n : n + step] = before[:, n : n + step] + lax.dot_general(
             flat[...],
             w_out[n : n + step, pl.ds(begin, share)],
             (((1,), (1,)), ((), ())),
             preferred_element_type=jnp.float32,
         )
-        hidden_a[:, n : n + step] = before[:half, n : n + step] + product[:half]
-        hidden_b[:, n : n + step] = before[half:, n : n + step] + product[half:]
 
 
 def gelu_slope(v):
@@ -430,25 +429,31 @@
         ],
     )(offsets, screen_size, canvas, dw_kernel, dw_bias, w_out)
     left_a, right_a = shift(mixed_a, 1), shift(mixed_a, -1)
-    cot_a, cot_b = shift(left[: slots // 2], 1), shift(right[slots // 2 :], -1)
-    right_b, left_b = shift(mixed_b, -1), shift(mixed_b, 1)
+    cot_a = shift(right[: slots // 2], -1)
+    second, right = lax.optimization_barrier((mixed_b, right))
+    left_b, right_b = shift(second, 1), shift(second, -1)
+    opp_a = shift(left_a, 1)
     canvas_like = struct((lanes, PAD_ROWS, PAD_COLS, 128), f32)
-    hidden, taken, near_in, sides = call(
+    hidden_a, hidden_b, taken, near_in, sides = call(
         hidden_kernel,
-        [struct((rows, hid), f32), canvas_like, struct(w_in.shape, bf16), struct((8, hid), f32)],
-        [SMEM] * 2 + [VMEM] * 8 + [HBM],
+        [struct((half, hid), f32), struct((half, hid), f32), canvas_like, struct(w_in.shape, bf16), struct((8, hid), f32)],
+        [SMEM] * 2 + [VMEM] * 9 + [HBM],
         [pltpu.VMEM((3, rows, share), bf16), pltpu.SemaphoreType.DMA(())],
     )(
-        offsets, tile_counts, cotangent, left, right, layer_scale, ln_gain, ln_bias, b_in, near_out, w_in
-    )
-    forward_a, forward_b, sides = lax.optimization_barrier((left_a, right_b, sides))
-    opp_a, opp_b = shift(forward_a, 1), shift(forward_b, -1)
-    hidden_a, hidden_b = call(
-        opposite_kernel,
-        [struct((half, hid), f32)] * 2,
-        [VMEM] * 5,
-        [pltpu.VMEM((rows, share), bf16)],
-    )(hidden, cot_a, cot_b, layer_scale, near_out)
+        offsets, tile_counts, cotangent, left, right, layer_scale, ln_gain, ln_bias, b_in, near_out, right_a, w_in
+    )
+    forward_b, forward_cot, sides = lax.optimization_barrier((left_b, right, sides))
+    cot_b = shift(forward_cot[slots // 2 :], -1)
+    opp_b = shift(forward_b, 1)
+
+    def with_opposite(hidden, cot):
+        return call(
+            opposite_kernel,
+            [struct((half, hid), f32)],
+            [VMEM] * 5,
+            [pltpu.VMEM((half, share), bf16)],
+        )(hidden, cot, layer_scale, near_out, right_b)[0]
+
     message = struct((half + 16, share), bf16)
 
     def block(blocks, hidden):
@@ -469,11 +474,11 @@
     def middle(come, keep):
         return call(middle_kernel, [message], [VMEM] * 2)(come, keep)[0]
 
-    away_a, act_a, centers_a, inverses_a = block((mixed_a, left_a, right_a, opp_a), hidden_a)
+    away_a, act_a, centers_a, inverses_a = block((mixed_a, left_a, right_a, opp_a), with_opposite(hidden_a, cot_a))
     come_a = shift(away_a, 1)
     keep_a, own_a, mine_a = parts(1, 3, act_a, away_a)
     got_a = shift(own_a, -1)
-    away_b, act_b, centers_b, inverses_b = block((mixed_b, left_b, right_b, opp_b), hidden_b)
+    away_b, act_b, centers_b, inverses_b = block((mixed_b, left_b, right_b, opp_b), with_opposite(hidden_b, cot_b))
     come_b = shift(away_b, -1)
     keep_b, own_b, mine_b = parts(3, 1, act_b, away_b)
     got_b = shift(own_b, 1)

time: 57.7 us -> 63.5 us (1.10)
  waiting for transfers between devices: 3.97 us -> 11.5 us
  starting transfers between devices: 23.9 us -> 21.9 us
    ppermute x16, waiting for transfers between devices: 3.97 us -> 11.5 us  [shift(): return lax.ppermute(x, 'ch', [(i, (i + by) % n) for i in range(n)])]
    ppermute x16, starting transfers between devices: 23.9 us -> 21.9 us  [shift(): return lax.ppermute(x, 'ch', [(i, (i + by) % n) for i in range(n)])]
    pallas_call x11 -> x12, Pallas kernels: 29.2 us -> 29 us  [held(): run(*(pltpu.with_memory_space_constraint(a, pltpu.VMEM if spec is VMEM el...]
  transfers between devices with their start and end apart: 16 -> 16, of which waited for: 3 -> 4; matrix products, arithmetic and copies ran while one was open for 0% -> 0% of each run, Pallas kernels for 43% -> 39%
where the time goes in v7:
time: 63.5 us; the launch traced here: 62.9 us
  Pallas kernels  29 us (46%)
  starting transfers between devices  21.9 us (34%)
  waiting for transfers between devices  11.5 us (18%)
    pallas_call x12, Pallas kernels, held(): run(*(pltpu.with_memory_space_constraint(a, pltpu.VMEM if spec is VMEM el...  29 us
    ppermute x16, starting transfers between devices, shift(): return lax.ppermute(x, 'ch', [(i, (i + by) % n) for i in range(n)])  21.9 us
    ppermute x16, waiting for transfers between devices, shift(): return lax.ppermute(x, 'ch', [(i, (i + by) % n) for i in range(n)])  11.5 us
  transfers between devices with their start and end apart: 16, of which 4 were waited for; matrix products, arithmetic and copies ran while one was open for 0% of the time, Pallas kernels for 39%

profile of v7, /device:TPU:28, one launch (start us, length us, event | category | flops | bytes accessed | tf_op | source)
XLA Modules:
  0.0 62.9 jit_solution(8432858959255600735)
XLA Ops:
  0.0 4.0 %collective-permute-start = (bf16[32,4,4,384]{3,2,1,0:T(4,128)(2,1)}, bf16[32,4,4,384]{3,2,1,0:T(4,128)(2,1)S(1)}, u32[]{:S(2)}, u32[]{:S(2)}) collective-permute-start(bf16[32,4,4,384]{3,2,1,0:T(4,128)(2,1)} %own.1), channel_id=1, source_target_pairs={{0,3},{1,0},{2,1},{3,2},{4,7},{5,4},{6,5},{7,6},{8,11},{9,8},{10,9... | collective-permute-start | bytes 1179656 | tf_op jit(solution)/shard_map/ppermute | solution.py:385
  4.0 0.0 collective-permute-start.3
  4.0 0.0 copy-start
  4.0 0.0 copy-start.1
  4.0 0.0 copy-start.2
  4.1 0.0 copy-start.3
  4.1 0.0 copy-start.4
  4.1 5.9 %shard_map.127 = (bf16[256,384]{1,0:T(8,128)(2,1)S(1)}, bf16[256,384]{1,0:T(8,128)(2,1)S(1)}, bf16[1536,1536]{1,0:T(8,128)(2,1)S(1)}, f32[3,28,8,128]{3,2,1,0:T(8,128)S(1)}) custom-call(s32[2,32]{1,0:T(2,128)} %bitcast.1, s32[1,2]{1,0:T(1,128)} %screen.3, bf16[32,32,384]{2,1,0:T(8,128)(2,1)} %canvas.1, bf16[49,384]{1,0:T(8,128)(2,1)} %dwk.1, f32[384]{0:T(512)} %bias.4, ...), custom_call_target="tpu_custom_call" | custom-call | tf_op jit(solution)/shard_map/pallas_call | solution.py:36
  10.0 0.1 collective-permute-start.10
  10.1 3.3 %collective-permute-start.4 = (bf16[256,384]{1,0:T(8,128)(2,1)S(1)}, bf16[256,384]{1,0:T(8,128)(2,1)S(1)}, u32[]{:S(2)}, u32[]{:S(2)}) collective-permute-start(bf16[256,384]{1,0:T(8,128)(2,1)S(1)} %get-tuple-element.37.own.mixed), channel_id=1, source_target_pairs={{0,3},{1,0},{2,1},{3,2},{4,7},{5,4},{6,5},{7,6},{8,11},{9,8},{10,9... | collective-permute-start | bytes 589832 | tf_op jit(solution)/shard_map/ppermute | solution.py:385
  13.4 0.0 collective-permute-done.right
  13.4 0.0 collective-permute-start.1
  13.4 8.3 %collective-permute-done.10.left = bf16[256,384]{1,0:T(8,128)(2,1)S(1)} collective-permute-done((bf16[256,384]{1,0:T(8,128)(2,1)S(1)}, bf16[256,384]{1,0:T(8,128)(2,1)S(1)}, u32[]{:S(2)}, u32[]{:S(2)}) %collective-permute-start.10) | collective-permute-done | bytes 196640 | tf_op jit(solution)/shard_map/ppermute | solution.py:385
  21.7 0.0 collective-permute-start.11
  21.7 3.2 %collective-permute-start.2 = (bf16[256,384]{1,0:T(8,128)(2,1)S(1)}, bf16[256,384]{1,0:T(8,128)(2,1)S(1)}, u32[]{:S(2)}, u32[]{:S(2)}) collective-permute-start(bf16[256,384]{1,0:T(8,128)(2,1)S(1)} %get-tuple-element.34.own.mixed), channel_id=1, source_target_pairs={{0,3},{1,0},{2,1},{3,2},{4,7},{5,4},{6,5},{7,6},{8,11},{9,8},{10,9... | collective-permute-start | bytes 589832 | tf_op jit(solution)/shard_map/ppermute | solution.py:385
  24.9 0.1 slice.8
  25.0 0.0 collective-permute-done.4.earlier.right
  25.0 0.1 collective-permute-start.12
  25.1 0.0 collective-permute-done.3.left
  25.1 0.0 copy-done
  25.1 0.0 copy-done.1
  25.1 0.0 copy-done.2
  25.2 0.0 copy-done.3
  25.2 0.0 copy-done.4
  25.2 4.7 %shard_map.128 = (f32[256,1536]{1,0:T(8,128)S(1)}, f32[256,1536]{1,0:T(8,128)S(1)}, f32[3,38,48,128]{3,2,1,0:T(8,128)S(1)}, bf16[1536,1536]{1,0:T(8,128)(2,1)S(1)}, f32[8,1536]{1,0:T(8,128)S(1)}) custom-call(s32[2,32]{1,0:T(2,128)} %bitcast.2, s32[32]{0:T(128)} %counts.5, bf16[32,4,4,384]{3,2,1,0:T(4,128)(2,1)S(1)} %copy-done, ...), custom_call_target="tpu_custom_call" | custom-call | tf_op jit(solution)/shard_map/pallas_call | solution.py:36
  29.9 0.0 collective-permute-done.1.left
  29.9 0.1 slice.6
  29.9 0.1 collective-permute-start.6
  30.0 2.1 %collective-permute-start.5 = (bf16[256,384]{1,0:T(8,128)(2,1)S(1)}, bf16[256,384]{1,0:T(8,128)(2,1)S(1)}, u32[]{:S(2)}, u32[]{:S(2)}) collective-permute-start(bf16[256,384]{1,0:T(8,128)(2,1)S(1)} %collective-permute-done.1.left), channel_id=1, source_target_pairs={{0,1},{1,2},{2,3},{3,0},{4,5},{5,6},{6,7},{7,4},{8,9},{9,10},{10,1... | collective-permute-start | bytes 589832 | tf_op jit(solution)/shard_map/ppermute | solution.py:385
  32.1 0.6 collective-permute-done.12.cot
  32.7 0.0 collective-permute-done.2.earlier.right
  32.7 0.7 %shard_map.133.hidden = f32[256,1536]{1,0:T(8,128)S(1)} custom-call(f32[256,1536]{1,0:T(8,128)S(1)} %get-tuple-element.52.before, bf16[16,4,4,384]{3,2,1,0:T(4,128)(2,1)S(1)} %collective-permute-done.12.cot, f32[1536]{0:T(1024)S(1)} %copy-done.2, bf16[1536,1536]{1,0:T(8,128)(2,1)S(1)} %get-tuple-element.36.w_out, ...), custom_call_target="tpu_custom_call" | custom-call | tf_op jit(solution)/shard_map/pallas_call | solution.py:36
  33.3 0.0 collective-permute-done.11.opp
  33.4 3.3 %shard_map.134 = (bf16[272,384]{1,0:T(8,128)(2,1)S(1)}, bf16[256,1536]{1,0:T(8,128)(2,1)S(1)}, f32[256,1]{1,0:T(8,128)S(1)}, f32[256,1]{1,0:T(8,128)S(1)}) custom-call(bf16[256,384]{1,0:T(8,128)(2,1)S(1)} %get-tuple-element.37.own.mixed, bf16[256,384]{1,0:T(8,128)(2,1)S(1)} %collective-permute-done.10.left, ...), custom_call_target="tpu_custom_call" | custom-call | tf_op jit(solution)/shard_map/pallas_call | solution.py:36
  36.7 1.6 %collective-permute-start.14 = (bf16[272,384]{1,0:T(8,128)(2,1)S(1)}, bf16[272,384]{1,0:T(8,128)(2,1)S(1)}, u32[]{:S(2)}, u32[]{:S(2)}) collective-permute-start(bf16[272,384]{1,0:T(8,128)(2,1)S(1)} %get-tuple-element.54.away), channel_id=1, source_target_pairs={{0,1},{1,2},{2,3},{3,0},{4,5},{5,6},{6,7},{7,4},{8,9},{9,10},{10,1... | collective-permute-start | bytes 626696 | tf_op jit(solution)/shard_map/ppermute | solution.py:385
  38.3 0.0 collective-permute-done.6.cot
  38.3 0.6 shard_map.129.hidden
  38.9 0.0 collective-permute-done.5.opp
  38.9 3.3 %shard_map.130 = (bf16[272,384]{1,0:T(8,128)(2,1)S(1)}, bf16[256,1536]{1,0:T(8,128)(2,1)S(1)}, f32[256,1]{1,0:T(8,128)S(1)}, f32[256,1]{1,0:T(8,128)S(1)}) custom-call(bf16[256,384]{1,0:T(8,128)(2,1)S(1)} %get-tuple-element.34.own.mixed, bf16[256,384]{1,0:T(8,128)(2,1)S(1)} %collective-permute-done.1.left, ...), custom_call_target="tpu_custom_call" | custom-call | tf_op jit(solution)/shard_map/pallas_call | solution.py:36
  42.2 2.3 %collective-permute-start.8 = (bf16[272,384]{1,0:T(8,128)(2,1)S(1)}, bf16[272,384]{1,0:T(8,128)(2,1)S(1)}, u32[]{:S(2)}, u32[]{:S(2)}) collective-permute-start(bf16[272,384]{1,0:T(8,128)(2,1)S(1)} %get-tuple-element.45.away), channel_id=1, source_target_pairs={{0,3},{1,0},{2,1},{3,2},{4,7},{5,4},{6,5},{7,6},{8,11},{9,8},{10,9... | collective-permute-start | bytes 626696 | tf_op jit(solution)/shard_map/ppermute | solution.py:385
  44.5 1.4 %shard_map.135 = (bf16[256,384]{1,0:T(8,128)(2,1)S(1)}, bf16[272,384]{1,0:T(8,128)(2,1)S(1)}, f32[256,384]{1,0:T(8,128)S(1)}) custom-call(bf16[256,1536]{1,0:T(8,128)(2,1)S(1)} %get-tuple-element.53.act, bf16[1536,1536]{1,0:T(8,128)(2,1)S(1)} %get-tuple-element.40.w_in, bf16[272,384]{1,0:T(8,128)(2,1)S(1)} %get-tuple-element.54.away), custom_call_target="tpu_custom_call" | custom-call | tf_op jit(solution)/shard_map/pallas_call | solution.py:36
  45.9 2.1 %collective-permute-start.13 = (bf16[272,384]{1,0:T(8,128)(2,1)S(1)}, bf16[272,384]{1,0:T(8,128)(2,1)S(1)}, u32[]{:S(2)}, u32[]{:S(2)}) collective-permute-start(bf16[272,384]{1,0:T(8,128)(2,1)S(1)} %get-tuple-element.56), channel_id=1, source_target_pairs={{0,3},{1,0},{2,1},{3,2},{4,7},{5,4},{6,5},{7,6},{8,11},{9,8},{10,9... | collective-permute-start | bytes 626696 | tf_op jit(solution)/shard_map/ppermute | solution.py:385
  48.0 0.0 collective-permute-done.14.come
  48.0 0.1 shard_map.136
  48.0 0.1 collective-permute-start.15
  48.1 1.4 %shard_map.131 = (bf16[256,384]{1,0:T(8,128)(2,1)S(1)}, bf16[272,384]{1,0:T(8,128)(2,1)S(1)}, f32[256,384]{1,0:T(8,128)S(1)}) custom-call(bf16[256,1536]{1,0:T(8,128)(2,1)S(1)} %get-tuple-element.44.act, bf16[1536,1536]{1,0:T(8,128)(2,1)S(1)} %get-tuple-element.40.w_in, bf16[272,384]{1,0:T(8,128)(2,1)S(1)} %get-tuple-element.45.away), custom_call_target="tpu_custom_call" | custom-call | tf_op jit(solution)/shard_map/pallas_call | solution.py:36
  49.5 0.1 collective-permute-start.7
  49.6 0.5 collective-permute-done.8.come
  50.1 0.1 shard_map.132
  50.1 2.9 %collective-permute-start.9 = (bf16[272,384]{1,0:T(8,128)(2,1)S(1)}, bf16[272,384]{1,0:T(8,128)(2,1)S(1)}, u32[]{:S(2)}, u32[]{:S(2)}) collective-permute-start(bf16[272,384]{1,0:T(8,128)(2,1)S(1)} %shard_map.132), channel_id=1, source_target_pairs={{0,3},{1,0},{2,1},{3,2},{4,7},{5,4},{6,5},{7,6},{8,11},{9,8},{10,9... | collective-permute-start | bytes 626696 | tf_op jit(solution)/shard_map/ppermute | solution.py:385
  53.0 0.0 collective-permute-done.13.got
  53.0 2.1 %collective-permute-done.15.total = bf16[272,384]{1,0:T(8,128)(2,1)S(1)} collective-permute-done((bf16[272,384]{1,0:T(8,128)(2,1)S(1)}, bf16[272,384]{1,0:T(8,128)(2,1)S(1)}, u32[]{:S(2)}, u32[]{:S(2)}) %collective-permute-start.15) | collective-permute-done | bytes 208928 | tf_op jit(solution)/shard_map/ppermute | solution.py:385
  55.1 3.4 %shard_map.137.before = f32[3,38,48,128]{3,2,1,0:T(8,128)S(1)} custom-call(s32[2,32]{1,0:T(2,128)} %bitcast.3, s32[32]{0:T(128)} %counts.5, f32[256,384]{1,0:T(8,128)S(1)} %get-tuple-element.55.mine, bf16[272,384]{1,0:T(8,128)(2,1)S(1)} %collective-permute-done.13.got, bf16[272,384]{1,0:T(8,128)(2,1)S(1)} %collective-permute-done.15.total, ...), custom_call_target="tpu_custom_call" | custom-call | tf_op jit(solution)/shard_map/pallas_call | solution.py:36
  58.5 0.0 collective-permute-done.7.got
  58.5 0.0 collective-permute-done.9.total
  58.5 4.2 %shard_map.138 = f32[32,32,384]{2,1,0:T(8,128)} custom-call(s32[2,32]{1,0:T(2,128)} %bitcast.4, s32[32]{0:T(128)} %counts.5, s32[1,2]{1,0:T(1,128)} %screen.3, f32[256,384]{1,0:T(8,128)S(1)} %get-tuple-element.46.mine, bf16[272,384]{1,0:T(8,128)(2,1)S(1)} %collective-permute-done.7.got, bf16[272,384]{1,0:T(8,128)(2,1)S(1)} %collective-permute-done.9.total, ...), custom_call_target="tpu_custom_call" | custom-call | tf_op jit(solution)/shard_map/pallas_call | solution.py:36
Async XLA Ops:
  0.0 13.4 %collective-permute-start = (bf16[32,4,4,384]{3,2,1,0:T(4,128)(2,1)}, bf16[32,4,4,384]{3,2,1,0:T(4,128)(2,1)S(1)}, u32[]{:S(2)}, u32[]{:S(2)}) collective-permute-start(bf16[32,4,4,384]{3,2,1,0:T(4,128)(2,1)} %own.1), channel_id=1, source_target_pairs={{0,3},{1,0},{2,1},{3,2},{4,7},{5,4},{6,5},{7,6},{8,11},{9,8},{10,9... | collective-permute-start | bytes 1179656 | tf_op jit(solution)/shard_map/ppermute | solution.py:385
  4.0 21.1 %collective-permute-start.3 = (bf16[32,4,4,384]{3,2,1,0:T(4,128)(2,1)}, bf16[32,4,4,384]{3,2,1,0:T(4,128)(2,1)S(1)}, u32[]{:S(2)}, u32[]{:S(2)}) collective-permute-start(bf16[32,4,4,384]{3,2,1,0:T(4,128)(2,1)} %own.1), channel_id=1, source_target_pairs={{0,1},{1,2},{2,3},{3,0},{4,5},{5,6},{6,7},{7,4},{8,9},{9,10},{10,1... | collective-permute-start | bytes 1179656 | tf_op jit(solution)/shard_map/ppermute | solution.py:385
  4.0 21.1 %copy-start = (bf16[32,4,4,384]{3,2,1,0:T(4,128)(2,1)S(1)}, bf16[32,4,4,384]{3,2,1,0:T(4,128)(2,1)}, u32[]{:S(2)}) copy-start(bf16[32,4,4,384]{3,2,1,0:T(4,128)(2,1)} %own.1) | copy-start | bytes 1179652
  4.0 21.1 %copy-start.1 = (f32[1536]{0:T(1024)S(1)}, f32[1536]{0:T(1024)}, u32[]{:S(2)}) copy-start(f32[1536]{0:T(1024)} %gain.9) | copy-start | bytes 18436
  4.0 21.1 %copy-start.2 = (f32[1536]{0:T(1024)S(1)}, f32[1536]{0:T(1024)}, u32[]{:S(2)}) copy-start(f32[1536]{0:T(1024)} %scale.5) | copy-start | bytes 18436
  4.1 21.1 %copy-start.3 = (f32[1536]{0:T(1024)S(1)}, f32[1536]{0:T(1024)}, u32[]{:S(2)}) copy-start(f32[1536]{0:T(1024)} %bias.7) | copy-start | bytes 18436
  4.1 21.1 %copy-start.4 = (f32[1536]{0:T(1024)S(1)}, f32[1536]{0:T(1024)}, u32[]{:S(2)}) copy-start(f32[1536]{0:T(1024)} %b_in.5) | copy-start | bytes 18436
  10.0 11.7 %collective-permute-start.10 = (bf16[256,384]{1,0:T(8,128)(2,1)S(1)}, bf16[256,384]{1,0:T(8,128)(2,1)S(1)}, u32[]{:S(2)}, u32[]{:S(2)}) collective-permute-start(bf16[256,384]{1,0:T(8,128)(2,1)S(1)} %get-tuple-element.37.own.mixed), channel_id=1, source_target_pairs={{0,1},{1,2},{2,3},{3,0},{4,5},{5,6},{6,7},{7,4},{8,9},{9,10},{10,1... | collective-permute-start | bytes 589832 | tf_op jit(solution)/shard_map/ppermute | solution.py:385
  10.1 14.9 %collective-permute-start.4 = (bf16[256,384]{1,0:T(8,128)(2,1)S(1)}, bf16[256,384]{1,0:T(8,128)(2,1)S(1)}, u32[]{:S(2)}, u32[]{:S(2)}) collective-permute-start(bf16[256,384]{1,0:T(8,128)(2,1)S(1)} %get-tuple-element.37.own.mixed), channel_id=1, source_target_pairs={{0,3},{1,0},{2,1},{3,2},{4,7},{5,4},{6,5},{7,6},{8,11},{9,8},{10,9... | collective-permute-start | bytes 589832 | tf_op jit(solution)/shard_map/ppermute | solution.py:385
  13.4 16.5 %collective-permute-start.1 = (bf16[256,384]{1,0:T(8,128)(2,1)S(1)}, bf16[256,384]{1,0:T(8,128)(2,1)S(1)}, u32[]{:S(2)}, u32[]{:S(2)}) collective-permute-start(bf16[256,384]{1,0:T(8,128)(2,1)S(1)} %get-tuple-element.34.own.mixed), channel_id=1, source_target_pairs={{0,1},{1,2},{2,3},{3,0},{4,5},{5,6},{6,7},{7,4},{8,9},{9,10},{10,1... | collective-permute-start | bytes 589832 | tf_op jit(solution)/shard_map/ppermute | solution.py:385
  21.7 11.6 %collective-permute-start.11 = (bf16[256,384]{1,0:T(8,128)(2,1)S(1)}, bf16[256,384]{1,0:T(8,128)(2,1)S(1)}, u32[]{:S(2)}, u32[]{:S(2)}) collective-permute-start(bf16[256,384]{1,0:T(8,128)(2,1)S(1)} %collective-permute-done.10.left), channel_id=1, source_target_pairs={{0,1},{1,2},{2,3},{3,0},{4,5},{5,6},{6,7},{7,4},{8,9},{9,10},{10,1... | collective-permute-start | bytes 589832 | tf_op jit(solution)/shard_map/ppermute | solution.py:385
  21.7 11.0 %collective-permute-start.2 = (bf16[256,384]{1,0:T(8,128)(2,1)S(1)}, bf16[256,384]{1,0:T(8,128)(2,1)S(1)}, u32[]{:S(2)}, u32[]{:S(2)}) collective-permute-start(bf16[256,384]{1,0:T(8,128)(2,1)S(1)} %get-tuple-element.34.own.mixed), channel_id=1, source_target_pairs={{0,3},{1,0},{2,1},{3,2},{4,7},{5,4},{6,5},{7,6},{8,11},{9,8},{10,9... | collective-permute-start | bytes 589832 | tf_op jit(solution)/shard_map/ppermute | solution.py:385
  25.0 7.6 %collective-permute-start.12 = (bf16[16,4,4,384]{3,2,1,0:T(4,128)(2,1)S(1)}, bf16[16,4,4,384]{3,2,1,0:T(4,128)(2,1)S(1)}, u32[]{:S(2)}, u32[]{:S(2)}) collective-permute-start(bf16[16,4,4,384]{3,2,1,0:T(4,128)(2,1)S(1)} %slice.8), channel_id=1, source_target_pairs={{0,3},{1,0},{2,1},{3,2},{4,7},{5,4},{6,5},{7,6},{8,11},{9,8},{10,9... | collective-permute-start | bytes 589832 | tf_op jit(solution)/shard_map/ppermute | solution.py:385
  29.9 8.3 %collective-permute-start.6 = (bf16[16,4,4,384]{3,2,1,0:T(4,128)(2,1)S(1)}, bf16[16,4,4,384]{3,2,1,0:T(4,128)(2,1)S(1)}, u32[]{:S(2)}, u32[]{:S(2)}) collective-permute-start(bf16[16,4,4,384]{3,2,1,0:T(4,128)(2,1)S(1)} %slice.6), channel_id=1, source_target_pairs={{0,3},{1,0},{2,1},{3,2},{4,7},{5,4},{6,5},{7,6},{8,11},{9,8},{10,9... | collective-permute-start | bytes 589832 | tf_op jit(solution)/shard_map/ppermute | solution.py:385
  30.0 8.9 %collective-permute-start.5 = (bf16[256,384]{1,0:T(8,128)(2,1)S(1)}, bf16[256,384]{1,0:T(8,128)(2,1)S(1)}, u32[]{:S(2)}, u32[]{:S(2)}) collective-permute-start(bf16[256,384]{1,0:T(8,128)(2,1)S(1)} %collective-permute-done.1.left), channel_id=1, source_target_pairs={{0,1},{1,2},{2,3},{3,0},{4,5},{5,6},{6,7},{7,4},{8,9},{9,10},{10,1... | collective-permute-start | bytes 589832 | tf_op jit(solution)/shard_map/ppermute | solution.py:385
  36.7 11.3 %collective-permute-start.14 = (bf16[272,384]{1,0:T(8,128)(2,1)S(1)}, bf16[272,384]{1,0:T(8,128)(2,1)S(1)}, u32[]{:S(2)}, u32[]{:S(2)}) collective-permute-start(bf16[272,384]{1,0:T(8,128)(2,1)S(1)} %get-tuple-element.54.away), channel_id=1, source_target_pairs={{0,1},{1,2},{2,3},{3,0},{4,5},{5,6},{6,7},{7,4},{8,9},{9,10},{10,1... | collective-permute-start | bytes 626696 | tf_op jit(solution)/shard_map/ppermute | solution.py:385
  42.2 7.8 %collective-permute-start.8 = (bf16[272,384]{1,0:T(8,128)(2,1)S(1)}, bf16[272,384]{1,0:T(8,128)(2,1)S(1)}, u32[]{:S(2)}, u32[]{:S(2)}) collective-permute-start(bf16[272,384]{1,0:T(8,128)(2,1)S(1)} %get-tuple-element.45.away), channel_id=1, source_target_pairs={{0,3},{1,0},{2,1},{3,2},{4,7},{5,4},{6,5},{7,6},{8,11},{9,8},{10,9... | collective-permute-start | bytes 626696 | tf_op jit(solution)/shard_map/ppermute | solution.py:385
  45.9 7.1 %collective-permute-start.13 = (bf16[272,384]{1,0:T(8,128)(2,1)S(1)}, bf16[272,384]{1,0:T(8,128)(2,1)S(1)}, u32[]{:S(2)}, u32[]{:S(2)}) collective-permute-start(bf16[272,384]{1,0:T(8,128)(2,1)S(1)} %get-tuple-element.56), channel_id=1, source_target_pairs={{0,3},{1,0},{2,1},{3,2},{4,7},{5,4},{6,5},{7,6},{8,11},{9,8},{10,9... | collective-permute-start | bytes 626696 | tf_op jit(solution)/shard_map/ppermute | solution.py:385
  48.0 7.1 %collective-permute-start.15 = (bf16[272,384]{1,0:T(8,128)(2,1)S(1)}, bf16[272,384]{1,0:T(8,128)(2,1)S(1)}, u32[]{:S(2)}, u32[]{:S(2)}) collective-permute-start(bf16[272,384]{1,0:T(8,128)(2,1)S(1)} %shard_map.136), channel_id=1, source_target_pairs={{0,1},{1,2},{2,3},{3,0},{4,5},{5,6},{6,7},{7,4},{8,9},{9,10},{10,1... | collective-permute-start | bytes 626696 | tf_op jit(solution)/shard_map/ppermute | solution.py:385
  49.5 9.0 %collective-permute-start.7 = (bf16[272,384]{1,0:T(8,128)(2,1)S(1)}, bf16[272,384]{1,0:T(8,128)(2,1)S(1)}, u32[]{:S(2)}, u32[]{:S(2)}) collective-permute-start(bf16[272,384]{1,0:T(8,128)(2,1)S(1)} %get-tuple-element.47), channel_id=1, source_target_pairs={{0,1},{1,2},{2,3},{3,0},{4,5},{5,6},{6,7},{7,4},{8,9},{9,10},{10,1... | collective-permute-start | bytes 626696 | tf_op jit(solution)/shard_map/ppermute | solution.py:385
  50.1 8.4 %collective-permute-start.9 = (bf16[272,384]{1,0:T(8,128)(2,1)S(1)}, bf16[272,384]{1,0:T(8,128)(2,1)S(1)}, u32[]{:S(2)}, u32[]{:S(2)}) collective-permute-start(bf16[272,384]{1,0:T(8,128)(2,1)S(1)} %shard_map.132), channel_id=1, source_target_pairs={{0,3},{1,0},{2,1},{3,2},{4,7},{5,4},{6,5},{7,6},{8,11},{9,8},{10,9... | collective-permute-start | bytes 626696 | tf_op jit(solution)/shard_map/ppermute | solution.py:385

commit v8 on v7

--- a/solution.py
+++ b/solution.py
@@ -139,10 +139,9 @@
 
 
 def hidden_kernel(
-    offsets, counts, own, left, right, scale, gain, bias, b_in, w_out, earlier, w_in,
+    offsets, counts, own, left, right, scale, gain, bias, b_in, w_out, w_in,
     hidden_a, hidden_b, taken, near_in, sides, flat, sem,
 ):
-    del earlier
     fetch = pltpu.make_async_copy(w_in, near_in, sem)
     fetch.start()
     share = own.shape[3]
@@ -162,6 +161,7 @@
         begins.append(channels_of(ahead, share))
         flat[k] = scaled_rows(cells, scale, begins[k])
     step = 512
+    half = hidden_a.shape[0]
     for n in range(0, hidden_a.shape[1], step):
         total = None
         for k, begin in enumerate(begins):
@@ -172,8 +172,8 @@
                 preferred_element_type=jnp.float32,
             )
             total = product if total is None else total + product
-        hidden_a[:, n : n + step] = total[: hidden_a.shape[0]]
-        hidden_b[:, n : n + step] = total[hidden_a.shape[0] :]
+        hidden_a[:, n : n + step] = total[:half]
+        hidden_b[:, n : n + step] = total[half:]
     width = gain.shape[0]
     lines = two_parts(gain[...][None]) + two_parts(bias[...][None])
     lines = jnp.concatenate(lines + [jnp.zeros((12, width), jnp.float32)], 0).astype(jnp.bfloat16)
@@ -183,8 +183,7 @@
     sides[1:2, :] = both[2:3] + both[3:4] + b_in[...][None]
 
 
-def opposite_kernel(before, cot, scale, w_out, earlier, hidden, flat):
-    del earlier
+def opposite_kernel(before, cot, scale, w_out, hidden, flat):
     share = flat.shape[1]
     begin = channels_of(2, share)
     flat[...] = scaled_rows(cot, scale, begin)
@@ -320,18 +319,21 @@
 
     def tile(t, carry):
         r, q = offsets[0, base + t], offsets[1, base + t]
+        doubled = []
         for b in range(share // 128):
-            doubled = []
+            twice = []
             for h in range(2):
                 pair = upstream[pl.ds(pl.multiple_of(t * 16 + 8 * h, 8), 8), b * 128 : (b + 1) * 128]
                 turned = pltpu.roll(pair, 4, 0)
-                doubled += [jnp.where(low, pair, turned), jnp.where(low, turned, pair)]
-            for j in range(4):
-                columns = pl.ds(q + (LEFT - 3 + j), 8)
+                twice += [jnp.where(low, pair, turned), jnp.where(low, turned, pair)]
+            doubled.append(twice)
+        for j in range(4):
+            columns = pl.ds(q + (LEFT - 3 + j), 8)
+            for b in range(share // 128):
                 for y in range(10):
                     more = None
                     for k in range(max(0, y - 6), min(3, y) + 1):
-                        term = doubled[k] * taps[b, (y - k) * 4 + j]
+                        term = doubled[b][k] * taps[b, (y - k) * 4 + j]
                         more = term if more is None else more + term
                     grown[b, r + y, columns, :] += more
         return carry
@@ -428,32 +430,34 @@
             pltpu.SemaphoreType.DMA((7,)),
         ],
     )(offsets, screen_size, canvas, dw_kernel, dw_bias, w_out)
-    left_a, right_a = shift(mixed_a, 1), shift(mixed_a, -1)
-    cot_a = shift(right[: slots // 2], -1)
-    second, right = lax.optimization_barrier((mixed_b, right))
-    left_b, right_b = shift(second, 1), shift(second, -1)
-    opp_a = shift(left_a, 1)
+    left_a, right_b = shift(mixed_a, 1), shift(mixed_b, -1)
+    cot_a, right_a = shift(left[: slots // 2], 1), shift(mixed_a, -1)
     canvas_like = struct((lanes, PAD_ROWS, PAD_COLS, 128), f32)
     hidden_a, hidden_b, taken, near_in, sides = call(
         hidden_kernel,
         [struct((half, hid), f32), struct((half, hid), f32), canvas_like, struct(w_in.shape, bf16), struct((8, hid), f32)],
-        [SMEM] * 2 + [VMEM] * 9 + [HBM],
+        [SMEM] * 2 + [VMEM] * 8 + [HBM],
         [pltpu.VMEM((3, rows, share), bf16), pltpu.SemaphoreType.DMA(())],
     )(
-        offsets, tile_counts, cotangent, left, right, layer_scale, ln_gain, ln_bias, b_in, near_out, right_a, w_in
-    )
-    forward_b, forward_cot, sides = lax.optimization_barrier((left_b, right, sides))
+        offsets, tile_counts, cotangent, left, right, layer_scale, ln_gain, ln_bias, b_in, near_out, w_in
+    )
+    forward_a, forward_b, forward_cot, sides = lax.optimization_barrier(
+        (left_a, right_b, right, sides)
+    )
+    opp_a, opp_b = shift(forward_a, 1), shift(forward_b, -1)
     cot_b = shift(forward_cot[slots // 2 :], -1)
-    opp_b = shift(forward_b, 1)
 
     def with_opposite(hidden, cot):
         return call(
             opposite_kernel,
             [struct((half, hid), f32)],
-            [VMEM] * 5,
+            [VMEM] * 4,
             [pltpu.VMEM((half, share), bf16)],
-        )(hidden, cot, layer_scale, near_out, right_b)[0]
-
+        )(hidden, cot, layer_scale, near_out)[0]
+
+    hidden_a, late_b = lax.optimization_barrier((with_opposite(hidden_a, cot_a), mixed_b))
+    left_b = shift(late_b, 1)
+    hidden_b = with_opposite(hidden_b, cot_b)
     message = struct((half + 16, share), bf16)
 
     def block(blocks, hidden):
@@ -474,11 +478,11 @@
     def middle(come, keep):
         return call(middle_kernel, [message], [VMEM] * 2)(come, keep)[0]
 
-    away_a, act_a, centers_a, inverses_a = block((mixed_a, left_a, right_a, opp_a), with_opposite(hidden_a, cot_a))
+    away_a, act_a, centers_a, inverses_a = block((mixed_a, left_a, right_a, opp_a), hidden_a)
     come_a = shift(away_a, 1)
     keep_a, own_a, mine_a = parts(1, 3, act_a, away_a)
     got_a = shift(own_a, -1)
-    away_b, act_b, centers_b, inverses_b = block((mixed_b, left_b, right_b, opp_b), with_opposite(hidden_b, cot_b))
+    away_b, act_b, centers_b, inverses_b = block((mixed_b, left_b, right_b, opp_b), hidden_b)
     come_b = shift(away_b, -1)
     keep_b, own_b, mine_b = parts(3, 1, act_b, away_b)
     got_b = shift(own_b, 1)

time: 63.5 us -> 57 us (0.90)
  the two profiles are of different devices: /device:TPU:28 before, /device:TPU:26 now
where the time goes in v8:
time: 57 us; the launch traced here: 56.8 us
  Pallas kernels  28.4 us (50%)
  starting transfers between devices  24 us (42%)
  waiting for transfers between devices  3.9 us (7%)
    pallas_call x12, Pallas kernels, held(): run(*(pltpu.with_memory_space_constraint(a, pltpu.VMEM if spec is VMEM el...  28.4 us
    ppermute x16, starting transfers between devices, shift(): return lax.ppermute(x, 'ch', [(i, (i + by) % n) for i in range(n)])  24 us
    ppermute x16, waiting for transfers between devices, shift(): return lax.ppermute(x, 'ch', [(i, (i + by) % n) for i in range(n)])  3.9 us
  transfers between devices with their start and end apart: 16, of which 4 were waited for; matrix products, arithmetic and copies ran while one was open for 0% of the time, Pallas kernels for 43%

profile of v8, /device:TPU:26, one launch (start us, length us, event | category | flops | bytes accessed | tf_op | source)
XLA Modules:
  0.0 56.8 jit_solution(18241647356797975864)
XLA Ops:
  0.0 1.9 %collective-permute-start = (bf16[32,4,4,384]{3,2,1,0:T(4,128)(2,1)}, bf16[32,4,4,384]{3,2,1,0:T(4,128)(2,1)S(1)}, u32[]{:S(2)}, u32[]{:S(2)}) collective-permute-start(bf16[32,4,4,384]{3,2,1,0:T(4,128)(2,1)} %own.1), channel_id=1, source_target_pairs={{0,1},{1,2},{2,3},{3,0},{4,5},{5,6},{6,7},{7,4},{8,9},{9,10},{10,1... | collective-permute-start | bytes 1179656 | tf_op jit(solution)/shard_map/ppermute | solution.py:387
  1.9 2.1 %collective-permute-start.1 = (bf16[32,4,4,384]{3,2,1,0:T(4,128)(2,1)}, bf16[32,4,4,384]{3,2,1,0:T(4,128)(2,1)S(1)}, u32[]{:S(2)}, u32[]{:S(2)}) collective-permute-start(bf16[32,4,4,384]{3,2,1,0:T(4,128)(2,1)} %own.1), channel_id=1, source_target_pairs={{0,3},{1,0},{2,1},{3,2},{4,7},{5,4},{6,5},{7,6},{8,11},{9,8},{10,9... | collective-permute-start | bytes 1179656 | tf_op jit(solution)/shard_map/ppermute | solution.py:387
  4.0 0.0 copy-start
  4.0 0.0 copy-start.1
  4.0 0.0 copy-start.2
  4.0 0.0 copy-start.3
  4.1 0.0 copy-start.4
  4.1 5.9 %shard_map.127 = (bf16[256,384]{1,0:T(8,128)(2,1)S(1)}, bf16[256,384]{1,0:T(8,128)(2,1)S(1)}, bf16[1536,1536]{1,0:T(8,128)(2,1)S(1)}, f32[3,28,8,128]{3,2,1,0:T(8,128)S(1)}) custom-call(s32[2,32]{1,0:T(2,128)} %bitcast.1, s32[1,2]{1,0:T(1,128)} %screen.3, bf16[32,32,384]{2,1,0:T(8,128)(2,1)} %canvas.1, bf16[49,384]{1,0:T(8,128)(2,1)} %dwk.1, f32[384]{0:T(512)} %bias.4, ...), custom_call_target="tpu_custom_call" | custom-call | tf_op jit(solution)/shard_map/pallas_call | solution.py:36
  10.0 2.1 %collective-permute-start.4 = (bf16[256,384]{1,0:T(8,128)(2,1)S(1)}, bf16[256,384]{1,0:T(8,128)(2,1)S(1)}, u32[]{:S(2)}, u32[]{:S(2)}) collective-permute-start(bf16[256,384]{1,0:T(8,128)(2,1)S(1)} %get-tuple-element.37.own.mixed), channel_id=1, source_target_pairs={{0,3},{1,0},{2,1},{3,2},{4,7},{5,4},{6,5},{7,6},{8,11},{9,8},{10,9... | collective-permute-start | bytes 589832 | tf_op jit(solution)/shard_map/ppermute | solution.py:387
  12.1 0.0 collective-permute-start.5
  12.1 1.3 %collective-permute-done.left = bf16[32,4,4,384]{3,2,1,0:T(4,128)(2,1)S(1)} collective-permute-done((bf16[32,4,4,384]{3,2,1,0:T(4,128)(2,1)}, bf16[32,4,4,384]{3,2,1,0:T(4,128)(2,1)S(1)}, u32[]{:S(2)}, u32[]{:S(2)}) %collective-permute-start) | collective-permute-done | bytes 393248 | tf_op jit(solution)/shard_map/ppermute | solution.py:387
  13.4 0.1 slice.8
  13.4 0.1 collective-permute-start.2
  13.5 3.2 %collective-permute-start.11 = (bf16[256,384]{1,0:T(8,128)(2,1)S(1)}, bf16[256,384]{1,0:T(8,128)(2,1)S(1)}, u32[]{:S(2)}, u32[]{:S(2)}) collective-permute-start(bf16[256,384]{1,0:T(8,128)(2,1)S(1)} %get-tuple-element.38.own.mixed), channel_id=1, source_target_pairs={{0,3},{1,0},{2,1},{3,2},{4,7},{5,4},{6,5},{7,6},{8,11},{9,8},{10,9... | collective-permute-start | bytes 589832 | tf_op jit(solution)/shard_map/ppermute | solution.py:387
  16.7 0.0 collective-permute-done.1.right
  16.7 0.0 copy-done
  16.7 0.0 copy-done.1
  16.8 0.0 copy-done.2
  16.8 0.0 copy-done.3
  16.8 0.0 copy-done.4
  16.8 4.7 %shard_map.128 = (f32[256,1536]{1,0:T(8,128)S(1)}, f32[256,1536]{1,0:T(8,128)S(1)}, f32[3,38,48,128]{3,2,1,0:T(8,128)S(1)}, bf16[1536,1536]{1,0:T(8,128)(2,1)S(1)}, f32[8,1536]{1,0:T(8,128)S(1)}) custom-call(s32[2,32]{1,0:T(2,128)} %bitcast.2, s32[32]{0:T(128)} %counts.5, bf16[32,4,4,384]{3,2,1,0:T(4,128)(2,1)S(1)} %copy-done, ...), custom_call_target="tpu_custom_call" | custom-call | tf_op jit(solution)/shard_map/pallas_call | solution.py:36
  21.5 0.0 collective-permute-done.4.right
  21.5 0.0 collective-permute-done.5.left
  21.5 0.1 collective-permute-start.12
  21.6 3.2 %collective-permute-start.6 = (bf16[256,384]{1,0:T(8,128)(2,1)S(1)}, bf16[256,384]{1,0:T(8,128)(2,1)S(1)}, u32[]{:S(2)}, u32[]{:S(2)}) collective-permute-start(bf16[256,384]{1,0:T(8,128)(2,1)S(1)} %collective-permute-done.4.right), channel_id=1, source_target_pairs={{0,3},{1,0},{2,1},{3,2},{4,7},{5,4},{6,5},{7,6},{8,11},{9,8},{10,9... | collective-permute-start | bytes 589832 | tf_op jit(solution)/shard_map/ppermute | solution.py:387
  24.8 0.1 slice.7
  24.9 0.4 collective-permute-start.7
  25.3 0.0 collective-permute-done.2.cot
  25.3 0.6 %shard_map.129.hidden = f32[256,1536]{1,0:T(8,128)S(1)} custom-call(f32[256,1536]{1,0:T(8,128)S(1)} %get-tuple-element.36.before, bf16[16,4,4,384]{3,2,1,0:T(4,128)(2,1)S(1)} %collective-permute-done.2.cot, f32[1536]{0:T(1024)S(1)} %copy-done.2, bf16[1536,1536]{1,0:T(8,128)(2,1)S(1)} %get-tuple-element.35.w_out), custom_call_target="tpu_custom_call" | custom-call | tf_op jit(solution)/shard_map/pallas_call | solution.py:36
  25.9 1.8 %collective-permute-start.3 = (bf16[256,384]{1,0:T(8,128)(2,1)S(1)}, bf16[256,384]{1,0:T(8,128)(2,1)S(1)}, u32[]{:S(2)}, u32[]{:S(2)}) collective-permute-start(bf16[256,384]{1,0:T(8,128)(2,1)S(1)} %get-tuple-element.37.own.mixed), channel_id=1, source_target_pairs={{0,1},{1,2},{2,3},{3,0},{4,5},{5,6},{6,7},{7,4},{8,9},{9,10},{10,1... | collective-permute-start | bytes 589832 | tf_op jit(solution)/shard_map/ppermute | solution.py:387
  27.7 0.0 collective-permute-done.11.right
  27.7 1.5 %collective-permute-done.12.opp = bf16[256,384]{1,0:T(8,128)(2,1)S(1)} collective-permute-done((bf16[256,384]{1,0:T(8,128)(2,1)S(1)}, bf16[256,384]{1,0:T(8,128)(2,1)S(1)}, u32[]{:S(2)}, u32[]{:S(2)}) %collective-permute-start.12) | collective-permute-done | bytes 196640 | tf_op jit(solution)/shard_map/ppermute | solution.py:387
  29.2 3.3 %shard_map.134 = (bf16[272,384]{1,0:T(8,128)(2,1)S(1)}, bf16[256,1536]{1,0:T(8,128)(2,1)S(1)}, f32[256,1]{1,0:T(8,128)S(1)}, f32[256,1]{1,0:T(8,128)S(1)}) custom-call(bf16[256,384]{1,0:T(8,128)(2,1)S(1)} %get-tuple-element.38.own.mixed, bf16[256,384]{1,0:T(8,128)(2,1)S(1)} %collective-permute-done.5.left, ...), custom_call_target="tpu_custom_call" | custom-call | tf_op jit(solution)/shard_map/pallas_call | solution.py:36
  32.5 0.3 collective-permute-start.14
  32.8 0.0 collective-permute-done.7.cot
  32.8 0.6 %shard_map.130.hidden = f32[256,1536]{1,0:T(8,128)S(1)} custom-call(f32[256,1536]{1,0:T(8,128)S(1)} %get-tuple-element.42.before, bf16[16,4,4,384]{3,2,1,0:T(4,128)(2,1)S(1)} %collective-permute-done.7.cot, f32[1536]{0:T(1024)S(1)} %copy-done.2, bf16[1536,1536]{1,0:T(8,128)(2,1)S(1)} %get-tuple-element.35.w_out), custom_call_target="tpu_custom_call" | custom-call | tf_op jit(solution)/shard_map/pallas_call | solution.py:36
  33.4 0.0 collective-permute-done.6.opp
  33.4 0.0 collective-permute-done.3.left
  33.4 3.3 %shard_map.131 = (bf16[272,384]{1,0:T(8,128)(2,1)S(1)}, bf16[256,1536]{1,0:T(8,128)(2,1)S(1)}, f32[256,1]{1,0:T(8,128)S(1)}, f32[256,1]{1,0:T(8,128)S(1)}) custom-call(bf16[256,384]{1,0:T(8,128)(2,1)S(1)} %get-tuple-element.37.own.mixed, bf16[256,384]{1,0:T(8,128)(2,1)S(1)} %collective-permute-done.3.left, ...), custom_call_target="tpu_custom_call" | custom-call | tf_op jit(solution)/shard_map/pallas_call | solution.py:36
  36.8 3.3 %collective-permute-start.9 = (bf16[272,384]{1,0:T(8,128)(2,1)S(1)}, bf16[272,384]{1,0:T(8,128)(2,1)S(1)}, u32[]{:S(2)}, u32[]{:S(2)}) collective-permute-start(bf16[272,384]{1,0:T(8,128)(2,1)S(1)} %get-tuple-element.46.away), channel_id=1, source_target_pairs={{0,3},{1,0},{2,1},{3,2},{4,7},{5,4},{6,5},{7,6},{8,11},{9,8},{10,9... | collective-permute-start | bytes 626696 | tf_op jit(solution)/shard_map/ppermute | solution.py:387
  40.1 1.4 %shard_map.135 = (bf16[256,384]{1,0:T(8,128)(2,1)S(1)}, bf16[272,384]{1,0:T(8,128)(2,1)S(1)}, f32[256,384]{1,0:T(8,128)S(1)}) custom-call(bf16[256,1536]{1,0:T(8,128)(2,1)S(1)} %get-tuple-element.55.act, bf16[1536,1536]{1,0:T(8,128)(2,1)S(1)} %get-tuple-element.41.w_in, bf16[272,384]{1,0:T(8,128)(2,1)S(1)} %get-tuple-element.56.away), custom_call_target="tpu_custom_call" | custom-call | tf_op jit(solution)/shard_map/pallas_call | solution.py:36
  41.4 0.4 collective-permute-start.13
  41.9 0.0 collective-permute-done.14.come
  41.9 0.1 shard_map.136
  42.0 1.7 %collective-permute-start.15 = (bf16[272,384]{1,0:T(8,128)(2,1)S(1)}, bf16[272,384]{1,0:T(8,128)(2,1)S(1)}, u32[]{:S(2)}, u32[]{:S(2)}) collective-permute-start(bf16[272,384]{1,0:T(8,128)(2,1)S(1)} %shard_map.136), channel_id=1, source_target_pairs={{0,1},{1,2},{2,3},{3,0},{4,5},{5,6},{6,7},{7,4},{8,9},{9,10},{10,1... | collective-permute-start | bytes 626696 | tf_op jit(solution)/shard_map/ppermute | solution.py:387
  43.7 1.4 %shard_map.132 = (bf16[256,384]{1,0:T(8,128)(2,1)S(1)}, bf16[272,384]{1,0:T(8,128)(2,1)S(1)}, f32[256,384]{1,0:T(8,128)S(1)}) custom-call(bf16[256,1536]{1,0:T(8,128)(2,1)S(1)} %get-tuple-element.45.act, bf16[1536,1536]{1,0:T(8,128)(2,1)S(1)} %get-tuple-element.41.w_in, bf16[272,384]{1,0:T(8,128)(2,1)S(1)} %get-tuple-element.46.away), custom_call_target="tpu_custom_call" | custom-call | tf_op jit(solution)/shard_map/pallas_call | solution.py:36
  45.1 0.1 collective-permute-start.8
  45.2 0.0 collective-permute-done.9.come
  45.2 0.1 shard_map.133
  45.2 3.3 %collective-permute-start.10 = (bf16[272,384]{1,0:T(8,128)(2,1)S(1)}, bf16[272,384]{1,0:T(8,128)(2,1)S(1)}, u32[]{:S(2)}, u32[]{:S(2)}) collective-permute-start(bf16[272,384]{1,0:T(8,128)(2,1)S(1)} %shard_map.133), channel_id=1, source_target_pairs={{0,3},{1,0},{2,1},{3,2},{4,7},{5,4},{6,5},{7,6},{8,11},{9,8},{10,9... | collective-permute-start | bytes 626696 | tf_op jit(solution)/shard_map/ppermute | solution.py:387
  48.5 0.9 %collective-permute-done.13.got = bf16[272,384]{1,0:T(8,128)(2,1)S(1)} collective-permute-done((bf16[272,384]{1,0:T(8,128)(2,1)S(1)}, bf16[272,384]{1,0:T(8,128)(2,1)S(1)}, u32[]{:S(2)}, u32[]{:S(2)}) %collective-permute-start.13) | collective-permute-done | bytes 208928 | tf_op jit(solution)/shard_map/ppermute | solution.py:387
  49.4 0.2 collective-permute-done.15.total
  49.6 2.9 %shard_map.137.before = f32[3,38,48,128]{3,2,1,0:T(8,128)S(1)} custom-call(s32[2,32]{1,0:T(2,128)} %bitcast.3, s32[32]{0:T(128)} %counts.5, f32[256,384]{1,0:T(8,128)S(1)} %get-tuple-element.57.mine, bf16[272,384]{1,0:T(8,128)(2,1)S(1)} %collective-permute-done.13.got, bf16[272,384]{1,0:T(8,128)(2,1)S(1)} %collective-permute-done.15.total, ...), custom_call_target="tpu_custom_call" | custom-call | tf_op jit(solution)/shard_map/pallas_call | solution.py:36
  52.5 0.0 collective-permute-done.8.got
  52.5 0.0 collective-permute-done.10.total
  52.6 4.1 %shard_map.138 = f32[32,32,384]{2,1,0:T(8,128)} custom-call(s32[2,32]{1,0:T(2,128)} %bitcast.4, s32[32]{0:T(128)} %counts.5, s32[1,2]{1,0:T(1,128)} %screen.3, f32[256,384]{1,0:T(8,128)S(1)} %get-tuple-element.47.mine, bf16[272,384]{1,0:T(8,128)(2,1)S(1)} %collective-permute-done.8.got, bf16[272,384]{1,0:T(8,128)(2,1)S(1)} %collective-permute-done.10.total, ...), custom_call_target="tpu_custom_call" | custom-call | tf_op jit(solution)/shard_map/pallas_call | solution.py:36
Async XLA Ops:
  0.0 13.4 %collective-permute-start = (bf16[32,4,4,384]{3,2,1,0:T(4,128)(2,1)}, bf16[32,4,4,384]{3,2,1,0:T(4,128)(2,1)S(1)}, u32[]{:S(2)}, u32[]{:S(2)}) collective-permute-start(bf16[32,4,4,384]{3,2,1,0:T(4,128)(2,1)} %own.1), channel_id=1, source_target_pairs={{0,1},{1,2},{2,3},{3,0},{4,5},{5,6},{6,7},{7,4},{8,9},{9,10},{10,1... | collective-permute-start | bytes 1179656 | tf_op jit(solution)/shard_map/ppermute | solution.py:387
  1.9 14.8 %collective-permute-start.1 = (bf16[32,4,4,384]{3,2,1,0:T(4,128)(2,1)}, bf16[32,4,4,384]{3,2,1,0:T(4,128)(2,1)S(1)}, u32[]{:S(2)}, u32[]{:S(2)}) collective-permute-start(bf16[32,4,4,384]{3,2,1,0:T(4,128)(2,1)} %own.1), channel_id=1, source_target_pairs={{0,3},{1,0},{2,1},{3,2},{4,7},{5,4},{6,5},{7,6},{8,11},{9,8},{10,9... | collective-permute-start | bytes 1179656 | tf_op jit(solution)/shard_map/ppermute | solution.py:387
  4.0 12.7 %copy-start = (bf16[32,4,4,384]{3,2,1,0:T(4,128)(2,1)S(1)}, bf16[32,4,4,384]{3,2,1,0:T(4,128)(2,1)}, u32[]{:S(2)}) copy-start(bf16[32,4,4,384]{3,2,1,0:T(4,128)(2,1)} %own.1) | copy-start | bytes 1179652
  4.0 12.7 %copy-start.1 = (f32[1536]{0:T(1024)S(1)}, f32[1536]{0:T(1024)}, u32[]{:S(2)}) copy-start(f32[1536]{0:T(1024)} %gain.9) | copy-start | bytes 18436
  4.0 12.7 %copy-start.2 = (f32[1536]{0:T(1024)S(1)}, f32[1536]{0:T(1024)}, u32[]{:S(2)}) copy-start(f32[1536]{0:T(1024)} %scale.5) | copy-start | bytes 18436
  4.0 12.7 %copy-start.3 = (f32[1536]{0:T(1024)S(1)}, f32[1536]{0:T(1024)}, u32[]{:S(2)}) copy-start(f32[1536]{0:T(1024)} %bias.7) | copy-start | bytes 18436
  4.1 12.7 %copy-start.4 = (f32[1536]{0:T(1024)S(1)}, f32[1536]{0:T(1024)}, u32[]{:S(2)}) copy-start(f32[1536]{0:T(1024)} %b_in.5) | copy-start | bytes 18436
  10.0 11.5 %collective-permute-start.4 = (bf16[256,384]{1,0:T(8,128)(2,1)S(1)}, bf16[256,384]{1,0:T(8,128)(2,1)S(1)}, u32[]{:S(2)}, u32[]{:S(2)}) collective-permute-start(bf16[256,384]{1,0:T(8,128)(2,1)S(1)} %get-tuple-element.37.own.mixed), channel_id=1, source_target_pairs={{0,3},{1,0},{2,1},{3,2},{4,7},{5,4},{6,5},{7,6},{8,11},{9,8},{10,9... | collective-permute-start | bytes 589832 | tf_op jit(solution)/shard_map/ppermute | solution.py:387
  12.1 9.4 %collective-permute-start.5 = (bf16[256,384]{1,0:T(8,128)(2,1)S(1)}, bf16[256,384]{1,0:T(8,128)(2,1)S(1)}, u32[]{:S(2)}, u32[]{:S(2)}) collective-permute-start(bf16[256,384]{1,0:T(8,128)(2,1)S(1)} %get-tuple-element.38.own.mixed), channel_id=1, source_target_pairs={{0,1},{1,2},{2,3},{3,0},{4,5},{5,6},{6,7},{7,4},{8,9},{9,10},{10,1... | collective-permute-start | bytes 589832 | tf_op jit(solution)/shard_map/ppermute | solution.py:387
  13.4 11.8 %collective-permute-start.2 = (bf16[16,4,4,384]{3,2,1,0:T(4,128)(2,1)S(1)}, bf16[16,4,4,384]{3,2,1,0:T(4,128)(2,1)S(1)}, u32[]{:S(2)}, u32[]{:S(2)}) collective-permute-start(bf16[16,4,4,384]{3,2,1,0:T(4,128)(2,1)S(1)} %slice.8), channel_id=1, source_target_pairs={{0,1},{1,2},{2,3},{3,0},{4,5},{5,6},{6,7},{7,4},{8,9},{9,10},{10,1... | collective-permute-start | bytes 589832 | tf_op jit(solution)/shard_map/ppermute | solution.py:387
  13.5 14.2 %collective-permute-start.11 = (bf16[256,384]{1,0:T(8,128)(2,1)S(1)}, bf16[256,384]{1,0:T(8,128)(2,1)S(1)}, u32[]{:S(2)}, u32[]{:S(2)}) collective-permute-start(bf16[256,384]{1,0:T(8,128)(2,1)S(1)} %get-tuple-element.38.own.mixed), channel_id=1, source_target_pairs={{0,3},{1,0},{2,1},{3,2},{4,7},{5,4},{6,5},{7,6},{8,11},{9,8},{10,9... | collective-permute-start | bytes 589832 | tf_op jit(solution)/shard_map/ppermute | solution.py:387
  21.5 7.7 %collective-permute-start.12 = (bf16[256,384]{1,0:T(8,128)(2,1)S(1)}, bf16[256,384]{1,0:T(8,128)(2,1)S(1)}, u32[]{:S(2)}, u32[]{:S(2)}) collective-permute-start(bf16[256,384]{1,0:T(8,128)(2,1)S(1)} %collective-permute-done.5.left), channel_id=1, source_target_pairs={{0,1},{1,2},{2,3},{3,0},{4,5},{5,6},{6,7},{7,4},{8,9},{9,10},{10,1... | collective-permute-start | bytes 589832 | tf_op jit(solution)/shard_map/ppermute | solution.py:387
  21.6 11.8 %collective-permute-start.6 = (bf16[256,384]{1,0:T(8,128)(2,1)S(1)}, bf16[256,384]{1,0:T(8,128)(2,1)S(1)}, u32[]{:S(2)}, u32[]{:S(2)}) collective-permute-start(bf16[256,384]{1,0:T(8,128)(2,1)S(1)} %collective-permute-done.4.right), channel_id=1, source_target_pairs={{0,3},{1,0},{2,1},{3,2},{4,7},{5,4},{6,5},{7,6},{8,11},{9,8},{10,9... | collective-permute-start | bytes 589832 | tf_op jit(solution)/shard_map/ppermute | solution.py:387
  24.9 7.9 %collective-permute-start.7 = (bf16[16,4,4,384]{3,2,1,0:T(4,128)(2,1)S(1)}, bf16[16,4,4,384]{3,2,1,0:T(4,128)(2,1)S(1)}, u32[]{:S(2)}, u32[]{:S(2)}) collective-permute-start(bf16[16,4,4,384]{3,2,1,0:T(4,128)(2,1)S(1)} %slice.7), channel_id=1, source_target_pairs={{0,3},{1,0},{2,1},{3,2},{4,7},{5,4},{6,5},{7,6},{8,11},{9,8},{10,9... | collective-permute-start | bytes 589832 | tf_op jit(solution)/shard_map/ppermute | solution.py:387
  25.9 7.5 %collective-permute-start.3 = (bf16[256,384]{1,0:T(8,128)(2,1)S(1)}, bf16[256,384]{1,0:T(8,128)(2,1)S(1)}, u32[]{:S(2)}, u32[]{:S(2)}) collective-permute-start(bf16[256,384]{1,0:T(8,128)(2,1)S(1)} %get-tuple-element.37.own.mixed), channel_id=1, source_target_pairs={{0,1},{1,2},{2,3},{3,0},{4,5},{5,6},{6,7},{7,4},{8,9},{9,10},{10,1... | collective-permute-start | bytes 589832 | tf_op jit(solution)/shard_map/ppermute | solution.py:387
  32.5 9.4 %collective-permute-start.14 = (bf16[272,384]{1,0:T(8,128)(2,1)S(1)}, bf16[272,384]{1,0:T(8,128)(2,1)S(1)}, u32[]{:S(2)}, u32[]{:S(2)}) collective-permute-start(bf16[272,384]{1,0:T(8,128)(2,1)S(1)} %get-tuple-element.56.away), channel_id=1, source_target_pairs={{0,1},{1,2},{2,3},{3,0},{4,5},{5,6},{6,7},{7,4},{8,9},{9,10},{10,1... | collective-permute-start | bytes 626696 | tf_op jit(solution)/shard_map/ppermute | solution.py:387
  36.8 8.4 %collective-permute-start.9 = (bf16[272,384]{1,0:T(8,128)(2,1)S(1)}, bf16[272,384]{1,0:T(8,128)(2,1)S(1)}, u32[]{:S(2)}, u32[]{:S(2)}) collective-permute-start(bf16[272,384]{1,0:T(8,128)(2,1)S(1)} %get-tuple-element.46.away), channel_id=1, source_target_pairs={{0,3},{1,0},{2,1},{3,2},{4,7},{5,4},{6,5},{7,6},{8,11},{9,8},{10,9... | collective-permute-start | bytes 626696 | tf_op jit(solution)/shard_map/ppermute | solution.py:387
  41.4 7.9 %collective-permute-start.13 = (bf16[272,384]{1,0:T(8,128)(2,1)S(1)}, bf16[272,384]{1,0:T(8,128)(2,1)S(1)}, u32[]{:S(2)}, u32[]{:S(2)}) collective-permute-start(bf16[272,384]{1,0:T(8,128)(2,1)S(1)} %get-tuple-element.58), channel_id=1, source_target_pairs={{0,3},{1,0},{2,1},{3,2},{4,7},{5,4},{6,5},{7,6},{8,11},{9,8},{10,9... | collective-permute-start | bytes 626696 | tf_op jit(solution)/shard_map/ppermute | solution.py:387
  42.0 7.6 %collective-permute-start.15 = (bf16[272,384]{1,0:T(8,128)(2,1)S(1)}, bf16[272,384]{1,0:T(8,128)(2,1)S(1)}, u32[]{:S(2)}, u32[]{:S(2)}) collective-permute-start(bf16[272,384]{1,0:T(8,128)(2,1)S(1)} %shard_map.136), channel_id=1, source_target_pairs={{0,1},{1,2},{2,3},{3,0},{4,5},{5,6},{6,7},{7,4},{8,9},{9,10},{10,1... | collective-permute-start | bytes 626696 | tf_op jit(solution)/shard_map/ppermute | solution.py:387
  45.1 7.5 %collective-permute-start.8 = (bf16[272,384]{1,0:T(8,128)(2,1)S(1)}, bf16[272,384]{1,0:T(8,128)(2,1)S(1)}, u32[]{:S(2)}, u32[]{:S(2)}) collective-permute-start(bf16[272,384]{1,0:T(8,128)(2,1)S(1)} %get-tuple-element.48), channel_id=1, source_target_pairs={{0,1},{1,2},{2,3},{3,0},{4,5},{5,6},{6,7},{7,4},{8,9},{9,10},{10,1... | collective-permute-start | bytes 626696 | tf_op jit(solution)/shard_map/ppermute | solution.py:387
  45.2 7.3 %collective-permute-start.10 = (bf16[272,384]{1,0:T(8,128)(2,1)S(1)}, bf16[272,384]{1,0:T(8,128)(2,1)S(1)}, u32[]{:S(2)}, u32[]{:S(2)}) collective-permute-start(bf16[272,384]{1,0:T(8,128)(2,1)S(1)} %shard_map.133), channel_id=1, source_target_pairs={{0,3},{1,0},{2,1},{3,2},{4,7},{5,4},{6,5},{7,6},{8,11},{9,8},{10,9... | collective-permute-start | bytes 626696 | tf_op jit(solution)/shard_map/ppermute | solution.py:387

commit v9 on v8

--- a/solution.py
+++ b/solution.py
@@ -1,5 +1,3 @@
-import functools
-
 import jax
 import jax.numpy as jnp
 from jax import lax
@@ -138,24 +136,28 @@
     return pl.multiple_of(lax.rem(lax.axis_index("ch") + ahead, 4) * share, 128)
 
 
-def hidden_kernel(
-    offsets, counts, own, left, right, scale, gain, bias, b_in, w_out, w_in,
-    hidden_a, hidden_b, taken, near_in, sides, flat, sem,
-):
-    fetch = pltpu.make_async_copy(w_in, near_in, sem)
-    fetch.start()
-    share = own.shape[3]
+def cotangent_kernel(offsets, counts, own, earlier, taken):
+    del earlier
     taken[...] = jnp.zeros_like(taken)
 
     def tile(t, carry):
         r, q = offsets[0, t], offsets[1, t]
         for y in range(4):
             cells = own[t, y].astype(jnp.float32)
-            for b in range(share // 128):
+            for b in range(own.shape[3] // 128):
                 taken[b, r + 3 + y, pl.ds(q + LEFT, 4), :] += cells[:, b * 128 : (b + 1) * 128]
         return carry
 
     lax.fori_loop(0, counts[lax.axis_index("img")], tile, 0)
+
+
+def hidden_kernel(
+    own, left, right, scale, gain, bias, b_in, w_out, w_in,
+    hidden_a, hidden_b, near_in, sides, flat, sem,
+):
+    fetch = pltpu.make_async_copy(w_in, near_in, sem)
+    fetch.start()
+    share = own.shape[3]
     begins = []
     for k, (cells, ahead) in enumerate(((own, 0), (left, 3), (right, 1))):
         begins.append(channels_of(ahead, share))
@@ -199,8 +201,9 @@
 
 def gelu_slope(v):
     square = v * v
-    t = jnp.tanh(slope_coef * (v + cubic_coef * square * v))
-    return 0.5 * (1.0 + t) + 0.5 * v * (1.0 - t * t) * slope_coef * (1.0 + 3.0 * cubic_coef * square)
+    t = jnp.tanh(v * (slope_coef + slope_coef * cubic_coef * square))
+    w = v * (0.5 * slope_coef + 1.5 * slope_coef * cubic_coef * square)
+    return (0.5 + 0.5 * t) + w * (1.0 - t * t)
 
 
 def as_rows(column):
@@ -238,8 +241,9 @@
 
 def block_kernel(
     own, left, right, opp, gain, bias, w_in, b_in, hidden, sides,
-    away, act, centers, inverses, full, scaled,
-):
+    *outs,
+):
+    *own_part, away, act, centers, inverses, full, scaled = outs
     rows, width = full.shape
     share = own.shape[1]
     for ref, ahead in ((own, 0), (left, 3), (right, 1), (opp, 2)):
@@ -277,13 +281,22 @@
     packed += [jnp.zeros((16 - 4 * (rows // 128), 128), jnp.float32)]
     away[rows : rows + 16, :] = jnp.zeros((16, share), jnp.bfloat16)
     away[rows : rows + 16, :128] = jnp.concatenate(packed, 0).astype(jnp.bfloat16)
-
-
-def parts_kernel(keep_ahead, own_ahead, act, w_in, away, keep, own, mine):
+    for own_out in own_part:
+        own_out[:rows, :] = part_of(act, w_in, 3).astype(jnp.bfloat16)
+        own_out[rows:, :] = away[rows:, :]
+
+
+def first_parts_kernel(act, w_in, earlier, keep, mine):
+    del earlier
+    keep[...] = part_of(act, w_in, 1).astype(jnp.bfloat16)
+    mine[...] = part_of(act, w_in, 0)
+
+
+def second_parts_kernel(act, w_in, away, keep, own, mine):
     rows = act.shape[0]
-    own[:rows, :] = part_of(act, w_in, own_ahead).astype(jnp.bfloat16)
+    own[:rows, :] = part_of(act, w_in, 1).astype(jnp.bfloat16)
     own[rows:, :] = away[rows:, :]
-    keep[...] = part_of(act, w_in, keep_ahead).astype(jnp.bfloat16)
+    keep[...] = part_of(act, w_in, 3).astype(jnp.bfloat16)
     mine[...] = part_of(act, w_in, 0)
 
 
@@ -431,16 +444,18 @@
         ],
     )(offsets, screen_size, canvas, dw_kernel, dw_bias, w_out)
     left_a, right_b = shift(mixed_a, 1), shift(mixed_b, -1)
+    canvas_like = struct((lanes, PAD_ROWS, PAD_COLS, 128), f32)
+    taken = call(cotangent_kernel, [canvas_like], [SMEM] * 2 + [VMEM] * 2)(
+        offsets, tile_counts, cotangent, mixed_a
+    )[0]
+    left, taken = lax.optimization_barrier((left, taken))
     cot_a, right_a = shift(left[: slots // 2], 1), shift(mixed_a, -1)
-    canvas_like = struct((lanes, PAD_ROWS, PAD_COLS, 128), f32)
-    hidden_a, hidden_b, taken, near_in, sides = call(
+    hidden_a, hidden_b, near_in, sides = call(
         hidden_kernel,
-        [struct((half, hid), f32), struct((half, hid), f32), canvas_like, struct(w_in.shape, bf16), struct((8, hid), f32)],
-        [SMEM] * 2 + [VMEM] * 8 + [HBM],
+        [struct((half, hid), f32), struct((half, hid), f32), struct(w_in.shape, bf16), struct((8, hid), f32)],
+        [VMEM] * 8 + [HBM],
         [pltpu.VMEM((3, rows, share), bf16), pltpu.SemaphoreType.DMA(())],
-    )(
-        offsets, tile_counts, cotangent, left, right, layer_scale, ln_gain, ln_bias, b_in, near_out, w_in
-    )
+    )(cotangent, left, right, layer_scale, ln_gain, ln_bias, b_in, near_out, w_in)
     forward_a, forward_b, forward_cot, sides = lax.optimization_barrier(
         (left_a, right_b, right, sides)
     )
@@ -460,31 +475,28 @@
     hidden_b = with_opposite(hidden_b, cot_b)
     message = struct((half + 16, share), bf16)
 
-    def block(blocks, hidden):
+    def block(own_parts, blocks, hidden):
         return call(
             block_kernel,
-            [message, struct((half, hid), bf16), struct((half, 1), f32), struct((half, 1), f32)],
+            [message] * (own_parts + 1)
+            + [struct((half, hid), bf16), struct((half, 1), f32), struct((half, 1), f32)],
             [VMEM] * 10,
             [pltpu.VMEM((half, width), bf16), pltpu.VMEM((half, width), bf16)],
         )(*blocks, ln_gain, ln_bias, near_in, b_in, hidden, sides)
 
-    def parts(keep_ahead, own_ahead, act, away):
-        return call(
-            functools.partial(parts_kernel, keep_ahead, own_ahead),
-            [struct((half, share), bf16), message, struct((half, share), f32)],
-            [VMEM] * 3,
-        )(act, near_in, away)
-
     def middle(come, keep):
         return call(middle_kernel, [message], [VMEM] * 2)(come, keep)[0]
 
-    away_a, act_a, centers_a, inverses_a = block((mixed_a, left_a, right_a, opp_a), hidden_a)
-    come_a = shift(away_a, 1)
-    keep_a, own_a, mine_a = parts(1, 3, act_a, away_a)
-    got_a = shift(own_a, -1)
-    away_b, act_b, centers_b, inverses_b = block((mixed_b, left_b, right_b, opp_b), hidden_b)
+    own_a, away_a, act_a, centers_a, inverses_a = block(1, (mixed_a, left_a, right_a, opp_a), hidden_a)
+    come_a, got_a = shift(away_a, 1), shift(own_a, -1)
+    away_b, act_b, centers_b, inverses_b = block(0, (mixed_b, left_b, right_b, opp_b), hidden_b)
     come_b = shift(away_b, -1)
-    keep_b, own_b, mine_b = parts(3, 1, act_b, away_b)
+    part = struct((half, share), bf16)
+    mine_like = struct((half, share), f32)
+    keep_a, mine_a = call(first_parts_kernel, [part, mine_like], [VMEM] * 3)(act_a, near_in, got_a)
+    keep_b, own_b, mine_b = call(second_parts_kernel, [part, message, mine_like], [VMEM] * 3)(
+        act_b, near_in, away_b
+    )
     got_b = shift(own_b, 1)
     total_a = shift(middle(come_a, keep_a), 1)
     total_b = shift(middle(come_b, keep_b), -1)

time: 57 us -> 56.7 us (level)
  the two profiles are of different devices: /device:TPU:26 before, /device:TPU:6 now
where the time goes in v9:
time: 56.7 us; the launch traced here: 56.6 us
  Pallas kernels  27.9 us (49%)
  starting transfers between devices  22.3 us (39%)
  waiting for transfers between devices  5.84 us (10%)
    pallas_call x13, Pallas kernels, held(): run(*(pltpu.with_memory_space_constraint(a, pltpu.VMEM if spec is VMEM el...  27.9 us
    ppermute x16, starting transfers between devices, shift(): return lax.ppermute(x, 'ch', [(i, (i + by) % n) for i in range(n)])  22.3 us
    ppermute x16, waiting for transfers between devices, shift(): return lax.ppermute(x, 'ch', [(i, (i + by) % n) for i in range(n)])  5.84 us
  transfers between devices with their start and end apart: 16, of which 6 were waited for; matrix products, arithmetic and copies ran while one was open for 0% of the time, Pallas kernels for 42%

profile of v9, /device:TPU:6, one launch (start us, length us, event | category | flops | bytes accessed | tf_op | source)
XLA Modules:
  0.0 56.6 jit_solution(15318564647139876536)
XLA Ops:
  0.0 0.0 copy-start
  0.0 1.9 %collective-permute-start = (bf16[32,4,4,384]{3,2,1,0:T(4,128)(2,1)}, bf16[32,4,4,384]{3,2,1,0:T(4,128)(2,1)S(1)}, u32[]{:S(2)}, u32[]{:S(2)}) collective-permute-start(bf16[32,4,4,384]{3,2,1,0:T(4,128)(2,1)} %own.3), channel_id=1, source_target_pairs={{0,1},{1,2},{2,3},{3,0},{4,5},{5,6},{6,7},{7,4},{8,9},{9,10},{10,1... | collective-permute-start | bytes 1179656 | tf_op jit(solution)/shard_map/ppermute | solution.py:400
  1.9 2.2 %collective-permute-start.1 = (bf16[32,4,4,384]{3,2,1,0:T(4,128)(2,1)}, bf16[32,4,4,384]{3,2,1,0:T(4,128)(2,1)S(1)}, u32[]{:S(2)}, u32[]{:S(2)}) collective-permute-start(bf16[32,4,4,384]{3,2,1,0:T(4,128)(2,1)} %own.3), channel_id=1, source_target_pairs={{0,3},{1,0},{2,1},{3,2},{4,7},{5,4},{6,5},{7,6},{8,11},{9,8},{10,9... | collective-permute-start | bytes 1179656 | tf_op jit(solution)/shard_map/ppermute | solution.py:400
  4.1 5.8 %shard_map.127 = (bf16[256,384]{1,0:T(8,128)(2,1)S(1)}, bf16[256,384]{1,0:T(8,128)(2,1)S(1)}, bf16[1536,1536]{1,0:T(8,128)(2,1)S(1)}, f32[3,28,8,128]{3,2,1,0:T(8,128)S(1)}) custom-call(s32[2,32]{1,0:T(2,128)} %bitcast.1, s32[1,2]{1,0:T(1,128)} %screen.3, bf16[32,32,384]{2,1,0:T(8,128)(2,1)} %canvas.1, bf16[49,384]{1,0:T(8,128)(2,1)} %dwk.1, f32[384]{0:T(512)} %bias.4, ...), custom_call_target="tpu_custom_call" | custom-call | tf_op jit(solution)/shard_map/pallas_call | solution.py:34
  9.9 0.0 copy-start.1
  9.9 0.0 copy-start.2
  9.9 0.0 copy-start.3
  9.9 0.0 copy-start.4
  9.9 2.0 %collective-permute-start.4 = (bf16[256,384]{1,0:T(8,128)(2,1)S(1)}, bf16[256,384]{1,0:T(8,128)(2,1)S(1)}, u32[]{:S(2)}, u32[]{:S(2)}) collective-permute-start(bf16[256,384]{1,0:T(8,128)(2,1)S(1)} %get-tuple-element.40.own.mixed), channel_id=1, source_target_pairs={{0,3},{1,0},{2,1},{3,2},{4,7},{5,4},{6,5},{7,6},{8,11},{9,8},{10,9... | collective-permute-start | bytes 589832 | tf_op jit(solution)/shard_map/ppermute | solution.py:400
  12.0 0.1 collective-permute-start.5
  12.0 0.0 copy-done
  12.0 1.3 %shard_map.128.before = f32[3,38,48,128]{3,2,1,0:T(8,128)S(1)} custom-call(s32[2,32]{1,0:T(2,128)} %bitcast.2, s32[32]{0:T(128)} %counts.5, bf16[32,4,4,384]{3,2,1,0:T(4,128)(2,1)S(1)} %copy-done, bf16[256,384]{1,0:T(8,128)(2,1)S(1)} %get-tuple-element.36.earlier.own.mixed), custom_call_target="tpu_custom_call" | custom-call | tf_op jit(solution)/shard_map/pallas_call | solution.py:34
  13.3 0.1 collective-permute-done.left
  13.4 0.1 slice.6
  13.5 0.1 collective-permute-start.2
  13.6 3.2 %collective-permute-start.11 = (bf16[256,384]{1,0:T(8,128)(2,1)S(1)}, bf16[256,384]{1,0:T(8,128)(2,1)S(1)}, u32[]{:S(2)}, u32[]{:S(2)}) collective-permute-start(bf16[256,384]{1,0:T(8,128)(2,1)S(1)} %get-tuple-element.36.earlier.own.mixed), channel_id=1, source_target_pairs={{0,3},{1,0},{2,1},{3,2},{4,7},{5,4},{6,5},{7,6},{8,11},{9,8},{10,9... | collective-permute-start | bytes 589832 | tf_op jit(solution)/shard_map/ppermute | solution.py:400
  16.8 0.0 collective-permute-done.1.right
  16.8 0.0 copy-done.1
  16.8 0.0 copy-done.2
  16.8 0.0 copy-done.3
  16.8 0.0 copy-done.4
  16.8 3.4 %shard_map.129 = (f32[256,1536]{1,0:T(8,128)S(1)}, f32[256,1536]{1,0:T(8,128)S(1)}, bf16[1536,1536]{1,0:T(8,128)(2,1)S(1)}, f32[8,1536]{1,0:T(8,128)S(1)}) custom-call(bf16[32,4,4,384]{3,2,1,0:T(4,128)(2,1)S(1)} %copy-done, bf16[32,4,4,384]{3,2,1,0:T(4,128)(2,1)S(1)} %collective-permute-done.left, bf16[32,4,4,384]{3,2,1,0:T(4,128)(2,1)S(1)} %collective-permute-done.1.right, ...), custom_call_target="tpu_custom_call" | custom-call | tf_op jit(solution)/shard_map/pallas_call | solution.py:34
  20.3 0.0 collective-permute-done.4.right
  20.3 0.7 %collective-permute-done.5.left = bf16[256,384]{1,0:T(8,128)(2,1)S(1)} collective-permute-done((bf16[256,384]{1,0:T(8,128)(2,1)S(1)}, bf16[256,384]{1,0:T(8,128)(2,1)S(1)}, u32[]{:S(2)}, u32[]{:S(2)}) %collective-permute-start.5) | collective-permute-done | bytes 196640 | tf_op jit(solution)/shard_map/ppermute | solution.py:400
  21.0 0.0 collective-permute-start.12
  21.0 3.2 %collective-permute-start.6 = (bf16[256,384]{1,0:T(8,128)(2,1)S(1)}, bf16[256,384]{1,0:T(8,128)(2,1)S(1)}, u32[]{:S(2)}, u32[]{:S(2)}) collective-permute-start(bf16[256,384]{1,0:T(8,128)(2,1)S(1)} %collective-permute-done.4.right), channel_id=1, source_target_pairs={{0,3},{1,0},{2,1},{3,2},{4,7},{5,4},{6,5},{7,6},{8,11},{9,8},{10,9... | collective-permute-start | bytes 589832 | tf_op jit(solution)/shard_map/ppermute | solution.py:400
  24.3 0.1 slice.7
  24.3 0.1 collective-permute-start.7
  24.4 0.0 collective-permute-done.2.cot
  24.4 0.7 %shard_map.130.hidden = f32[256,1536]{1,0:T(8,128)S(1)} custom-call(f32[256,1536]{1,0:T(8,128)S(1)} %get-tuple-element.39.before, bf16[16,4,4,384]{3,2,1,0:T(4,128)(2,1)S(1)} %collective-permute-done.2.cot, f32[1536]{0:T(1024)S(1)} %copy-done.2, bf16[1536,1536]{1,0:T(8,128)(2,1)S(1)} %get-tuple-element.38.w_out), custom_call_target="tpu_custom_call" | custom-call | tf_op jit(solution)/shard_map/pallas_call | solution.py:34
  25.1 2.0 %collective-permute-start.3 = (bf16[256,384]{1,0:T(8,128)(2,1)S(1)}, bf16[256,384]{1,0:T(8,128)(2,1)S(1)}, u32[]{:S(2)}, u32[]{:S(2)}) collective-permute-start(bf16[256,384]{1,0:T(8,128)(2,1)S(1)} %get-tuple-element.40.own.mixed), channel_id=1, source_target_pairs={{0,1},{1,2},{2,3},{3,0},{4,5},{5,6},{6,7},{7,4},{8,9},{9,10},{10,1... | collective-permute-start | bytes 589832 | tf_op jit(solution)/shard_map/ppermute | solution.py:400
  27.1 0.0 collective-permute-done.11.right
  27.1 2.2 %collective-permute-done.12.opp = bf16[256,384]{1,0:T(8,128)(2,1)S(1)} collective-permute-done((bf16[256,384]{1,0:T(8,128)(2,1)S(1)}, bf16[256,384]{1,0:T(8,128)(2,1)S(1)}, u32[]{:S(2)}, u32[]{:S(2)}) %collective-permute-start.12) | collective-permute-done | bytes 196640 | tf_op jit(solution)/shard_map/ppermute | solution.py:400
  29.4 3.5 %shard_map.135 = (bf16[272,384]{1,0:T(8,128)(2,1)S(1)}, bf16[272,384]{1,0:T(8,128)(2,1)S(1)}, bf16[256,1536]{1,0:T(8,128)(2,1)S(1)}, f32[256,1]{1,0:T(8,128)S(1)}, f32[256,1]{1,0:T(8,128)S(1)}) custom-call(bf16[256,384]{1,0:T(8,128)(2,1)S(1)} %get-tuple-element.36.earlier.own.mixed, bf16[256,384]{1,0:T(8,128)(2,1)S(1)} %collective-permute-done.5.left, ...), custom_call_target="tpu_custom_call" | custom-call | tf_op jit(solution)/shard_map/pallas_call | solution.py:34
  32.8 0.6 %collective-permute-start.13 = (bf16[272,384]{1,0:T(8,128)(2,1)S(1)}, bf16[272,384]{1,0:T(8,128)(2,1)S(1)}, u32[]{:S(2)}, u32[]{:S(2)}) collective-permute-start(bf16[272,384]{1,0:T(8,128)(2,1)S(1)} %get-tuple-element.58), channel_id=1, source_target_pairs={{0,3},{1,0},{2,1},{3,2},{4,7},{5,4},{6,5},{7,6},{8,11},{9,8},{10,9... | collective-permute-start | bytes 626696 | tf_op jit(solution)/shard_map/ppermute | solution.py:400
  33.5 1.5 %collective-permute-start.14 = (bf16[272,384]{1,0:T(8,128)(2,1)S(1)}, bf16[272,384]{1,0:T(8,128)(2,1)S(1)}, u32[]{:S(2)}, u32[]{:S(2)}) collective-permute-start(bf16[272,384]{1,0:T(8,128)(2,1)S(1)} %get-tuple-element.60.away), channel_id=1, source_target_pairs={{0,1},{1,2},{2,3},{3,0},{4,5},{5,6},{6,7},{7,4},{8,9},{9,10},{10,1... | collective-permute-start | bytes 626696 | tf_op jit(solution)/shard_map/ppermute | solution.py:400
  34.9 0.0 collective-permute-done.7.cot
  34.9 0.7 %shard_map.131.hidden = f32[256,1536]{1,0:T(8,128)S(1)} custom-call(f32[256,1536]{1,0:T(8,128)S(1)} %get-tuple-element.44.before, bf16[16,4,4,384]{3,2,1,0:T(4,128)(2,1)S(1)} %collective-permute-done.7.cot, f32[1536]{0:T(1024)S(1)} %copy-done.2, bf16[1536,1536]{1,0:T(8,128)(2,1)S(1)} %get-tuple-element.38.w_out), custom_call_target="tpu_custom_call" | custom-call | tf_op jit(solution)/shard_map/pallas_call | solution.py:34
  35.6 0.0 collective-permute-done.6.opp
  35.6 0.0 collective-permute-done.3.left
  35.6 3.2 %shard_map.132 = (bf16[272,384]{1,0:T(8,128)(2,1)S(1)}, bf16[256,1536]{1,0:T(8,128)(2,1)S(1)}, f32[256,1]{1,0:T(8,128)S(1)}, f32[256,1]{1,0:T(8,128)S(1)}) custom-call(bf16[256,384]{1,0:T(8,128)(2,1)S(1)} %get-tuple-element.40.own.mixed, bf16[256,384]{1,0:T(8,128)(2,1)S(1)} %collective-permute-done.3.left, ...), custom_call_target="tpu_custom_call" | custom-call | tf_op jit(solution)/shard_map/pallas_call | solution.py:34
  38.8 1.8 %collective-permute-start.9 = (bf16[272,384]{1,0:T(8,128)(2,1)S(1)}, bf16[272,384]{1,0:T(8,128)(2,1)S(1)}, u32[]{:S(2)}, u32[]{:S(2)}) collective-permute-start(bf16[272,384]{1,0:T(8,128)(2,1)S(1)} %get-tuple-element.48.away), channel_id=1, source_target_pairs={{0,3},{1,0},{2,1},{3,2},{4,7},{5,4},{6,5},{7,6},{8,11},{9,8},{10,9... | collective-permute-start | bytes 626696 | tf_op jit(solution)/shard_map/ppermute | solution.py:400
  40.7 0.1 collective-permute-done.13.earlier.got
  40.7 1.0 %shard_map.136 = (bf16[256,384]{1,0:T(8,128)(2,1)S(1)}, f32[256,384]{1,0:T(8,128)S(1)}) custom-call(bf16[256,1536]{1,0:T(8,128)(2,1)S(1)} %get-tuple-element.57.act, bf16[1536,1536]{1,0:T(8,128)(2,1)S(1)} %get-tuple-element.43.w_in, bf16[272,384]{1,0:T(8,128)(2,1)S(1)} %collective-permute-done.13.earlier.got), custom_call_target="tpu_custom_call" | custom-call | tf_op jit(solution)/shard_map/pallas_call | solution.py:34
  41.7 0.0 collective-permute-done.14.come
  41.7 0.1 shard_map.137
  41.8 0.3 collective-permute-start.15
  42.1 1.4 %shard_map.133 = (bf16[256,384]{1,0:T(8,128)(2,1)S(1)}, bf16[272,384]{1,0:T(8,128)(2,1)S(1)}, f32[256,384]{1,0:T(8,128)S(1)}) custom-call(bf16[256,1536]{1,0:T(8,128)(2,1)S(1)} %get-tuple-element.47.act, bf16[1536,1536]{1,0:T(8,128)(2,1)S(1)} %get-tuple-element.43.w_in, bf16[272,384]{1,0:T(8,128)(2,1)S(1)} %get-tuple-element.48.away), custom_call_target="tpu_custom_call" | custom-call | tf_op jit(solution)/shard_map/pallas_call | solution.py:34
  43.4 0.1 collective-permute-start.8
  43.5 2.3 %collective-permute-done.9.come = bf16[272,384]{1,0:T(8,128)(2,1)S(1)} collective-permute-done((bf16[272,384]{1,0:T(8,128)(2,1)S(1)}, bf16[272,384]{1,0:T(8,128)(2,1)S(1)}, u32[]{:S(2)}, u32[]{:S(2)}) %collective-permute-start.9) | collective-permute-done | bytes 208928 | tf_op jit(solution)/shard_map/ppermute | solution.py:400
  45.8 0.1 shard_map.134
  45.9 3.1 %collective-permute-start.10 = (bf16[272,384]{1,0:T(8,128)(2,1)S(1)}, bf16[272,384]{1,0:T(8,128)(2,1)S(1)}, u32[]{:S(2)}, u32[]{:S(2)}) collective-permute-start(bf16[272,384]{1,0:T(8,128)(2,1)S(1)} %shard_map.134), channel_id=1, source_target_pairs={{0,3},{1,0},{2,1},{3,2},{4,7},{5,4},{6,5},{7,6},{8,11},{9,8},{10,9... | collective-permute-start | bytes 626696 | tf_op jit(solution)/shard_map/ppermute | solution.py:400
  49.0 0.0 collective-permute-done.15.total
  49.0 2.9 %shard_map.138.before = f32[3,38,48,128]{3,2,1,0:T(8,128)S(1)} custom-call(s32[2,32]{1,0:T(2,128)} %bitcast.3, s32[32]{0:T(128)} %counts.5, f32[256,384]{1,0:T(8,128)S(1)} %get-tuple-element.59.mine, bf16[272,384]{1,0:T(8,128)(2,1)S(1)} %collective-permute-done.13.earlier.got, bf16[272,384]{1,0:T(8,128)(2,1)S(1)} %collective-permute-done.15.total, ...), custom_call_target="tpu_custom_call" | custom-call | tf_op jit(solution)/shard_map/pallas_call | solution.py:34
  51.9 0.0 collective-permute-done.8.got
  51.9 0.4 collective-permute-done.10.total
  52.3 4.1 %shard_map.139 = f32[32,32,384]{2,1,0:T(8,128)} custom-call(s32[2,32]{1,0:T(2,128)} %bitcast.4, s32[32]{0:T(128)} %counts.5, s32[1,2]{1,0:T(1,128)} %screen.3, f32[256,384]{1,0:T(8,128)S(1)} %get-tuple-element.49.mine, bf16[272,384]{1,0:T(8,128)(2,1)S(1)} %collective-permute-done.8.got, bf16[272,384]{1,0:T(8,128)(2,1)S(1)} %collective-permute-done.10.total, ...), custom_call_target="tpu_custom_call" | custom-call | tf_op jit(solution)/shard_map/pallas_call | solution.py:34
Async XLA Ops:
  0.0 12.0 %copy-start = (bf16[32,4,4,384]{3,2,1,0:T(4,128)(2,1)S(1)}, bf16[32,4,4,384]{3,2,1,0:T(4,128)(2,1)}, u32[]{:S(2)}) copy-start(bf16[32,4,4,384]{3,2,1,0:T(4,128)(2,1)} %own.3) | copy-start | bytes 1179652
  0.0 13.4 %collective-permute-start = (bf16[32,4,4,384]{3,2,1,0:T(4,128)(2,1)}, bf16[32,4,4,384]{3,2,1,0:T(4,128)(2,1)S(1)}, u32[]{:S(2)}, u32[]{:S(2)}) collective-permute-start(bf16[32,4,4,384]{3,2,1,0:T(4,128)(2,1)} %own.3), channel_id=1, source_target_pairs={{0,1},{1,2},{2,3},{3,0},{4,5},{5,6},{6,7},{7,4},{8,9},{9,10},{10,1... | collective-permute-start | bytes 1179656 | tf_op jit(solution)/shard_map/ppermute | solution.py:400
  1.9 14.9 %collective-permute-start.1 = (bf16[32,4,4,384]{3,2,1,0:T(4,128)(2,1)}, bf16[32,4,4,384]{3,2,1,0:T(4,128)(2,1)S(1)}, u32[]{:S(2)}, u32[]{:S(2)}) collective-permute-start(bf16[32,4,4,384]{3,2,1,0:T(4,128)(2,1)} %own.3), channel_id=1, source_target_pairs={{0,3},{1,0},{2,1},{3,2},{4,7},{5,4},{6,5},{7,6},{8,11},{9,8},{10,9... | collective-permute-start | bytes 1179656 | tf_op jit(solution)/shard_map/ppermute | solution.py:400
  9.9 6.9 %copy-start.1 = (f32[1536]{0:T(1024)S(1)}, f32[1536]{0:T(1024)}, u32[]{:S(2)}) copy-start(f32[1536]{0:T(1024)} %gain.9) | copy-start | bytes 18436
  9.9 6.9 %copy-start.2 = (f32[1536]{0:T(1024)S(1)}, f32[1536]{0:T(1024)}, u32[]{:S(2)}) copy-start(f32[1536]{0:T(1024)} %scale.5) | copy-start | bytes 18436
  9.9 6.9 %copy-start.3 = (f32[1536]{0:T(1024)S(1)}, f32[1536]{0:T(1024)}, u32[]{:S(2)}) copy-start(f32[1536]{0:T(1024)} %bias.7) | copy-start | bytes 18436
  9.9 6.9 %copy-start.4 = (f32[1536]{0:T(1024)S(1)}, f32[1536]{0:T(1024)}, u32[]{:S(2)}) copy-start(f32[1536]{0:T(1024)} %b_in.5) | copy-start | bytes 18436
  9.9 10.3 %collective-permute-start.4 = (bf16[256,384]{1,0:T(8,128)(2,1)S(1)}, bf16[256,384]{1,0:T(8,128)(2,1)S(1)}, u32[]{:S(2)}, u32[]{:S(2)}) collective-permute-start(bf16[256,384]{1,0:T(8,128)(2,1)S(1)} %get-tuple-element.40.own.mixed), channel_id=1, source_target_pairs={{0,3},{1,0},{2,1},{3,2},{4,7},{5,4},{6,5},{7,6},{8,11},{9,8},{10,9... | collective-permute-start | bytes 589832 | tf_op jit(solution)/shard_map/ppermute | solution.py:400
  12.0 9.0 %collective-permute-start.5 = (bf16[256,384]{1,0:T(8,128)(2,1)S(1)}, bf16[256,384]{1,0:T(8,128)(2,1)S(1)}, u32[]{:S(2)}, u32[]{:S(2)}) collective-permute-start(bf16[256,384]{1,0:T(8,128)(2,1)S(1)} %get-tuple-element.36.earlier.own.mixed), channel_id=1, source_target_pairs={{0,1},{1,2},{2,3},{3,0},{4,5},{5,6},{6,7},{7,4},{8,9},{9,10},{10,1... | collective-permute-start | bytes 589832 | tf_op jit(solution)/shard_map/ppermute | solution.py:400
  13.5 10.9 %collective-permute-start.2 = (bf16[16,4,4,384]{3,2,1,0:T(4,128)(2,1)S(1)}, bf16[16,4,4,384]{3,2,1,0:T(4,128)(2,1)S(1)}, u32[]{:S(2)}, u32[]{:S(2)}) collective-permute-start(bf16[16,4,4,384]{3,2,1,0:T(4,128)(2,1)S(1)} %slice.6), channel_id=1, source_target_pairs={{0,1},{1,2},{2,3},{3,0},{4,5},{5,6},{6,7},{7,4},{8,9},{9,10},{10,1... | collective-permute-start | bytes 589832 | tf_op jit(solution)/shard_map/ppermute | solution.py:400
  13.6 13.5 %collective-permute-start.11 = (bf16[256,384]{1,0:T(8,128)(2,1)S(1)}, bf16[256,384]{1,0:T(8,128)(2,1)S(1)}, u32[]{:S(2)}, u32[]{:S(2)}) collective-permute-start(bf16[256,384]{1,0:T(8,128)(2,1)S(1)} %get-tuple-element.36.earlier.own.mixed), channel_id=1, source_target_pairs={{0,3},{1,0},{2,1},{3,2},{4,7},{5,4},{6,5},{7,6},{8,11},{9,8},{10,9... | collective-permute-start | bytes 589832 | tf_op jit(solution)/shard_map/ppermute | solution.py:400
  21.0 8.4 %collective-permute-start.12 = (bf16[256,384]{1,0:T(8,128)(2,1)S(1)}, bf16[256,384]{1,0:T(8,128)(2,1)S(1)}, u32[]{:S(2)}, u32[]{:S(2)}) collective-permute-start(bf16[256,384]{1,0:T(8,128)(2,1)S(1)} %collective-permute-done.5.left), channel_id=1, source_target_pairs={{0,1},{1,2},{2,3},{3,0},{4,5},{5,6},{6,7},{7,4},{8,9},{9,10},{10,1... | collective-permute-start | bytes 589832 | tf_op jit(solution)/shard_map/ppermute | solution.py:400
  21.0 14.6 %collective-permute-start.6 = (bf16[256,384]{1,0:T(8,128)(2,1)S(1)}, bf16[256,384]{1,0:T(8,128)(2,1)S(1)}, u32[]{:S(2)}, u32[]{:S(2)}) collective-permute-start(bf16[256,384]{1,0:T(8,128)(2,1)S(1)} %collective-permute-done.4.right), channel_id=1, source_target_pairs={{0,3},{1,0},{2,1},{3,2},{4,7},{5,4},{6,5},{7,6},{8,11},{9,8},{10,9... | collective-permute-start | bytes 589832 | tf_op jit(solution)/shard_map/ppermute | solution.py:400
  24.3 10.6 %collective-permute-start.7 = (bf16[16,4,4,384]{3,2,1,0:T(4,128)(2,1)S(1)}, bf16[16,4,4,384]{3,2,1,0:T(4,128)(2,1)S(1)}, u32[]{:S(2)}, u32[]{:S(2)}) collective-permute-start(bf16[16,4,4,384]{3,2,1,0:T(4,128)(2,1)S(1)} %slice.7), channel_id=1, source_target_pairs={{0,3},{1,0},{2,1},{3,2},{4,7},{5,4},{6,5},{7,6},{8,11},{9,8},{10,9... | collective-permute-start | bytes 589832 | tf_op jit(solution)/shard_map/ppermute | solution.py:400
  25.1 10.5 %collective-permute-start.3 = (bf16[256,384]{1,0:T(8,128)(2,1)S(1)}, bf16[256,384]{1,0:T(8,128)(2,1)S(1)}, u32[]{:S(2)}, u32[]{:S(2)}) collective-permute-start(bf16[256,384]{1,0:T(8,128)(2,1)S(1)} %get-tuple-element.40.own.mixed), channel_id=1, source_target_pairs={{0,1},{1,2},{2,3},{3,0},{4,5},{5,6},{6,7},{7,4},{8,9},{9,10},{10,1... | collective-permute-start | bytes 589832 | tf_op jit(solution)/shard_map/ppermute | solution.py:400
  32.8 7.9 %collective-permute-start.13 = (bf16[272,384]{1,0:T(8,128)(2,1)S(1)}, bf16[272,384]{1,0:T(8,128)(2,1)S(1)}, u32[]{:S(2)}, u32[]{:S(2)}) collective-permute-start(bf16[272,384]{1,0:T(8,128)(2,1)S(1)} %get-tuple-element.58), channel_id=1, source_target_pairs={{0,3},{1,0},{2,1},{3,2},{4,7},{5,4},{6,5},{7,6},{8,11},{9,8},{10,9... | collective-permute-start | bytes 626696 | tf_op jit(solution)/shard_map/ppermute | solution.py:400
  33.5 8.2 %collective-permute-start.14 = (bf16[272,384]{1,0:T(8,128)(2,1)S(1)}, bf16[272,384]{1,0:T(8,128)(2,1)S(1)}, u32[]{:S(2)}, u32[]{:S(2)}) collective-permute-start(bf16[272,384]{1,0:T(8,128)(2,1)S(1)} %get-tuple-element.60.away), channel_id=1, source_target_pairs={{0,1},{1,2},{2,3},{3,0},{4,5},{5,6},{6,7},{7,4},{8,9},{9,10},{10,1... | collective-permute-start | bytes 626696 | tf_op jit(solution)/shard_map/ppermute | solution.py:400
  38.8 7.0 %collective-permute-start.9 = (bf16[272,384]{1,0:T(8,128)(2,1)S(1)}, bf16[272,384]{1,0:T(8,128)(2,1)S(1)}, u32[]{:S(2)}, u32[]{:S(2)}) collective-permute-start(bf16[272,384]{1,0:T(8,128)(2,1)S(1)} %get-tuple-element.48.away), channel_id=1, source_target_pairs={{0,3},{1,0},{2,1},{3,2},{4,7},{5,4},{6,5},{7,6},{8,11},{9,8},{10,9... | collective-permute-start | bytes 626696 | tf_op jit(solution)/shard_map/ppermute | solution.py:400
  41.8 7.2 %collective-permute-start.15 = (bf16[272,384]{1,0:T(8,128)(2,1)S(1)}, bf16[272,384]{1,0:T(8,128)(2,1)S(1)}, u32[]{:S(2)}, u32[]{:S(2)}) collective-permute-start(bf16[272,384]{1,0:T(8,128)(2,1)S(1)} %shard_map.137), channel_id=1, source_target_pairs={{0,1},{1,2},{2,3},{3,0},{4,5},{5,6},{6,7},{7,4},{8,9},{9,10},{10,1... | collective-permute-start | bytes 626696 | tf_op jit(solution)/shard_map/ppermute | solution.py:400
  43.4 8.4 %collective-permute-start.8 = (bf16[272,384]{1,0:T(8,128)(2,1)S(1)}, bf16[272,384]{1,0:T(8,128)(2,1)S(1)}, u32[]{:S(2)}, u32[]{:S(2)}) collective-permute-start(bf16[272,384]{1,0:T(8,128)(2,1)S(1)} %get-tuple-element.50), channel_id=1, source_target_pairs={{0,1},{1,2},{2,3},{3,0},{4,5},{5,6},{6,7},{7,4},{8,9},{9,10},{10,1... | collective-permute-start | bytes 626696 | tf_op jit(solution)/shard_map/ppermute | solution.py:400
  45.9 6.4 %collective-permute-start.10 = (bf16[272,384]{1,0:T(8,128)(2,1)S(1)}, bf16[272,384]{1,0:T(8,128)(2,1)S(1)}, u32[]{:S(2)}, u32[]{:S(2)}) collective-permute-start(bf16[272,384]{1,0:T(8,128)(2,1)S(1)} %shard_map.134), channel_id=1, source_target_pairs={{0,3},{1,0},{2,1},{3,2},{4,7},{5,4},{6,5},{7,6},{8,11},{9,8},{10,9... | collective-permute-start | bytes 626696 | tf_op jit(solution)/shard_map/ppermute | solution.py:400

commit v10 on v9

--- a/solution.py
+++ b/solution.py
@@ -185,10 +185,22 @@
     sides[1:2, :] = both[2:3] + both[3:4] + b_in[...][None]
 
 
-def opposite_kernel(before, cot, scale, w_out, hidden, flat):
-    share = flat.shape[1]
+def join_kernel(mixed, cells, joined):
+    half = mixed.shape[0]
+    joined[:half, :] = mixed[...]
+    last = cells[cells.shape[0] // 2 :].astype(jnp.float32)
+    joined[half:, :] = last.reshape(half, mixed.shape[1]).astype(jnp.bfloat16)
+
+
+def opposite_kernel(before, cot, scale, w_out, earlier, hidden, flat):
+    del earlier
+    rows, share = flat.shape
     begin = channels_of(2, share)
-    flat[...] = scaled_rows(cot, scale, begin)
+    if len(cot.shape) == 4:
+        flat[...] = scaled_rows(cot, scale, begin)
+    else:
+        cells = cot[rows:, :].astype(jnp.float32)
+        flat[...] = (scale[pl.ds(begin, share)][None] * cells).astype(jnp.bfloat16)
     step = 512
     for n in range(0, before.shape[1], step):
         hidden[:, n : n + step] = before[:, n : n + step] + lax.dot_general(
@@ -247,7 +259,7 @@
     rows, width = full.shape
     share = own.shape[1]
     for ref, ahead in ((own, 0), (left, 3), (right, 1), (opp, 2)):
-        full[:, pl.ds(channels_of(ahead, share), share)] = ref[...]
+        full[:, pl.ds(channels_of(ahead, share), share)] = ref[:rows, :]
     step = 64
     for m in range(0, rows, step):
         values = full[m : m + step, :].astype(jnp.float32)
@@ -459,20 +471,22 @@
     forward_a, forward_b, forward_cot, sides = lax.optimization_barrier(
         (left_a, right_b, right, sides)
     )
-    opp_a, opp_b = shift(forward_a, 1), shift(forward_b, -1)
-    cot_b = shift(forward_cot[slots // 2 :], -1)
-
-    def with_opposite(hidden, cot):
+    opp_a = shift(forward_a, 1)
+    beyond = shift(
+        call(join_kernel, [struct((rows, share), bf16)], [VMEM] * 2)(forward_b, forward_cot)[0], -1
+    )
+
+    def with_opposite(hidden, cot, earlier):
         return call(
             opposite_kernel,
             [struct((half, hid), f32)],
-            [VMEM] * 4,
+            [VMEM] * 5,
             [pltpu.VMEM((half, share), bf16)],
-        )(hidden, cot, layer_scale, near_out)[0]
-
-    hidden_a, late_b = lax.optimization_barrier((with_opposite(hidden_a, cot_a), mixed_b))
+        )(hidden, cot, layer_scale, near_out, earlier)[0]
+
+    hidden_a, late_b = lax.optimization_barrier((with_opposite(hidden_a, cot_a, right_a), mixed_b))
     left_b = shift(late_b, 1)
-    hidden_b = with_opposite(hidden_b, cot_b)
+    hidden_b = with_opposite(hidden_b, beyond, right_b)
     message = struct((half + 16, share), bf16)
 
     def block(own_parts, blocks, hidden):
@@ -489,7 +503,7 @@
 
     own_a, away_a, act_a, centers_a, inverses_a = block(1, (mixed_a, left_a, right_a, opp_a), hidden_a)
     come_a, got_a = shift(away_a, 1), shift(own_a, -1)
-    away_b, act_b, centers_b, inverses_b = block(0, (mixed_b, left_b, right_b, opp_b), hidden_b)
+    away_b, act_b, centers_b, inverses_b = block(0, (mixed_b, left_b, right_b, beyond), hidden_b)
     come_b = shift(away_b, -1)
     part = struct((half, share), bf16)
     mine_like = struct((half, share), f32)

time: 56.7 us -> 58.4 us (1.030)
  the two profiles are of different devices: /device:TPU:6 before, /device:TPU:2 now
where the time goes in v10:
time: 58.4 us; the launch traced here: 58.3 us
  Pallas kernels  27.9 us (48%)
  starting transfers between devices  21 us (36%)
  waiting for transfers between devices  8.78 us (15%)
    pallas_call x14, Pallas kernels, held(): run(*(pltpu.with_memory_space_constraint(a, pltpu.VMEM if spec is VMEM el...  27.9 us
    ppermute x15, starting transfers between devices, shift(): return lax.ppermute(x, 'ch', [(i, (i + by) % n) for i in range(n)])  21 us
    ppermute x15, waiting for transfers between devices, shift(): return lax.ppermute(x, 'ch', [(i, (i + by) % n) for i in range(n)])  8.78 us
  transfers between devices with their start and end apart: 15, of which 5 were waited for; matrix products, arithmetic and copies ran while one was open for 0% of the time, Pallas kernels for 41%

profile of v10, /device:TPU:2, one launch (start us, length us, event | category | flops | bytes accessed | tf_op | source)
XLA Modules:
  0.0 58.3 jit_solution(4429931361291204527)
XLA Ops:
  0.0 0.0 copy-start
  0.0 1.9 %collective-permute-start = (bf16[32,4,4,384]{3,2,1,0:T(4,128)(2,1)}, bf16[32,4,4,384]{3,2,1,0:T(4,128)(2,1)S(1)}, u32[]{:S(2)}, u32[]{:S(2)}) collective-permute-start(bf16[32,4,4,384]{3,2,1,0:T(4,128)(2,1)} %own.3), channel_id=1, source_target_pairs={{0,1},{1,2},{2,3},{3,0},{4,5},{5,6},{6,7},{7,4},{8,9},{9,10},{10,1... | collective-permute-start | bytes 1179656 | tf_op jit(solution)/shard_map/ppermute | solution.py:412
  1.9 2.2 %collective-permute-start.1 = (bf16[32,4,4,384]{3,2,1,0:T(4,128)(2,1)}, bf16[32,4,4,384]{3,2,1,0:T(4,128)(2,1)S(1)}, u32[]{:S(2)}, u32[]{:S(2)}) collective-permute-start(bf16[32,4,4,384]{3,2,1,0:T(4,128)(2,1)} %own.3), channel_id=1, source_target_pairs={{0,3},{1,0},{2,1},{3,2},{4,7},{5,4},{6,5},{7,6},{8,11},{9,8},{10,9... | collective-permute-start | bytes 1179656 | tf_op jit(solution)/shard_map/ppermute | solution.py:412
  4.1 5.8 %shard_map.127 = (bf16[256,384]{1,0:T(8,128)(2,1)S(1)}, bf16[256,384]{1,0:T(8,128)(2,1)S(1)}, bf16[1536,1536]{1,0:T(8,128)(2,1)S(1)}, f32[3,28,8,128]{3,2,1,0:T(8,128)S(1)}) custom-call(s32[2,32]{1,0:T(2,128)} %bitcast.1, s32[1,2]{1,0:T(1,128)} %screen.3, bf16[32,32,384]{2,1,0:T(8,128)(2,1)} %canvas.1, bf16[49,384]{1,0:T(8,128)(2,1)} %dwk.1, f32[384]{0:T(512)} %bias.4, ...), custom_call_target="tpu_custom_call" | custom-call | tf_op jit(solution)/shard_map/pallas_call | solution.py:34
  9.9 0.0 copy-start.1
  9.9 0.0 copy-start.2
  9.9 0.0 copy-start.3
  9.9 0.0 copy-start.4
  9.9 2.0 %collective-permute-start.5 = (bf16[256,384]{1,0:T(8,128)(2,1)S(1)}, bf16[256,384]{1,0:T(8,128)(2,1)S(1)}, u32[]{:S(2)}, u32[]{:S(2)}) collective-permute-start(bf16[256,384]{1,0:T(8,128)(2,1)S(1)} %get-tuple-element.40.own.mixed), channel_id=1, source_target_pairs={{0,3},{1,0},{2,1},{3,2},{4,7},{5,4},{6,5},{7,6},{8,11},{9,8},{10,9... | collective-permute-start | bytes 589832 | tf_op jit(solution)/shard_map/ppermute | solution.py:412
  12.0 0.1 collective-permute-start.6
  12.0 3.2 %collective-permute-start.3 = (bf16[256,384]{1,0:T(8,128)(2,1)S(1)}, bf16[256,384]{1,0:T(8,128)(2,1)S(1)}, u32[]{:S(2)}, u32[]{:S(2)}) collective-permute-start(bf16[256,384]{1,0:T(8,128)(2,1)S(1)} %get-tuple-element.36.earlier.own.mixed), channel_id=1, source_target_pairs={{0,3},{1,0},{2,1},{3,2},{4,7},{5,4},{6,5},{7,6},{8,11},{9,8},{10,9... | collective-permute-start | bytes 589832 | tf_op jit(solution)/shard_map/ppermute | solution.py:412
  15.2 0.0 copy-done
  15.2 1.3 %shard_map.128.before = f32[3,38,48,128]{3,2,1,0:T(8,128)S(1)} custom-call(s32[2,32]{1,0:T(2,128)} %bitcast.2, s32[32]{0:T(128)} %counts.5, bf16[32,4,4,384]{3,2,1,0:T(4,128)(2,1)S(1)} %copy-done, bf16[256,384]{1,0:T(8,128)(2,1)S(1)} %get-tuple-element.36.earlier.own.mixed), custom_call_target="tpu_custom_call" | custom-call | tf_op jit(solution)/shard_map/pallas_call | solution.py:34
  16.5 0.0 collective-permute-done.left
  16.5 0.1 slice.3
  16.6 0.1 collective-permute-start.2
  16.7 0.0 collective-permute-done.1.right.cells
  16.7 0.0 copy-done.1
  16.7 0.0 copy-done.2
  16.7 0.0 copy-done.3
  16.7 0.0 copy-done.4
  16.7 3.4 %shard_map.129 = (f32[256,1536]{1,0:T(8,128)S(1)}, f32[256,1536]{1,0:T(8,128)S(1)}, bf16[1536,1536]{1,0:T(8,128)(2,1)S(1)}, f32[8,1536]{1,0:T(8,128)S(1)}) custom-call(bf16[32,4,4,384]{3,2,1,0:T(4,128)(2,1)S(1)} %copy-done, bf16[32,4,4,384]{3,2,1,0:T(4,128)(2,1)S(1)} %collective-permute-done.left, ...), custom_call_target="tpu_custom_call" | custom-call | tf_op jit(solution)/shard_map/pallas_call | solution.py:34
  20.1 0.0 collective-permute-done.5.mixed.earlier.right
  20.2 0.0 collective-permute-done.6.left
  20.2 0.1 shard_map.131
  20.2 3.3 %collective-permute-start.7 = (bf16[512,384]{1,0:T(8,128)(2,1)S(1)}, bf16[512,384]{1,0:T(8,128)(2,1)S(1)}, u32[]{:S(2)}, u32[]{:S(2)}) collective-permute-start(bf16[512,384]{1,0:T(8,128)(2,1)S(1)} %shard_map.131), channel_id=1, source_target_pairs={{0,3},{1,0},{2,1},{3,2},{4,7},{5,4},{6,5},{7,6},{8,11},{9,8},{10,9... | collective-permute-start | bytes 1179656 | tf_op jit(solution)/shard_map/ppermute | solution.py:412
  23.5 0.0 collective-permute-start.11
  23.5 0.0 collective-permute-done.3.earlier.right
  23.5 0.0 collective-permute-done.2.cot
  23.5 0.7 %shard_map.130.hidden = f32[256,1536]{1,0:T(8,128)S(1)} custom-call(f32[256,1536]{1,0:T(8,128)S(1)} %get-tuple-element.39.before, bf16[16,4,4,384]{3,2,1,0:T(4,128)(2,1)S(1)} %collective-permute-done.2.cot, f32[1536]{0:T(1024)S(1)} %copy-done.2, bf16[1536,1536]{1,0:T(8,128)(2,1)S(1)} %get-tuple-element.38.w_out, ...), custom_call_target="tpu_custom_call" | custom-call | tf_op jit(solution)/shard_map/pallas_call | solution.py:34
  24.2 1.0 %collective-permute-start.4 = (bf16[256,384]{1,0:T(8,128)(2,1)S(1)}, bf16[256,384]{1,0:T(8,128)(2,1)S(1)}, u32[]{:S(2)}, u32[]{:S(2)}) collective-permute-start(bf16[256,384]{1,0:T(8,128)(2,1)S(1)} %get-tuple-element.40.own.mixed), channel_id=1, source_target_pairs={{0,1},{1,2},{2,3},{3,0},{4,5},{5,6},{6,7},{7,4},{8,9},{9,10},{10,1... | collective-permute-start | bytes 589832 | tf_op jit(solution)/shard_map/ppermute | solution.py:412
  25.2 6.0 %collective-permute-done.11.opp = bf16[256,384]{1,0:T(8,128)(2,1)S(1)} collective-permute-done((bf16[256,384]{1,0:T(8,128)(2,1)S(1)}, bf16[256,384]{1,0:T(8,128)(2,1)S(1)}, u32[]{:S(2)}, u32[]{:S(2)}) %collective-permute-start.11) | collective-permute-done | bytes 196640 | tf_op jit(solution)/shard_map/ppermute | solution.py:412
  31.2 3.5 %shard_map.136 = (bf16[272,384]{1,0:T(8,128)(2,1)S(1)}, bf16[272,384]{1,0:T(8,128)(2,1)S(1)}, bf16[256,1536]{1,0:T(8,128)(2,1)S(1)}, f32[256,1]{1,0:T(8,128)S(1)}, f32[256,1]{1,0:T(8,128)S(1)}) custom-call(bf16[256,384]{1,0:T(8,128)(2,1)S(1)} %get-tuple-element.36.earlier.own.mixed, bf16[256,384]{1,0:T(8,128)(2,1)S(1)} %collective-permute-done.6.left, ...), custom_call_target="tpu_custom_call" | custom-call | tf_op jit(solution)/shard_map/pallas_call | solution.py:34
  34.7 0.1 collective-permute-start.12
  34.8 2.0 %collective-permute-start.13 = (bf16[272,384]{1,0:T(8,128)(2,1)S(1)}, bf16[272,384]{1,0:T(8,128)(2,1)S(1)}, u32[]{:S(2)}, u32[]{:S(2)}) collective-permute-start(bf16[272,384]{1,0:T(8,128)(2,1)S(1)} %get-tuple-element.60.away), channel_id=1, source_target_pairs={{0,1},{1,2},{2,3},{3,0},{4,5},{5,6},{6,7},{7,4},{8,9},{9,10},{10,1... | collective-permute-start | bytes 626696 | tf_op jit(solution)/shard_map/ppermute | solution.py:412
  36.8 0.0 collective-permute-done.7.cot.opp
  36.8 0.6 %shard_map.132.hidden = f32[256,1536]{1,0:T(8,128)S(1)} custom-call(f32[256,1536]{1,0:T(8,128)S(1)} %get-tuple-element.45.before, bf16[512,384]{1,0:T(8,128)(2,1)S(1)} %collective-permute-done.7.cot.opp, f32[1536]{0:T(1024)S(1)} %copy-done.2, bf16[1536,1536]{1,0:T(8,128)(2,1)S(1)} %get-tuple-element.38.w_out, ...), custom_call_target="tpu_custom_call" | custom-call | tf_op jit(solution)/shard_map/pallas_call | solution.py:34
  37.4 0.0 collective-permute-done.4.left
  37.4 3.2 %shard_map.133 = (bf16[272,384]{1,0:T(8,128)(2,1)S(1)}, bf16[256,1536]{1,0:T(8,128)(2,1)S(1)}, f32[256,1]{1,0:T(8,128)S(1)}, f32[256,1]{1,0:T(8,128)S(1)}) custom-call(bf16[256,384]{1,0:T(8,128)(2,1)S(1)} %get-tuple-element.40.own.mixed, bf16[256,384]{1,0:T(8,128)(2,1)S(1)} %collective-permute-done.4.left, ...), custom_call_target="tpu_custom_call" | custom-call | tf_op jit(solution)/shard_map/pallas_call | solution.py:34
  40.6 1.5 %collective-permute-start.9 = (bf16[272,384]{1,0:T(8,128)(2,1)S(1)}, bf16[272,384]{1,0:T(8,128)(2,1)S(1)}, u32[]{:S(2)}, u32[]{:S(2)}) collective-permute-start(bf16[272,384]{1,0:T(8,128)(2,1)S(1)} %get-tuple-element.48.away), channel_id=1, source_target_pairs={{0,3},{1,0},{2,1},{3,2},{4,7},{5,4},{6,5},{7,6},{8,11},{9,8},{10,9... | collective-permute-start | bytes 626696 | tf_op jit(solution)/shard_map/ppermute | solution.py:412
  42.1 0.6 %collective-permute-done.12.earlier.got = bf16[272,384]{1,0:T(8,128)(2,1)S(1)} collective-permute-done((bf16[272,384]{1,0:T(8,128)(2,1)S(1)}, bf16[272,384]{1,0:T(8,128)(2,1)S(1)}, u32[]{:S(2)}, u32[]{:S(2)}) %collective-permute-start.12) | collective-permute-done | bytes 208928 | tf_op jit(solution)/shard_map/ppermute | solution.py:412
  42.8 1.0 %shard_map.137 = (bf16[256,384]{1,0:T(8,128)(2,1)S(1)}, f32[256,384]{1,0:T(8,128)S(1)}) custom-call(bf16[256,1536]{1,0:T(8,128)(2,1)S(1)} %get-tuple-element.57.act, bf16[1536,1536]{1,0:T(8,128)(2,1)S(1)} %get-tuple-element.44.w_in, bf16[272,384]{1,0:T(8,128)(2,1)S(1)} %collective-permute-done.12.earlier.got), custom_call_target="tpu_custom_call" | custom-call | tf_op jit(solution)/shard_map/pallas_call | solution.py:34
  43.7 0.0 collective-permute-done.13.come
  43.8 0.1 shard_map.138
  43.8 0.2 collective-permute-start.14
  44.1 1.4 %shard_map.134 = (bf16[256,384]{1,0:T(8,128)(2,1)S(1)}, bf16[272,384]{1,0:T(8,128)(2,1)S(1)}, f32[256,384]{1,0:T(8,128)S(1)}) custom-call(bf16[256,1536]{1,0:T(8,128)(2,1)S(1)} %get-tuple-element.47.act, bf16[1536,1536]{1,0:T(8,128)(2,1)S(1)} %get-tuple-element.44.w_in, bf16[272,384]{1,0:T(8,128)(2,1)S(1)} %get-tuple-element.48.away), custom_call_target="tpu_custom_call" | custom-call | tf_op jit(solution)/shard_map/pallas_call | solution.py:34
  45.4 0.1 collective-permute-start.8
  45.5 1.8 %collective-permute-done.9.come = bf16[272,384]{1,0:T(8,128)(2,1)S(1)} collective-permute-done((bf16[272,384]{1,0:T(8,128)(2,1)S(1)}, bf16[272,384]{1,0:T(8,128)(2,1)S(1)}, u32[]{:S(2)}, u32[]{:S(2)}) %collective-permute-start.9) | collective-permute-done | bytes 208928 | tf_op jit(solution)/shard_map/ppermute | solution.py:412
  47.3 0.1 shard_map.135
  47.4 3.3 %collective-permute-start.10 = (bf16[272,384]{1,0:T(8,128)(2,1)S(1)}, bf16[272,384]{1,0:T(8,128)(2,1)S(1)}, u32[]{:S(2)}, u32[]{:S(2)}) collective-permute-start(bf16[272,384]{1,0:T(8,128)(2,1)S(1)} %shard_map.135), channel_id=1, source_target_pairs={{0,3},{1,0},{2,1},{3,2},{4,7},{5,4},{6,5},{7,6},{8,11},{9,8},{10,9... | collective-permute-start | bytes 626696 | tf_op jit(solution)/shard_map/ppermute | solution.py:412
  50.7 0.2 collective-permute-done.14.total
  50.9 2.9 %shard_map.139.before = f32[3,38,48,128]{3,2,1,0:T(8,128)S(1)} custom-call(s32[2,32]{1,0:T(2,128)} %bitcast.3, s32[32]{0:T(128)} %counts.5, f32[256,384]{1,0:T(8,128)S(1)} %get-tuple-element.59.mine, bf16[272,384]{1,0:T(8,128)(2,1)S(1)} %collective-permute-done.12.earlier.got, bf16[272,384]{1,0:T(8,128)(2,1)S(1)} %collective-permute-done.14.total, ...), custom_call_target="tpu_custom_call" | custom-call | tf_op jit(solution)/shard_map/pallas_call | solution.py:34
  53.8 0.0 collective-permute-done.8.got
  53.8 0.2 collective-permute-done.10.total
  54.0 4.1 %shard_map.140 = f32[32,32,384]{2,1,0:T(8,128)} custom-call(s32[2,32]{1,0:T(2,128)} %bitcast.4, s32[32]{0:T(128)} %counts.5, s32[1,2]{1,0:T(1,128)} %screen.3, f32[256,384]{1,0:T(8,128)S(1)} %get-tuple-element.49.mine, bf16[272,384]{1,0:T(8,128)(2,1)S(1)} %collective-permute-done.8.got, bf16[272,384]{1,0:T(8,128)(2,1)S(1)} %collective-permute-done.10.total, ...), custom_call_target="tpu_custom_call" | custom-call | tf_op jit(solution)/shard_map/pallas_call | solution.py:34
Async XLA Ops:
  0.0 15.2 %copy-start = (bf16[32,4,4,384]{3,2,1,0:T(4,128)(2,1)S(1)}, bf16[32,4,4,384]{3,2,1,0:T(4,128)(2,1)}, u32[]{:S(2)}) copy-start(bf16[32,4,4,384]{3,2,1,0:T(4,128)(2,1)} %own.3) | copy-start | bytes 1179652
  0.0 16.5 %collective-permute-start = (bf16[32,4,4,384]{3,2,1,0:T(4,128)(2,1)}, bf16[32,4,4,384]{3,2,1,0:T(4,128)(2,1)S(1)}, u32[]{:S(2)}, u32[]{:S(2)}) collective-permute-start(bf16[32,4,4,384]{3,2,1,0:T(4,128)(2,1)} %own.3), channel_id=1, source_target_pairs={{0,1},{1,2},{2,3},{3,0},{4,5},{5,6},{6,7},{7,4},{8,9},{9,10},{10,1... | collective-permute-start | bytes 1179656 | tf_op jit(solution)/shard_map/ppermute | solution.py:412
  1.9 14.8 %collective-permute-start.1 = (bf16[32,4,4,384]{3,2,1,0:T(4,128)(2,1)}, bf16[32,4,4,384]{3,2,1,0:T(4,128)(2,1)S(1)}, u32[]{:S(2)}, u32[]{:S(2)}) collective-permute-start(bf16[32,4,4,384]{3,2,1,0:T(4,128)(2,1)} %own.3), channel_id=1, source_target_pairs={{0,3},{1,0},{2,1},{3,2},{4,7},{5,4},{6,5},{7,6},{8,11},{9,8},{10,9... | collective-permute-start | bytes 1179656 | tf_op jit(solution)/shard_map/ppermute | solution.py:412
  9.9 6.8 %copy-start.1 = (f32[1536]{0:T(1024)S(1)}, f32[1536]{0:T(1024)}, u32[]{:S(2)}) copy-start(f32[1536]{0:T(1024)} %gain.9) | copy-start | bytes 18436
  9.9 6.8 %copy-start.2 = (f32[1536]{0:T(1024)S(1)}, f32[1536]{0:T(1024)}, u32[]{:S(2)}) copy-start(f32[1536]{0:T(1024)} %scale.5) | copy-start | bytes 18436
  9.9 6.8 %copy-start.3 = (f32[1536]{0:T(1024)S(1)}, f32[1536]{0:T(1024)}, u32[]{:S(2)}) copy-start(f32[1536]{0:T(1024)} %bias.7) | copy-start | bytes 18436
  9.9 6.8 %copy-start.4 = (f32[1536]{0:T(1024)S(1)}, f32[1536]{0:T(1024)}, u32[]{:S(2)}) copy-start(f32[1536]{0:T(1024)} %b_in.5) | copy-start | bytes 18436
  9.9 10.2 %collective-permute-start.5 = (bf16[256,384]{1,0:T(8,128)(2,1)S(1)}, bf16[256,384]{1,0:T(8,128)(2,1)S(1)}, u32[]{:S(2)}, u32[]{:S(2)}) collective-permute-start(bf16[256,384]{1,0:T(8,128)(2,1)S(1)} %get-tuple-element.40.own.mixed), channel_id=1, source_target_pairs={{0,3},{1,0},{2,1},{3,2},{4,7},{5,4},{6,5},{7,6},{8,11},{9,8},{10,9... | collective-permute-start | bytes 589832 | tf_op jit(solution)/shard_map/ppermute | solution.py:412
  12.0 8.2 %collective-permute-start.6 = (bf16[256,384]{1,0:T(8,128)(2,1)S(1)}, bf16[256,384]{1,0:T(8,128)(2,1)S(1)}, u32[]{:S(2)}, u32[]{:S(2)}) collective-permute-start(bf16[256,384]{1,0:T(8,128)(2,1)S(1)} %get-tuple-element.36.earlier.own.mixed), channel_id=1, source_target_pairs={{0,1},{1,2},{2,3},{3,0},{4,5},{5,6},{6,7},{7,4},{8,9},{9,10},{10,1... | collective-permute-start | bytes 589832 | tf_op jit(solution)/shard_map/ppermute | solution.py:412
  12.0 11.5 %collective-permute-start.3 = (bf16[256,384]{1,0:T(8,128)(2,1)S(1)}, bf16[256,384]{1,0:T(8,128)(2,1)S(1)}, u32[]{:S(2)}, u32[]{:S(2)}) collective-permute-start(bf16[256,384]{1,0:T(8,128)(2,1)S(1)} %get-tuple-element.36.earlier.own.mixed), channel_id=1, source_target_pairs={{0,3},{1,0},{2,1},{3,2},{4,7},{5,4},{6,5},{7,6},{8,11},{9,8},{10,9... | collective-permute-start | bytes 589832 | tf_op jit(solution)/shard_map/ppermute | solution.py:412
  16.6 7.0 %collective-permute-start.2 = (bf16[16,4,4,384]{3,2,1,0:T(4,128)(2,1)S(1)}, bf16[16,4,4,384]{3,2,1,0:T(4,128)(2,1)S(1)}, u32[]{:S(2)}, u32[]{:S(2)}) collective-permute-start(bf16[16,4,4,384]{3,2,1,0:T(4,128)(2,1)S(1)} %slice.3), channel_id=1, source_target_pairs={{0,1},{1,2},{2,3},{3,0},{4,5},{5,6},{6,7},{7,4},{8,9},{9,10},{10,1... | collective-permute-start | bytes 589832 | tf_op jit(solution)/shard_map/ppermute | solution.py:412
  20.2 16.5 %collective-permute-start.7 = (bf16[512,384]{1,0:T(8,128)(2,1)S(1)}, bf16[512,384]{1,0:T(8,128)(2,1)S(1)}, u32[]{:S(2)}, u32[]{:S(2)}) collective-permute-start(bf16[512,384]{1,0:T(8,128)(2,1)S(1)} %shard_map.131), channel_id=1, source_target_pairs={{0,3},{1,0},{2,1},{3,2},{4,7},{5,4},{6,5},{7,6},{8,11},{9,8},{10,9... | collective-permute-start | bytes 1179656 | tf_op jit(solution)/shard_map/ppermute | solution.py:412
  23.5 7.7 %collective-permute-start.11 = (bf16[256,384]{1,0:T(8,128)(2,1)S(1)}, bf16[256,384]{1,0:T(8,128)(2,1)S(1)}, u32[]{:S(2)}, u32[]{:S(2)}) collective-permute-start(bf16[256,384]{1,0:T(8,128)(2,1)S(1)} %collective-permute-done.6.left), channel_id=1, source_target_pairs={{0,1},{1,2},{2,3},{3,0},{4,5},{5,6},{6,7},{7,4},{8,9},{9,10},{10,1... | collective-permute-start | bytes 589832 | tf_op jit(solution)/shard_map/ppermute | solution.py:412
  24.2 13.2 %collective-permute-start.4 = (bf16[256,384]{1,0:T(8,128)(2,1)S(1)}, bf16[256,384]{1,0:T(8,128)(2,1)S(1)}, u32[]{:S(2)}, u32[]{:S(2)}) collective-permute-start(bf16[256,384]{1,0:T(8,128)(2,1)S(1)} %get-tuple-element.40.own.mixed), channel_id=1, source_target_pairs={{0,1},{1,2},{2,3},{3,0},{4,5},{5,6},{6,7},{7,4},{8,9},{9,10},{10,1... | collective-permute-start | bytes 589832 | tf_op jit(solution)/shard_map/ppermute | solution.py:412
  34.7 8.1 %collective-permute-start.12 = (bf16[272,384]{1,0:T(8,128)(2,1)S(1)}, bf16[272,384]{1,0:T(8,128)(2,1)S(1)}, u32[]{:S(2)}, u32[]{:S(2)}) collective-permute-start(bf16[272,384]{1,0:T(8,128)(2,1)S(1)} %get-tuple-element.58), channel_id=1, source_target_pairs={{0,3},{1,0},{2,1},{3,2},{4,7},{5,4},{6,5},{7,6},{8,11},{9,8},{10,9... | collective-permute-start | bytes 626696 | tf_op jit(solution)/shard_map/ppermute | solution.py:412
  34.8 9.0 %collective-permute-start.13 = (bf16[272,384]{1,0:T(8,128)(2,1)S(1)}, bf16[272,384]{1,0:T(8,128)(2,1)S(1)}, u32[]{:S(2)}, u32[]{:S(2)}) collective-permute-start(bf16[272,384]{1,0:T(8,128)(2,1)S(1)} %get-tuple-element.60.away), channel_id=1, source_target_pairs={{0,1},{1,2},{2,3},{3,0},{4,5},{5,6},{6,7},{7,4},{8,9},{9,10},{10,1... | collective-permute-start | bytes 626696 | tf_op jit(solution)/shard_map/ppermute | solution.py:412
  40.6 6.7 %collective-permute-start.9 = (bf16[272,384]{1,0:T(8,128)(2,1)S(1)}, bf16[272,384]{1,0:T(8,128)(2,1)S(1)}, u32[]{:S(2)}, u32[]{:S(2)}) collective-permute-start(bf16[272,384]{1,0:T(8,128)(2,1)S(1)} %get-tuple-element.48.away), channel_id=1, source_target_pairs={{0,3},{1,0},{2,1},{3,2},{4,7},{5,4},{6,5},{7,6},{8,11},{9,8},{10,9... | collective-permute-start | bytes 626696 | tf_op jit(solution)/shard_map/ppermute | solution.py:412
  43.8 7.1 %collective-permute-start.14 = (bf16[272,384]{1,0:T(8,128)(2,1)S(1)}, bf16[272,384]{1,0:T(8,128)(2,1)S(1)}, u32[]{:S(2)}, u32[]{:S(2)}) collective-permute-start(bf16[272,384]{1,0:T(8,128)(2,1)S(1)} %shard_map.138), channel_id=1, source_target_pairs={{0,1},{1,2},{2,3},{3,0},{4,5},{5,6},{6,7},{7,4},{8,9},{9,10},{10,1... | collective-permute-start | bytes 626696 | tf_op jit(solution)/shard_map/ppermute | solution.py:412
  45.4 8.4 %collective-permute-start.8 = (bf16[272,384]{1,0:T(8,128)(2,1)S(1)}, bf16[272,384]{1,0:T(8,128)(2,1)S(1)}, u32[]{:S(2)}, u32[]{:S(2)}) collective-permute-start(bf16[272,384]{1,0:T(8,128)(2,1)S(1)} %get-tuple-element.50), channel_id=1, source_target_pairs={{0,1},{1,2},{2,3},{3,0},{4,5},{5,6},{6,7},{7,4},{8,9},{9,10},{10,1... | collective-permute-start | bytes 626696 | tf_op jit(solution)/shard_map/ppermute | solution.py:412
  47.4 6.6 %collective-permute-start.10 = (bf16[272,384]{1,0:T(8,128)(2,1)S(1)}, bf16[272,384]{1,0:T(8,128)(2,1)S(1)}, u32[]{:S(2)}, u32[]{:S(2)}) collective-permute-start(bf16[272,384]{1,0:T(8,128)(2,1)S(1)} %shard_map.135), channel_id=1, source_target_pairs={{0,3},{1,0},{2,1},{3,2},{4,7},{5,4},{6,5},{7,6},{8,11},{9,8},{10,9... | collective-permute-start | bytes 626696 | tf_op jit(solution)/shard_map/ppermute | solution.py:412

commit v11 on v9

--- a/solution.py
+++ b/solution.py
@@ -97,13 +97,14 @@
         rows_in[g].wait()
         lax.fori_loop(g * deep, (g + 1) * deep, fill, 0, unroll=4)
     count = mixed_a.shape[0] // 16
-    for b in range(lanes):
-        cut = slice(b * 128, (b + 1) * 128)
-        start = jnp.broadcast_to(bias_row[cut][None], (8, 128))
-        for mixed, base in ((mixed_a, 0), (mixed_b, count)):
-
-            def tile(t, carry):
-                r, q = offsets[0, base + t], offsets[1, base + t]
+    for mixed, base in ((mixed_a, 0), (mixed_b, count)):
+
+        def tile(t, carry):
+            r, q = offsets[0, base + t], offsets[1, base + t]
+            rows = pl.ds(pl.multiple_of(t * 16, 16), 16)
+            for b in range(lanes):
+                cut = slice(b * 128, (b + 1) * 128)
+                start = jnp.broadcast_to(bias_row[cut][None], (8, 128))
                 sums = [None] * 4
                 for p in range(10):
                     for j in range(4):
@@ -113,11 +114,10 @@
                             sums[y] = term if sums[y] is None else sums[y] + term
                 folded = [s + pltpu.roll(s, 4, 0) + start for s in sums]
                 pair = [jnp.where(low, folded[y], folded[y + 1]) for y in (0, 2)]
-                rows = pl.ds(pl.multiple_of(t * 16, 16), 16)
                 mixed[rows, cut] = jnp.concatenate(pair, 0).astype(jnp.bfloat16)
-                return carry
-
-            lax.fori_loop(0, count, tile, 0, unroll=2)
+            return carry
+
+        lax.fori_loop(0, count, tile, 0)
     weights.wait()
 
 

time: 56.7 us -> 56.6 us (level)
  the two profiles are of different devices: /device:TPU:6 before, /device:TPU:28 now
where the time goes in v11:
time: 56.6 us; the launch traced here: 56.2 us
  Pallas kernels  27.7 us (49%)
  starting transfers between devices  22.3 us (39%)
  waiting for transfers between devices  5.67 us (10%)
    pallas_call x13, Pallas kernels, held(): run(*(pltpu.with_memory_space_constraint(a, pltpu.VMEM if spec is VMEM el...  27.7 us
    ppermute x16, starting transfers between devices, shift(): return lax.ppermute(x, 'ch', [(i, (i + by) % n) for i in range(n)])  22.3 us
    ppermute x16, waiting for transfers between devices, shift(): return lax.ppermute(x, 'ch', [(i, (i + by) % n) for i in range(n)])  5.67 us
  transfers between devices with their start and end apart: 16, of which 5 were waited for; matrix products, arithmetic and copies ran while one was open for 0% of the time, Pallas kernels for 42%

profile of v11, /device:TPU:28, one launch (start us, length us, event | category | flops | bytes accessed | tf_op | source)
XLA Modules:
  0.0 56.2 jit_solution(12136166992181267890)
XLA Ops:
  0.0 0.0 copy-start
  0.0 1.9 %collective-permute-start = (bf16[32,4,4,384]{3,2,1,0:T(4,128)(2,1)}, bf16[32,4,4,384]{3,2,1,0:T(4,128)(2,1)S(1)}, u32[]{:S(2)}, u32[]{:S(2)}) collective-permute-start(bf16[32,4,4,384]{3,2,1,0:T(4,128)(2,1)} %own.3), channel_id=1, source_target_pairs={{0,1},{1,2},{2,3},{3,0},{4,5},{5,6},{6,7},{7,4},{8,9},{9,10},{10,1... | collective-permute-start | bytes 1179656 | tf_op jit(solution)/shard_map/ppermute | solution.py:400
  1.9 2.2 %collective-permute-start.1 = (bf16[32,4,4,384]{3,2,1,0:T(4,128)(2,1)}, bf16[32,4,4,384]{3,2,1,0:T(4,128)(2,1)S(1)}, u32[]{:S(2)}, u32[]{:S(2)}) collective-permute-start(bf16[32,4,4,384]{3,2,1,0:T(4,128)(2,1)} %own.3), channel_id=1, source_target_pairs={{0,3},{1,0},{2,1},{3,2},{4,7},{5,4},{6,5},{7,6},{8,11},{9,8},{10,9... | collective-permute-start | bytes 1179656 | tf_op jit(solution)/shard_map/ppermute | solution.py:400
  4.1 5.6 %shard_map.127 = (bf16[256,384]{1,0:T(8,128)(2,1)S(1)}, bf16[256,384]{1,0:T(8,128)(2,1)S(1)}, bf16[1536,1536]{1,0:T(8,128)(2,1)S(1)}, f32[3,28,8,128]{3,2,1,0:T(8,128)S(1)}) custom-call(s32[2,32]{1,0:T(2,128)} %bitcast.1, s32[1,2]{1,0:T(1,128)} %screen.3, bf16[32,32,384]{2,1,0:T(8,128)(2,1)} %canvas.1, bf16[49,384]{1,0:T(8,128)(2,1)} %dwk.1, f32[384]{0:T(512)} %bias.4, ...), custom_call_target="tpu_custom_call" | custom-call | tf_op jit(solution)/shard_map/pallas_call | solution.py:34
  9.8 0.0 copy-start.1
  9.8 0.0 copy-start.2
  9.8 0.0 copy-start.3
  9.8 0.0 copy-start.4
  9.8 2.0 %collective-permute-start.4 = (bf16[256,384]{1,0:T(8,128)(2,1)S(1)}, bf16[256,384]{1,0:T(8,128)(2,1)S(1)}, u32[]{:S(2)}, u32[]{:S(2)}) collective-permute-start(bf16[256,384]{1,0:T(8,128)(2,1)S(1)} %get-tuple-element.40.own.mixed), channel_id=1, source_target_pairs={{0,3},{1,0},{2,1},{3,2},{4,7},{5,4},{6,5},{7,6},{8,11},{9,8},{10,9... | collective-permute-start | bytes 589832 | tf_op jit(solution)/shard_map/ppermute | solution.py:400
  11.8 0.1 collective-permute-start.5
  11.9 0.0 copy-done
  11.9 1.3 %shard_map.128.before = f32[3,38,48,128]{3,2,1,0:T(8,128)S(1)} custom-call(s32[2,32]{1,0:T(2,128)} %bitcast.2, s32[32]{0:T(128)} %counts.5, bf16[32,4,4,384]{3,2,1,0:T(4,128)(2,1)S(1)} %copy-done, bf16[256,384]{1,0:T(8,128)(2,1)S(1)} %get-tuple-element.36.earlier.own.mixed), custom_call_target="tpu_custom_call" | custom-call | tf_op jit(solution)/shard_map/pallas_call | solution.py:34
  13.2 0.2 collective-permute-done.left
  13.4 0.1 slice.6
  13.5 0.1 collective-permute-start.2
  13.6 3.2 %collective-permute-start.11 = (bf16[256,384]{1,0:T(8,128)(2,1)S(1)}, bf16[256,384]{1,0:T(8,128)(2,1)S(1)}, u32[]{:S(2)}, u32[]{:S(2)}) collective-permute-start(bf16[256,384]{1,0:T(8,128)(2,1)S(1)} %get-tuple-element.36.earlier.own.mixed), channel_id=1, source_target_pairs={{0,3},{1,0},{2,1},{3,2},{4,7},{5,4},{6,5},{7,6},{8,11},{9,8},{10,9... | collective-permute-start | bytes 589832 | tf_op jit(solution)/shard_map/ppermute | solution.py:400
  16.8 0.0 collective-permute-done.1.right
  16.8 0.0 copy-done.1
  16.8 0.0 copy-done.2
  16.8 0.0 copy-done.3
  16.8 0.0 copy-done.4
  16.8 3.4 %shard_map.129 = (f32[256,1536]{1,0:T(8,128)S(1)}, f32[256,1536]{1,0:T(8,128)S(1)}, bf16[1536,1536]{1,0:T(8,128)(2,1)S(1)}, f32[8,1536]{1,0:T(8,128)S(1)}) custom-call(bf16[32,4,4,384]{3,2,1,0:T(4,128)(2,1)S(1)} %copy-done, bf16[32,4,4,384]{3,2,1,0:T(4,128)(2,1)S(1)} %collective-permute-done.left, bf16[32,4,4,384]{3,2,1,0:T(4,128)(2,1)S(1)} %collective-permute-done.1.right, ...), custom_call_target="tpu_custom_call" | custom-call | tf_op jit(solution)/shard_map/pallas_call | solution.py:34
  20.3 0.0 collective-permute-done.4.right
  20.3 0.6 %collective-permute-done.5.left = bf16[256,384]{1,0:T(8,128)(2,1)S(1)} collective-permute-done((bf16[256,384]{1,0:T(8,128)(2,1)S(1)}, bf16[256,384]{1,0:T(8,128)(2,1)S(1)}, u32[]{:S(2)}, u32[]{:S(2)}) %collective-permute-start.5) | collective-permute-done | bytes 196640 | tf_op jit(solution)/shard_map/ppermute | solution.py:400
  20.9 0.0 collective-permute-start.12
  20.9 3.2 %collective-permute-start.6 = (bf16[256,384]{1,0:T(8,128)(2,1)S(1)}, bf16[256,384]{1,0:T(8,128)(2,1)S(1)}, u32[]{:S(2)}, u32[]{:S(2)}) collective-permute-start(bf16[256,384]{1,0:T(8,128)(2,1)S(1)} %collective-permute-done.4.right), channel_id=1, source_target_pairs={{0,3},{1,0},{2,1},{3,2},{4,7},{5,4},{6,5},{7,6},{8,11},{9,8},{10,9... | collective-permute-start | bytes 589832 | tf_op jit(solution)/shard_map/ppermute | solution.py:400
  24.1 0.1 slice.7
  24.2 0.1 collective-permute-start.7
  24.3 0.0 collective-permute-done.2.cot
  24.3 0.7 %shard_map.130.hidden = f32[256,1536]{1,0:T(8,128)S(1)} custom-call(f32[256,1536]{1,0:T(8,128)S(1)} %get-tuple-element.39.before, bf16[16,4,4,384]{3,2,1,0:T(4,128)(2,1)S(1)} %collective-permute-done.2.cot, f32[1536]{0:T(1024)S(1)} %copy-done.2, bf16[1536,1536]{1,0:T(8,128)(2,1)S(1)} %get-tuple-element.38.w_out), custom_call_target="tpu_custom_call" | custom-call | tf_op jit(solution)/shard_map/pallas_call | solution.py:34
  25.0 2.0 %collective-permute-start.3 = (bf16[256,384]{1,0:T(8,128)(2,1)S(1)}, bf16[256,384]{1,0:T(8,128)(2,1)S(1)}, u32[]{:S(2)}, u32[]{:S(2)}) collective-permute-start(bf16[256,384]{1,0:T(8,128)(2,1)S(1)} %get-tuple-element.40.own.mixed), channel_id=1, source_target_pairs={{0,1},{1,2},{2,3},{3,0},{4,5},{5,6},{6,7},{7,4},{8,9},{9,10},{10,1... | collective-permute-start | bytes 589832 | tf_op jit(solution)/shard_map/ppermute | solution.py:400
  27.0 0.0 collective-permute-done.11.right
  27.0 2.1 %collective-permute-done.12.opp = bf16[256,384]{1,0:T(8,128)(2,1)S(1)} collective-permute-done((bf16[256,384]{1,0:T(8,128)(2,1)S(1)}, bf16[256,384]{1,0:T(8,128)(2,1)S(1)}, u32[]{:S(2)}, u32[]{:S(2)}) %collective-permute-start.12) | collective-permute-done | bytes 196640 | tf_op jit(solution)/shard_map/ppermute | solution.py:400
  29.1 3.5 %shard_map.135 = (bf16[272,384]{1,0:T(8,128)(2,1)S(1)}, bf16[272,384]{1,0:T(8,128)(2,1)S(1)}, bf16[256,1536]{1,0:T(8,128)(2,1)S(1)}, f32[256,1]{1,0:T(8,128)S(1)}, f32[256,1]{1,0:T(8,128)S(1)}) custom-call(bf16[256,384]{1,0:T(8,128)(2,1)S(1)} %get-tuple-element.36.earlier.own.mixed, bf16[256,384]{1,0:T(8,128)(2,1)S(1)} %collective-permute-done.5.left, ...), custom_call_target="tpu_custom_call" | custom-call | tf_op jit(solution)/shard_map/pallas_call | solution.py:34
  32.6 0.7 %collective-permute-start.13 = (bf16[272,384]{1,0:T(8,128)(2,1)S(1)}, bf16[272,384]{1,0:T(8,128)(2,1)S(1)}, u32[]{:S(2)}, u32[]{:S(2)}) collective-permute-start(bf16[272,384]{1,0:T(8,128)(2,1)S(1)} %get-tuple-element.58), channel_id=1, source_target_pairs={{0,3},{1,0},{2,1},{3,2},{4,7},{5,4},{6,5},{7,6},{8,11},{9,8},{10,9... | collective-permute-start | bytes 626696 | tf_op jit(solution)/shard_map/ppermute | solution.py:400
  33.3 1.4 %collective-permute-start.14 = (bf16[272,384]{1,0:T(8,128)(2,1)S(1)}, bf16[272,384]{1,0:T(8,128)(2,1)S(1)}, u32[]{:S(2)}, u32[]{:S(2)}) collective-permute-start(bf16[272,384]{1,0:T(8,128)(2,1)S(1)} %get-tuple-element.60.away), channel_id=1, source_target_pairs={{0,1},{1,2},{2,3},{3,0},{4,5},{5,6},{6,7},{7,4},{8,9},{9,10},{10,1... | collective-permute-start | bytes 626696 | tf_op jit(solution)/shard_map/ppermute | solution.py:400
  34.7 0.0 collective-permute-done.7.cot
  34.7 0.7 %shard_map.131.hidden = f32[256,1536]{1,0:T(8,128)S(1)} custom-call(f32[256,1536]{1,0:T(8,128)S(1)} %get-tuple-element.44.before, bf16[16,4,4,384]{3,2,1,0:T(4,128)(2,1)S(1)} %collective-permute-done.7.cot, f32[1536]{0:T(1024)S(1)} %copy-done.2, bf16[1536,1536]{1,0:T(8,128)(2,1)S(1)} %get-tuple-element.38.w_out), custom_call_target="tpu_custom_call" | custom-call | tf_op jit(solution)/shard_map/pallas_call | solution.py:34
  35.3 0.0 collective-permute-done.6.opp
  35.3 0.0 collective-permute-done.3.left
  35.3 3.2 %shard_map.132 = (bf16[272,384]{1,0:T(8,128)(2,1)S(1)}, bf16[256,1536]{1,0:T(8,128)(2,1)S(1)}, f32[256,1]{1,0:T(8,128)S(1)}, f32[256,1]{1,0:T(8,128)S(1)}) custom-call(bf16[256,384]{1,0:T(8,128)(2,1)S(1)} %get-tuple-element.40.own.mixed, bf16[256,384]{1,0:T(8,128)(2,1)S(1)} %collective-permute-done.3.left, ...), custom_call_target="tpu_custom_call" | custom-call | tf_op jit(solution)/shard_map/pallas_call | solution.py:34
  38.5 1.9 %collective-permute-start.9 = (bf16[272,384]{1,0:T(8,128)(2,1)S(1)}, bf16[272,384]{1,0:T(8,128)(2,1)S(1)}, u32[]{:S(2)}, u32[]{:S(2)}) collective-permute-start(bf16[272,384]{1,0:T(8,128)(2,1)S(1)} %get-tuple-element.48.away), channel_id=1, source_target_pairs={{0,3},{1,0},{2,1},{3,2},{4,7},{5,4},{6,5},{7,6},{8,11},{9,8},{10,9... | collective-permute-start | bytes 626696 | tf_op jit(solution)/shard_map/ppermute | solution.py:400
  40.4 0.0 collective-permute-done.13.earlier.got
  40.4 1.0 %shard_map.136 = (bf16[256,384]{1,0:T(8,128)(2,1)S(1)}, f32[256,384]{1,0:T(8,128)S(1)}) custom-call(bf16[256,1536]{1,0:T(8,128)(2,1)S(1)} %get-tuple-element.57.act, bf16[1536,1536]{1,0:T(8,128)(2,1)S(1)} %get-tuple-element.43.w_in, bf16[272,384]{1,0:T(8,128)(2,1)S(1)} %collective-permute-done.13.earlier.got), custom_call_target="tpu_custom_call" | custom-call | tf_op jit(solution)/shard_map/pallas_call | solution.py:34
  41.4 0.0 collective-permute-done.14.come
  41.5 0.1 shard_map.137
  41.5 0.3 collective-permute-start.15
  41.8 1.4 %shard_map.133 = (bf16[256,384]{1,0:T(8,128)(2,1)S(1)}, bf16[272,384]{1,0:T(8,128)(2,1)S(1)}, f32[256,384]{1,0:T(8,128)S(1)}) custom-call(bf16[256,1536]{1,0:T(8,128)(2,1)S(1)} %get-tuple-element.47.act, bf16[1536,1536]{1,0:T(8,128)(2,1)S(1)} %get-tuple-element.43.w_in, bf16[272,384]{1,0:T(8,128)(2,1)S(1)} %get-tuple-element.48.away), custom_call_target="tpu_custom_call" | custom-call | tf_op jit(solution)/shard_map/pallas_call | solution.py:34
  43.2 0.1 collective-permute-start.8
  43.3 2.4 %collective-permute-done.9.come = bf16[272,384]{1,0:T(8,128)(2,1)S(1)} collective-permute-done((bf16[272,384]{1,0:T(8,128)(2,1)S(1)}, bf16[272,384]{1,0:T(8,128)(2,1)S(1)}, u32[]{:S(2)}, u32[]{:S(2)}) %collective-permute-start.9) | collective-permute-done | bytes 208928 | tf_op jit(solution)/shard_map/ppermute | solution.py:400
  45.6 0.1 shard_map.134
  45.7 3.1 %collective-permute-start.10 = (bf16[272,384]{1,0:T(8,128)(2,1)S(1)}, bf16[272,384]{1,0:T(8,128)(2,1)S(1)}, u32[]{:S(2)}, u32[]{:S(2)}) collective-permute-start(bf16[272,384]{1,0:T(8,128)(2,1)S(1)} %shard_map.134), channel_id=1, source_target_pairs={{0,3},{1,0},{2,1},{3,2},{4,7},{5,4},{6,5},{7,6},{8,11},{9,8},{10,9... | collective-permute-start | bytes 626696 | tf_op jit(solution)/shard_map/ppermute | solution.py:400
  48.8 0.0 collective-permute-done.15.total
  48.8 2.9 %shard_map.138.before = f32[3,38,48,128]{3,2,1,0:T(8,128)S(1)} custom-call(s32[2,32]{1,0:T(2,128)} %bitcast.3, s32[32]{0:T(128)} %counts.5, f32[256,384]{1,0:T(8,128)S(1)} %get-tuple-element.59.mine, bf16[272,384]{1,0:T(8,128)(2,1)S(1)} %collective-permute-done.13.earlier.got, bf16[272,384]{1,0:T(8,128)(2,1)S(1)} %collective-permute-done.15.total, ...), custom_call_target="tpu_custom_call" | custom-call | tf_op jit(solution)/shard_map/pallas_call | solution.py:34
  51.7 0.0 collective-permute-done.8.got
  51.7 0.4 collective-permute-done.10.total
  52.1 4.0 %shard_map.139 = f32[32,32,384]{2,1,0:T(8,128)} custom-call(s32[2,32]{1,0:T(2,128)} %bitcast.4, s32[32]{0:T(128)} %counts.5, s32[1,2]{1,0:T(1,128)} %screen.3, f32[256,384]{1,0:T(8,128)S(1)} %get-tuple-element.49.mine, bf16[272,384]{1,0:T(8,128)(2,1)S(1)} %collective-permute-done.8.got, bf16[272,384]{1,0:T(8,128)(2,1)S(1)} %collective-permute-done.10.total, ...), custom_call_target="tpu_custom_call" | custom-call | tf_op jit(solution)/shard_map/pallas_call | solution.py:34
Async XLA Ops:
  0.0 11.9 %copy-start = (bf16[32,4,4,384]{3,2,1,0:T(4,128)(2,1)S(1)}, bf16[32,4,4,384]{3,2,1,0:T(4,128)(2,1)}, u32[]{:S(2)}) copy-start(bf16[32,4,4,384]{3,2,1,0:T(4,128)(2,1)} %own.3) | copy-start | bytes 1179652
  0.0 13.4 %collective-permute-start = (bf16[32,4,4,384]{3,2,1,0:T(4,128)(2,1)}, bf16[32,4,4,384]{3,2,1,0:T(4,128)(2,1)S(1)}, u32[]{:S(2)}, u32[]{:S(2)}) collective-permute-start(bf16[32,4,4,384]{3,2,1,0:T(4,128)(2,1)} %own.3), channel_id=1, source_target_pairs={{0,1},{1,2},{2,3},{3,0},{4,5},{5,6},{6,7},{7,4},{8,9},{9,10},{10,1... | collective-permute-start | bytes 1179656 | tf_op jit(solution)/shard_map/ppermute | solution.py:400
  1.9 14.9 %collective-permute-start.1 = (bf16[32,4,4,384]{3,2,1,0:T(4,128)(2,1)}, bf16[32,4,4,384]{3,2,1,0:T(4,128)(2,1)S(1)}, u32[]{:S(2)}, u32[]{:S(2)}) collective-permute-start(bf16[32,4,4,384]{3,2,1,0:T(4,128)(2,1)} %own.3), channel_id=1, source_target_pairs={{0,3},{1,0},{2,1},{3,2},{4,7},{5,4},{6,5},{7,6},{8,11},{9,8},{10,9... | collective-permute-start | bytes 1179656 | tf_op jit(solution)/shard_map/ppermute | solution.py:400
  9.8 7.1 %copy-start.1 = (f32[1536]{0:T(1024)S(1)}, f32[1536]{0:T(1024)}, u32[]{:S(2)}) copy-start(f32[1536]{0:T(1024)} %gain.9) | copy-start | bytes 18436
  9.8 7.1 %copy-start.2 = (f32[1536]{0:T(1024)S(1)}, f32[1536]{0:T(1024)}, u32[]{:S(2)}) copy-start(f32[1536]{0:T(1024)} %scale.5) | copy-start | bytes 18436
  9.8 7.1 %copy-start.3 = (f32[1536]{0:T(1024)S(1)}, f32[1536]{0:T(1024)}, u32[]{:S(2)}) copy-start(f32[1536]{0:T(1024)} %bias.7) | copy-start | bytes 18436
  9.8 7.0 %copy-start.4 = (f32[1536]{0:T(1024)S(1)}, f32[1536]{0:T(1024)}, u32[]{:S(2)}) copy-start(f32[1536]{0:T(1024)} %b_in.5) | copy-start | bytes 18436
  9.8 10.5 %collective-permute-start.4 = (bf16[256,384]{1,0:T(8,128)(2,1)S(1)}, bf16[256,384]{1,0:T(8,128)(2,1)S(1)}, u32[]{:S(2)}, u32[]{:S(2)}) collective-permute-start(bf16[256,384]{1,0:T(8,128)(2,1)S(1)} %get-tuple-element.40.own.mixed), channel_id=1, source_target_pairs={{0,3},{1,0},{2,1},{3,2},{4,7},{5,4},{6,5},{7,6},{8,11},{9,8},{10,9... | collective-permute-start | bytes 589832 | tf_op jit(solution)/shard_map/ppermute | solution.py:400
  11.8 9.1 %collective-permute-start.5 = (bf16[256,384]{1,0:T(8,128)(2,1)S(1)}, bf16[256,384]{1,0:T(8,128)(2,1)S(1)}, u32[]{:S(2)}, u32[]{:S(2)}) collective-permute-start(bf16[256,384]{1,0:T(8,128)(2,1)S(1)} %get-tuple-element.36.earlier.own.mixed), channel_id=1, source_target_pairs={{0,1},{1,2},{2,3},{3,0},{4,5},{5,6},{6,7},{7,4},{8,9},{9,10},{10,1... | collective-permute-start | bytes 589832 | tf_op jit(solution)/shard_map/ppermute | solution.py:400
  13.5 10.8 %collective-permute-start.2 = (bf16[16,4,4,384]{3,2,1,0:T(4,128)(2,1)S(1)}, bf16[16,4,4,384]{3,2,1,0:T(4,128)(2,1)S(1)}, u32[]{:S(2)}, u32[]{:S(2)}) collective-permute-start(bf16[16,4,4,384]{3,2,1,0:T(4,128)(2,1)S(1)} %slice.6), channel_id=1, source_target_pairs={{0,1},{1,2},{2,3},{3,0},{4,5},{5,6},{6,7},{7,4},{8,9},{9,10},{10,1... | collective-permute-start | bytes 589832 | tf_op jit(solution)/shard_map/ppermute | solution.py:400
  13.6 13.4 %collective-permute-start.11 = (bf16[256,384]{1,0:T(8,128)(2,1)S(1)}, bf16[256,384]{1,0:T(8,128)(2,1)S(1)}, u32[]{:S(2)}, u32[]{:S(2)}) collective-permute-start(bf16[256,384]{1,0:T(8,128)(2,1)S(1)} %get-tuple-element.36.earlier.own.mixed), channel_id=1, source_target_pairs={{0,3},{1,0},{2,1},{3,2},{4,7},{5,4},{6,5},{7,6},{8,11},{9,8},{10,9... | collective-permute-start | bytes 589832 | tf_op jit(solution)/shard_map/ppermute | solution.py:400
  20.9 8.2 %collective-permute-start.12 = (bf16[256,384]{1,0:T(8,128)(2,1)S(1)}, bf16[256,384]{1,0:T(8,128)(2,1)S(1)}, u32[]{:S(2)}, u32[]{:S(2)}) collective-permute-start(bf16[256,384]{1,0:T(8,128)(2,1)S(1)} %collective-permute-done.5.left), channel_id=1, source_target_pairs={{0,1},{1,2},{2,3},{3,0},{4,5},{5,6},{6,7},{7,4},{8,9},{9,10},{10,1... | collective-permute-start | bytes 589832 | tf_op jit(solution)/shard_map/ppermute | solution.py:400
  20.9 14.4 %collective-permute-start.6 = (bf16[256,384]{1,0:T(8,128)(2,1)S(1)}, bf16[256,384]{1,0:T(8,128)(2,1)S(1)}, u32[]{:S(2)}, u32[]{:S(2)}) collective-permute-start(bf16[256,384]{1,0:T(8,128)(2,1)S(1)} %collective-permute-done.4.right), channel_id=1, source_target_pairs={{0,3},{1,0},{2,1},{3,2},{4,7},{5,4},{6,5},{7,6},{8,11},{9,8},{10,9... | collective-permute-start | bytes 589832 | tf_op jit(solution)/shard_map/ppermute | solution.py:400
  24.2 10.5 %collective-permute-start.7 = (bf16[16,4,4,384]{3,2,1,0:T(4,128)(2,1)S(1)}, bf16[16,4,4,384]{3,2,1,0:T(4,128)(2,1)S(1)}, u32[]{:S(2)}, u32[]{:S(2)}) collective-permute-start(bf16[16,4,4,384]{3,2,1,0:T(4,128)(2,1)S(1)} %slice.7), channel_id=1, source_target_pairs={{0,3},{1,0},{2,1},{3,2},{4,7},{5,4},{6,5},{7,6},{8,11},{9,8},{10,9... | collective-permute-start | bytes 589832 | tf_op jit(solution)/shard_map/ppermute | solution.py:400
  25.0 10.4 %collective-permute-start.3 = (bf16[256,384]{1,0:T(8,128)(2,1)S(1)}, bf16[256,384]{1,0:T(8,128)(2,1)S(1)}, u32[]{:S(2)}, u32[]{:S(2)}) collective-permute-start(bf16[256,384]{1,0:T(8,128)(2,1)S(1)} %get-tuple-element.40.own.mixed), channel_id=1, source_target_pairs={{0,1},{1,2},{2,3},{3,0},{4,5},{5,6},{6,7},{7,4},{8,9},{9,10},{10,1... | collective-permute-start | bytes 589832 | tf_op jit(solution)/shard_map/ppermute | solution.py:400
  32.6 7.9 %collective-permute-start.13 = (bf16[272,384]{1,0:T(8,128)(2,1)S(1)}, bf16[272,384]{1,0:T(8,128)(2,1)S(1)}, u32[]{:S(2)}, u32[]{:S(2)}) collective-permute-start(bf16[272,384]{1,0:T(8,128)(2,1)S(1)} %get-tuple-element.58), channel_id=1, source_target_pairs={{0,3},{1,0},{2,1},{3,2},{4,7},{5,4},{6,5},{7,6},{8,11},{9,8},{10,9... | collective-permute-start | bytes 626696 | tf_op jit(solution)/shard_map/ppermute | solution.py:400
  33.3 8.2 %collective-permute-start.14 = (bf16[272,384]{1,0:T(8,128)(2,1)S(1)}, bf16[272,384]{1,0:T(8,128)(2,1)S(1)}, u32[]{:S(2)}, u32[]{:S(2)}) collective-permute-start(bf16[272,384]{1,0:T(8,128)(2,1)S(1)} %get-tuple-element.60.away), channel_id=1, source_target_pairs={{0,1},{1,2},{2,3},{3,0},{4,5},{5,6},{6,7},{7,4},{8,9},{9,10},{10,1... | collective-permute-start | bytes 626696 | tf_op jit(solution)/shard_map/ppermute | solution.py:400
  38.5 7.1 %collective-permute-start.9 = (bf16[272,384]{1,0:T(8,128)(2,1)S(1)}, bf16[272,384]{1,0:T(8,128)(2,1)S(1)}, u32[]{:S(2)}, u32[]{:S(2)}) collective-permute-start(bf16[272,384]{1,0:T(8,128)(2,1)S(1)} %get-tuple-element.48.away), channel_id=1, source_target_pairs={{0,3},{1,0},{2,1},{3,2},{4,7},{5,4},{6,5},{7,6},{8,11},{9,8},{10,9... | collective-permute-start | bytes 626696 | tf_op jit(solution)/shard_map/ppermute | solution.py:400
  41.5 7.3 %collective-permute-start.15 = (bf16[272,384]{1,0:T(8,128)(2,1)S(1)}, bf16[272,384]{1,0:T(8,128)(2,1)S(1)}, u32[]{:S(2)}, u32[]{:S(2)}) collective-permute-start(bf16[272,384]{1,0:T(8,128)(2,1)S(1)} %shard_map.137), channel_id=1, source_target_pairs={{0,1},{1,2},{2,3},{3,0},{4,5},{5,6},{6,7},{7,4},{8,9},{9,10},{10,1... | collective-permute-start | bytes 626696 | tf_op jit(solution)/shard_map/ppermute | solution.py:400
  43.2 8.5 %collective-permute-start.8 = (bf16[272,384]{1,0:T(8,128)(2,1)S(1)}, bf16[272,384]{1,0:T(8,128)(2,1)S(1)}, u32[]{:S(2)}, u32[]{:S(2)}) collective-permute-start(bf16[272,384]{1,0:T(8,128)(2,1)S(1)} %get-tuple-element.50), channel_id=1, source_target_pairs={{0,1},{1,2},{2,3},{3,0},{4,5},{5,6},{6,7},{7,4},{8,9},{9,10},{10,1... | collective-permute-start | bytes 626696 | tf_op jit(solution)/shard_map/ppermute | solution.py:400
  45.7 6.4 %collective-permute-start.10 = (bf16[272,384]{1,0:T(8,128)(2,1)S(1)}, bf16[272,384]{1,0:T(8,128)(2,1)S(1)}, u32[]{:S(2)}, u32[]{:S(2)}) collective-permute-start(bf16[272,384]{1,0:T(8,128)(2,1)S(1)} %shard_map.134), channel_id=1, source_target_pairs={{0,3},{1,0},{2,1},{3,2},{4,7},{5,4},{6,5},{7,6},{8,11},{9,8},{10,9... | collective-permute-start | bytes 626696 | tf_op jit(solution)/shard_map/ppermute | solution.py:400
